TPU v7x, 32 devices: a whole 2x2x4 slice. The times are simulated.
32 devices in a mesh: dp: 4 (over y, x), tensor: 8 (over z, core).
Axes of the slice: x: 2, y: 2, z: 4, core: 2. Of those that a mesh axis runs over, the one named last changes fastest.
Arguments:
- tokens: bfloat16 [4096, 1280], P(('dp', 'tensor'))
- cotangent: bfloat16 [4096, 1280], P(('dp', 'tensor')), may hold values from -6 to 6
- gate_weights: float32 [4096, 2], P(('dp', 'tensor')), may hold values from 0.2 to 1
- routes: int32 [4096, 2], P(('dp', 'tensor')), may hold values from 0 to 7, as said below
- slot_index: int32 [4096, 2], P(('dp', 'tensor')), may hold values from -1 to 1, as said below
- qkv_weight: bfloat16 [1280, 16, 240], P(None, 'tensor'), may hold values from -0.15625 to 0.15625
- proj_weight: bfloat16 [16, 80, 1280], P('tensor'), may hold values from -1.25 to 1.25
- up_weight: bfloat16 [8, 1280, 5120], P('dp', None, 'tensor'), may hold values from -0.15625 to 0.15625
- down_weight: bfloat16 [8, 5120, 1280], P('dp', 'tensor'), may hold values from -0.078125 to 0.078125
Outputs:
- layer_out: bfloat16 [4096, 1280], P(('dp', 'tensor'))
- gate_grad: float32 [4096, 2], P(('dp', 'tensor'))
- grad_qkv: float32 [1280, 16, 240], P('dp', 'tensor')
- grad_proj: float32 [16, 80, 1280], P('tensor', None, 'dp')
- grad_up: bfloat16 [8, 1280, 5120], P('dp', None, 'tensor')
- grad_down: bfloat16 [8, 5120, 1280], P('dp', 'tensor')
Inputs may be any that keep to these rules, and one draw needn't show every extreme that they name: `routes`: the two experts of a row differ. `slot_index`: -1 marks a dropped pair; within the rows of one device (aligned blocks of 128 rows) and one expert, the kept pairs hold the slots 0, 1, 2, ... without gaps, each at most once.
All inputs are finite; a program needn't handle non-finite values.
Results may differ from a plain program's by a relative error of at most 0.035.
Values may be sent and summed in bfloat16 or wider, within the bound.
No kernel may reach another device: no remote copies, remote signals or barrier semaphores. Data moves between devices by JAX's collectives and lax.ppermute only.
A program may use at most 128 MiB of HBM per device.

v0:
```python
from functools import partial
import math

import jax
import jax.numpy as jnp
from jax import lax
from jax.sharding import PartitionSpec as P

CAP = 2


epsilon = 1e-06
half_root = 1.0 / math.sqrt(2.0)
bell_scale = 1.0 / math.sqrt(2.0 * math.pi)


def norm_parts(row_block):
    widened = row_block.astype(jnp.float32)
    center = widened - jnp.mean(widened, axis=-1, keepdims=True)
    factor = lax.rsqrt(jnp.mean(center * center, axis=-1, keepdims=True) + epsilon)
    return (center * factor, factor)


def norm_back(normal_rows, factor, upstream):
    mean_up = jnp.mean(upstream, axis=-1, keepdims=True)
    mean_mix = jnp.mean(upstream * normal_rows, axis=-1, keepdims=True)
    return factor * (upstream - mean_up - normal_rows * mean_mix)


def gelu_value(pre_act):
    return 0.5 * pre_act * (1.0 + lax.erf(pre_act * half_root))


def gelu_slope(pre_act):
    return (
        0.5 * (1.0 + lax.erf(pre_act * half_root))
        + pre_act * jnp.exp(-0.5 * pre_act * pre_act) * bell_scale
    )


def block_shares(query_block, key_rows, score_scale):
    scores = (
        jnp.einsum("qk,tk->qt", query_block, key_rows, preferred_element_type=jnp.float32)
        * score_scale
    )
    raised = jnp.exp(scores)
    return raised / jnp.sum(raised, axis=-1, keepdims=True)


def attend_head(queries, key_rows, value_rows, block_rows, score_scale):
    block_count = queries.shape[0] // block_rows

    def attend_one_block(query_block):
        shares = block_shares(query_block, key_rows, score_scale)
        context = jnp.dot(
            shares.astype(jnp.bfloat16), value_rows, preferred_element_type=jnp.float32
        )
        return context.astype(jnp.bfloat16)

    outputs = lax.map(attend_one_block, queries.reshape(block_count, block_rows, queries.shape[1]))
    return outputs.reshape(queries.shape)


def head_backward(queries, key_rows, value_rows, grad_context, block_rows, score_scale):
    block_count = queries.shape[0] // block_rows

    def head_one_block(carry, pieces):
        grad_keys, grad_values = carry
        query_block, grad_block = pieces
        shares = block_shares(query_block, key_rows, score_scale)
        grad_shares = jnp.einsum(
            "qk,tk->qt", grad_block, value_rows, preferred_element_type=jnp.float32
        )
        grad_scores = (
            shares
            * (grad_shares - jnp.sum(shares * grad_shares, axis=-1, keepdims=True))
            * score_scale
        ).astype(jnp.bfloat16)
        grad_query = jnp.dot(grad_scores, key_rows, preferred_element_type=jnp.float32).astype(
            jnp.bfloat16
        )
        grad_keys = grad_keys + jnp.einsum(
            "qt,qk->tk", grad_scores, query_block, preferred_element_type=jnp.float32
        )
        grad_values = grad_values + jnp.einsum(
            "qt,qk->tk", shares.astype(jnp.bfloat16), grad_block, preferred_element_type=jnp.float32
        )
        return ((grad_keys, grad_values), grad_query)

    zeros_rows = jnp.zeros(key_rows.shape, jnp.float32)
    shaped = (
        queries.reshape(block_count, block_rows, queries.shape[1]),
        grad_context.reshape(block_count, block_rows, queries.shape[1]),
    )
    (grad_keys, grad_values), grad_queries = lax.scan(
        head_one_block, (zeros_rows, zeros_rows), shaped
    )
    return (
        grad_queries.reshape(queries.shape),
        grad_keys.astype(jnp.bfloat16),
        grad_values.astype(jnp.bfloat16),
    )


def return_slots(expert_partial):
    summed = lax.psum_scatter(
        expert_partial.astype(jnp.bfloat16), "tensor", scatter_dimension=0, tiled=True
    ).astype(jnp.float32)
    returned = lax.all_to_all(
        summed[0].astype(jnp.bfloat16), "dp", split_axis=0, concat_axis=0, tiled=True
    )
    return returned.reshape(
        returned.shape[0] * returned.shape[1] * returned.shape[2], returned.shape[3]
    )


def shards(
    tokens,
    cotangent,
    gate_weights,
    routes,
    slot_index,
    qkv_weight,
    proj_weight,
    up_weight,
    down_weight,
):
    rows_dev, model_width = tokens.shape
    head_size = qkv_weight.shape[2] // 3
    score_scale = head_size ** (-0.5)
    group_count = lax.axis_size("dp")
    local_experts = up_weight.shape[0]
    places = group_count * local_experts * CAP
    normal_in, factor_in = norm_parts(tokens)
    normed = normal_in.astype(jnp.bfloat16)
    full_norm = lax.all_gather(normed, "tensor", axis=0, tiled=True)
    seq_len = full_norm.shape[0]
    block_rows = min(512, seq_len)
    qkv_rows = jnp.einsum(
        "sd,dhc->hsc", full_norm, qkv_weight, preferred_element_type=jnp.float32
    ).astype(jnp.bfloat16)
    queries = qkv_rows[:, :, :head_size]
    key_rows = qkv_rows[:, :, head_size : 2 * head_size]
    value_rows = qkv_rows[:, :, 2 * head_size :]
    context = jax.vmap(partial(attend_head, block_rows=block_rows, score_scale=score_scale))(
        queries, key_rows, value_rows
    )
    attention = lax.psum_scatter(
        jnp.einsum("hsk,hkd->sd", context, proj_weight, preferred_element_type=jnp.float32).astype(
            jnp.bfloat16
        ),
        "tensor",
        scatter_dimension=0,
        tiled=True,
    ).astype(jnp.float32)
    mid = (tokens.astype(jnp.float32) + attention).astype(jnp.bfloat16)
    normal_mid, factor_mid = norm_parts(mid)
    mid_normed = normal_mid.astype(jnp.bfloat16)
    slot_code = jnp.where(slot_index >= 0, routes * CAP + slot_index, -1)
    positions = jnp.arange(places, dtype=jnp.int32)
    pick_both = (slot_code[None, :, :] == positions[:, None, None]).astype(jnp.bfloat16)
    pick_first = pick_both[:, :, 0]
    pick_second = pick_both[:, :, 1]
    dispatch_rows = pick_first + pick_second
    outgoing = jnp.dot(dispatch_rows, mid_normed, preferred_element_type=jnp.float32).astype(
        jnp.bfloat16
    )
    outgoing = outgoing.reshape(group_count, local_experts, CAP, model_width)
    landed = lax.all_to_all(outgoing, "dp", split_axis=0, concat_axis=0, tiled=True)
    arrived = lax.all_gather(landed[None], "tensor", axis=0, tiled=True)
    pre_act = jnp.einsum("tsecd,edf->tsecf", arrived, up_weight, preferred_element_type=jnp.float32)
    hidden = gelu_value(pre_act).astype(jnp.bfloat16)
    expert_partial = jnp.einsum(
        "tsecf,efd->tsecd", hidden, down_weight, preferred_element_type=jnp.float32
    )
    returned = return_slots(expert_partial)
    expert_first = jnp.einsum("pr,pd->rd", pick_first, returned, preferred_element_type=jnp.float32)
    expert_second = jnp.einsum(
        "pr,pd->rd", pick_second, returned, preferred_element_type=jnp.float32
    )
    mixed_rows = gate_weights[:, 0:1] * expert_first + gate_weights[:, 1:2] * expert_second
    layer_out = (mid.astype(jnp.float32) + mixed_rows).astype(jnp.bfloat16)
    upstream = cotangent.astype(jnp.float32)
    gate_grad = jnp.stack(
        [jnp.sum(upstream * expert_first, axis=-1), jnp.sum(upstream * expert_second, axis=-1)],
        axis=1,
    )
    grad_first = (gate_weights[:, 0:1] * upstream).astype(jnp.bfloat16)
    grad_second = (gate_weights[:, 1:2] * upstream).astype(jnp.bfloat16)
    grad_outgoing = jnp.dot(pick_first, grad_first, preferred_element_type=jnp.float32) + jnp.dot(
        pick_second, grad_second, preferred_element_type=jnp.float32
    )
    grad_outgoing = grad_outgoing.astype(jnp.bfloat16).reshape(
        group_count, local_experts, CAP, model_width
    )
    grad_landed = lax.all_to_all(grad_outgoing, "dp", split_axis=0, concat_axis=0, tiled=True)
    grad_arrived = lax.all_gather(grad_landed[None], "tensor", axis=0, tiled=True)
    grad_hidden = jnp.einsum(
        "tsecd,efd->tsecf", grad_arrived, down_weight, preferred_element_type=jnp.float32
    )
    grad_pre = (grad_hidden * gelu_slope(pre_act)).astype(jnp.bfloat16)
    grad_down = jnp.einsum(
        "tsecf,tsecd->efd", hidden, grad_arrived, preferred_element_type=jnp.float32
    ).astype(jnp.bfloat16)
    grad_up = jnp.einsum(
        "tsecd,tsecf->edf", arrived, grad_pre, preferred_element_type=jnp.float32
    ).astype(jnp.bfloat16)
    grad_partial = jnp.einsum(
        "tsecf,edf->tsecd", grad_pre, up_weight, preferred_element_type=jnp.float32
    )
    grad_back = return_slots(grad_partial)
    grad_norm = jnp.einsum(
        "pr,pd->rd", dispatch_rows, grad_back, preferred_element_type=jnp.float32
    )
    grad_mid = (upstream + norm_back(normal_mid, factor_mid, grad_norm)).astype(jnp.bfloat16)
    full_grad = lax.all_gather(grad_mid, "tensor", axis=0, tiled=True)
    grad_context = jnp.einsum(
        "sd,hkd->hsk", full_grad, proj_weight, preferred_element_type=jnp.float32
    ).astype(jnp.bfloat16)
    grad_proj = jnp.einsum("hsk,sd->hkd", context, full_grad, preferred_element_type=jnp.float32)
    grad_queries, grad_keys, grad_values = jax.vmap(
        partial(head_backward, block_rows=block_rows, score_scale=score_scale)
    )(queries, key_rows, value_rows, grad_context)
    grad_rows = jnp.concatenate([grad_queries, grad_keys, grad_values], axis=-1)
    grad_qkv = jnp.einsum("sd,hsc->dhc", full_norm, grad_rows, preferred_element_type=jnp.float32)
    grad_qkv, grad_proj = (
        lax.psum_scatter(
            grad_qkv.astype(jnp.bfloat16), "dp", scatter_dimension=0, tiled=True
        ).astype(jnp.float32),
        lax.psum_scatter(
            grad_proj.astype(jnp.bfloat16), "dp", scatter_dimension=2, tiled=True
        ).astype(jnp.float32),
    )
    return (layer_out, gate_grad, grad_qkv, grad_proj, grad_up, grad_down)


def solution(mesh):
    return jax.shard_map(
        shards,
        mesh=mesh,
        in_specs=(
            P(("dp", "tensor"), None),
            P(("dp", "tensor"), None),
            P(("dp", "tensor"), None),
            P(("dp", "tensor"), None),
            P(("dp", "tensor"), None),
            P(None, "tensor", None),
            P("tensor", None, None),
            P("dp", None, "tensor"),
            P("dp", "tensor", None),
        ),
        out_specs=(
            P(("dp", "tensor"), None),
            P(("dp", "tensor"), None),
            P("dp", "tensor", None),
            P("tensor", None, "dp"),
            P("dp", None, "tensor"),
            P("dp", "tensor", None),
        ),
        check_vma=False,
    )
```

profile of v0, /device:TPU:0, one launch (start us, length us, event | category | flops | bytes accessed | tf_op | source)
XLA Modules:
  0.0 381.7 jit_solution(2948682413308738826)
XLA Ops:
  11.7 36.7 %all-gather.5.cloned.1.call-done = bf16[1024,1280]{1,0:T(8,128)(2,1)} async-done(((bf16[128,1280]{1,0:T(8,128)(2,1)}), bf16[1024,1280]{1,0:T(8,128)(2,1)}) %all-gather.5.cloned.1.call-update) | async-done | bytes 2621456 | tf_op jit(solution)/shard_map/all_gather | solution.py:136
  48.4 3.5 fusion.162
  54.6 7.5 %while.25 = (s32[]{:T(128)}, bf16[2,2,512,80]{2,3,1,0:T(8,128)(2,1)}, bf16[2,2,512,80]{2,3,1,0:T(8,128)(2,1)}, bf16[2,1024,80]{1,2,0:T(8,128)(2,1)}, bf16[2,1024,80]{1,2,0:T(8,128)(2,1)}, /*index=5*/s32[]{:T(128)}) while((s32[]{:T(128)}, bf16[2,2,512,80]{2,3,1,0:T(8,128)(2,1)}, bf16[2,2,512,80]{2,3,1,0:T(8,128)(2,1)}, ...), condition=%wide.region_4.5_spmd, body=%wide.region_2.4_spmd.sunk | while | flops 340868096 | bytes 13312169 | solution.py:60
  63.8 3.4 bitcast_convert_fusion.2
  70.4 3.6 all-to-all-start.2
  74.1 29.8 %reduce-scatter.6.cloned.1.call-done = bf16[128,1280]{1,0:T(8,128)(2,1)} async-done(((bf16[1024,1280]{1,0:T(8,128)(2,1)}), bf16[128,1280]{1,0:T(8,128)(2,1)}) %reduce-scatter.6.cloned.1.call-update) | async-done | bytes 327696 | tf_op jit(solution)/shard_map/reduce_scatter | solution.py:148
  106.8 3.5 all-to-all-start
  110.3 15.4 %all-gather.1 = bf16[32,2,2,1280]{3,2,1,0:T(2,128)(2,1)} all-gather(bf16[4,2,2,1280]{3,2,1,0:T(2,128)(2,1)S(1)} %all-to-all-done.2), channel_id=3, replica_groups=mesh['dp'=4,'tensor'=8] {'tensor'}, dimensions={0}, use_global_device_ids=true | all-gather | bytes 368640 | tf_op jit(solution)/shard_map/all_gather | solution.py:197
  125.7 14.5 %all-gather = bf16[32,2,2,1280]{3,2,1,0:T(2,128)(2,1)S(1)} all-gather(bf16[4,2,2,1280]{3,2,1,0:T(2,128)(2,1)S(1)} %all-to-all-done), channel_id=2, replica_groups=mesh['dp'=4,'tensor'=8] {'tensor'}, dimensions={0}, use_global_device_ids=true | all-gather | bytes 368640 | tf_op jit(solution)/shard_map/all_gather | solution.py:170
  146.9 55.5 %all-reduce.5.cloned.1.call-done = (bf16[8,4,2,2,1280]{4,1,3,2,0:T(4,128)(2,1)}, bf16[8,4,2,2,1280]{4,1,3,2,0:T(4,128)(2,1)}) async-done(((bf16[8,4,2,2,1280]{4,1,3,2,0:T(4,128)(2,1)}, bf16[8,4,2,2,1280]{4,1,3,2,0:T(4,128)(2,1)}), (bf16[8,4,2,2,1280]{4,1,3,2,0:T(4,128)(2,1)}, bf16[8,4,2,2,1280]{4,1,3,2,0:T(4,128)(2,1)})) %all-reduce.5.cloned.1.call-update) | async-done | bytes 655376
  204.6 3.6 all-to-all-start.3
  210.3 2.7 all-to-all-done.3
  213.0 3.3 all-to-all-start.1
  221.3 2.6 fusion.128
  224.2 31.1 %all-gather.7.cloned.1.call-done = bf16[1024,1280]{1,0:T(8,128)(2,1)} async-done(((bf16[128,1280]{1,0:T(8,128)(2,1)}), bf16[1024,1280]{1,0:T(8,128)(2,1)}) %all-gather.7.cloned.1.call-update) | async-done | bytes 2621456 | tf_op jit(solution)/shard_map/all_gather | solution.py:216
  255.3 2.9 fusion.93
  262.5 2.6 reshape.96
  265.9 70.5 %while.26 = (s32[]{:T(128)}, f32[2,1024,80]{1,2,0:T(8,128)}, f32[2,1024,80]{1,2,0:T(8,128)}, bf16[2,2,512,80]{2,3,1,0:T(8,128)(2,1)}, bf16[2,2,512,80]{2,3,1,0:T...) while((s32[]{:T(128)}, f32[2,1024,80]{1,2,0:T(8,128)}, ...), condition=%wide.region_17.18_spmd.clone, body=%wide.region_14.17_spmd.clone.sunk | while | flops 863718400 | bytes 53207232 | solution.py:95
  265.9 3.8 fusion.210
  269.7 2.8 fusion.211
  272.6 12.1 %fusion.214 = bf16[2,2,512,80]{2,3,1,0:T(8,128)(2,1)} fusion(bf16[2,2,512,80]{2,3,1,0:T(8,128)(2,1)} %get-tuple-element.297, s32[]{:T(128)S(6)} %copy.103, bf16[2,1024,80]{1,2,0:T(8,128)(2,1)} %get-tuple-element.309, f32[2,512,1024]{2,1,0:T(8,128)} %fusion.210, f32[2,512,1024]{2,1,0:T(8,128)} %get-tuple-element.264, f32[2,512]{1,0:T(2,128)S(1)} %get-tuple-element.265), kind=kOutput, calls=%fused_computation.29.clone.1 | convolution fusion | flops 177293312 | bytes 17276932 | tf_op jit(solution)/shard_map/vmap()/while/body/eval_jaxpr/dot_general | solution.py:79
  284.7 12.5 %fusion.212 = f32[2,1024,80]{1,2,0:T(8,128)} fusion(f32[2,512,1024]{2,1,0:T(8,128)} %fusion.210, f32[2,1024,80]{1,2,0:T(8,128)} %get-tuple-element.295, pred[]{:T(512)S(6)} %compare.3, bf16[2,2,512,80]{2,3,1,0:T(8,128)(2,1)} %get-tuple-element.308, s32[]{:T(128)S(6)} %copy.103, f32[2,512,1024]{2,1,0:T(8,128)} %get-tuple-element.264, ...), kind=kOutput, calls=%fused_computation.26.clone.1 | convolution fusion | flops 177539072 | bytes 18259972 | tf_op jit(solution)/shard_map/vmap()/while/body/eval_jaxpr/qt,qk->tk/dot_general | solution.py:82
  297.1 4.0 %fusion.213 = f32[2,1024,80]{1,2,0:T(8,128)} fusion(f32[2,1024,80]{1,2,0:T(8,128)} %get-tuple-element.296, pred[]{:T(512)S(6)} %compare.3, bf16[2,2,512,80]{2,3,1,0:T(8,128)(2,1)} %get-tuple-element.310, s32[]{:T(128)S(6)} %copy.103, f32[2,512,1024]{2,1,0:T(8,128)} %get-tuple-element.264, f32[2,512]{1,0:T(2,128)S(1)} %get-tuple-element.265), kind=kOutput, calls=%fused_computation.25.clone.1 | convolution fusion | flops 171245568 | bytes 5672965 | tf_op jit(solution)/shard_map/vmap()/while/body/eval_jaxpr/qt,qk->tk/dot_general | solution.py:85
  301.2 3.8 fusion.210
  305.0 2.8 fusion.211
  307.8 11.9 %fusion.214 = bf16[2,2,512,80]{2,3,1,0:T(8,128)(2,1)} fusion(bf16[2,2,512,80]{2,3,1,0:T(8,128)(2,1)} %get-tuple-element.297, s32[]{:T(128)S(6)} %copy.103, bf16[2,1024,80]{1,2,0:T(8,128)(2,1)} %get-tuple-element.309, f32[2,512,1024]{2,1,0:T(8,128)} %fusion.210, f32[2,512,1024]{2,1,0:T(8,128)} %get-tuple-element.264, f32[2,512]{1,0:T(2,128)S(1)} %get-tuple-element.265), kind=kOutput, calls=%fused_computation.29.clone.1 | convolution fusion | flops 177293312 | bytes 17276932 | tf_op jit(solution)/shard_map/vmap()/while/body/eval_jaxpr/dot_general | solution.py:79
  319.7 12.5 %fusion.212 = f32[2,1024,80]{1,2,0:T(8,128)} fusion(f32[2,512,1024]{2,1,0:T(8,128)} %fusion.210, f32[2,1024,80]{1,2,0:T(8,128)} %get-tuple-element.295, pred[]{:T(512)S(6)} %compare.3, bf16[2,2,512,80]{2,3,1,0:T(8,128)(2,1)} %get-tuple-element.308, s32[]{:T(128)S(6)} %copy.103, f32[2,512,1024]{2,1,0:T(8,128)} %get-tuple-element.264, ...), kind=kOutput, calls=%fused_computation.26.clone.1 | convolution fusion | flops 177539072 | bytes 18259972 | tf_op jit(solution)/shard_map/vmap()/while/body/eval_jaxpr/qt,qk->tk/dot_general | solution.py:82
  332.2 4.2 %fusion.213 = f32[2,1024,80]{1,2,0:T(8,128)} fusion(f32[2,1024,80]{1,2,0:T(8,128)} %get-tuple-element.296, pred[]{:T(512)S(6)} %compare.3, bf16[2,2,512,80]{2,3,1,0:T(8,128)(2,1)} %get-tuple-element.310, s32[]{:T(128)S(6)} %copy.103, f32[2,512,1024]{2,1,0:T(8,128)} %get-tuple-element.264, f32[2,512]{1,0:T(2,128)S(1)} %get-tuple-element.265), kind=kOutput, calls=%fused_computation.25.clone.1 | convolution fusion | flops 171245568 | bytes 5672965 | tf_op jit(solution)/shard_map/vmap()/while/body/eval_jaxpr/qt,qk->tk/dot_general | solution.py:85
  339.7 4.4 %convolution_convert_fusion = bf16[1280,2,240]{2,0,1:T(8,128)(2,1)} fusion(bf16[1024,1280]{1,0:T(8,128)(2,1)} %all-gather.5.cloned.1.call-done, bf16[2,1024,80]{1,2,0:T(8,128)(2,1)S(1)} %convert_element_type.154, bf16[2,1024,80]{1,2,0:T(8,128)(2,1)S(1)} %convert_element_type.153, bf16[2,1024,80]{1,2,0:T(8,128)(2,1)S(1)} %bitcast.203), kind=kOutput, calls=%fused_computation.59 | convolution fusion | flops 1261854720 | bytes 4833280 | tf_op jit(solution)/shard_map/sd,hsc->dhc/dot_general | solution.py:225
  344.1 3.9 %bitcast_convert_fusion = bf16[2,640,1280]{2,1,0:T(8,128)(2,1)} fusion(bf16[8,4,2,2,1280]{4,3,2,1,0:T(2,128)(2,1)} %bitcast.199, bf16[8,4,2,2,640]{4,0,3,1,2:T(8,128)(2,1)} %copy-done.20), kind=kOutput, calls=%fused_computation.48 | convolution fusion | flops 211353600 | bytes 3768320 | tf_op jit(solution)/shard_map/tsecf,tsecd->efd/dot_general | solution.py:202
  348.0 2.8 bitcast_convert_fusion.1
  354.8 17.9 %reduce-scatter.8.cloned.1.call-done = bf16[320,2,240]{2,0,1:T(8,128)(2,1)} async-done(((bf16[1280,2,240]{2,0,1:T(8,128)(2,1)}), bf16[320,2,240]{2,0,1:T(8,128)(2,1)}) %reduce-scatter.8.cloned.1.call-update) | async-done | bytes 307216 | tf_op jit(solution)/shard_map/reduce_scatter | solution.py:227
  (124 shorter events, 53.0 us)
Async XLA Ops:
  7.2 133.7 %copy-start = (bf16[2,1280,640]{2,1,0:T(8,128)(2,1)S(1)}, bf16[2,1280,640]{2,1,0:T(8,128)(2,1)}, u32[]{:S(2)}) copy-start(bf16[2,1280,640]{2,1,0:T(8,128)(2,1)} %param.20) | copy-start | bytes 9830404
  7.2 41.2 %all-gather.5.cloned.1.call-start = ((), (), s32[]{:S(2)}) async-start(), calls=%async_computation.7 | async-start | bytes 2949120 | tf_op jit(solution)/shard_map/all_gather | solution.py:136
  11.6 92.2 %reduce-scatter.6.cloned.1.call-start = ((), (), s32[]{:S(2)}) async-start(), calls=%async_computation.8 | async-start | bytes 2949120 | tf_op jit(solution)/shard_map/reduce_scatter | solution.py:148
  54.6 2.1 copy-start.3
  54.6 2.1 copy-start.8
  57.6 0.7 copy-start.9
  58.3 2.0 copy-start.3
  58.3 2.1 copy-start.8
  62.1 5.2 %copy-start.15 = (f32[128,2]{0,1:T(2,128)S(1)}, f32[128,2]{0,1:T(2,128)}, u32[]{:S(2)}) copy-start(f32[128,2]{0,1:T(2,128)} %param.15) | copy-start | bytes 3076
  62.1 5.2 %copy-start.13 = (s32[128,2]{0,1:T(2,128)S(1)}, s32[128,2]{0,1:T(2,128)}, u32[]{:S(2)}) copy-start(s32[128,2]{0,1:T(2,128)} %param.17) | copy-start | bytes 3076
  62.1 5.2 %copy-start.14 = (s32[128,2]{0,1:T(2,128)S(1)}, s32[128,2]{0,1:T(2,128)}, u32[]{:S(2)}) copy-start(s32[128,2]{0,1:T(2,128)} %param.16) | copy-start | bytes 3076
  70.4 36.4 %all-to-all-start.2 = ((bf16[4,2,2,1280]{3,2,1,0:T(2,128)(2,1)}), bf16[4,2,2,1280]{3,2,1,0:T(2,128)(2,1)S(1)}, u32[]{:S(2)}, u32[]{:S(2)}) async-start(bf16[4,2,2,1280]{3,2,1,0:T(2,128)(2,1)} %reshape.81), calls=%async_computation.3 | async-start | bytes 81920 | tf_op jit(solution)/shard_map/all_to_all | solution.py:196
  106.8 18.9 %all-to-all-start = ((bf16[4,2,2,1280]{3,2,1,0:T(2,128)(2,1)}), bf16[4,2,2,1280]{3,2,1,0:T(2,128)(2,1)S(1)}, u32[]{:S(2)}, u32[]{:S(2)}) async-start(bf16[4,2,2,1280]{3,2,1,0:T(2,128)(2,1)} %reshape.79), calls=%async_computation.1 | async-start | bytes 81920 | tf_op jit(solution)/shard_map/all_to_all | solution.py:169
  110.3 92.2 %all-reduce.5.cloned.1.call-start = ((), (), s32[]{:S(2)}) async-start(), calls=%async_computation.12 | async-start | bytes 1310720
  125.7 15.9 %copy-start.10 = (bf16[32,2,2,1280]{3,2,1,0:T(2,128)(2,1)S(1)}, bf16[32,2,2,1280]{3,2,1,0:T(2,128)(2,1)}, u32[]{:S(2)}) copy-start(bf16[32,2,2,1280]{3,2,1,0:T(2,128)(2,1)} %all-gather.1) | copy-start | bytes 983044
  125.7 15.9 %copy-start.16 = (bf16[2,640,1280]{2,1,0:T(8,128)(2,1)S(1)}, bf16[2,640,1280]{2,1,0:T(8,128)(2,1)}, u32[]{:S(2)}) copy-start(bf16[2,640,1280]{2,1,0:T(8,128)(2,1)} %param.21) | copy-start | bytes 9830404
  141.6 3.2 copy-start.20
  142.7 2.8 copy-start.18
  143.8 2.5 copy-start.17
  204.6 8.4 %all-to-all-start.3 = ((bf16[4,2,2,1280]{3,2,1,0:T(2,128)(2,1)}), bf16[4,2,2,1280]{3,2,1,0:T(2,128)(2,1)S(1)}, u32[]{:S(2)}, u32[]{:S(2)}) async-start(bf16[4,2,2,1280]{3,2,1,0:T(2,128)(2,1)} %bitcast.163), calls=%async_computation.4 | async-start | bytes 81920 | tf_op jit(solution)/shard_map/all_to_all | solution.py:109
  213.0 8.0 %all-to-all-start.1 = ((bf16[4,2,2,1280]{3,2,1,0:T(2,128)(2,1)}), bf16[4,2,2,1280]{3,2,1,0:T(2,128)(2,1)S(1)}, u32[]{:S(2)}, u32[]{:S(2)}) async-start(bf16[4,2,2,1280]{3,2,1,0:T(2,128)(2,1)} %bitcast.164), calls=%async_computation.2 | async-start | bytes 81920 | tf_op jit(solution)/shard_map/all_to_all | solution.py:109
  216.3 39.1 %all-gather.7.cloned.1.call-start = ((), (), s32[]{:S(2)}) async-start(), calls=%async_computation.9 | async-start | bytes 2949120 | tf_op jit(solution)/shard_map/all_gather | solution.py:216
  224.0 127.4 %reduce-scatter.10.cloned.1.call-start = ((), (), s32[]{:S(2)}) async-start(), calls=%async_computation.11 | async-start | bytes 819200
  255.3 3.7 copy-start.5
  255.3 3.7 copy-start.7
  265.1 107.6 %reduce-scatter.8.cloned.1.call-start = ((), (), s32[]{:S(2)}) async-start(), calls=%async_computation.10 | async-start | bytes 1638400 | tf_op jit(solution)/shard_map/reduce_scatter | solution.py:227
  265.9 3.8 copy-start.1
  265.9 3.8 copy-start.2
  301.2 3.8 copy-start.1
  301.2 3.8 copy-start.2
  344.1 3.9 %copy-start.12 = (bf16[32,2,2,1280]{3,2,1,0:T(2,128)(2,1)S(1)}, bf16[32,2,2,1280]{3,2,1,0:T(2,128)(2,1)}, u32[]{:S(2)}) copy-start(bf16[32,2,2,1280]{3,2,1,0:T(2,128)(2,1)} %copy-done.11) | copy-start | bytes 983044
  344.1 3.9 %copy-start.19 = (bf16[8,4,2,2,640]{4,0,3,1,2:T(8,128)(2,1)S(1)}, bf16[8,4,2,2,640]{4,0,3,1,2:T(8,128)(2,1)}, u32[]{:S(2)}) copy-start(bf16[8,4,2,2,640]{4,0,3,1,2:T(8,128)(2,1)} %copy-done.18) | copy-start | bytes 491524
  (4 other events, 2.9 us)
Sparse Core Ops, SparseCore 0:
  11.8 36.5 all-gather.4
  67.4 36.4 reduce-scatter.5
  146.5 55.9 all-reduce.4
  224.1 31.2 all-gather.6
  265.2 24.4 reduce-scatter.9
  344.2 28.4 reduce-scatter.7
where the time goes:
time: 383 us; the launch traced here: 382 us
  waiting for transfers between devices  176 us (46%)
  matrix products  110 us (29%)
  blocking collectives  29.9 us (8%)
  local copies, waits for them, and re-layouts  26.1 us (7%)
  starting transfers between devices  14.5 us (4%)
  between operations  14.4 us (4%)
  other arithmetic  10.5 us (3%)
    unnamed x8, waiting for transfers between devices  55.6 us
    all_gather x1, waiting for transfers between devices, shards(): full_norm = lax.all_gather(normed, 'tensor', axis=0, tiled=True)  36.7 us
    all_gather x1, waiting for transfers between devices, shards(): full_grad = lax.all_gather(grad_mid, 'tensor', axis=0, tiled=True)  31.1 us
    reduce_scatter x1, waiting for transfers between devices, shards(): lax.psum_scatter(jnp.einsum('hsk,hkd->sd', context, proj_weight, preferre...  29.8 us
    dot_general x2, matrix products, head_one_block(): jnp.einsum('qt,qk->tk', grad_scores, query_block, preferred_element_type=...  25 us
    dot_general x2, matrix products, head_one_block(): jnp.dot(grad_scores, key_rows, preferred_element_type=jnp.float32)  24 us
    reduce_scatter x1, waiting for transfers between devices, shards(): lax.psum_scatter(grad_qkv.astype(jnp.bfloat16), 'dp', scatter_dimension=0...  17.9 us
    all_gather x1, blocking collectives, shards(): lax.all_gather(grad_landed[None], 'tensor', axis=0, tiled=True)  15.4 us
  transfers between devices with their start and end apart: 10, of which 7 were waited for; matrix products, arithmetic and copies ran while one was open for 26% of the time, Pallas kernels for 0%

commit v1 on v0

v1 whole, which is shorter than its diff:
```python
import math

import jax
import jax.numpy as jnp
from jax import lax
from jax.experimental import pallas as pl
from jax.experimental.pallas import tpu as pltpu
from jax.sharding import PartitionSpec as P

CAP = 2
LANES = 128
epsilon = 1e-06
half_root = 1.0 / math.sqrt(2.0)
bell_scale = 1.0 / math.sqrt(2.0 * math.pi)
f32 = jnp.float32
bf16 = jnp.bfloat16


def norm_parts(row_block):
    widened = row_block.astype(f32)
    center = widened - jnp.mean(widened, axis=-1, keepdims=True)
    factor = lax.rsqrt(jnp.mean(center * center, axis=-1, keepdims=True) + epsilon)
    return (center * factor, factor)


def norm_back(normal_rows, factor, upstream):
    mean_up = jnp.mean(upstream, axis=-1, keepdims=True)
    mean_mix = jnp.mean(upstream * normal_rows, axis=-1, keepdims=True)
    return factor * (upstream - mean_up - normal_rows * mean_mix)


def dot(a, b):
    return lax.dot_general(a, b, (((1,), (0,)), ((), ())), preferred_element_type=f32)


def dot_nt(a, b):
    return lax.dot_general(a, b, (((1,), (1,)), ((), ())), preferred_element_type=f32)


def dot_tn(a, b):
    return lax.dot_general(a, b, (((0,), (0,)), ((), ())), preferred_element_type=f32)


def run(body, outs, ins, name, flops=0, mib=48, smem=()):
    specs = [
        pl.BlockSpec(memory_space=pltpu.SMEM if i in smem else pltpu.VMEM) for i in range(len(ins))
    ]
    sizes = [math.prod(x.shape) * x.dtype.itemsize for x in list(ins) + list(outs)]
    return pl.pallas_call(
        body,
        out_shape=list(outs),
        in_specs=specs,
        out_specs=[pl.BlockSpec(memory_space=pltpu.VMEM)] * len(outs),
        compiler_params=pltpu.CompilerParams(vmem_limit_bytes=mib * 2**20),
        cost_estimate=pl.CostEstimate(
            flops=int(flops), bytes_accessed=int(sum(sizes)), transcendentals=0
        ),
        name=name,
    )(*ins)


def shape(dims, dtype=bf16):
    return jax.ShapeDtypeStruct(tuple(dims), dtype)


def block_of(rows, most=256):
    return max(b for b in range(16, most + 1, 16) if rows % b == 0)


def hop(x, axis, mask):
    size = lax.axis_size(axis)
    return lax.ppermute(x, axis, [(i, i ^ mask) for i in range(size)])


def gather_rel(x):
    size = lax.axis_size("tensor")
    even = [x] + [hop(x, "tensor", m) for m in range(2, size, 2)]
    odd = [hop(e, "tensor", 1) for e in even]
    return [y for pair in zip(even, odd) for y in pair]


def prologue_body(group, tok, cot, gate, routes, slots, *outs):
    normed_o, cot_o, tok_o, perm_o, pick0_o, pick1_o, link_o, gout_o = outs
    rows = tok.shape[0]
    places = pick0_o.shape[1]
    code = jnp.where(slots[...] >= 0, (routes[...] ^ group[0]) * CAP + slots[...], -1)
    lane = lax.broadcasted_iota(jnp.int32, (rows, LANES), 1)
    wide0 = (code[:, 0:1] == lane).astype(f32)
    wide1 = (code[:, 1:2] == lane).astype(f32)
    kept0 = (code[:, 0:1] >= 0).astype(f32)
    prim = wide0 + wide1 * (1.0 - kept0)
    plain = 1.0 - jnp.sum(prim, axis=1, keepdims=True)
    open_at = 1.0 - jnp.sum(prim, axis=0, keepdims=True)
    ri = lax.broadcasted_iota(jnp.int32, (rows, rows), 0)
    ci = lax.broadcasted_iota(jnp.int32, (rows, rows), 1)
    row_rank = dot(
        (ci < ri).astype(bf16), jnp.broadcast_to(plain, (rows, rows)).astype(bf16)
    )
    place_rank = dot(
        jnp.broadcast_to(open_at, (rows, rows)).astype(bf16), (ri < ci).astype(bf16)
    )
    filler = plain * open_at * (row_rank == place_rank).astype(f32)
    perm = (prim + filler).astype(bf16)
    perm_o[...] = perm
    normal, _ = norm_parts(tok[...])
    normed_o[...] = dot_tn(perm, normal.astype(bf16)).astype(bf16)
    cot_o[...] = dot_tn(perm, cot[...]).astype(bf16)
    tok_o[...] = dot_tn(perm, tok[...]).astype(bf16)
    pick0 = wide0.astype(bf16)
    pick1 = wide1.astype(bf16)
    pick0_o[...] = pick0[:, :places]
    pick1_o[...] = pick1[:, :places]
    link_o[...] = dot_tn((pick0 + pick1), prim.astype(bf16))[:places, :places].astype(bf16)
    upstream = cot[...].astype(f32)
    g0 = (gate[:, 0:1] * upstream).astype(bf16)
    g1 = (gate[:, 1:2] * upstream).astype(bf16)
    gout_o[...] = (dot_tn(pick0, g0) + dot_tn(pick1, g1))[:places].astype(bf16)


def probs_of(queries, keys, scale):
    raised = jnp.exp(dot_nt(queries, keys) * scale)
    return raised * (1.0 / jnp.sum(raised, axis=-1, keepdims=True))


def part_of(ref, rows, which, head):
    at = (3 * head + which) * LANES
    return ref[rows, at : at + LANES]


def make_front(count, places, heads, scale):
    def body(*refs):
        shards, (wqkv, proj) = refs[:count], refs[count : count + 2]
        fn, qkv, ctx, part = refs[count + 2 :]
        rows = shards[0].shape[0]
        cold = rows - places
        hot_all = count * places
        for k in range(count):
            fn[k * places : (k + 1) * places] = shards[k][:places]
            if cold:
                fn[hot_all + k * cold : hot_all + (k + 1) * cold] = shards[k][places:]
        total = fn.shape[0]
        step = block_of(total)

        def chunk(i, _):
            at = pl.ds(pl.multiple_of(i * step, 16), step)
            qkv[at, :] = dot(fn[at, :], wqkv[...]).astype(bf16)
            return 0

        lax.fori_loop(0, total // step, chunk, 0)
        every = slice(None)
        hot = slice(0, hot_all)
        for h in range(heads):
            shares = probs_of(part_of(qkv, hot, 0, h), part_of(qkv, every, 1, h), scale)
            ctx[:, h * LANES : (h + 1) * LANES] = dot(
                shares.astype(bf16), part_of(qkv, every, 2, h)
            ).astype(bf16)
        part[...] = dot(ctx[...], proj[...]).astype(bf16)

    return body


def make_cold(hot_all, heads, scale):
    def body(qkv, proj, ctx, part):
        total = ctx.shape[0]
        step = block_of(total)
        every = slice(None)

        def chunk(i, _):
            at = pl.ds(pl.multiple_of(i * step, 16), step)
            src = pl.ds(pl.multiple_of(hot_all + i * step, 16), step)
            for h in range(heads):
                shares = probs_of(part_of(qkv, src, 0, h), part_of(qkv, every, 1, h), scale)
                ctx[at, h * LANES : (h + 1) * LANES] = dot(
                    shares.astype(bf16), part_of(qkv, every, 2, h)
                ).astype(bf16)
            part[at, :] = dot(ctx[at, :], proj[...]).astype(bf16)
            return 0

        lax.fori_loop(0, total // step, chunk, 0)

    return body


def back_block(qkv, src, grad_ctx, head, scale):
    every = slice(None)
    queries = part_of(qkv, src, 0, head)
    keys = part_of(qkv, every, 1, head)
    shares = probs_of(queries, keys, scale)
    grad_shares = dot_nt(grad_ctx, part_of(qkv, every, 2, head))
    mix = jnp.sum(shares * grad_shares, axis=-1, keepdims=True)
    grad_scores = (shares * (grad_shares - mix) * scale).astype(bf16)
    return (
        dot(grad_scores, keys),
        dot_tn(queries, grad_scores),
        dot_tn(grad_ctx, shares.astype(bf16)),
    )


def make_cold_back(count, places, heads, scale):
    def body(*refs):
        shards, (qkv, proj, ctx) = refs[:count], refs[count : count + 3]
        gq, gk, gv, gp, cots = refs[count + 3 :]
        cold = shards[0].shape[0]
        hot_all = count * places
        for k in range(count):
            cots[k * cold : (k + 1) * cold] = shards[k][...]
        total = cots.shape[0]
        step = block_of(total)
        gk[...] = jnp.zeros_like(gk)
        gv[...] = jnp.zeros_like(gv)
        gp[...] = jnp.zeros_like(gp)

        def chunk(i, _):
            at = pl.ds(pl.multiple_of(i * step, 16), step)
            src = pl.ds(pl.multiple_of(hot_all + i * step, 16), step)
            grad_ctx = dot_nt(cots[at, :], proj[...]).astype(bf16)
            gp[...] += dot_tn(ctx[at, :], cots[at, :])
            for h in range(heads):
                cut = slice(h * LANES, (h + 1) * LANES)
                a, b, c = back_block(qkv, src, grad_ctx[:, cut], h, scale)
                gq[at, cut] = a.astype(bf16)
                gk[cut, :] += b
                gv[cut, :] += c
            return 0

        lax.fori_loop(0, total // step, chunk, 0)

    return body


def make_hot_back(count, heads, size, groups, scale):
    def body(*refs):
        shards = refs[:count]
        qkv, proj, ctx, gq, gk, gv, gp, fn, out, rows_t = refs[count:]
        grads = jnp.concatenate([s[...] for s in shards], axis=0)
        hot_all = grads.shape[0]
        grad_ctx = dot_nt(grads, proj[...]).astype(bf16)
        proj_grad = gp[...] + dot_tn(ctx[...], grads)
        width = fn.shape[1] // groups
        base = heads * 3 * size
        for h in range(heads):
            cut = slice(h * LANES, (h + 1) * LANES)
            a, b, c = back_block(qkv, slice(0, hot_all), grad_ctx[:, cut], h, scale)
            at = h * 3 * size
            rows_t[at : at + size, :hot_all] = a.T[:size].astype(bf16)
            rows_t[at : at + size, hot_all:] = gq[:, cut].T[:size]
            rows_t[at + size : at + 2 * size, :] = (gk[cut, :] + b)[:size].astype(bf16)
            rows_t[at + 2 * size : at + 3 * size, :] = (gv[cut, :] + c)[:size].astype(bf16)
            for g in range(groups):
                out[g, base + h * size : base + (h + 1) * size, :] = proj_grad[
                    h * LANES : h * LANES + size, g * width : (g + 1) * width
                ].astype(bf16)
        for h in range(heads):
            part = slice(h * 3 * size, (h + 1) * 3 * size)
            whole = dot(rows_t[part, :], fn[...])
            for g in range(groups):
                out[g, part, :] = whole[:, g * width : (g + 1) * width].astype(bf16)

    return body


def make_fold(count):
    def body(mine, theirs, *outs):
        rows = outs[0].shape[0]
        for i in range(count):
            at = slice(i * rows, (i + 1) * rows)
            outs[i][...] = (mine[at].astype(f32) + theirs[at].astype(f32)).astype(bf16)

    return body


def total_of(refs):
    total = refs[0][...].astype(f32)
    for r in refs[1:]:
        total = total + r[...].astype(f32)
    return total


def make_mid(count, groups):
    def body(*refs):
        parts, (tok, link) = refs[:count], refs[count : count + 2]
        mid_o, normal_o, factor_o = refs[count + 2 : count + 5]
        outs = refs[count + 5 :]
        mid = (tok[...].astype(f32) + total_of(parts)).astype(bf16)
        normal, factor = norm_parts(mid)
        mid_o[...] = mid
        normal_o[...] = normal
        factor_o[...] = factor
        slot_in = dot(link[...], normal.astype(bf16))
        each = slot_in.shape[0] // groups
        for g in range(groups):
            outs[g][...] = slot_in[g * each : (g + 1) * each].astype(bf16)

    return body


def slot_mask(rows, experts, e):
    row = lax.broadcasted_iota(jnp.int32, (rows, 1), 0)
    return (row // CAP) % experts == e


def make_expert_grad(count, experts):
    def body(*refs):
        shards, down, grads, out = refs[:count], refs[count], refs[count + 1], refs[count + 2]
        grads[...] = jnp.concatenate([s[...] for s in shards], axis=0)
        for e in range(experts):
            out[e] = dot_nt(grads[...], down[e])

    return body


def make_expert(count, experts):
    def body(*refs):
        shards = refs[:count]
        up, down, grad_hidden, arrived, hid_o, pre_o, even, odd = refs[count:]
        arrived[...] = jnp.concatenate([s[...] for s in shards], axis=0)
        rows = arrived.shape[0]
        forth = None
        back = None
        for e in range(experts):
            keep = slot_mask(rows, experts, e)
            pre = dot(arrived[...], up[e])
            cdf = 0.5 * (1.0 + lax.erf(pre * half_root))
            hidden = jnp.where(keep, pre * cdf, 0.0).astype(bf16)
            slope = cdf + pre * jnp.exp(-0.5 * pre * pre) * bell_scale
            grad_pre = jnp.where(keep, grad_hidden[e] * slope, 0.0).astype(bf16)
            hid_o[e] = hidden
            pre_o[e] = grad_pre
            a = dot(hidden, down[e])
            b = dot_nt(grad_pre, up[e])
            forth = a if forth is None else forth + a
            back = b if back is None else back + b
        both = jnp.concatenate([back, forth], axis=1).astype(bf16)
        each = rows // count
        for k in range(count):
            to = even if k % 2 == 0 else odd
            to[(k // 2) * each : (k // 2 + 1) * each] = both[k * each : (k + 1) * each]

    return body


def make_weight_grads(experts):
    def body(arrived, grads, hidden, grad_pre, up_o, down_o):
        for e in range(experts):
            up_o[e] = dot_tn(arrived[...], grad_pre[e]).astype(bf16)
            down_o[e] = dot_tn(hidden[e], grads[...]).astype(bf16)

    return body


def make_split(count, groups):
    def body(*refs):
        parts, outs = refs[:count], refs[count:]
        total = total_of(parts)
        each = total.shape[0] // groups
        for g in range(groups):
            outs[g][...] = total[g * each : (g + 1) * each].astype(bf16)

    return body


def make_mid_back(groups):
    def body(*refs):
        parts = refs[:groups]
        link, cot, normal, factor, grad_o, expert_o = refs[groups:]
        both = jnp.concatenate([p[...].astype(f32) for p in parts], axis=0).astype(bf16)
        width = cot.shape[1]
        expert_o[...] = both[:, width:]
        grad_norm = dot_tn(link[...], both[:, :width])
        grad_o[...] = (
            cot[...].astype(f32) + norm_back(normal[...], factor[...], grad_norm)
        ).astype(bf16)

    return body


def make_epilogue(count):
    def body(*refs):
        parts = refs[:count]
        tok, mid_hot, perm, pick0, pick1, experts, gate, cot, out, gate_o = refs[count:]
        cold = (tok[...].astype(f32) + total_of(parts)).astype(bf16)
        ordered = jnp.concatenate([mid_hot[...], cold], axis=0)
        mid = dot(perm[...], ordered)
        first = dot(pick0[...], experts[...])
        second = dot(pick1[...], experts[...])
        out[...] = (mid + gate[:, 0:1] * first + gate[:, 1:2] * second).astype(bf16)
        upstream = cot[...].astype(f32)
        gate_o[:, 0:1] = jnp.sum(upstream * first, axis=-1, keepdims=True)
        gate_o[:, 1:2] = jnp.sum(upstream * second, axis=-1, keepdims=True)

    return body


def fold_scatter(even, odd, rows, name):
    count = lax.axis_size("tensor") // 2
    theirs = hop(odd, "tensor", 1)
    sums = run(
        make_fold(count), [shape((rows, even.shape[1]))] * count, [even, theirs], name, mib=24
    )
    return [sums[0]] + [hop(sums[i], "tensor", 2 * i) for i in range(1, count)]


def shards(
    tokens,
    cotangent,
    gate_weights,
    routes,
    slot_index,
    qkv_weight,
    proj_weight,
    up_weight,
    down_weight,
):
    rows, width = tokens.shape
    heads, size = qkv_weight.shape[1], qkv_weight.shape[2] // 3
    scale = size ** (-0.5)
    groups = lax.axis_size("dp")
    count = lax.axis_size("tensor")
    experts, _, hidden_dev = up_weight.shape
    each = experts * CAP
    places = groups * each
    cold = rows - places
    hot_all = count * places
    total = count * rows
    slots = count * places

    wqkv = jnp.pad(
        qkv_weight.reshape(width, heads, 3, size), ((0, 0), (0, 0), (0, 0), (0, LANES - size))
    ).reshape(width, heads * 3 * LANES)
    proj = jnp.pad(proj_weight, ((0, 0), (0, LANES - size), (0, 0))).reshape(heads * LANES, width)

    group = (lax.axis_index("dp") * experts).astype(jnp.int32).reshape(1)
    normed, cot, tok, perm, pick0, pick1, link, grad_out = run(
        prologue_body,
        [
            shape((rows, width)),
            shape((rows, width)),
            shape((rows, width)),
            shape((rows, rows)),
            shape((rows, places)),
            shape((rows, places)),
            shape((places, places)),
            shape((places, width)),
        ],
        [group, tokens, cotangent, gate_weights, routes, slot_index],
        "prologue",
        smem=(0,),
        mib=24,
    )
    normed_all = gather_rel(normed)
    fn, qkv, ctx_hot, part_hot = run(
        make_front(count, places, heads, scale),
        [
            shape((total, width)),
            shape((total, heads * 3 * LANES)),
            shape((hot_all, heads * LANES)),
            shape((hot_all, width)),
        ],
        normed_all + [wqkv, proj],
        "front",
        flops=2 * total * width * heads * 3 * LANES,
    )

    def parity(x, n):
        blocks = x.reshape(count // 2, 2, n, x.shape[1])
        return (
            blocks[:, 0].reshape(count // 2 * n, x.shape[1]),
            blocks[:, 1].reshape(count // 2 * n, x.shape[1]),
        )

    even, odd = parity(part_hot, places)
    hot_sums = fold_scatter(even, odd, places, "fold_hot")

    pieces = [grad_out[g * each : (g + 1) * each] for g in range(groups)]
    landed = jnp.concatenate(
        [pieces[0]] + [hop(pieces[g], "dp", g) for g in range(1, groups)], axis=0
    )
    grads_all = gather_rel(landed)
    slot_grads, grad_hidden = run(
        make_expert_grad(count, experts),
        [shape((slots, width)), shape((experts, slots, hidden_dev), f32)],
        grads_all + [down_weight],
        "slot_grads",
        flops=2 * slots * width * hidden_dev * experts,
        mib=24,
    )

    outs = run(
        make_mid(count // 2, groups),
        [shape((places, width)), shape((places, width), f32), shape((places, 1), f32)]
        + [shape((each, width))] * groups,
        hot_sums + [tok[:places], link],
        "mid_hot",
        mib=16,
    )
    mid_hot, normal_hot, factor_hot = outs[:3]
    pieces = outs[3:]
    landed = jnp.concatenate(
        [pieces[0]] + [hop(pieces[g], "dp", g) for g in range(1, groups)], axis=0
    )
    arrived_all = gather_rel(landed)
    arrived, hidden, grad_pre, even, odd = run(
        make_expert(count, experts),
        [
            shape((slots, width)),
            shape((experts, slots, hidden_dev)),
            shape((experts, slots, hidden_dev)),
            shape((slots // 2, 2 * width)),
            shape((slots // 2, 2 * width)),
        ],
        arrived_all + [up_weight, down_weight, grad_hidden],
        "experts",
        flops=6 * slots * width * hidden_dev * experts,
        mib=32,
    )
    sums = fold_scatter(even, odd, places, "fold_slots")
    pieces = run(
        make_split(count // 2, groups),
        [shape((each, 2 * width))] * groups,
        sums,
        "split_slots",
        mib=16,
    )
    back = [pieces[0]] + [hop(pieces[g], "dp", g) for g in range(1, groups)]
    grad_hot, expert_out = run(
        make_mid_back(groups),
        [shape((places, width)), shape((places, width))],
        back + [link, cot[:places], normal_hot, factor_hot],
        "mid_back",
        mib=16,
    )
    grad_hot_all = gather_rel(grad_hot)

    ctx_cold, part_cold = run(
        make_cold(hot_all, heads, scale),
        [shape((count * cold, heads * LANES)), shape((count * cold, width))],
        [qkv, proj],
        "cold",
        flops=4 * total * total * heads * LANES,
    )
    even, odd = parity(part_cold, cold)
    cold_sums = fold_scatter(even, odd, cold, "fold_cold")
    cot_all = gather_rel(cot[places:])
    gq, gk, gv, gp = run(
        lambda *refs: make_cold_back(count, places, heads, scale)(*refs),
        [
            shape((count * cold, heads * LANES)),
            shape((heads * LANES, total), f32),
            shape((heads * LANES, total), f32),
            shape((heads * LANES, width), f32),
            shape((count * cold, width)),
        ],
        cot_all + [qkv, proj, ctx_cold],
        "cold_back",
        flops=10 * total * total * heads * LANES,
    )[:4]
    grad_up, grad_down = run(
        make_weight_grads(experts),
        [shape(up_weight.shape), shape(down_weight.shape)],
        [arrived, slot_grads, hidden, grad_pre],
        "weight_grads",
        flops=4 * slots * width * hidden_dev * experts,
        mib=32,
    )

    sums, _ = run(
        make_hot_back(count, heads, size, groups, scale),
        [
            shape((groups, heads * 4 * size, width // groups)),
            shape((heads * 3 * size, total)),
        ],
        grad_hot_all + [qkv, proj, ctx_hot, gq, gk, gv, gp, fn],
        "hot_back",
        flops=2 * total * width * heads * 3 * LANES,
    )
    me = lax.axis_index("dp")
    mine = lax.dynamic_index_in_dim(sums, me, 0, False).astype(f32)
    for g in range(1, groups):
        piece = lax.dynamic_index_in_dim(sums, me ^ g, 0, False)
        mine = mine + hop(piece, "dp", g).astype(f32)
    base = heads * 3 * size
    grad_qkv = mine[:base].T.reshape(width // groups, heads, 3 * size)
    grad_proj = mine[base:].reshape(heads, size, width // groups)

    layer_out, gate_grad = run(
        make_epilogue(count // 2),
        [shape((rows, width)), shape((rows, 2), f32)],
        cold_sums
        + [tok[places:], mid_hot, perm, pick0, pick1, expert_out, gate_weights, cotangent],
        "epilogue",
        mib=24,
    )
    return (layer_out, gate_grad, grad_qkv, grad_proj, grad_up, grad_down)


def solution(mesh):
    return jax.shard_map(
        shards,
        mesh=mesh,
        in_specs=(
            P(("dp", "tensor"), None),
            P(("dp", "tensor"), None),
            P(("dp", "tensor"), None),
            P(("dp", "tensor"), None),
            P(("dp", "tensor"), None),
            P(None, "tensor", None),
            P("tensor", None, None),
            P("dp", None, "tensor"),
            P("dp", "tensor", None),
        ),
        out_specs=(
            P(("dp", "tensor"), None),
            P(("dp", "tensor"), None),
            P("dp", "tensor", None),
            P("tensor", None, "dp"),
            P("dp", None, "tensor"),
            P("dp", "tensor", None),
        ),
        check_vma=False,
    )
```

time: 383 us -> 220 us (0.57)
  matrix products: 110 us -> 0 us
  waiting for transfers between devices: 176 us -> 76 us
  starting transfers between devices: 14.5 us -> 58 us
  Pallas kernels: 0 us -> 40.9 us
  blocking collectives: 29.9 us -> 0 us
  between operations: 14.4 us -> 1.19 us
  local copies, waits for them, and re-layouts: 26.1 us -> 39 us
  other arithmetic: 10.5 us -> 1.76 us
    dot_general x30 -> x0, matrix products: 106 us -> none  [the longest x2 25 us: head_one_block(): jnp.einsum('qt,qk->tk', grad_scores, query_block, preferred_element_type=...]
    ppermute x0 -> x59, waiting for transfers between devices: none -> 76 us  [hop(): return lax.ppermute(x, axis, [(i, i ^ mask) for i in range(size)])]
    all_gather x2 -> x0, waiting for transfers between devices: 67.8 us -> none  [the longest x1 36.7 us: shards(): full_norm = lax.all_gather(normed, 'tensor', axis=0, tiled=True)]
    ppermute x0 -> x59, starting transfers between devices: none -> 58 us  [hop(): return lax.ppermute(x, axis, [(i, i ^ mask) for i in range(size)])]
    unnamed x8 -> x0, waiting for transfers between devices: 55.6 us -> none
    reduce_scatter x2 -> x0, waiting for transfers between devices: 47.8 us -> none  [the longest x1 29.8 us: shards(): lax.psum_scatter(jnp.einsum('hsk,hkd->sd', context, proj_weight, preferre...]
    pallas_call x0 -> x15, Pallas kernels: none -> 40.9 us  [run(): pl.pallas_call(body, out_shape=list(outs), in_specs=specs, out_specs=[pl....]
    all_gather x2 -> x0, blocking collectives: 29.9 us -> none  [the longest x1 15.4 us: shards(): lax.all_gather(grad_landed[None], 'tensor', axis=0, tiled=True)]
  transfers between devices with their start and end apart: 10 -> 59, of which waited for: 7 -> 16; matrix products, arithmetic and copies ran while one was open for 26% -> 8% of each run, Pallas kernels for 0% -> 14%
where the time goes in v1:
time: 220 us; the launch traced here: 217 us
  waiting for transfers between devices  76 us (35%)
  starting transfers between devices  58 us (26%)
  Pallas kernels  40.9 us (19%)
  local copies, waits for them, and re-layouts  39 us (18%)
    ppermute x59, waiting for transfers between devices, hop(): return lax.ppermute(x, axis, [(i, i ^ mask) for i in range(size)])  76 us
    ppermute x59, starting transfers between devices, hop(): return lax.ppermute(x, axis, [(i, i ^ mask) for i in range(size)])  58 us
    pallas_call x15, Pallas kernels, run(): pl.pallas_call(body, out_shape=list(outs), in_specs=specs, out_specs=[pl....  40.9 us
    unnamed x99, local copies, waits for them, and re-layouts  26.1 us
  transfers between devices with their start and end apart: 59, of which 16 were waited for; matrix products, arithmetic and copies ran while one was open for 8% of the time, Pallas kernels for 14%

profile of v1, /device:TPU:0, one launch (start us, length us, event | category | flops | bytes accessed | tf_op | source)
XLA Modules:
  0.0 216.9 jit_solution(14009716980843646819)
XLA Ops:
  7.2 3.1 %collective-permute-start.1 = (bf16[128,1280]{1,0:T(8,128)(2,1)S(1)}, bf16[128,1280]{1,0:T(8,128)(2,1)S(1)}, u32[]{:S(2)}, u32[]{:S(2)}) collective-permute-start(bf16[128,1280]{1,0:T(8,128)(2,1)S(1)} %get-tuple-element.61.refs_0_), channel_id=1, source_target_pairs={{0,2},{1,3},{2,0},{3,1},{4,6},{5,7},{6,4},{7,5},{8,10},{9,11},{10,... | collective-permute-start | bytes 983048 | tf_op jit(solution)/shard_map/ppermute | solution.py:72
  10.3 2.6 %collective-permute-start.3 = (bf16[128,1280]{1,0:T(8,128)(2,1)S(1)}, bf16[128,1280]{1,0:T(8,128)(2,1)S(1)}, u32[]{:S(2)}, u32[]{:S(2)}) collective-permute-start(bf16[128,1280]{1,0:T(8,128)(2,1)S(1)} %get-tuple-element.61.refs_0_), channel_id=1, source_target_pairs={{0,4},{1,5},{2,6},{3,7},{4,0},{5,1},{6,2},{7,3},{8,12},{9,13},{10,... | collective-permute-start | bytes 983048 | tf_op jit(solution)/shard_map/ppermute | solution.py:72
  12.9 11.4 %collective-permute-done.1.refs_2_ = bf16[128,1280]{1,0:T(8,128)(2,1)S(1)} collective-permute-done((bf16[128,1280]{1,0:T(8,128)(2,1)S(1)}, bf16[128,1280]{1,0:T(8,128)(2,1)S(1)}, u32[]{:S(2)}, u32[]{:S(2)}) %collective-permute-start.1) | collective-permute-done | bytes 327712 | tf_op jit(solution)/shard_map/ppermute | solution.py:72
  24.2 11.6 %collective-permute-done.3.refs_4_ = bf16[128,1280]{1,0:T(8,128)(2,1)S(1)} collective-permute-done((bf16[128,1280]{1,0:T(8,128)(2,1)S(1)}, bf16[128,1280]{1,0:T(8,128)(2,1)S(1)}, u32[]{:S(2)}, u32[]{:S(2)}) %collective-permute-start.3) | collective-permute-done | bytes 327712 | tf_op jit(solution)/shard_map/ppermute | solution.py:72
  36.4 2.7 %pad.8 = bf16[1280,2,3,128]{0,3,2,1:T(8,128)(2,1)} pad(bf16[1280,2,3,80]{0,3,2,1:T(8,128)(2,1)} %bitcast.41, bf16[]{:T(256)} %constant.21.clone.1), padding=0_0x0_0x0_0x0_48 | pad | bytes 3194882 | tf_op jit(solution)/shard_map/jit(_pad)/pad | solution.py:427
  39.1 4.0 %copy.29.refs_8_ = bf16[1280,768]{1,0:T(8,128)(2,1)} copy(bf16[1280,768]{0,1:T(8,128)(2,1)} %bitcast.39) | data formatting | bytes 3932160 | tf_op jit(solution)/shard_map/reshape | solution.py:429
  47.1 6.1 %front.1 = (bf16[1024,1280]{1,0:T(8,128)(2,1)}, bf16[1024,768]{1,0:T(8,128)(2,1)S(1)}, bf16[128,256]{1,0:T(8,128)(2,1)S(1)}, bf16[128,1280]{1,0:T(8,128)(2,1)S(1)}) custom-call(bf16[128,1280]{1,0:T(8,128)(2,1)S(1)} %copy-done.27, bf16[128,1280]{1,0:T(8,128)(2,1)} %collective-permute-done.refs_1_, bf16[128,1280]{1,0:T(8,128)(2,1)S(1)} %copy-done.29, ...), custom_call_target="tpu_custom_call" | custom-call | flops 2013265920 | bytes 9830400 | tf_op jit(solution)/shard_map/front/pallas_call | solution.py:49
  53.4 2.5 %collective-permute-start.27 = (bf16[4,1280]{1,0:T(4,128)(2,1)S(1)}, bf16[4,1280]{1,0:T(4,128)(2,1)S(1)}, u32[]{:S(2)}, u32[]{:S(2)}) collective-permute-start(bf16[4,1280]{1,0:T(4,128)(2,1)S(1)} %get-tuple-element.136), channel_id=1, source_target_pairs={{0,24},{8,16},{16,8},{24,0},{1,25},{9,17},{17,9},{25,1},{2,26},{10... | collective-permute-start | bytes 30728 | tf_op jit(solution)/shard_map/ppermute | solution.py:72
  57.1 6.0 %collective-permute-start.12 = (bf16[16,1280]{1,0:T(8,128)(2,1)S(1)}, bf16[16,1280]{1,0:T(8,128)(2,1)S(1)}, u32[]{:S(2)}, u32[]{:S(2)}) collective-permute-start(bf16[16,1280]{1,0:T(8,128)(2,1)S(1)} %get-tuple-element.71), channel_id=1, source_target_pairs={{0,2},{1,3},{2,0},{3,1},{4,6},{5,7},{6,4},{7,5},{8,10},{9,11},{10,... | collective-permute-start | bytes 122888 | tf_op jit(solution)/shard_map/ppermute | solution.py:72
  66.7 2.0 collective-permute-start.31
  70.5 2.5 %collective-permute-start.17 = (bf16[4,1280]{1,0:T(4,128)(2,1)S(1)}, bf16[4,1280]{1,0:T(4,128)(2,1)S(1)}, u32[]{:S(2)}, u32[]{:S(2)}) collective-permute-start(bf16[4,1280]{1,0:T(4,128)(2,1)S(1)} %get-tuple-element.82), channel_id=1, source_target_pairs={{0,24},{8,16},{16,8},{24,0},{1,25},{9,17},{17,9},{25,1},{2,26},{10... | collective-permute-start | bytes 30728 | tf_op jit(solution)/shard_map/ppermute | solution.py:72
  83.3 2.4 %collective-permute-done.23.refs_6_ = bf16[16,1280]{1,0:T(8,128)(2,1)S(1)} collective-permute-done((bf16[16,1280]{1,0:T(8,128)(2,1)S(1)}, bf16[16,1280]{1,0:T(8,128)(2,1)S(1)}, u32[]{:S(2)}, u32[]{:S(2)}) %collective-permute-start.23) | collective-permute-done | bytes 40992 | tf_op jit(solution)/shard_map/ppermute | solution.py:72
  87.0 2.4 %experts.1 = (bf16[128,1280]{1,0:T(8,128)(2,1)S(1)}, bf16[2,128,640]{2,1,0:T(8,128)(2,1)S(1)}, bf16[2,128,640]{2,1,0:T(8,128)(2,1)S(1)}, bf16[64,2560]{1,0:T(8,128)(2,1)S(1)}, bf16[64,2560]{1,0:T(8,128)(2,1)S(1)}) custom-call(bf16[16,1280]{1,0:T(8,128)(2,1)S(1)} %pad_maximum_fusion.refs_0_, bf16[16,1280]{1,0:T(8,128)(2,1)S(1)} %collective-permute-done.18.refs_1_, ...), custom_call_target="tpu_custom_call" | custom-call | flops 1258291200 | bytes 9175040 | tf_op jit(solution)/shard_map/experts/pallas_call | solution.py:49
  90.0 2.3 %collective-permute-start.52 = (bf16[112,1280]{1,0:T(8,128)(2,1)S(1)}, bf16[112,1280]{1,0:T(8,128)(2,1)S(1)}, u32[]{:S(2)}, u32[]{:S(2)}) collective-permute-start(bf16[112,1280]{1,0:T(8,128)(2,1)S(1)} %slice.53.refs_0_), channel_id=1, source_target_pairs={{0,4},{1,5},{2,6},{3,7},{4,0},{5,1},{6,2},{7,3},{8,12},{9,13},{10,... | collective-permute-start | bytes 860168 | tf_op jit(solution)/shard_map/ppermute | solution.py:72
  92.4 2.0 collective-permute-start.54
  94.6 2.3 %collective-permute-start.37 = (bf16[16,2560]{1,0:T(8,128)(2,1)S(1)}, bf16[16,2560]{1,0:T(8,128)(2,1)S(1)}, u32[]{:S(2)}, u32[]{:S(2)}) collective-permute-start(bf16[16,2560]{1,0:T(8,128)(2,1)S(1)} %get-tuple-element.89), channel_id=1, source_target_pairs={{0,4},{1,5},{2,6},{3,7},{4,0},{5,1},{6,2},{7,3},{8,12},{9,13},{10,... | collective-permute-start | bytes 245768 | tf_op jit(solution)/shard_map/ppermute | solution.py:72
  96.9 15.7 %collective-permute-done.36.refs_1_ = bf16[16,2560]{1,0:T(8,128)(2,1)S(1)} collective-permute-done((bf16[16,2560]{1,0:T(8,128)(2,1)S(1)}, bf16[16,2560]{1,0:T(8,128)(2,1)S(1)}, u32[]{:S(2)}, u32[]{:S(2)}) %collective-permute-start.36) | collective-permute-done | bytes 81952 | tf_op jit(solution)/shard_map/ppermute | solution.py:72
  114.4 10.0 %collective-permute-done.37.refs_2_ = bf16[16,2560]{1,0:T(8,128)(2,1)S(1)} collective-permute-done((bf16[16,2560]{1,0:T(8,128)(2,1)S(1)}, bf16[16,2560]{1,0:T(8,128)(2,1)S(1)}, u32[]{:S(2)}, u32[]{:S(2)}) %collective-permute-start.37) | collective-permute-done | bytes 81952 | tf_op jit(solution)/shard_map/ppermute | solution.py:72
  124.5 1.9 collective-permute-start.39
  127.9 5.3 %cold.1 = (bf16[896,256]{1,0:T(8,128)(2,1)S(1)}, bf16[896,1280]{1,0:T(8,128)(2,1)S(1)}) custom-call(bf16[1024,768]{1,0:T(8,128)(2,1)S(1)} %get-tuple-element.62.qkv.refs_8_, bf16[256,1280]{1,0:T(8,128)(2,1)S(1)} %bitcast.33), custom_call_target="tpu_custom_call" | custom-call | flops 1073741824 | bytes 4980736 | tf_op jit(solution)/shard_map/cold/pallas_call | solution.py:49
  136.5 3.3 %collective-permute-done.41.refs_3_ = bf16[4,2560]{1,0:T(4,128)(2,1)S(1)} collective-permute-done((bf16[4,2560]{1,0:T(4,128)(2,1)S(1)}, bf16[4,2560]{1,0:T(4,128)(2,1)S(1)}, u32[]{:S(2)}, u32[]{:S(2)}) %collective-permute-start.41) | collective-permute-done | bytes 20512 | tf_op jit(solution)/shard_map/ppermute | solution.py:72
  145.0 2.4 %collective-permute-start.47 = (bf16[16,1280]{1,0:T(8,128)(2,1)S(1)}, bf16[16,1280]{1,0:T(8,128)(2,1)}, u32[]{:S(2)}, u32[]{:S(2)}) collective-permute-start(bf16[16,1280]{1,0:T(8,128)(2,1)S(1)} %get-tuple-element.101.refs_0_), channel_id=1, source_target_pairs={{0,6},{1,7},{2,4},{3,5},{4,2},{5,3},{6,0},{7,1},{8,14},{9,15},{10,... | collective-permute-start | bytes 122888 | tf_op jit(solution)/shard_map/ppermute | solution.py:72
  148.0 2.1 collective-permute-done.45.refs_4_
  156.9 10.6 %cold_back.1 = (bf16[896,256]{1,0:T(8,128)(2,1)S(1)}, f32[256,1024]{1,0:T(8,128)S(1)}, f32[256,1024]{1,0:T(8,128)S(1)}, f32[256,1280]{1,0:T(8,128)}, bf16[896,1280]{1,0:T(8,128)(2,1)}) custom-call(bf16[112,1280]{1,0:T(8,128)(2,1)S(1)} %copy-done.11, bf16[112,1280]{1,0:T(8,128)(2,1)S(1)} %copy-done.39, bf16[112,1280]{1,0:T(8,128)(2,1)S(1)} %copy-done.35, ...), custom_call_target="tpu_custom_call" | custom-call | flops 2684354560 | bytes 11141120 | tf_op jit(solution)/shard_map/cold_back/pallas_call | solution.py:49
  168.8 6.9 %hot_back.1 = (bf16[4,640,320]{2,1,0:T(8,128)(2,1)}, bf16[480,1024]{1,0:T(8,128)(2,1)}) custom-call(bf16[16,1280]{1,0:T(8,128)(2,1)S(1)} %get-tuple-element.101.refs_0_, bf16[16,1280]{1,0:T(8,128)(2,1)S(1)} %collective-permute-done.42.refs_1_, bf16[16,1280]{1,0:T(8,128)(2,1)S(1)} %collective-permute-done.43.refs_2_, ...), custom_call_target="tpu_custom_call" | custom-call | flops 2013265920 | bytes 11730944 | tf_op jit(solution)/shard_map/hot_back/pallas_call | solution.py:49
  175.7 2.5 %dynamic-slice_bitcast_fusion.2 = (bf16[640,320]{1,0:T(8,128)(2,1)}, bf16[640,320]{1,0:T(8,128)(2,1)}, bf16[640,320]{1,0:T(8,128)(2,1)}) fusion(bf16[4,640,320]{2,1,0:T(8,128)(2,1)} %get-tuple-element.109, s32[]{:T(128)S(6)} %select_n.14, s32[]{:T(128)S(6)} %select_n.16, s32[]{:T(128)S(6)} %select_n.15), kind=kLoop, calls=%fused_computation.5 | loop fusion | bytes 2457612 | tf_op jit(solution)/shard_map/jit(dynamic_index_in_dim)/squeeze | solution.py:579
  185.7 4.3 %weight_grads.1 = (bf16[2,1280,640]{2,1,0:T(8,128)(2,1)}, bf16[2,640,1280]{2,1,0:T(8,128)(2,1)}) custom-call(bf16[128,1280]{1,0:T(8,128)(2,1)S(1)} %copy-done.21, bf16[128,1280]{1,0:T(8,128)(2,1)S(1)} %copy-done.19, bf16[2,128,640]{2,1,0:T(8,128)(2,1)S(1)} %copy-done.23, bf16[2,128,640]{2,1,0:T(8,128)(2,1)S(1)} %copy-done.25), custom_call_target="tpu_custom_call" | custom-call | flops 838860800 | bytes 7864320 | tf_op jit(solution)/shard_map/weight_grads/pallas_call | solution.py:49
  191.7 2.3 %collective-permute-start.9 = (bf16[112,1280]{1,0:T(8,128)(2,1)}, bf16[112,1280]{1,0:T(8,128)(2,1)S(1)}, u32[]{:S(2)}, u32[]{:S(2)}) collective-permute-start(bf16[112,1280]{1,0:T(8,128)(2,1)} %get-tuple-element.66), channel_id=1, source_target_pairs={{0,4},{1,5},{2,6},{3,7},{4,0},{5,1},{6,2},{7,3},{8,12},{9,13},{10,... | collective-permute-start | bytes 860168 | tf_op jit(solution)/shard_map/ppermute | solution.py:72
  193.9 2.0 collective-permute-start.10
  195.9 7.0 %collective-permute-done.57 = bf16[640,320]{1,0:T(8,128)(2,1)} collective-permute-done((bf16[640,320]{1,0:T(8,128)(2,1)}, bf16[640,320]{1,0:T(8,128)(2,1)}, u32[]{:S(2)}, u32[]{:S(2)}) %collective-permute-start.57) | collective-permute-done | bytes 409632 | tf_op jit(solution)/shard_map/ppermute | solution.py:72
  206.3 2.1 copy.36
  208.4 6.5 %collective-permute-done.9.refs_2_ = bf16[112,1280]{1,0:T(8,128)(2,1)S(1)} collective-permute-done((bf16[112,1280]{1,0:T(8,128)(2,1)}, bf16[112,1280]{1,0:T(8,128)(2,1)S(1)}, u32[]{:S(2)}, u32[]{:S(2)}) %collective-permute-start.9) | collective-permute-done | bytes 286752 | tf_op jit(solution)/shard_map/ppermute | solution.py:72
  (216 shorter events, 64.6 us)
Async XLA Ops:
  7.2 17.1 %collective-permute-start.1 = (bf16[128,1280]{1,0:T(8,128)(2,1)S(1)}, bf16[128,1280]{1,0:T(8,128)(2,1)S(1)}, u32[]{:S(2)}, u32[]{:S(2)}) collective-permute-start(bf16[128,1280]{1,0:T(8,128)(2,1)S(1)} %get-tuple-element.61.refs_0_), channel_id=1, source_target_pairs={{0,2},{1,3},{2,0},{3,1},{4,6},{5,7},{6,4},{7,5},{8,10},{9,11},{10,... | collective-permute-start | bytes 983048 | tf_op jit(solution)/shard_map/ppermute | solution.py:72
  10.3 25.6 %collective-permute-start.3 = (bf16[128,1280]{1,0:T(8,128)(2,1)S(1)}, bf16[128,1280]{1,0:T(8,128)(2,1)S(1)}, u32[]{:S(2)}, u32[]{:S(2)}) collective-permute-start(bf16[128,1280]{1,0:T(8,128)(2,1)S(1)} %get-tuple-element.61.refs_0_), channel_id=1, source_target_pairs={{0,4},{1,5},{2,6},{3,7},{4,0},{5,1},{6,2},{7,3},{8,12},{9,13},{10,... | collective-permute-start | bytes 983048 | tf_op jit(solution)/shard_map/ppermute | solution.py:72
  12.8 23.0 %collective-permute-start.5 = (bf16[128,1280]{1,0:T(8,128)(2,1)S(1)}, bf16[128,1280]{1,0:T(8,128)(2,1)S(1)}, u32[]{:S(2)}, u32[]{:S(2)}) collective-permute-start(bf16[128,1280]{1,0:T(8,128)(2,1)S(1)} %get-tuple-element.61.refs_0_), channel_id=1, source_target_pairs={{0,6},{1,7},{2,4},{3,5},{4,2},{5,3},{6,0},{7,1},{8,14},{9,15},{10,... | collective-permute-start | bytes 983048 | tf_op jit(solution)/shard_map/ppermute | solution.py:72
  12.8 30.3 %collective-permute-start = (bf16[128,1280]{1,0:T(8,128)(2,1)S(1)}, bf16[128,1280]{1,0:T(8,128)(2,1)}, u32[]{:S(2)}, u32[]{:S(2)}) collective-permute-start(bf16[128,1280]{1,0:T(8,128)(2,1)S(1)} %get-tuple-element.61.refs_0_), channel_id=1, source_target_pairs={{0,1},{1,0},{2,3},{3,2},{4,5},{5,4},{6,7},{7,6},{8,9},{9,8},{10,11... | collective-permute-start | bytes 983048 | tf_op jit(solution)/shard_map/ppermute | solution.py:72
  24.2 18.9 %collective-permute-start.2 = (bf16[128,1280]{1,0:T(8,128)(2,1)S(1)}, bf16[128,1280]{1,0:T(8,128)(2,1)}, u32[]{:S(2)}, u32[]{:S(2)}) collective-permute-start(bf16[128,1280]{1,0:T(8,128)(2,1)S(1)} %collective-permute-done.1.refs_2_), channel_id=1, source_target_pairs={{0,1},{1,0},{2,3},{3,2},{4,5},{5,4},{6,7},{7,6},{8,9},{9,8},{10,11... | collective-permute-start | bytes 983048 | tf_op jit(solution)/shard_map/ppermute | solution.py:72
  53.4 10.8 %collective-permute-start.27 = (bf16[4,1280]{1,0:T(4,128)(2,1)S(1)}, bf16[4,1280]{1,0:T(4,128)(2,1)S(1)}, u32[]{:S(2)}, u32[]{:S(2)}) collective-permute-start(bf16[4,1280]{1,0:T(4,128)(2,1)S(1)} %get-tuple-element.136), channel_id=1, source_target_pairs={{0,24},{8,16},{16,8},{24,0},{1,25},{9,17},{17,9},{25,1},{2,26},{10... | collective-permute-start | bytes 30728 | tf_op jit(solution)/shard_map/ppermute | solution.py:72
  56.0 9.7 %collective-permute-start.26 = (bf16[4,1280]{1,0:T(4,128)(2,1)S(1)}, bf16[4,1280]{1,0:T(4,128)(2,1)S(1)}, u32[]{:S(2)}, u32[]{:S(2)}) collective-permute-start(bf16[4,1280]{1,0:T(4,128)(2,1)S(1)} %get-tuple-element.137), channel_id=1, source_target_pairs={{0,16},{8,24},{16,0},{24,8},{1,17},{9,25},{17,1},{25,9},{2,18},{10... | collective-permute-start | bytes 30728 | tf_op jit(solution)/shard_map/ppermute | solution.py:72
  56.5 9.1 %collective-permute-start.25 = (bf16[4,1280]{1,0:T(4,128)(2,1)S(1)}, bf16[4,1280]{1,0:T(4,128)(2,1)S(1)}, u32[]{:S(2)}, u32[]{:S(2)}) collective-permute-start(bf16[4,1280]{1,0:T(4,128)(2,1)S(1)} %get-tuple-element.138), channel_id=1, source_target_pairs={{0,8},{8,0},{16,24},{24,16},{1,9},{9,1},{17,25},{25,17},{2,10},{10... | collective-permute-start | bytes 30728 | tf_op jit(solution)/shard_map/ppermute | solution.py:72
  57.1 11.7 %collective-permute-start.12 = (bf16[16,1280]{1,0:T(8,128)(2,1)S(1)}, bf16[16,1280]{1,0:T(8,128)(2,1)S(1)}, u32[]{:S(2)}, u32[]{:S(2)}) collective-permute-start(bf16[16,1280]{1,0:T(8,128)(2,1)S(1)} %get-tuple-element.71), channel_id=1, source_target_pairs={{0,2},{1,3},{2,0},{3,1},{4,6},{5,7},{6,4},{7,5},{8,10},{9,11},{10,... | collective-permute-start | bytes 122888 | tf_op jit(solution)/shard_map/ppermute | solution.py:72
  65.7 8.4 %collective-permute-start.29 = (bf16[16,1280]{1,0:T(8,128)(2,1)S(1)}, bf16[16,1280]{1,0:T(8,128)(2,1)S(1)}, u32[]{:S(2)}, u32[]{:S(2)}) collective-permute-start(bf16[16,1280]{1,0:T(8,128)(2,1)S(1)} %pad_maximum_fusion.1.refs_0_), channel_id=1, source_target_pairs={{0,2},{1,3},{2,0},{3,1},{4,6},{5,7},{6,4},{7,5},{8,10},{9,11},{10,... | collective-permute-start | bytes 122888 | tf_op jit(solution)/shard_map/ppermute | solution.py:72
  89.9 44.1 %collective-permute-start.50 = (bf16[112,1280]{1,0:T(8,128)(2,1)S(1)}, bf16[112,1280]{1,0:T(8,128)(2,1)S(1)}, u32[]{:S(2)}, u32[]{:S(2)}) collective-permute-start(bf16[112,1280]{1,0:T(8,128)(2,1)S(1)} %slice.53.refs_0_), channel_id=1, source_target_pairs={{0,2},{1,3},{2,0},{3,1},{4,6},{5,7},{6,4},{7,5},{8,10},{9,11},{10,... | collective-permute-start | bytes 860168 | tf_op jit(solution)/shard_map/ppermute | solution.py:72
  90.0 44.1 %collective-permute-start.52 = (bf16[112,1280]{1,0:T(8,128)(2,1)S(1)}, bf16[112,1280]{1,0:T(8,128)(2,1)S(1)}, u32[]{:S(2)}, u32[]{:S(2)}) collective-permute-start(bf16[112,1280]{1,0:T(8,128)(2,1)S(1)} %slice.53.refs_0_), channel_id=1, source_target_pairs={{0,4},{1,5},{2,6},{3,7},{4,0},{5,1},{6,2},{7,3},{8,12},{9,13},{10,... | collective-permute-start | bytes 860168 | tf_op jit(solution)/shard_map/ppermute | solution.py:72
  92.4 42.3 %collective-permute-start.54 = (bf16[112,1280]{1,0:T(8,128)(2,1)S(1)}, bf16[112,1280]{1,0:T(8,128)(2,1)}, u32[]{:S(2)}, u32[]{:S(2)}) collective-permute-start(bf16[112,1280]{1,0:T(8,128)(2,1)S(1)} %slice.53.refs_0_), channel_id=1, source_target_pairs={{0,6},{1,7},{2,4},{3,5},{4,2},{5,3},{6,0},{7,1},{8,14},{9,15},{10,... | collective-permute-start | bytes 860168 | tf_op jit(solution)/shard_map/ppermute | solution.py:72
  94.5 18.1 %collective-permute-start.36 = (bf16[16,2560]{1,0:T(8,128)(2,1)S(1)}, bf16[16,2560]{1,0:T(8,128)(2,1)S(1)}, u32[]{:S(2)}, u32[]{:S(2)}) collective-permute-start(bf16[16,2560]{1,0:T(8,128)(2,1)S(1)} %get-tuple-element.88), channel_id=1, source_target_pairs={{0,2},{1,3},{2,0},{3,1},{4,6},{5,7},{6,4},{7,5},{8,10},{9,11},{10,... | collective-permute-start | bytes 245768 | tf_op jit(solution)/shard_map/ppermute | solution.py:72
  94.6 29.9 %collective-permute-start.37 = (bf16[16,2560]{1,0:T(8,128)(2,1)S(1)}, bf16[16,2560]{1,0:T(8,128)(2,1)S(1)}, u32[]{:S(2)}, u32[]{:S(2)}) collective-permute-start(bf16[16,2560]{1,0:T(8,128)(2,1)S(1)} %get-tuple-element.89), channel_id=1, source_target_pairs={{0,4},{1,5},{2,6},{3,7},{4,0},{5,1},{6,2},{7,3},{8,12},{9,13},{10,... | collective-permute-start | bytes 245768 | tf_op jit(solution)/shard_map/ppermute | solution.py:72
  112.6 11.9 %collective-permute-start.38 = (bf16[16,2560]{1,0:T(8,128)(2,1)S(1)}, bf16[16,2560]{1,0:T(8,128)(2,1)S(1)}, u32[]{:S(2)}, u32[]{:S(2)}) collective-permute-start(bf16[16,2560]{1,0:T(8,128)(2,1)S(1)} %get-tuple-element.90), channel_id=1, source_target_pairs={{0,6},{1,7},{2,4},{3,5},{4,2},{5,3},{6,0},{7,1},{8,14},{9,15},{10,... | collective-permute-start | bytes 245768 | tf_op jit(solution)/shard_map/ppermute | solution.py:72
  124.5 10.2 %collective-permute-start.39 = (bf16[4,2560]{1,0:T(4,128)(2,1)S(1)}, bf16[4,2560]{1,0:T(4,128)(2,1)S(1)}, u32[]{:S(2)}, u32[]{:S(2)}) collective-permute-start(bf16[4,2560]{1,0:T(4,128)(2,1)S(1)} %get-tuple-element.92), channel_id=1, source_target_pairs={{0,8},{8,0},{16,24},{24,16},{1,9},{9,1},{17,25},{25,17},{2,10},{10... | collective-permute-start | bytes 61448 | tf_op jit(solution)/shard_map/ppermute | solution.py:72
  126.4 8.7 %collective-permute-start.40 = (bf16[4,2560]{1,0:T(4,128)(2,1)S(1)}, bf16[4,2560]{1,0:T(4,128)(2,1)S(1)}, u32[]{:S(2)}, u32[]{:S(2)}) collective-permute-start(bf16[4,2560]{1,0:T(4,128)(2,1)S(1)} %get-tuple-element.93), channel_id=1, source_target_pairs={{0,16},{8,24},{16,0},{24,8},{1,17},{9,25},{17,1},{25,9},{2,18},{10... | collective-permute-start | bytes 61448 | tf_op jit(solution)/shard_map/ppermute | solution.py:72
  134.2 8.9 %collective-permute-start.51 = (bf16[112,1280]{1,0:T(8,128)(2,1)S(1)}, bf16[112,1280]{1,0:T(8,128)(2,1)S(1)}, u32[]{:S(2)}, u32[]{:S(2)}) collective-permute-start(bf16[112,1280]{1,0:T(8,128)(2,1)S(1)} %collective-permute-done.50.refs_2_), channel_id=1, source_target_pairs={{0,1},{1,0},{2,3},{3,2},{4,5},{5,4},{6,7},{7,6},{8,9},{9,8},{10,11... | collective-permute-start | bytes 860168 | tf_op jit(solution)/shard_map/ppermute | solution.py:72
  134.6 9.7 %collective-permute-start.53 = (bf16[112,1280]{1,0:T(8,128)(2,1)S(1)}, bf16[112,1280]{1,0:T(8,128)(2,1)S(1)}, u32[]{:S(2)}, u32[]{:S(2)}) collective-permute-start(bf16[112,1280]{1,0:T(8,128)(2,1)S(1)} %collective-permute-done.52.refs_4_), channel_id=1, source_target_pairs={{0,1},{1,0},{2,3},{3,2},{4,5},{5,4},{6,7},{7,6},{8,9},{9,8},{10,11... | collective-permute-start | bytes 860168 | tf_op jit(solution)/shard_map/ppermute | solution.py:72
  134.7 12.7 %collective-permute-start.55 = (bf16[112,1280]{1,0:T(8,128)(2,1)}, bf16[112,1280]{1,0:T(8,128)(2,1)}, u32[]{:S(2)}, u32[]{:S(2)}) collective-permute-start(bf16[112,1280]{1,0:T(8,128)(2,1)} %collective-permute-done.54.refs_6_), channel_id=1, source_target_pairs={{0,1},{1,0},{2,3},{3,2},{4,5},{5,4},{6,7},{7,6},{8,9},{9,8},{10,11... | collective-permute-start | bytes 860168 | tf_op jit(solution)/shard_map/ppermute | solution.py:72
  139.8 50.2 %collective-permute-start.7 = (bf16[448,1280]{1,0:T(8,128)(2,1)}, bf16[448,1280]{1,0:T(8,128)(2,1)S(1)}, u32[]{:S(2)}, u32[]{:S(2)}) collective-permute-start(bf16[448,1280]{1,0:T(8,128)(2,1)} %bitcast.6), channel_id=1, source_target_pairs={{0,1},{1,0},{2,3},{3,2},{4,5},{5,4},{6,7},{7,6},{8,9},{9,8},{10,11... | collective-permute-start | bytes 3440648 | tf_op jit(solution)/shard_map/ppermute | solution.py:72
  147.5 20.0 %collective-permute-start.42 = (bf16[16,1280]{1,0:T(8,128)(2,1)S(1)}, bf16[16,1280]{1,0:T(8,128)(2,1)S(1)}, u32[]{:S(2)}, u32[]{:S(2)}) collective-permute-start(bf16[16,1280]{1,0:T(8,128)(2,1)S(1)} %get-tuple-element.101.refs_0_), channel_id=1, source_target_pairs={{0,1},{1,0},{2,3},{3,2},{4,5},{5,4},{6,7},{7,6},{8,9},{9,8},{10,11... | collective-permute-start | bytes 122888 | tf_op jit(solution)/shard_map/ppermute | solution.py:72
  147.5 20.0 %collective-permute-start.44 = (bf16[16,1280]{1,0:T(8,128)(2,1)S(1)}, bf16[16,1280]{1,0:T(8,128)(2,1)S(1)}, u32[]{:S(2)}, u32[]{:S(2)}) collective-permute-start(bf16[16,1280]{1,0:T(8,128)(2,1)S(1)} %collective-permute-done.43.refs_2_), channel_id=1, source_target_pairs={{0,1},{1,0},{2,3},{3,2},{4,5},{5,4},{6,7},{7,6},{8,9},{9,8},{10,11... | collective-permute-start | bytes 122888 | tf_op jit(solution)/shard_map/ppermute | solution.py:72
  150.1 17.4 %collective-permute-start.46 = (bf16[16,1280]{1,0:T(8,128)(2,1)}, bf16[16,1280]{1,0:T(8,128)(2,1)S(1)}, u32[]{:S(2)}, u32[]{:S(2)}) collective-permute-start(bf16[16,1280]{1,0:T(8,128)(2,1)} %collective-permute-done.45.refs_4_), channel_id=1, source_target_pairs={{0,1},{1,0},{2,3},{3,2},{4,5},{5,4},{6,7},{7,6},{8,9},{9,8},{10,11... | collective-permute-start | bytes 122888 | tf_op jit(solution)/shard_map/ppermute | solution.py:72
  151.1 16.5 %collective-permute-start.48 = (bf16[16,1280]{1,0:T(8,128)(2,1)}, bf16[16,1280]{1,0:T(8,128)(2,1)S(1)}, u32[]{:S(2)}, u32[]{:S(2)}) collective-permute-start(bf16[16,1280]{1,0:T(8,128)(2,1)} %collective-permute-done.47.refs_6_), channel_id=1, source_target_pairs={{0,1},{1,0},{2,3},{3,2},{4,5},{5,4},{6,7},{7,6},{8,9},{9,8},{10,11... | collective-permute-start | bytes 122888 | tf_op jit(solution)/shard_map/ppermute | solution.py:72
  178.3 15.7 %collective-permute-start.58 = (bf16[640,320]{1,0:T(8,128)(2,1)}, bf16[640,320]{1,0:T(8,128)(2,1)}, u32[]{:S(2)}, u32[]{:S(2)}) collective-permute-start(bf16[640,320]{1,0:T(8,128)(2,1)} %get-tuple-element.131), channel_id=1, source_target_pairs={{0,24},{8,16},{16,8},{24,0},{1,25},{9,17},{17,9},{25,1},{2,26},{10... | collective-permute-start | bytes 1228808 | tf_op jit(solution)/shard_map/ppermute | solution.py:72
  178.7 24.2 %collective-permute-start.57 = (bf16[640,320]{1,0:T(8,128)(2,1)}, bf16[640,320]{1,0:T(8,128)(2,1)}, u32[]{:S(2)}, u32[]{:S(2)}) collective-permute-start(bf16[640,320]{1,0:T(8,128)(2,1)} %get-tuple-element.132), channel_id=1, source_target_pairs={{0,16},{8,24},{16,0},{24,8},{1,17},{9,25},{17,1},{25,9},{2,18},{10... | collective-permute-start | bytes 1228808 | tf_op jit(solution)/shard_map/ppermute | solution.py:72
  180.3 22.6 %collective-permute-start.56 = (bf16[640,320]{1,0:T(8,128)(2,1)}, bf16[640,320]{1,0:T(8,128)(2,1)}, u32[]{:S(2)}, u32[]{:S(2)}) collective-permute-start(bf16[640,320]{1,0:T(8,128)(2,1)} %get-tuple-element.130), channel_id=1, source_target_pairs={{0,8},{8,0},{16,24},{24,16},{1,9},{9,1},{17,25},{25,17},{2,10},{10... | collective-permute-start | bytes 1228808 | tf_op jit(solution)/shard_map/ppermute | solution.py:72
  191.0 17.3 %collective-permute-start.8 = (bf16[112,1280]{1,0:T(8,128)(2,1)}, bf16[112,1280]{1,0:T(8,128)(2,1)S(1)}, u32[]{:S(2)}, u32[]{:S(2)}) collective-permute-start(bf16[112,1280]{1,0:T(8,128)(2,1)} %get-tuple-element.65), channel_id=1, source_target_pairs={{0,2},{1,3},{2,0},{3,1},{4,6},{5,7},{6,4},{7,5},{8,10},{9,11},{10,... | collective-permute-start | bytes 860168 | tf_op jit(solution)/shard_map/ppermute | solution.py:72
  191.7 23.2 %collective-permute-start.9 = (bf16[112,1280]{1,0:T(8,128)(2,1)}, bf16[112,1280]{1,0:T(8,128)(2,1)S(1)}, u32[]{:S(2)}, u32[]{:S(2)}) collective-permute-start(bf16[112,1280]{1,0:T(8,128)(2,1)} %get-tuple-element.66), channel_id=1, source_target_pairs={{0,4},{1,5},{2,6},{3,7},{4,0},{5,1},{6,2},{7,3},{8,12},{9,13},{10,... | collective-permute-start | bytes 860168 | tf_op jit(solution)/shard_map/ppermute | solution.py:72
  193.9 20.9 %collective-permute-start.10 = (bf16[112,1280]{1,0:T(8,128)(2,1)S(1)}, bf16[112,1280]{1,0:T(8,128)(2,1)S(1)}, u32[]{:S(2)}, u32[]{:S(2)}) collective-permute-start(bf16[112,1280]{1,0:T(8,128)(2,1)S(1)} %get-tuple-element.67), channel_id=1, source_target_pairs={{0,6},{1,7},{2,4},{3,5},{4,2},{5,3},{6,0},{7,1},{8,14},{9,15},{10,... | collective-permute-start | bytes 860168 | tf_op jit(solution)/shard_map/ppermute | solution.py:72
  (74 other events, 777.5 us)

commit v2 on v1

v2 whole, which is shorter than its diff:
```python
import math

import jax
import jax.numpy as jnp
from jax import lax
from jax.experimental import pallas as pl
from jax.experimental.pallas import tpu as pltpu
from jax.sharding import PartitionSpec as P

CAP = 2
LANES = 128
epsilon = 1e-06
half_root = 1.0 / math.sqrt(2.0)
bell_scale = 1.0 / math.sqrt(2.0 * math.pi)
LOG2E = math.log2(math.e)
f32 = jnp.float32
bf16 = jnp.bfloat16


def norm_parts(row_block):
    widened = row_block.astype(f32)
    center = widened - jnp.mean(widened, axis=-1, keepdims=True)
    factor = lax.rsqrt(jnp.mean(center * center, axis=-1, keepdims=True) + epsilon)
    return (center * factor, factor)


def norm_back(normal_rows, factor, upstream):
    mean_up = jnp.mean(upstream, axis=-1, keepdims=True)
    mean_mix = jnp.mean(upstream * normal_rows, axis=-1, keepdims=True)
    return factor * (upstream - mean_up - normal_rows * mean_mix)


def dot(a, b):
    return lax.dot_general(a, b, (((1,), (0,)), ((), ())), preferred_element_type=f32)


def dot_nt(a, b):
    return lax.dot_general(a, b, (((1,), (1,)), ((), ())), preferred_element_type=f32)


def dot_tn(a, b):
    return lax.dot_general(a, b, (((0,), (0,)), ((), ())), preferred_element_type=f32)


def run(body, outs, ins, name, flops=0, mib=48, smem=(), loose=0, scratch=()):
    specs = [
        pl.BlockSpec(
            memory_space=pl.ANY if i < loose else pltpu.SMEM if i in smem else pltpu.VMEM
        )
        for i in range(len(ins))
    ]
    sizes = [math.prod(x.shape) * x.dtype.itemsize for x in list(ins) + list(outs)]
    return pl.pallas_call(
        body,
        out_shape=list(outs),
        in_specs=specs,
        out_specs=[pl.BlockSpec(memory_space=pltpu.VMEM)] * len(outs),
        scratch_shapes=list(scratch),
        compiler_params=pltpu.CompilerParams(vmem_limit_bytes=mib * 2**20),
        cost_estimate=pl.CostEstimate(
            flops=int(flops), bytes_accessed=int(sum(sizes)), transcendentals=0
        ),
        name=name,
    )(*ins)


def after(x, *others):
    return lax.optimization_barrier((x, others))[0]


def pull(pairs, sems):
    copies = [pltpu.make_async_copy(a, b, sems.at[i]) for i, (a, b) in enumerate(pairs)]
    for c in copies:
        c.start()
    for c in copies:
        c.wait()


def shape(dims, dtype=bf16):
    return jax.ShapeDtypeStruct(tuple(dims), dtype)


def block_of(rows, most=256):
    return max(b for b in range(16, most + 1, 16) if rows % b == 0)


def hop(x, axis, mask):
    size = lax.axis_size(axis)
    return lax.ppermute(x, axis, [(i, i ^ mask) for i in range(size)])


def gather_rel(x, hold=None, firm=()):
    size = lax.axis_size("tensor")
    have = {0: x}
    odd = {}
    mask = size // 2
    while mask > 1:
        have.update({k ^ mask: hop(y, "tensor", mask) for k, y in list(have.items())})
        mask //= 2
    if hold is not None:
        held = hold(have)
        last = size - 2
        have[last] = after(have[last], held)
    return [hop(have[k - 1], "tensor", 1) if k % 2 else have[k] for k in range(size)]


def fold_order(count):
    keys = range(0, count, 2)
    return sorted(keys, key=lambda k: tuple((k >> b) & 1 for b in range(1, 8)))


def prologue_body(tok_in, cot_in, group, gate_t, routes_t, slots_t, *outs):
    normed_o, cot_o, tok_o, perm_o, pick0_o, pick1_o, link_o, gout_o, tok, cot, sems = outs
    half = tok.shape[0] // 2
    pairs = [(tok_in, tok), (cot_in, cot)]
    copies = [
        pltpu.make_async_copy(
            a.at[i * half : (i + 1) * half], b.at[i * half : (i + 1) * half], sems.at[2 * n + i]
        )
        for n, (a, b) in enumerate(pairs)
        for i in range(2)
    ]
    for c in copies:
        c.start()
    rows = tok.shape[0]
    places = pick0_o.shape[1]
    code_t = jnp.where(slots_t[...] >= 0, (routes_t[...] ^ group[0]) * CAP + slots_t[...], -1)
    packed = jnp.concatenate(
        [code_t.astype(f32), gate_t[...], jnp.zeros((4, rows), f32)], axis=0
    ).T
    code = packed[:, 0:2].astype(jnp.int32)
    gate = packed[:, 2:4]
    lane = lax.broadcasted_iota(jnp.int32, (rows, LANES), 1)
    wide0 = (code[:, 0:1] == lane).astype(f32)
    wide1 = (code[:, 1:2] == lane).astype(f32)
    kept0 = (code[:, 0:1] >= 0).astype(f32)
    prim = wide0 + wide1 * (1.0 - kept0)
    plain = 1.0 - jnp.sum(prim, axis=1, keepdims=True)
    open_at = 1.0 - jnp.sum(prim, axis=0, keepdims=True)
    ri = lax.broadcasted_iota(jnp.int32, (rows, rows), 0)
    ci = lax.broadcasted_iota(jnp.int32, (rows, rows), 1)
    row_rank = dot(
        (ci < ri).astype(bf16), jnp.broadcast_to(plain, (rows, rows)).astype(bf16)
    )
    place_rank = dot(
        jnp.broadcast_to(open_at, (rows, rows)).astype(bf16), (ri < ci).astype(bf16)
    )
    filler = plain * open_at * (row_rank == place_rank).astype(f32)
    perm = (prim + filler).astype(bf16)
    perm_o[...] = perm
    for c in copies:
        c.wait()
    normal, _ = norm_parts(tok[...])
    normed_o[...] = dot_tn(perm, normal.astype(bf16)).astype(bf16)
    cot_o[...] = dot_tn(perm, cot[...]).astype(bf16)
    tok_o[...] = dot_tn(perm, tok[...]).astype(bf16)
    pick0 = wide0.astype(bf16)
    pick1 = wide1.astype(bf16)
    pick0_o[...] = pick0[:, :places]
    pick1_o[...] = pick1[:, :places]
    link_o[...] = dot_tn((pick0 + pick1), prim.astype(bf16))[:places, :places].astype(bf16)
    upstream = cot[...].astype(f32)
    g0 = (gate[:, 0:1] * upstream).astype(bf16)
    g1 = (gate[:, 1:2] * upstream).astype(bf16)
    gout_o[...] = (dot_tn(pick0, g0) + dot_tn(pick1, g1))[:places].astype(bf16)


def make_prep(heads, size):
    def body(w, p, wo, po):
        wo[...] = jnp.zeros_like(wo)
        po[...] = jnp.zeros_like(po)
        for h in range(heads):
            for i in range(3):
                at = (3 * h + i) * LANES
                wo[at : at + size] = w[h, i * size : (i + 1) * size]
            po[h * LANES : h * LANES + size] = p[h]

    return body


def spare_lanes(dims, size):
    lane = lax.broadcasted_iota(jnp.int32, dims, 1) % LANES
    return (lane >= size) & (lane < size + 3)


def with_term(rows, term, size):
    lane = lax.broadcasted_iota(jnp.int32, rows.shape, 1)
    first = term.astype(bf16).astype(f32)
    second = (term - first).astype(bf16).astype(f32)
    third = term - first - second
    term = jnp.where(lane == size, first, jnp.where(lane == size + 1, second, third))
    return jnp.where(spare_lanes(rows.shape, size), term, rows.astype(f32)).astype(bf16)


def project(rows, weights, heads, size, scale):
    raw = dot_nt(rows, weights)
    part = lax.broadcasted_iota(jnp.int32, raw.shape, 1) // LANES % 3
    factor = jnp.where(part == 0, scale * LOG2E, 1.0)
    ones = ((part != 0) & spare_lanes(raw.shape, size)).astype(f32)
    return (raw * factor + ones).astype(bf16)


def attend(queries, keys, values, size):
    raised = jnp.exp2(dot_nt(queries, keys))
    total = jnp.sum(raised, axis=-1, keepdims=True)
    shares = raised * (1.0 / total)
    return dot(shares.astype(bf16), values).astype(bf16), with_term(queries, -jnp.log2(total), size)


def part_of(ref, rows, which, head):
    at = (3 * head + which) * LANES
    return ref[rows, at : at + LANES]


def pieces_of(ref, first, count, every, lo, hi, at):
    return jnp.concatenate(
        [ref[(first + k) * every + lo : (first + k) * every + hi, at] for k in range(count)], axis=0
    )


def make_half(count, heads, size, scale):
    def body(*refs):
        shards, (weights, qkv, fn_t, fn, sems) = refs[:count], refs[count:]
        rows = shards[0].shape[0]
        pull([(shards[k], fn.at[k * rows : (k + 1) * rows]) for k in range(count)], sems)
        for k in range(count):
            at = slice(k * rows, (k + 1) * rows)
            fn_t[:, at] = fn[at, :].T
        step = block_of(fn.shape[0])

        def chunk(i, _):
            at = pl.ds(pl.multiple_of(i * step, 16), step)
            qkv[at, :] = project(fn[at, :], weights[...], heads, size, scale)
            return 0

        lax.fori_loop(0, fn.shape[0] // step, chunk, 0)

    return body


def make_turn(count):
    def body(*refs):
        shards, fn_t = refs[:count], refs[count]
        rows = shards[0].shape[0]
        for k in range(count):
            fn_t[:, k * rows : (k + 1) * rows] = shards[k][...].T

    return body


def make_front(count, places, heads, size, scale):
    def body(*refs):
        half = count // 2
        shards, (first, weights, proj) = refs[:half], refs[half : half + 3]
        qkv, ctx, ask, even, odd, fn, sems = refs[half + 3 :]
        rows = shards[0].shape[0]
        pull([(shards[k], fn.at[k * rows : (k + 1) * rows]) for k in range(half)], sems)
        done = first.shape[0]
        qkv[:done] = first[...]
        step = block_of(fn.shape[0])

        def chunk(i, _):
            at = pl.ds(pl.multiple_of(i * step, 16), step)
            to = pl.ds(pl.multiple_of(done + i * step, 16), step)
            qkv[to, :] = project(fn[at, :], weights[...], heads, size, scale)
            return 0

        lax.fori_loop(0, fn.shape[0] // step, chunk, 0)
        every = slice(None)
        for h in range(heads):
            cut = slice(h * LANES, (h + 1) * LANES)
            queries = pieces_of(
                qkv, 0, count, rows, 0, places, slice(3 * h * LANES, (3 * h + 1) * LANES)
            )
            ctx[:, cut], ask[:, cut] = attend(
                queries, part_of(qkv, every, 1, h), part_of(qkv, every, 2, h), size
            )
        part = dot(ctx[...], proj[...]).astype(bf16)
        for i, k in enumerate(range(0, count, 2)):
            even[i * places : (i + 1) * places] = part[k * places : (k + 1) * places]
            odd[i * places : (i + 1) * places] = part[(k + 1) * places : (k + 2) * places]

    return body


def make_cold(count, places, heads, size):
    def body(qkv, proj, ctx, ask, even, odd):
        rows = qkv.shape[0] // count
        cold = rows - places
        every = slice(None)
        group = min(4, count)
        order = fold_order(count)
        for first in range(0, count, group):
            at = slice(first * cold, (first + group) * cold)
            for h in range(heads):
                cut = slice(h * LANES, (h + 1) * LANES)
                queries = pieces_of(
                    qkv, first, group, rows, places, rows, slice(3 * h * LANES, (3 * h + 1) * LANES)
                )
                ctx[at, cut], ask[at, cut] = attend(
                    queries, part_of(qkv, every, 1, h), part_of(qkv, every, 2, h), size
                )
            part = dot(ctx[at, :], proj[...]).astype(bf16)
            for k in range(first, first + group):
                to = odd if k % 2 else even
                i = order.index(k // 2 * 2)
                to[i * cold : (i + 1) * cold] = part[(k - first) * cold : (k - first + 1) * cold]

    return body


def back_block(ask, keys, values, ctx, grad_ctx, size):
    shares = jnp.exp2(dot_nt(ask, keys))
    mix = jnp.sum(grad_ctx.astype(f32) * ctx.astype(f32), axis=-1, keepdims=True)
    grad_ctx = with_term(grad_ctx, -mix, size)
    grad_scores = (shares * dot_nt(grad_ctx, values)).astype(bf16)
    return (
        dot(grad_scores, keys),
        dot_tn(ask, grad_scores),
        dot_tn(grad_ctx, shares.astype(bf16)),
    )


def make_cold_back(count, places, heads, size, scale):
    def body(*refs):
        shards, (qkv, proj, ctx, ask) = refs[:count], refs[count : count + 4]
        gq, gk, gv, gp, cots, sems = refs[count + 4 :]
        cold = shards[0].shape[0]
        pull([(shards[k], cots.at[k * cold : (k + 1) * cold]) for k in range(count)], sems)
        every = slice(None)
        group = min(4, count)
        for first in range(0, count, group):
            at = slice(first * cold, (first + group) * cold)
            grad_ctx = dot_nt(cots[at, :], proj[...]).astype(bf16)
            proj_grad = dot_tn(ctx[at, :], cots[at, :])
            for h in range(heads):
                cut = slice(h * LANES, (h + 1) * LANES)
                a, b, c = back_block(
                    ask[at, cut],
                    part_of(qkv, every, 1, h),
                    part_of(qkv, every, 2, h),
                    ctx[at, cut],
                    grad_ctx[:, cut],
                    size,
                )
                gq[at, cut] = (a * scale).astype(bf16)
                if first:
                    gk[cut, :] += b
                    gv[cut, :] += c
                else:
                    gk[cut, :] = b
                    gv[cut, :] = c
            if first:
                gp[...] += proj_grad
            else:
                gp[...] = proj_grad

    return body


def make_hot_back(count, heads, size, groups, scale):
    def body(*refs):
        shards = refs[:count]
        place, qkv, proj, ctx, ask, gq, gk, gv, gp, fn_a, fn_b = refs[count : count + 11]
        outs = refs[count + 11 : count + 11 + groups]
        rows_t, grad_q, whole = refs[count + 11 + groups :]
        grads = jnp.concatenate([s[...] for s in shards], axis=0)
        places = shards[0].shape[0]
        rows = qkv.shape[0] // count
        cold = rows - places
        grad_ctx = dot_nt(grads, proj[...]).astype(bf16)
        proj_grad = gp[...] + dot_tn(ctx[...], grads)
        base = heads * 3 * size
        every = slice(None)
        proj_rows = []
        for h in range(heads):
            cut = slice(h * LANES, (h + 1) * LANES)
            a, b, c = back_block(
                ask[:, cut],
                part_of(qkv, every, 1, h),
                part_of(qkv, every, 2, h),
                ctx[:, cut],
                grad_ctx[:, cut],
                size,
            )
            a = (a * scale).astype(bf16)
            for k in range(count):
                grad_q[k * rows : k * rows + places] = a[k * places : (k + 1) * places]
                grad_q[k * rows + places : (k + 1) * rows] = gq[k * cold : (k + 1) * cold, cut]
            at = h * 3 * size
            rows_t[at : at + size, :] = grad_q[...].T[:size]
            rows_t[at + size : at + 2 * size, :] = ((gk[cut, :] + b) * (1.0 / LOG2E))[
                :size
            ].astype(bf16)
            rows_t[at + 2 * size : at + 3 * size, :] = (gv[cut, :] + c)[:size].astype(bf16)
            proj_rows.append(proj_grad[h * LANES : h * LANES + size].astype(bf16))
        done = fn_a.shape[1]
        turned = rows_t[...].T
        whole[:, :base] = (dot(fn_a[...], turned[:done]) + dot(fn_b[...], turned[done:])).astype(
            bf16
        )
        whole[:, base:] = jnp.concatenate(proj_rows, axis=0).T
        each = whole.shape[0] // groups
        for g in range(groups):
            at = pl.multiple_of((place[0] ^ g) * each, 16)
            outs[g][...] = whole[pl.ds(at, each), :]

    return body


def make_last(heads, size, groups):
    def body(*refs):
        parts, (qkv_o, proj_o) = refs[:groups], refs[groups:]
        total = total_of(parts)
        base = heads * 3 * size
        turned = total[:, base:].T
        for h in range(heads):
            qkv_o[:, h, :] = total[:, h * 3 * size : (h + 1) * 3 * size]
            proj_o[h] = turned[h * size : (h + 1) * size]

    return body


def make_fold(count):
    def body(mine, theirs, *outs):
        rows = outs[0].shape[0]
        for i in range(count):
            at = slice(i * rows, (i + 1) * rows)
            outs[i][...] = (mine[at].astype(f32) + theirs[at].astype(f32)).astype(bf16)

    return body


def total_of(refs):
    total = refs[0][...].astype(f32)
    for r in refs[1:]:
        total = total + r[...].astype(f32)
    return total


def make_mid(count, groups):
    def body(*refs):
        parts, (tok, link) = refs[:count], refs[count : count + 2]
        mid_o, normal_o, factor_o = refs[count + 2 : count + 5]
        outs = refs[count + 5 :]
        mid = (tok[...].astype(f32) + total_of(parts)).astype(bf16)
        normal, factor = norm_parts(mid)
        mid_o[...] = mid
        normal_o[...] = normal
        factor_o[...] = factor
        slot_in = dot(link[...], normal.astype(bf16))
        each = slot_in.shape[0] // groups
        for g in range(groups):
            outs[g][...] = slot_in[g * each : (g + 1) * each].astype(bf16)

    return body


def slot_mask(rows, experts, e):
    row = lax.broadcasted_iota(jnp.int32, (rows, 1), 0)
    return (row // CAP) % experts == e


def make_expert_grad(count, experts):
    def body(*refs):
        shards, down, grads, out = refs[:count], refs[count], refs[count + 1], refs[count + 2]
        grads[...] = jnp.concatenate([s[...] for s in shards], axis=0)
        for e in range(experts):
            out[e] = dot_nt(grads[...], down[e])

    return body


def make_expert(count, experts):
    def body(*refs):
        shards = refs[:count]
        up, down, grad_hidden, arrived, hid_o, pre_o, even, odd = refs[count:]
        arrived[...] = jnp.concatenate([s[...] for s in shards], axis=0)
        rows = arrived.shape[0]
        forth = None
        back = None
        for e in range(experts):
            keep = slot_mask(rows, experts, e)
            pre = dot(arrived[...], up[e])
            cdf = 0.5 * (1.0 + lax.erf(pre * half_root))
            hidden = jnp.where(keep, pre * cdf, 0.0).astype(bf16)
            slope = cdf + pre * jnp.exp(-0.5 * pre * pre) * bell_scale
            grad_pre = jnp.where(keep, grad_hidden[e] * slope, 0.0).astype(bf16)
            hid_o[e] = hidden
            pre_o[e] = grad_pre
            a = dot(hidden, down[e])
            b = dot_nt(grad_pre, up[e])
            forth = a if forth is None else forth + a
            back = b if back is None else back + b
        both = jnp.concatenate([back, forth], axis=1).astype(bf16)
        each = rows // count
        for k in range(count):
            to = odd if k % 2 else even
            to[(k // 2) * each : (k // 2 + 1) * each] = both[k * each : (k + 1) * each]

    return body


def make_weight_grads(experts):
    def body(arrived, grads, hidden, grad_pre, up_o, down_o):
        for e in range(experts):
            up_o[e] = dot_tn(arrived[...], grad_pre[e]).astype(bf16)
            down_o[e] = dot_tn(hidden[e], grads[...]).astype(bf16)

    return body


def make_split(count, groups):
    def body(*refs):
        parts, outs = refs[:count], refs[count:]
        total = total_of(parts)
        each = total.shape[0] // groups
        for g in range(groups):
            outs[g][...] = total[g * each : (g + 1) * each].astype(bf16)

    return body


def make_mid_back(groups):
    def body(*refs):
        parts = refs[:groups]
        link, cot, normal, factor, grad_o, expert_o = refs[groups:]
        both = jnp.concatenate([p[...].astype(f32) for p in parts], axis=0).astype(bf16)
        width = cot.shape[1]
        expert_o[...] = both[:, width:]
        grad_norm = dot_tn(link[...], both[:, :width])
        grad_o[...] = (
            cot[...].astype(f32) + norm_back(normal[...], factor[...], grad_norm)
        ).astype(bf16)

    return body


def make_epilogue(count):
    def body(*refs):
        parts = refs[:count]
        tok, mid_hot, perm, pick0, pick1, experts, gate_t, cot, out, gate_o = refs[count:]
        cold = (tok[...].astype(f32) + total_of(parts)).astype(bf16)
        ordered = jnp.concatenate([mid_hot[...], cold], axis=0)
        mid = dot(perm[...], ordered)
        gate = jnp.concatenate([gate_t[...], jnp.zeros((6, gate_t.shape[1]), f32)], axis=0).T
        first = dot(pick0[...], experts[...])
        second = dot(pick1[...], experts[...])
        out[...] = (mid + gate[:, 0:1] * first + gate[:, 1:2] * second).astype(bf16)
        upstream = cot[...].astype(f32)
        lane = lax.broadcasted_iota(jnp.int32, (upstream.shape[0], LANES), 1)
        one = jnp.sum(upstream * first, axis=-1, keepdims=True)
        two = jnp.sum(upstream * second, axis=-1, keepdims=True)
        gate_o[...] = jnp.where(lane == 0, one, two).T[:2]

    return body


def fold_scatter(even, odd, rows, name):
    count = lax.axis_size("tensor") // 2
    theirs = hop(odd, "tensor", 1)
    sums = run(
        make_fold(count), [shape((rows, even.shape[1]))] * count, [even, theirs], name, mib=24
    )
    return [sums[0]] + [hop(sums[i], "tensor", 2 * i) for i in range(1, count)]


def halving_scatter(even, odd, name):
    mine, mask, theirs = even, 1, odd
    while True:
        theirs = hop(theirs, "tensor", mask)
        if mine.shape[0] == even.shape[0] * 2 // lax.axis_size("tensor"):
            return [mine, theirs]
        half = (mine.shape[0] // 2, mine.shape[1])
        mine, theirs = run(
            make_fold(2), [shape(half), shape(half)], [mine, theirs], f"{name}_{mask}", mib=24
        )
        mask *= 2


def shards(
    tokens,
    cotangent,
    gate_weights,
    routes,
    slot_index,
    qkv_weight,
    proj_weight,
    up_weight,
    down_weight,
):
    rows, width = tokens.shape
    heads, size = qkv_weight.shape[1], qkv_weight.shape[2] // 3
    scale = size ** (-0.5)
    groups = lax.axis_size("dp")
    count = lax.axis_size("tensor")
    experts, _, hidden_dev = up_weight.shape
    each = experts * CAP
    places = groups * each
    cold = rows - places
    hot_all = count * places
    total = count * rows
    slots = count * places

    wqkv, proj = run(
        make_prep(heads, size),
        [shape((heads * 3 * LANES, width)), shape((heads * LANES, width))],
        [qkv_weight.transpose(1, 2, 0), proj_weight],
        "prep",
        mib=24,
    )
    group = (lax.axis_index("dp") * experts).astype(jnp.int32).reshape(1)
    normed, cot, tok, perm, pick0, pick1, link, grad_out = run(
        prologue_body,
        [
            shape((rows, width)),
            shape((rows, width)),
            shape((rows, width)),
            shape((rows, rows)),
            shape((rows, places)),
            shape((rows, places)),
            shape((places, places)),
            shape((places, width)),
        ],
        [tokens, cotangent, group, gate_weights.T, routes.T, slot_index.T],
        "prologue",
        smem=(2,),
        loose=2,
        mib=24,
        scratch=[
            pltpu.VMEM((rows, width), bf16),
            pltpu.VMEM((rows, width), bf16),
            pltpu.SemaphoreType.DMA((4,)),
        ],
    )
    half = count // 2
    cot_cold = cot[places:]

    def first_half(have):
        near = [
            hop(have[k - 1], "tensor", 1) if k % 2 else have[k] for k in range(half)
        ]
        return run(
            make_half(half, heads, size, scale),
            [shape((half * rows, heads * 3 * LANES)), shape((width, half * rows))],
            near + [wqkv],
            "half",
            flops=2 * half * rows * width * heads * 3 * LANES,
            loose=half,
            mib=40,
            scratch=[
                pltpu.VMEM((half * rows, width), bf16),
                pltpu.SemaphoreType.DMA((half,)),
            ],
        )

    box = []

    def hold(have):
        box.append((have, first_half(have)))
        return box[0][1]

    normed_all = gather_rel(normed, hold)
    have, (qkv_a, fn_a) = box[0]

    pieces = [grad_out[g * each : (g + 1) * each] for g in range(groups)]
    landed = jnp.concatenate(
        [pieces[0]] + [hop(pieces[g], "dp", g) for g in range(1, groups)], axis=0
    )
    grads_all = gather_rel(landed)
    slot_grads, grad_hidden = run(
        make_expert_grad(count, experts),
        [shape((slots, width)), shape((experts, slots, hidden_dev), f32)],
        grads_all + [down_weight],
        "slot_grads",
        flops=2 * slots * width * hidden_dev * experts,
        mib=24,
    )
    far = count // 2
    cots = {0: cot_cold}
    mask = 2
    while mask < far:
        cots.update({k ^ mask: hop(y, "tensor", mask) for k, y in list(cots.items())})
        mask *= 2
    near_cots = list(cots.values())

    qkv, ctx_hot, ask_hot, even, odd = run(
        make_front(count, places, heads, size, scale),
        [
            shape((total, heads * 3 * LANES)),
            shape((hot_all, heads * LANES)),
            shape((hot_all, heads * LANES)),
            shape((hot_all // 2, width)),
            shape((hot_all // 2, width)),
        ],
        after(normed_all[half:], grad_hidden, near_cots) + [qkv_a, wqkv, proj],
        "front",
        flops=2 * total * width * heads * 3 * LANES,
        loose=half,
        scratch=[
            pltpu.VMEM((half * rows, width), bf16),
            pltpu.SemaphoreType.DMA((half,)),
        ],
    )
    cots[far] = hop(after(cot_cold, have[far]), "tensor", far)
    odd = after(odd, cots[far])
    hot_sums = fold_scatter(even, odd, places, "fold_hot")

    outs = run(
        make_mid(count // 2, groups),
        [shape((places, width)), shape((places, width), f32), shape((places, 1), f32)]
        + [shape((each, width))] * groups,
        hot_sums + [tok[:places], link],
        "mid_hot",
        mib=16,
    )
    mid_hot, normal_hot, factor_hot = outs[:3]
    pieces = outs[3:]

    ctx_cold, ask_cold, even_cold, odd_cold = run(
        make_cold(count, places, heads, size),
        [
            shape((count * cold, heads * LANES)),
            shape((count * cold, heads * LANES)),
            shape((count * cold // 2, width)),
            shape((count * cold // 2, width)),
        ],
        [after(qkv, mid_hot), proj],
        "cold",
        flops=4 * total * total * heads * LANES,
    )
    start = after(cots[far], mid_hot)
    rest = {far: start}
    mask = 2
    while mask < far:
        rest.update({k ^ mask: hop(y, "tensor", mask) for k, y in list(rest.items())})
        mask *= 2
    cots.update(rest)
    landed = jnp.concatenate(
        [pieces[0]] + [hop(pieces[g], "dp", g) for g in range(1, groups)], axis=0
    )
    landed = after(landed, ctx_cold, list(cots.values()))
    arrived_all = gather_rel(landed)
    arrived, hidden, grad_pre, even, odd = run(
        make_expert(count, experts),
        [
            shape((slots, width)),
            shape((experts, slots, hidden_dev)),
            shape((experts, slots, hidden_dev)),
            shape((slots // 2, 2 * width)),
            shape((slots // 2, 2 * width)),
        ],
        arrived_all + [up_weight, down_weight, grad_hidden],
        "experts",
        flops=6 * slots * width * hidden_dev * experts,
        mib=32,
    )
    sums = fold_scatter(even, odd, places, "fold_slots")

    pieces = run(
        make_split(count // 2, groups),
        [shape((each, 2 * width))] * groups,
        sums,
        "split_slots",
        mib=16,
    )
    back = [pieces[0]] + [hop(pieces[g], "dp", g) for g in range(1, groups)]
    cot_all = [hop(cots[k - 1], "tensor", 1) if k % 2 else cots[k] for k in range(count)]
    gq, gk, gv, gp = run(
        make_cold_back(count, places, heads, size, scale),
        [
            shape((count * cold, heads * LANES)),
            shape((heads * LANES, total), f32),
            shape((heads * LANES, total), f32),
            shape((heads * LANES, width), f32),
        ],
        cot_all + [after(qkv, pieces[0]), proj, ctx_cold, ask_cold],
        "cold_back",
        flops=10 * total * total * heads * LANES,
        loose=count,
        scratch=[
            pltpu.VMEM((count * cold, width), bf16),
            pltpu.SemaphoreType.DMA((count,)),
        ],
    )
    back = after(back, gp)
    grad_hot, expert_out = run(
        make_mid_back(groups),
        [shape((places, width)), shape((places, width))],
        back + [link, cot[:places], normal_hot, factor_hot],
        "mid_back",
        mib=16,
    )
    box.clear()

    def turn(_):
        box.append(
            run(
                make_turn(half),
                [shape((width, half * rows))],
                after(normed_all[half:], grad_hot),
                "turn",
                mib=24,
            )[0]
        )
        return box[0]

    grad_hot_all = gather_rel(grad_hot, turn)
    fn_b = box[0]
    cold_sums = halving_scatter(even_cold, after(odd_cold, grad_hot_all), "fold_cold")

    me = lax.axis_index("dp").astype(jnp.int32).reshape(1)
    pieces = run(
        make_hot_back(count, heads, size, groups, scale),
        [shape((width // groups, heads * 4 * size))] * groups,
        grad_hot_all + [me, qkv, proj, ctx_hot, ask_hot, gq, gk, gv, gp, fn_a, fn_b],
        "hot_back",
        flops=2 * total * width * heads * 3 * LANES,
        smem=(count,),
        scratch=[
            pltpu.VMEM((heads * 3 * size, total), bf16),
            pltpu.VMEM((total, LANES), bf16),
            pltpu.VMEM((width, heads * 4 * size), bf16),
        ],
    )
    grad_up, grad_down = run(
        make_weight_grads(experts),
        [shape(up_weight.shape), shape(down_weight.shape)],
        [after(arrived, pieces[0]), slot_grads, hidden, grad_pre],
        "weight_grads",
        flops=4 * slots * width * hidden_dev * experts,
        mib=32,
    )
    parts = [pieces[0]] + [hop(pieces[g], "dp", g) for g in range(1, groups)]
    layer_out, gate_grad = run(
        make_epilogue(2),
        [shape((rows, width)), shape((2, rows), f32)],
        cold_sums
        + [tok[places:], mid_hot, perm, pick0, pick1, expert_out, gate_weights.T, cotangent],
        "epilogue",
        mib=24,
    )
    grad_qkv, grad_proj = run(
        make_last(heads, size, groups),
        [shape((width // groups, heads, 3 * size), f32), shape((heads, size, width // groups), f32)],
        after(parts, layer_out, grad_up),
        "last",
        mib=24,
    )
    return (layer_out, gate_grad.T, grad_qkv, grad_proj, grad_up, grad_down)


def solution(mesh):
    return jax.shard_map(
        shards,
        mesh=mesh,
        in_specs=(
            P(("dp", "tensor"), None),
            P(("dp", "tensor"), None),
            P(("dp", "tensor"), None),
            P(("dp", "tensor"), None),
            P(("dp", "tensor"), None),
            P(None, "tensor", None),
            P("tensor", None, None),
            P("dp", None, "tensor"),
            P("dp", "tensor", None),
        ),
        out_specs=(
            P(("dp", "tensor"), None),
            P(("dp", "tensor"), None),
            P("dp", "tensor", None),
            P("tensor", None, "dp"),
            P("dp", None, "tensor"),
            P("dp", "tensor", None),
        ),
        check_vma=False,
    )
```

time: 220 us -> 184 us (0.84); the launches traced: 217 us -> 183 us
  local copies, waits for them, and re-layouts: 39 us -> 15.8 us
  starting transfers between devices: 58 us -> 46.6 us
  waiting for transfers between devices: 76 us -> 78.3 us
    ppermute x59 -> x58, starting transfers between devices: 58 us -> 46.6 us  [hop(): return lax.ppermute(x, axis, [(i, i ^ mask) for i in range(size)])]
    unnamed x99 -> x92, local copies, waits for them, and re-layouts: 26.1 us -> 15.8 us
    reshape x1 -> x0, local copies, waits for them, and re-layouts: 4 us -> none  [shards(): wqkv = jnp.pad(qkv_weight.reshape(width, heads, 3, size), ((0, 0), (0, 0)...]
    slice x5 -> x1, local copies, waits for them, and re-layouts: 2.86 us -> 0.02 us  [shards(): cot_cold = cot[places:]]
    pad x2 -> x0, local copies, waits for them, and re-layouts: 2.74 us -> none  [the longest x1 2.7 us: shards(): jnp.pad(qkv_weight.reshape(width, heads, 3, size), ((0, 0), (0, 0), (0, 0...]
    squeeze x1 -> x0, local copies, waits for them, and re-layouts: 2.53 us -> none  [shards(): piece = lax.dynamic_index_in_dim(sums, me ^ g, 0, False)]
    ppermute x59 -> x58, waiting for transfers between devices: 76 us -> 78.3 us  [hop(): return lax.ppermute(x, axis, [(i, i ^ mask) for i in range(size)])]
    pallas_call x15 -> x20, Pallas kernels: 40.9 us -> 41.1 us  [run(): pl.pallas_call(body, out_shape=list(outs), in_specs=specs, out_specs=[pl....]
  transfers between devices with their start and end apart: 59 -> 58, of which waited for: 16 -> 23; matrix products, arithmetic and copies ran while one was open for 8% -> 0% of each run, Pallas kernels for 14% -> 19%
where the time goes in v2:
time: 184 us; the launch traced here: 183 us
  waiting for transfers between devices  78.3 us (43%)
  starting transfers between devices  46.6 us (25%)
  Pallas kernels  41.1 us (22%)
  local copies, waits for them, and re-layouts  15.8 us (9%)
    ppermute x58, waiting for transfers between devices, hop(): return lax.ppermute(x, axis, [(i, i ^ mask) for i in range(size)])  78.3 us
    ppermute x58, starting transfers between devices, hop(): return lax.ppermute(x, axis, [(i, i ^ mask) for i in range(size)])  46.6 us
    pallas_call x20, Pallas kernels, run(): pl.pallas_call(body, out_shape=list(outs), in_specs=specs, out_specs=[pl....  41.1 us
    unnamed x92, local copies, waits for them, and re-layouts  15.8 us
  transfers between devices with their start and end apart: 58, of which 23 were waited for; matrix products, arithmetic and copies ran while one was open for 0% of the time, Pallas kernels for 19%

profile of v2, /device:TPU:0, one launch (start us, length us, event | category | flops | bytes accessed | tf_op | source)
XLA Modules:
  0.0 183.1 jit_solution(16689037666821047524)
XLA Ops:
  4.6 2.2 %prologue.1 = (bf16[128,1280]{1,0:T(8,128)(2,1)S(1)}, bf16[128,1280]{1,0:T(8,128)(2,1)S(1)}, bf16[128,1280]{1,0:T(8,128)(2,1)S(1)}, bf16[128,128]{1,0:T(8,128)(2...) custom-call(bf16[128,1280]{1,0:T(8,128)(2,1)S(1)} %copy-done.10, ...), custom_call_target="tpu_custom_call" | custom-call | bytes 1723908 | tf_op jit(solution)/shard_map/prologue/pallas_call | solution.py:53
  6.8 3.1 %collective-permute-start.4 = (bf16[128,1280]{1,0:T(8,128)(2,1)S(1)}, bf16[128,1280]{1,0:T(8,128)(2,1)S(1)}, u32[]{:S(2)}, u32[]{:S(2)}) collective-permute-start(bf16[128,1280]{1,0:T(8,128)(2,1)S(1)} %get-tuple-element.99.refs_0_), channel_id=1, source_target_pairs={{0,2},{1,3},{2,0},{3,1},{4,6},{5,7},{6,4},{7,5},{8,10},{9,11},{10,... | collective-permute-start | bytes 983048 | tf_op jit(solution)/shard_map/ppermute | solution.py:89
  9.9 2.6 %collective-permute-start = (bf16[128,1280]{1,0:T(8,128)(2,1)S(1)}, bf16[128,1280]{1,0:T(8,128)(2,1)S(1)}, u32[]{:S(2)}, u32[]{:S(2)}) collective-permute-start(bf16[128,1280]{1,0:T(8,128)(2,1)S(1)} %get-tuple-element.99.refs_0_), channel_id=1, source_target_pairs={{0,4},{1,5},{2,6},{3,7},{4,0},{5,1},{6,2},{7,3},{8,12},{9,13},{10,... | collective-permute-start | bytes 983048 | tf_op jit(solution)/shard_map/ppermute | solution.py:89
  12.5 12.0 %collective-permute-done.4.refs_2_ = bf16[128,1280]{1,0:T(8,128)(2,1)S(1)} collective-permute-done((bf16[128,1280]{1,0:T(8,128)(2,1)S(1)}, bf16[128,1280]{1,0:T(8,128)(2,1)S(1)}, u32[]{:S(2)}, u32[]{:S(2)}) %collective-permute-start.4) | collective-permute-done | bytes 327712 | tf_op jit(solution)/shard_map/ppermute | solution.py:89
  24.5 2.5 %collective-permute-done.refs_0_ = bf16[128,1280]{1,0:T(8,128)(2,1)S(1)} collective-permute-done((bf16[128,1280]{1,0:T(8,128)(2,1)S(1)}, bf16[128,1280]{1,0:T(8,128)(2,1)S(1)}, u32[]{:S(2)}, u32[]{:S(2)}) %collective-permute-start) | collective-permute-done | bytes 327712 | tf_op jit(solution)/shard_map/ppermute | solution.py:89
  27.5 2.5 %collective-permute-start.9 = (bf16[4,1280]{1,0:T(4,128)(2,1)S(1)}, bf16[4,1280]{1,0:T(4,128)(2,1)S(1)}, u32[]{:S(2)}, u32[]{:S(2)}) collective-permute-start(bf16[4,1280]{1,0:T(4,128)(2,1)S(1)} %get-tuple-element.193), channel_id=1, source_target_pairs={{0,24},{8,16},{16,8},{24,0},{1,25},{9,17},{17,9},{25,1},{2,26},{10... | collective-permute-start | bytes 30728 | tf_op jit(solution)/shard_map/ppermute | solution.py:89
  34.1 2.3 %half.1 = (bf16[512,768]{1,0:T(8,128)(2,1)S(1)}, bf16[1280,512]{1,0:T(8,128)(2,1)S(1)}) custom-call(bf16[128,1280]{1,0:T(8,128)(2,1)S(1)} %get-tuple-element.99.refs_0_, bf16[128,1280]{1,0:T(8,128)(2,1)S(1)} %collective-permute-done.3.refs_1_, bf16[128,1280]{1,0:T(8,128)(2,1)S(1)} %collective-permute-done.4.refs_2_, ...), custom_call_target="tpu_custom_call" | custom-call | flops 1006632960 | bytes 5373952 | tf_op jit(solution)/shard_map/half/pallas_call | solution.py:53
  37.0 1.8 collective-permute-start.13
  38.8 2.5 %collective-permute-start.11 = (bf16[16,1280]{1,0:T(8,128)(2,1)S(1)}, bf16[16,1280]{1,0:T(8,128)(2,1)S(1)}, u32[]{:S(2)}, u32[]{:S(2)}) collective-permute-start(bf16[16,1280]{1,0:T(8,128)(2,1)S(1)} %pad_maximum_fusion.refs_0_), channel_id=1, source_target_pairs={{0,2},{1,3},{2,0},{3,1},{4,6},{5,7},{6,4},{7,5},{8,10},{9,11},{10,... | collective-permute-start | bytes 122888 | tf_op jit(solution)/shard_map/ppermute | solution.py:89
  43.3 2.0 %collective-permute-start.15 = (bf16[16,1280]{1,0:T(8,128)(2,1)S(1)}, bf16[16,1280]{1,0:T(8,128)(2,1)S(1)}, u32[]{:S(2)}, u32[]{:S(2)}) collective-permute-start(bf16[16,1280]{1,0:T(8,128)(2,1)S(1)} %collective-permute-done.13.refs_4_), channel_id=1, source_target_pairs={{0,2},{1,3},{2,0},{3,1},{4,6},{5,7},{6,4},{7,5},{8,10},{9,11},{10,... | collective-permute-start | bytes 122888 | tf_op jit(solution)/shard_map/ppermute | solution.py:89
  45.3 2.0 %collective-permute-done.15.refs_6_ = bf16[16,1280]{1,0:T(8,128)(2,1)S(1)} collective-permute-done((bf16[16,1280]{1,0:T(8,128)(2,1)S(1)}, bf16[16,1280]{1,0:T(8,128)(2,1)S(1)}, u32[]{:S(2)}, u32[]{:S(2)}) %collective-permute-start.15) | collective-permute-done | bytes 40992 | tf_op jit(solution)/shard_map/ppermute | solution.py:89
  51.6 4.8 %front.1 = (bf16[1024,768]{1,0:T(8,128)(2,1)S(1)}, bf16[128,256]{1,0:T(8,128)(2,1)S(1)}, bf16[128,256]{1,0:T(8,128)(2,1)S(1)}, bf16[64,1280]{1,0:T(8,128)(2,1)S(1)}, bf16[64,1280]{1,0:T(8,128)(2,1)S(1)}) custom-call(bf16[128,1280]{1,0:T(8,128)(2,1)S(1)} %collective-permute-done.refs_0_, bf16[128,1280]{1,0:T(8,128)(2,1)S(1)} %collective-permute-done.1.refs_1_, ...), custom_call_target="tpu_custom_call" | custom-call | flops 2013265920 | bytes 6750208 | tf_op jit(solution)/shard_map/front/pallas_call | solution.py:53
  57.1 6.5 %collective-permute-done.18.refs_4_ = bf16[112,1280]{1,0:T(8,128)(2,1)S(1)} collective-permute-done((bf16[112,1280]{1,0:T(8,128)(2,1)S(1)}, bf16[112,1280]{1,0:T(8,128)(2,1)S(1)}, u32[]{:S(2)}, u32[]{:S(2)}) %collective-permute-start.18) | collective-permute-done | bytes 286752 | tf_op jit(solution)/shard_map/ppermute | solution.py:89
  65.1 2.7 %collective-permute-start.21 = (bf16[16,1280]{1,0:T(8,128)(2,1)S(1)}, bf16[16,1280]{1,0:T(8,128)(2,1)S(1)}, u32[]{:S(2)}, u32[]{:S(2)}) collective-permute-start(bf16[16,1280]{1,0:T(8,128)(2,1)S(1)} %get-tuple-element.119), channel_id=1, source_target_pairs={{0,4},{1,5},{2,6},{3,7},{4,0},{5,1},{6,2},{7,3},{8,12},{9,13},{10,... | collective-permute-start | bytes 122888 | tf_op jit(solution)/shard_map/ppermute | solution.py:89
  70.8 2.7 %collective-permute-done.22.refs_3_ = bf16[16,1280]{1,0:T(8,128)(2,1)S(1)} collective-permute-done((bf16[16,1280]{1,0:T(8,128)(2,1)S(1)}, bf16[16,1280]{1,0:T(8,128)(2,1)S(1)}, u32[]{:S(2)}, u32[]{:S(2)}) %collective-permute-start.22) | collective-permute-done | bytes 40992 | tf_op jit(solution)/shard_map/ppermute | solution.py:89
  78.0 4.0 %cold.1 = (bf16[896,256]{1,0:T(8,128)(2,1)S(1)}, bf16[896,256]{1,0:T(8,128)(2,1)S(1)}, bf16[448,1280]{1,0:T(8,128)(2,1)S(1)}, bf16[448,1280]{1,0:T(8,128)(2,1)S(1)}) custom-call(bf16[1024,768]{1,0:T(8,128)(2,1)S(1)} %get-tuple-element.144.qkv.refs_8_.refs_9_, bf16[256,1280]{1,0:T(8,128)(2,1)S(1)} %get-tuple-element.111.refs_6_.proj.refs_9_.refs_10_), custom_call_target="tpu_custom_call" | custom-call | flops 1073741824 | bytes 5439488 | tf_op jit(solution)/shard_map/cold/pallas_call | solution.py:53
  86.9 3.1 %collective-permute-done.30.refs_4_ = bf16[16,1280]{1,0:T(8,128)(2,1)S(1)} collective-permute-done((bf16[16,1280]{1,0:T(8,128)(2,1)S(1)}, bf16[16,1280]{1,0:T(8,128)(2,1)S(1)}, u32[]{:S(2)}, u32[]{:S(2)}) %collective-permute-start.30) | collective-permute-done | bytes 40992 | tf_op jit(solution)/shard_map/ppermute | solution.py:89
  90.8 3.2 %collective-permute-done.32.refs_6_ = bf16[16,1280]{1,0:T(8,128)(2,1)S(1)} collective-permute-done((bf16[16,1280]{1,0:T(8,128)(2,1)S(1)}, bf16[16,1280]{1,0:T(8,128)(2,1)S(1)}, u32[]{:S(2)}, u32[]{:S(2)}) %collective-permute-start.32) | collective-permute-done | bytes 40992 | tf_op jit(solution)/shard_map/ppermute | solution.py:89
  95.2 2.3 %experts.1 = (bf16[128,1280]{1,0:T(8,128)(2,1)S(1)}, bf16[2,128,640]{2,1,0:T(8,128)(2,1)S(1)}, bf16[2,128,640]{2,1,0:T(8,128)(2,1)S(1)}, bf16[64,2560]{1,0:T(8,128)(2,1)S(1)}, bf16[64,2560]{1,0:T(8,128)(2,1)S(1)}) custom-call(bf16[16,1280]{1,0:T(8,128)(2,1)S(1)} %pad_maximum_fusion.1.refs_0_, bf16[16,1280]{1,0:T(8,128)(2,1)S(1)} %collective-permute-done.27.refs_1_, ...), custom_call_target="tpu_custom_call" | custom-call | flops 1258291200 | bytes 9175040 | tf_op jit(solution)/shard_map/experts/pallas_call | solution.py:53
  99.9 4.4 %collective-permute-done.35.refs_1_ = bf16[16,2560]{1,0:T(8,128)(2,1)S(1)} collective-permute-done((bf16[16,2560]{1,0:T(8,128)(2,1)S(1)}, bf16[16,2560]{1,0:T(8,128)(2,1)S(1)}, u32[]{:S(2)}, u32[]{:S(2)}) %collective-permute-start.35) | collective-permute-done | bytes 81952 | tf_op jit(solution)/shard_map/ppermute | solution.py:89
  105.1 5.5 %collective-permute-done.36.refs_2_ = bf16[16,2560]{1,0:T(8,128)(2,1)S(1)} collective-permute-done((bf16[16,2560]{1,0:T(8,128)(2,1)S(1)}, bf16[16,2560]{1,0:T(8,128)(2,1)S(1)}, u32[]{:S(2)}, u32[]{:S(2)}) %collective-permute-start.36) | collective-permute-done | bytes 81952 | tf_op jit(solution)/shard_map/ppermute | solution.py:89
  110.6 2.0 %collective-permute-start.37 = (bf16[16,2560]{1,0:T(8,128)(2,1)S(1)}, bf16[16,2560]{1,0:T(8,128)(2,1)S(1)}, u32[]{:S(2)}, u32[]{:S(2)}) collective-permute-start(bf16[16,2560]{1,0:T(8,128)(2,1)S(1)} %get-tuple-element.139), channel_id=1, source_target_pairs={{0,6},{1,7},{2,4},{3,5},{4,2},{5,3},{6,0},{7,1},{8,14},{9,15},{10,... | collective-permute-start | bytes 245768 | tf_op jit(solution)/shard_map/ppermute | solution.py:89
  112.6 4.3 %collective-permute-done.37.refs_3_ = bf16[16,2560]{1,0:T(8,128)(2,1)S(1)} collective-permute-done((bf16[16,2560]{1,0:T(8,128)(2,1)S(1)}, bf16[16,2560]{1,0:T(8,128)(2,1)S(1)}, u32[]{:S(2)}, u32[]{:S(2)}) %collective-permute-start.37) | collective-permute-done | bytes 81952 | tf_op jit(solution)/shard_map/ppermute | solution.py:89
  126.4 9.7 %cold_back.1 = (bf16[896,256]{1,0:T(8,128)(2,1)S(1)}, f32[256,1024]{1,0:T(8,128)S(1)}, f32[256,1024]{1,0:T(8,128)}, f32[256,1280]{1,0:T(8,128)}) custom-call(bf16[112,1280]{1,0:T(8,128)(2,1)S(1)} %copy-done.12, bf16[112,1280]{1,0:T(8,128)(2,1)S(1)} %collective-permute-done.41.refs_1_, bf16[112,1280]{1,0:T(8,128)(2,1)S(1)} %copy-done.37, ...), custom_call_target="tpu_custom_call" | custom-call | flops 2684354560 | bytes 9306112 | tf_op jit(solution)/shard_map/cold_back/pallas_call | solution.py:53
  136.5 2.5 %collective-permute-start.46 = (bf16[16,1280]{1,0:T(8,128)(2,1)S(1)}, bf16[16,1280]{1,0:T(8,128)(2,1)S(1)}, u32[]{:S(2)}, u32[]{:S(2)}) collective-permute-start(bf16[16,1280]{1,0:T(8,128)(2,1)S(1)} %get-tuple-element.153.refs_0_), channel_id=1, source_target_pairs={{0,2},{1,3},{2,0},{3,1},{4,6},{5,7},{6,4},{7,5},{8,10},{9,11},{10,... | collective-permute-start | bytes 122888 | tf_op jit(solution)/shard_map/ppermute | solution.py:89
  139.0 2.5 %collective-permute-done.48.refs_4_ = bf16[16,1280]{1,0:T(8,128)(2,1)S(1)} collective-permute-done((bf16[16,1280]{1,0:T(8,128)(2,1)S(1)}, bf16[16,1280]{1,0:T(8,128)(2,1)S(1)}, u32[]{:S(2)}, u32[]{:S(2)}) %collective-permute-start.48) | collective-permute-done | bytes 40992 | tf_op jit(solution)/shard_map/ppermute | solution.py:89
  143.5 1.9 %collective-permute-done.50.refs_6_ = bf16[16,1280]{1,0:T(8,128)(2,1)S(1)} collective-permute-done((bf16[16,1280]{1,0:T(8,128)(2,1)S(1)}, bf16[16,1280]{1,0:T(8,128)(2,1)S(1)}, u32[]{:S(2)}, u32[]{:S(2)}) %collective-permute-start.50) | collective-permute-done | bytes 40992 | tf_op jit(solution)/shard_map/ppermute | solution.py:89
  146.9 2.6 %collective-permute-done.52.theirs = bf16[448,1280]{1,0:T(8,128)(2,1)S(1)} collective-permute-done((bf16[448,1280]{1,0:T(8,128)(2,1)S(1)}, bf16[448,1280]{1,0:T(8,128)(2,1)S(1)}, u32[]{:S(2)}, u32[]{:S(2)}) %collective-permute-start.52) | collective-permute-done | bytes 1146912 | tf_op jit(solution)/shard_map/ppermute | solution.py:89
  150.0 5.8 %hot_back.1 = (bf16[320,640]{1,0:T(8,128)(2,1)S(1)}, bf16[320,640]{1,0:T(8,128)(2,1)S(1)}, bf16[320,640]{1,0:T(8,128)(2,1)S(1)}, bf16[320,640]{1,0:T(8,128)(2,1)S(1)}) custom-call(bf16[16,1280]{1,0:T(8,128)(2,1)S(1)} %get-tuple-element.153.refs_0_, bf16[16,1280]{1,0:T(8,128)(2,1)S(1)} %collective-permute-done.45.refs_1_, ...), custom_call_target="tpu_custom_call" | custom-call | flops 2013265920 | bytes 10813444 | tf_op jit(solution)/shard_map/hot_back/pallas_call | solution.py:53
  159.3 5.5 %collective-permute-done.53.theirs = bf16[224,1280]{1,0:T(8,128)(2,1)S(1)} collective-permute-done((bf16[224,1280]{1,0:T(8,128)(2,1)S(1)}, bf16[224,1280]{1,0:T(8,128)(2,1)S(1)}, u32[]{:S(2)}, u32[]{:S(2)}) %collective-permute-start.53) | collective-permute-done | bytes 573472 | tf_op jit(solution)/shard_map/ppermute | solution.py:89
  166.0 4.3 %weight_grads.1 = (bf16[2,1280,640]{2,1,0:T(8,128)(2,1)}, bf16[2,640,1280]{2,1,0:T(8,128)(2,1)}) custom-call(bf16[128,1280]{1,0:T(8,128)(2,1)S(1)} %get-tuple-element.180.arrived, bf16[128,1280]{1,0:T(8,128)(2,1)S(1)} %copy-done.35, bf16[2,128,640]{2,1,0:T(8,128)(2,1)S(1)} %get-tuple-element.182.hidden, bf16[2,128,640]{2,1,0:T(8,128)(2,1)S(1)} %get-tuple-element.183.grad_pre), custom_call_target="tpu_custom_call" | custom-call | flops 838860800 | bytes 7864320 | tf_op jit(solution)/shard_map/weight_grads/pallas_call | solution.py:53
  170.3 9.8 %collective-permute-done.54.refs_1_ = bf16[112,1280]{1,0:T(8,128)(2,1)S(1)} collective-permute-done((bf16[112,1280]{1,0:T(8,128)(2,1)S(1)}, bf16[112,1280]{1,0:T(8,128)(2,1)S(1)}, u32[]{:S(2)}, u32[]{:S(2)}) %collective-permute-start.54) | collective-permute-done | bytes 286752 | tf_op jit(solution)/shard_map/ppermute | solution.py:89
  (203 shorter events, 56.3 us)
Async XLA Ops:
  6.8 17.7 %collective-permute-start.4 = (bf16[128,1280]{1,0:T(8,128)(2,1)S(1)}, bf16[128,1280]{1,0:T(8,128)(2,1)S(1)}, u32[]{:S(2)}, u32[]{:S(2)}) collective-permute-start(bf16[128,1280]{1,0:T(8,128)(2,1)S(1)} %get-tuple-element.99.refs_0_), channel_id=1, source_target_pairs={{0,2},{1,3},{2,0},{3,1},{4,6},{5,7},{6,4},{7,5},{8,10},{9,11},{10,... | collective-permute-start | bytes 983048 | tf_op jit(solution)/shard_map/ppermute | solution.py:89
  9.9 17.1 %collective-permute-start = (bf16[128,1280]{1,0:T(8,128)(2,1)S(1)}, bf16[128,1280]{1,0:T(8,128)(2,1)S(1)}, u32[]{:S(2)}, u32[]{:S(2)}) collective-permute-start(bf16[128,1280]{1,0:T(8,128)(2,1)S(1)} %get-tuple-element.99.refs_0_), channel_id=1, source_target_pairs={{0,4},{1,5},{2,6},{3,7},{4,0},{5,1},{6,2},{7,3},{8,12},{9,13},{10,... | collective-permute-start | bytes 983048 | tf_op jit(solution)/shard_map/ppermute | solution.py:89
  12.5 19.4 %collective-permute-start.3 = (bf16[128,1280]{1,0:T(8,128)(2,1)S(1)}, bf16[128,1280]{1,0:T(8,128)(2,1)S(1)}, u32[]{:S(2)}, u32[]{:S(2)}) collective-permute-start(bf16[128,1280]{1,0:T(8,128)(2,1)S(1)} %get-tuple-element.99.refs_0_), channel_id=1, source_target_pairs={{0,1},{1,0},{2,3},{3,2},{4,5},{5,4},{6,7},{7,6},{8,9},{9,8},{10,11... | collective-permute-start | bytes 983048 | tf_op jit(solution)/shard_map/ppermute | solution.py:89
  24.5 8.0 %collective-permute-start.5 = (bf16[128,1280]{1,0:T(8,128)(2,1)S(1)}, bf16[128,1280]{1,0:T(8,128)(2,1)S(1)}, u32[]{:S(2)}, u32[]{:S(2)}) collective-permute-start(bf16[128,1280]{1,0:T(8,128)(2,1)S(1)} %collective-permute-done.4.refs_2_), channel_id=1, source_target_pairs={{0,1},{1,0},{2,3},{3,2},{4,5},{5,4},{6,7},{7,6},{8,9},{9,8},{10,11... | collective-permute-start | bytes 983048 | tf_op jit(solution)/shard_map/ppermute | solution.py:89
  27.1 9.3 %collective-permute-start.2 = (bf16[128,1280]{1,0:T(8,128)(2,1)S(1)}, bf16[128,1280]{1,0:T(8,128)(2,1)S(1)}, u32[]{:S(2)}, u32[]{:S(2)}) collective-permute-start(bf16[128,1280]{1,0:T(8,128)(2,1)S(1)} %collective-permute-done.refs_0_), channel_id=1, source_target_pairs={{0,2},{1,3},{2,0},{3,1},{4,6},{5,7},{6,4},{7,5},{8,10},{9,11},{10,... | collective-permute-start | bytes 983048 | tf_op jit(solution)/shard_map/ppermute | solution.py:89
  27.5 9.0 %collective-permute-start.9 = (bf16[4,1280]{1,0:T(4,128)(2,1)S(1)}, bf16[4,1280]{1,0:T(4,128)(2,1)S(1)}, u32[]{:S(2)}, u32[]{:S(2)}) collective-permute-start(bf16[4,1280]{1,0:T(4,128)(2,1)S(1)} %get-tuple-element.193), channel_id=1, source_target_pairs={{0,24},{8,16},{16,8},{24,0},{1,25},{9,17},{17,9},{25,1},{2,26},{10... | collective-permute-start | bytes 30728 | tf_op jit(solution)/shard_map/ppermute | solution.py:89
  30.0 6.9 %collective-permute-start.8 = (bf16[4,1280]{1,0:T(4,128)(2,1)S(1)}, bf16[4,1280]{1,0:T(4,128)(2,1)S(1)}, u32[]{:S(2)}, u32[]{:S(2)}) collective-permute-start(bf16[4,1280]{1,0:T(4,128)(2,1)S(1)} %get-tuple-element.194), channel_id=1, source_target_pairs={{0,16},{8,24},{16,0},{24,8},{1,17},{9,25},{17,1},{25,9},{2,18},{10... | collective-permute-start | bytes 30728 | tf_op jit(solution)/shard_map/ppermute | solution.py:89
  32.5 19.1 %collective-permute-start.17 = (bf16[112,1280]{1,0:T(8,128)(2,1)S(1)}, bf16[112,1280]{1,0:T(8,128)(2,1)S(1)}, u32[]{:S(2)}, u32[]{:S(2)}) collective-permute-start(bf16[112,1280]{1,0:T(8,128)(2,1)S(1)} %slice.28.refs_0_), channel_id=1, source_target_pairs={{0,2},{1,3},{2,0},{3,1},{4,6},{5,7},{6,4},{7,5},{8,10},{9,11},{10,... | collective-permute-start | bytes 860168 | tf_op jit(solution)/shard_map/ppermute | solution.py:89
  36.4 15.2 %collective-permute-start.1 = (bf16[128,1280]{1,0:T(8,128)(2,1)S(1)}, bf16[128,1280]{1,0:T(8,128)(2,1)S(1)}, u32[]{:S(2)}, u32[]{:S(2)}) collective-permute-start(bf16[128,1280]{1,0:T(8,128)(2,1)S(1)} %collective-permute-done.refs_0_), channel_id=1, source_target_pairs={{0,1},{1,0},{2,3},{3,2},{4,5},{5,4},{6,7},{7,6},{8,9},{9,8},{10,11... | collective-permute-start | bytes 983048 | tf_op jit(solution)/shard_map/ppermute | solution.py:89
  36.5 15.1 %collective-permute-start.6 = (bf16[128,1280]{1,0:T(8,128)(2,1)S(1)}, bf16[128,1280]{1,0:T(8,128)(2,1)S(1)}, u32[]{:S(2)}, u32[]{:S(2)}) collective-permute-start(bf16[128,1280]{1,0:T(8,128)(2,1)S(1)} %collective-permute-done.2.refs_2_), channel_id=1, source_target_pairs={{0,1},{1,0},{2,3},{3,2},{4,5},{5,4},{6,7},{7,6},{8,9},{9,8},{10,11... | collective-permute-start | bytes 983048 | tf_op jit(solution)/shard_map/ppermute | solution.py:89
  47.3 16.3 %collective-permute-start.18 = (bf16[112,1280]{1,0:T(8,128)(2,1)S(1)}, bf16[112,1280]{1,0:T(8,128)(2,1)S(1)}, u32[]{:S(2)}, u32[]{:S(2)}) collective-permute-start(bf16[112,1280]{1,0:T(8,128)(2,1)S(1)} %slice.28.refs_0_), channel_id=1, source_target_pairs={{0,4},{1,5},{2,6},{3,7},{4,0},{5,1},{6,2},{7,3},{8,12},{9,13},{10,... | collective-permute-start | bytes 860168 | tf_op jit(solution)/shard_map/ppermute | solution.py:89
  65.1 5.7 %collective-permute-start.21 = (bf16[16,1280]{1,0:T(8,128)(2,1)S(1)}, bf16[16,1280]{1,0:T(8,128)(2,1)S(1)}, u32[]{:S(2)}, u32[]{:S(2)}) collective-permute-start(bf16[16,1280]{1,0:T(8,128)(2,1)S(1)} %get-tuple-element.119), channel_id=1, source_target_pairs={{0,4},{1,5},{2,6},{3,7},{4,0},{5,1},{6,2},{7,3},{8,12},{9,13},{10,... | collective-permute-start | bytes 122888 | tf_op jit(solution)/shard_map/ppermute | solution.py:89
  67.8 5.8 %collective-permute-start.22 = (bf16[16,1280]{1,0:T(8,128)(2,1)S(1)}, bf16[16,1280]{1,0:T(8,128)(2,1)S(1)}, u32[]{:S(2)}, u32[]{:S(2)}) collective-permute-start(bf16[16,1280]{1,0:T(8,128)(2,1)S(1)} %get-tuple-element.120), channel_id=1, source_target_pairs={{0,6},{1,7},{2,4},{3,5},{4,2},{5,3},{6,0},{7,1},{8,14},{9,15},{10,... | collective-permute-start | bytes 122888 | tf_op jit(solution)/shard_map/ppermute | solution.py:89
  74.5 8.6 %collective-permute-start.23 = (bf16[4,1280]{1,0:T(4,128)(2,1)S(1)}, bf16[4,1280]{1,0:T(4,128)(2,1)S(1)}, u32[]{:S(2)}, u32[]{:S(2)}) collective-permute-start(bf16[4,1280]{1,0:T(4,128)(2,1)S(1)} %get-tuple-element.128), channel_id=1, source_target_pairs={{0,8},{8,0},{16,24},{24,16},{1,9},{9,1},{17,25},{25,17},{2,10},{10... | collective-permute-start | bytes 30728 | tf_op jit(solution)/shard_map/ppermute | solution.py:89
  76.0 7.1 %collective-permute-start.24 = (bf16[4,1280]{1,0:T(4,128)(2,1)S(1)}, bf16[4,1280]{1,0:T(4,128)(2,1)S(1)}, u32[]{:S(2)}, u32[]{:S(2)}) collective-permute-start(bf16[4,1280]{1,0:T(4,128)(2,1)S(1)} %get-tuple-element.129), channel_id=1, source_target_pairs={{0,16},{8,24},{16,0},{24,8},{1,17},{9,25},{17,1},{25,9},{2,18},{10... | collective-permute-start | bytes 30728 | tf_op jit(solution)/shard_map/ppermute | solution.py:89
  77.5 5.6 %collective-permute-start.25 = (bf16[4,1280]{1,0:T(4,128)(2,1)S(1)}, bf16[4,1280]{1,0:T(4,128)(2,1)S(1)}, u32[]{:S(2)}, u32[]{:S(2)}) collective-permute-start(bf16[4,1280]{1,0:T(4,128)(2,1)S(1)} %get-tuple-element.130), channel_id=1, source_target_pairs={{0,24},{8,16},{16,8},{24,0},{1,25},{9,17},{17,9},{25,1},{2,26},{10... | collective-permute-start | bytes 30728 | tf_op jit(solution)/shard_map/ppermute | solution.py:89
  78.0 6.6 %collective-permute-start.26 = (bf16[112,1280]{1,0:T(8,128)(2,1)S(1)}, bf16[112,1280]{1,0:T(8,128)(2,1)S(1)}, u32[]{:S(2)}, u32[]{:S(2)}) collective-permute-start(bf16[112,1280]{1,0:T(8,128)(2,1)S(1)} %collective-permute-done.18.refs_4_), channel_id=1, source_target_pairs={{0,2},{1,3},{2,0},{3,1},{4,6},{5,7},{6,4},{7,5},{8,10},{9,11},{10,... | collective-permute-start | bytes 860168 | tf_op jit(solution)/shard_map/ppermute | solution.py:89
  97.7 20.7 %collective-permute-start.41 = (bf16[112,1280]{1,0:T(8,128)(2,1)S(1)}, bf16[112,1280]{1,0:T(8,128)(2,1)S(1)}, u32[]{:S(2)}, u32[]{:S(2)}) collective-permute-start(bf16[112,1280]{1,0:T(8,128)(2,1)S(1)} %slice.28.refs_0_), channel_id=1, source_target_pairs={{0,1},{1,0},{2,3},{3,2},{4,5},{5,4},{6,7},{7,6},{8,9},{9,8},{10,11... | collective-permute-start | bytes 860168 | tf_op jit(solution)/shard_map/ppermute | solution.py:89
  98.1 21.9 %collective-permute-start.42 = (bf16[112,1280]{1,0:T(8,128)(2,1)S(1)}, bf16[112,1280]{1,0:T(8,128)(2,1)S(1)}, u32[]{:S(2)}, u32[]{:S(2)}) collective-permute-start(bf16[112,1280]{1,0:T(8,128)(2,1)S(1)} %collective-permute-done.17.refs_2_), channel_id=1, source_target_pairs={{0,1},{1,0},{2,3},{3,2},{4,5},{5,4},{6,7},{7,6},{8,9},{9,8},{10,11... | collective-permute-start | bytes 860168 | tf_op jit(solution)/shard_map/ppermute | solution.py:89
  98.3 22.2 %collective-permute-start.43 = (bf16[112,1280]{1,0:T(8,128)(2,1)S(1)}, bf16[112,1280]{1,0:T(8,128)(2,1)S(1)}, u32[]{:S(2)}, u32[]{:S(2)}) collective-permute-start(bf16[112,1280]{1,0:T(8,128)(2,1)S(1)} %collective-permute-done.18.refs_4_), channel_id=1, source_target_pairs={{0,1},{1,0},{2,3},{3,2},{4,5},{5,4},{6,7},{7,6},{8,9},{9,8},{10,11... | collective-permute-start | bytes 860168 | tf_op jit(solution)/shard_map/ppermute | solution.py:89
  99.3 21.2 %collective-permute-start.44 = (bf16[112,1280]{1,0:T(8,128)(2,1)S(1)}, bf16[112,1280]{1,0:T(8,128)(2,1)S(1)}, u32[]{:S(2)}, u32[]{:S(2)}) collective-permute-start(bf16[112,1280]{1,0:T(8,128)(2,1)S(1)} %collective-permute-done.26.refs_6_), channel_id=1, source_target_pairs={{0,1},{1,0},{2,3},{3,2},{4,5},{5,4},{6,7},{7,6},{8,9},{9,8},{10,11... | collective-permute-start | bytes 860168 | tf_op jit(solution)/shard_map/ppermute | solution.py:89
  104.3 6.3 %collective-permute-start.36 = (bf16[16,2560]{1,0:T(8,128)(2,1)S(1)}, bf16[16,2560]{1,0:T(8,128)(2,1)S(1)}, u32[]{:S(2)}, u32[]{:S(2)}) collective-permute-start(bf16[16,2560]{1,0:T(8,128)(2,1)S(1)} %get-tuple-element.138), channel_id=1, source_target_pairs={{0,4},{1,5},{2,6},{3,7},{4,0},{5,1},{6,2},{7,3},{8,12},{9,13},{10,... | collective-permute-start | bytes 245768 | tf_op jit(solution)/shard_map/ppermute | solution.py:89
  110.6 6.2 %collective-permute-start.37 = (bf16[16,2560]{1,0:T(8,128)(2,1)S(1)}, bf16[16,2560]{1,0:T(8,128)(2,1)S(1)}, u32[]{:S(2)}, u32[]{:S(2)}) collective-permute-start(bf16[16,2560]{1,0:T(8,128)(2,1)S(1)} %get-tuple-element.139), channel_id=1, source_target_pairs={{0,6},{1,7},{2,4},{3,5},{4,2},{5,3},{6,0},{7,1},{8,14},{9,15},{10,... | collective-permute-start | bytes 245768 | tf_op jit(solution)/shard_map/ppermute | solution.py:89
  116.9 19.2 %collective-permute-start.38 = (bf16[4,2560]{1,0:T(4,128)(2,1)S(1)}, bf16[4,2560]{1,0:T(4,128)(2,1)S(1)}, u32[]{:S(2)}, u32[]{:S(2)}) collective-permute-start(bf16[4,2560]{1,0:T(4,128)(2,1)S(1)} %get-tuple-element.141), channel_id=1, source_target_pairs={{0,8},{8,0},{16,24},{24,16},{1,9},{9,1},{17,25},{25,17},{2,10},{10... | collective-permute-start | bytes 61448 | tf_op jit(solution)/shard_map/ppermute | solution.py:89
  118.5 17.6 %collective-permute-start.39 = (bf16[4,2560]{1,0:T(4,128)(2,1)S(1)}, bf16[4,2560]{1,0:T(4,128)(2,1)S(1)}, u32[]{:S(2)}, u32[]{:S(2)}) collective-permute-start(bf16[4,2560]{1,0:T(4,128)(2,1)S(1)} %get-tuple-element.142), channel_id=1, source_target_pairs={{0,16},{8,24},{16,0},{24,8},{1,17},{9,25},{17,1},{25,9},{2,18},{10... | collective-permute-start | bytes 61448 | tf_op jit(solution)/shard_map/ppermute | solution.py:89
  120.0 16.1 %collective-permute-start.40 = (bf16[4,2560]{1,0:T(4,128)(2,1)S(1)}, bf16[4,2560]{1,0:T(4,128)(2,1)S(1)}, u32[]{:S(2)}, u32[]{:S(2)}) collective-permute-start(bf16[4,2560]{1,0:T(4,128)(2,1)S(1)} %get-tuple-element.143), channel_id=1, source_target_pairs={{0,24},{8,16},{16,8},{24,0},{1,25},{9,17},{17,9},{25,1},{2,26},{10... | collective-permute-start | bytes 61448 | tf_op jit(solution)/shard_map/ppermute | solution.py:89
  136.5 7.0 %collective-permute-start.46 = (bf16[16,1280]{1,0:T(8,128)(2,1)S(1)}, bf16[16,1280]{1,0:T(8,128)(2,1)S(1)}, u32[]{:S(2)}, u32[]{:S(2)}) collective-permute-start(bf16[16,1280]{1,0:T(8,128)(2,1)S(1)} %get-tuple-element.153.refs_0_), channel_id=1, source_target_pairs={{0,2},{1,3},{2,0},{3,1},{4,6},{5,7},{6,4},{7,5},{8,10},{9,11},{10,... | collective-permute-start | bytes 122888 | tf_op jit(solution)/shard_map/ppermute | solution.py:89
  149.8 15.1 %collective-permute-start.53 = (bf16[224,1280]{1,0:T(8,128)(2,1)S(1)}, bf16[224,1280]{1,0:T(8,128)(2,1)S(1)}, u32[]{:S(2)}, u32[]{:S(2)}) collective-permute-start(bf16[224,1280]{1,0:T(8,128)(2,1)S(1)} %get-tuple-element.161), channel_id=1, source_target_pairs={{0,2},{1,3},{2,0},{3,1},{4,6},{5,7},{6,4},{7,5},{8,10},{9,11},{10,... | collective-permute-start | bytes 1720328 | tf_op jit(solution)/shard_map/ppermute | solution.py:89
  155.8 25.7 %collective-permute-start.55 = (bf16[320,640]{1,0:T(8,128)(2,1)S(1)}, bf16[320,640]{1,0:T(8,128)(2,1)S(1)}, u32[]{:S(2)}, u32[]{:S(2)}) collective-permute-start(bf16[320,640]{1,0:T(8,128)(2,1)S(1)} %get-tuple-element.176), channel_id=1, source_target_pairs={{0,8},{8,0},{16,24},{24,16},{1,9},{9,1},{17,25},{25,17},{2,10},{10... | collective-permute-start | bytes 1228808 | tf_op jit(solution)/shard_map/ppermute | solution.py:89
  157.3 24.2 %collective-permute-start.56 = (bf16[320,640]{1,0:T(8,128)(2,1)S(1)}, bf16[320,640]{1,0:T(8,128)(2,1)S(1)}, u32[]{:S(2)}, u32[]{:S(2)}) collective-permute-start(bf16[320,640]{1,0:T(8,128)(2,1)S(1)} %get-tuple-element.177), channel_id=1, source_target_pairs={{0,16},{8,24},{16,0},{24,8},{1,17},{9,25},{17,1},{25,9},{2,18},{10... | collective-permute-start | bytes 1228808 | tf_op jit(solution)/shard_map/ppermute | solution.py:89
  158.8 22.6 %collective-permute-start.57 = (bf16[320,640]{1,0:T(8,128)(2,1)S(1)}, bf16[320,640]{1,0:T(8,128)(2,1)S(1)}, u32[]{:S(2)}, u32[]{:S(2)}) collective-permute-start(bf16[320,640]{1,0:T(8,128)(2,1)S(1)} %get-tuple-element.178), channel_id=1, source_target_pairs={{0,24},{8,16},{16,8},{24,0},{1,25},{9,17},{17,9},{25,1},{2,26},{10... | collective-permute-start | bytes 1228808 | tf_op jit(solution)/shard_map/ppermute | solution.py:89
  165.0 15.2 %collective-permute-start.54 = (bf16[112,1280]{1,0:T(8,128)(2,1)S(1)}, bf16[112,1280]{1,0:T(8,128)(2,1)S(1)}, u32[]{:S(2)}, u32[]{:S(2)}) collective-permute-start(bf16[112,1280]{1,0:T(8,128)(2,1)S(1)} %get-tuple-element.163), channel_id=1, source_target_pairs={{0,4},{1,5},{2,6},{3,7},{4,0},{5,1},{6,2},{7,3},{8,12},{9,13},{10,... | collective-permute-start | bytes 860168 | tf_op jit(solution)/shard_map/ppermute | solution.py:89
  (72 other events, 648.6 us)

commit v3 on v2

--- a/solution.py
+++ b/solution.py
@@ -42,21 +42,23 @@
     return lax.dot_general(a, b, (((0,), (0,)), ((), ())), preferred_element_type=f32)
 
 
-def run(body, outs, ins, name, flops=0, mib=48, smem=(), loose=0, scratch=()):
+def run(body, outs, ins, name, flops=0, extra=1, smem=(), loose=0, scratch=()):
     specs = [
         pl.BlockSpec(
             memory_space=pl.ANY if i < loose else pltpu.SMEM if i in smem else pltpu.VMEM
         )
         for i in range(len(ins))
     ]
-    sizes = [math.prod(x.shape) * x.dtype.itemsize for x in list(ins) + list(outs)]
+    sizes = [math.prod(x.shape) * x.dtype.itemsize for x in list(ins)[loose:] + list(outs)]
+    sizes += [math.prod(x.shape) * x.dtype.itemsize for x in scratch if x.dtype in (f32, bf16)]
+    limit = int(sum(sizes) * 1.2) + extra * 2**20
     return pl.pallas_call(
         body,
         out_shape=list(outs),
         in_specs=specs,
         out_specs=[pl.BlockSpec(memory_space=pltpu.VMEM)] * len(outs),
         scratch_shapes=list(scratch),
-        compiler_params=pltpu.CompilerParams(vmem_limit_bytes=mib * 2**20),
+        compiler_params=pltpu.CompilerParams(vmem_limit_bytes=limit),
         cost_estimate=pl.CostEstimate(
             flops=int(flops), bytes_accessed=int(sum(sizes)), transcendentals=0
         ),
@@ -104,9 +106,9 @@
     return [hop(have[k - 1], "tensor", 1) if k % 2 else have[k] for k in range(size)]
 
 
-def fold_order(count):
-    keys = range(0, count, 2)
-    return sorted(keys, key=lambda k: tuple((k >> b) & 1 for b in range(1, 8)))
+def fold_order(keys, flip=False):
+    bits = range(7, -1, -1) if flip else range(8)
+    return sorted(keys, key=lambda k: tuple((k >> b) & 1 for b in bits))
 
 
 def prologue_body(tok_in, cot_in, group, gate_t, routes_t, slots_t, *outs):
@@ -289,7 +291,7 @@
         cold = rows - places
         every = slice(None)
         group = min(4, count)
-        order = fold_order(count)
+        order = fold_order(range(0, count, 2))
         for first in range(0, count, group):
             at = slice(first * cold, (first + group) * cold)
             for h in range(heads):
@@ -362,8 +364,8 @@
     def body(*refs):
         shards = refs[:count]
         place, qkv, proj, ctx, ask, gq, gk, gv, gp, fn_a, fn_b = refs[count : count + 11]
-        outs = refs[count + 11 : count + 11 + groups]
-        rows_t, grad_q, whole = refs[count + 11 + groups :]
+        outs = refs[count + 11 : count + 15]
+        rows_t, grad_q, whole = refs[count + 15 :]
         grads = jnp.concatenate([s[...] for s in shards], axis=0)
         places = shards[0].shape[0]
         rows = qkv.shape[0] // count
@@ -401,17 +403,25 @@
         )
         whole[:, base:] = jnp.concatenate(proj_rows, axis=0).T
         each = whole.shape[0] // groups
-        for g in range(groups):
-            at = pl.multiple_of((place[0] ^ g) * each, 16)
-            outs[g][...] = whole[pl.ds(at, each), :]
-
-    return body
-
-
-def make_last(heads, size, groups):
-    def body(*refs):
-        parts, (qkv_o, proj_o) = refs[:groups], refs[groups:]
-        total = total_of(parts)
+        cuts = (0, near_rows(each), each)
+        for n in range(2):
+            size_n = cuts[n + 1] - cuts[n]
+            for i, g in enumerate(fold_order(range(groups), n == 1)):
+                at = pl.multiple_of((place[0] ^ g) * each + cuts[n], 16)
+                to = outs[2 * n + i // (groups // 2)]
+                i = i % (groups // 2)
+                to[i * size_n : (i + 1) * size_n] = whole[pl.ds(at, size_n), :]
+
+    return body
+
+
+def near_rows(rows):
+    return (rows // 2 + 15) // 16 * 16
+
+
+def make_last(heads, size):
+    def body(a, b, c, d, qkv_o, proj_o):
+        total = jnp.concatenate([total_of([a, b]), total_of([c, d])], axis=0)
         base = heads * 3 * size
         turned = total[:, base:].T
         for h in range(heads):
@@ -440,9 +450,9 @@
 
 def make_mid(count, groups):
     def body(*refs):
-        parts, (tok, link) = refs[:count], refs[count : count + 2]
-        mid_o, normal_o, factor_o = refs[count + 2 : count + 5]
-        outs = refs[count + 5 :]
+        parts, (tok, link, grads) = refs[:count], refs[count : count + 3]
+        mid_o, normal_o, factor_o = refs[count + 3 : count + 6]
+        outs = refs[count + 6 :]
         mid = (tok[...].astype(f32) + total_of(parts)).astype(bf16)
         normal, factor = norm_parts(mid)
         mid_o[...] = mid
@@ -451,7 +461,9 @@
         slot_in = dot(link[...], normal.astype(bf16))
         each = slot_in.shape[0] // groups
         for g in range(groups):
-            outs[g][...] = slot_in[g * each : (g + 1) * each].astype(bf16)
+            at = slice(g * each, (g + 1) * each)
+            both = jnp.concatenate([slot_in[at], grads[at].astype(f32)], axis=1)
+            outs[g][...] = both.astype(bf16)
 
     return body
 
@@ -461,21 +473,13 @@
     return (row // CAP) % experts == e
 
 
-def make_expert_grad(count, experts):
-    def body(*refs):
-        shards, down, grads, out = refs[:count], refs[count], refs[count + 1], refs[count + 2]
-        grads[...] = jnp.concatenate([s[...] for s in shards], axis=0)
-        for e in range(experts):
-            out[e] = dot_nt(grads[...], down[e])
-
-    return body
-
-
 def make_expert(count, experts):
     def body(*refs):
         shards = refs[:count]
-        up, down, grad_hidden, arrived, hid_o, pre_o, even, odd = refs[count:]
-        arrived[...] = jnp.concatenate([s[...] for s in shards], axis=0)
+        up, down, arrived, grads, hid_o, pre_o, even, odd = refs[count:]
+        width = arrived.shape[1]
+        arrived[...] = jnp.concatenate([s[:, :width] for s in shards], axis=0)
+        grads[...] = jnp.concatenate([s[:, width:] for s in shards], axis=0)
         rows = arrived.shape[0]
         forth = None
         back = None
@@ -485,7 +489,7 @@
             cdf = 0.5 * (1.0 + lax.erf(pre * half_root))
             hidden = jnp.where(keep, pre * cdf, 0.0).astype(bf16)
             slope = cdf + pre * jnp.exp(-0.5 * pre * pre) * bell_scale
-            grad_pre = jnp.where(keep, grad_hidden[e] * slope, 0.0).astype(bf16)
+            grad_pre = jnp.where(keep, dot_nt(grads[...], down[e]) * slope, 0.0).astype(bf16)
             hid_o[e] = hidden
             pre_o[e] = grad_pre
             a = dot(hidden, down[e])
@@ -560,22 +564,14 @@
     count = lax.axis_size("tensor") // 2
     theirs = hop(odd, "tensor", 1)
     sums = run(
-        make_fold(count), [shape((rows, even.shape[1]))] * count, [even, theirs], name, mib=24
+        make_fold(count), [shape((rows, even.shape[1]))] * count, [even, theirs], name
     )
     return [sums[0]] + [hop(sums[i], "tensor", 2 * i) for i in range(1, count)]
 
 
-def halving_scatter(even, odd, name):
-    mine, mask, theirs = even, 1, odd
-    while True:
-        theirs = hop(theirs, "tensor", mask)
-        if mine.shape[0] == even.shape[0] * 2 // lax.axis_size("tensor"):
-            return [mine, theirs]
-        half = (mine.shape[0] // 2, mine.shape[1])
-        mine, theirs = run(
-            make_fold(2), [shape(half), shape(half)], [mine, theirs], f"{name}_{mask}", mib=24
-        )
-        mask *= 2
+def halve(mine, theirs, name):
+    half = (mine.shape[0] // 2, mine.shape[1])
+    return run(make_fold(2), [shape(half), shape(half)], [mine, theirs], name)
 
 
 def shards(
@@ -607,7 +603,6 @@
         [shape((heads * 3 * LANES, width)), shape((heads * LANES, width))],
         [qkv_weight.transpose(1, 2, 0), proj_weight],
         "prep",
-        mib=24,
     )
     group = (lax.axis_index("dp") * experts).astype(jnp.int32).reshape(1)
     normed, cot, tok, perm, pick0, pick1, link, grad_out = run(
@@ -624,9 +619,9 @@
         ],
         [tokens, cotangent, group, gate_weights.T, routes.T, slot_index.T],
         "prologue",
+        extra=4,
         smem=(2,),
         loose=2,
-        mib=24,
         scratch=[
             pltpu.VMEM((rows, width), bf16),
             pltpu.VMEM((rows, width), bf16),
@@ -635,6 +630,12 @@
     )
     half = count // 2
     cot_cold = cot[places:]
+    cots = {0: cot_cold}
+    mask = 2
+    while mask < half:
+        cots.update({k ^ mask: hop(y, "tensor", mask) for k, y in list(cots.items())})
+        mask *= 2
+    near_cots = list(cots.values())
 
     def first_half(have):
         near = [
@@ -643,11 +644,10 @@
         return run(
             make_half(half, heads, size, scale),
             [shape((half * rows, heads * 3 * LANES)), shape((width, half * rows))],
-            near + [wqkv],
+            after(near, near_cots) + [wqkv],
             "half",
-            flops=2 * half * rows * width * heads * 3 * LANES,
+        extra=6,
             loose=half,
-            mib=40,
             scratch=[
                 pltpu.VMEM((half * rows, width), bf16),
                 pltpu.SemaphoreType.DMA((half,)),
@@ -663,27 +663,7 @@
     normed_all = gather_rel(normed, hold)
     have, (qkv_a, fn_a) = box[0]
 
-    pieces = [grad_out[g * each : (g + 1) * each] for g in range(groups)]
-    landed = jnp.concatenate(
-        [pieces[0]] + [hop(pieces[g], "dp", g) for g in range(1, groups)], axis=0
-    )
-    grads_all = gather_rel(landed)
-    slot_grads, grad_hidden = run(
-        make_expert_grad(count, experts),
-        [shape((slots, width)), shape((experts, slots, hidden_dev), f32)],
-        grads_all + [down_weight],
-        "slot_grads",
-        flops=2 * slots * width * hidden_dev * experts,
-        mib=24,
-    )
     far = count // 2
-    cots = {0: cot_cold}
-    mask = 2
-    while mask < far:
-        cots.update({k ^ mask: hop(y, "tensor", mask) for k, y in list(cots.items())})
-        mask *= 2
-    near_cots = list(cots.values())
-
     qkv, ctx_hot, ask_hot, even, odd = run(
         make_front(count, places, heads, size, scale),
         [
@@ -693,9 +673,9 @@
             shape((hot_all // 2, width)),
             shape((hot_all // 2, width)),
         ],
-        after(normed_all[half:], grad_hidden, near_cots) + [qkv_a, wqkv, proj],
+        normed_all[half:] + [qkv_a, wqkv, proj],
         "front",
-        flops=2 * total * width * heads * 3 * LANES,
+        extra=8,
         loose=half,
         scratch=[
             pltpu.VMEM((half * rows, width), bf16),
@@ -709,10 +689,9 @@
     outs = run(
         make_mid(count // 2, groups),
         [shape((places, width)), shape((places, width), f32), shape((places, 1), f32)]
-        + [shape((each, width))] * groups,
-        hot_sums + [tok[:places], link],
+        + [shape((each, 2 * width))] * groups,
+        hot_sums + [tok[:places], link, grad_out],
         "mid_hot",
-        mib=16,
     )
     mid_hot, normal_hot, factor_hot = outs[:3]
     pieces = outs[3:]
@@ -727,6 +706,7 @@
         ],
         [after(qkv, mid_hot), proj],
         "cold",
+        extra=14,
         flops=4 * total * total * heads * LANES,
     )
     start = after(cots[far], mid_hot)
@@ -739,21 +719,23 @@
     landed = jnp.concatenate(
         [pieces[0]] + [hop(pieces[g], "dp", g) for g in range(1, groups)], axis=0
     )
+    cold_theirs = hop(after(odd_cold, ctx_cold), "tensor", 1)
     landed = after(landed, ctx_cold, list(cots.values()))
     arrived_all = gather_rel(landed)
-    arrived, hidden, grad_pre, even, odd = run(
+    arrived, slot_grads, hidden, grad_pre, even, odd = run(
         make_expert(count, experts),
         [
+            shape((slots, width)),
             shape((slots, width)),
             shape((experts, slots, hidden_dev)),
             shape((experts, slots, hidden_dev)),
             shape((slots // 2, 2 * width)),
             shape((slots // 2, 2 * width)),
         ],
-        arrived_all + [up_weight, down_weight, grad_hidden],
+        arrived_all + [up_weight, down_weight],
         "experts",
+        extra=8,
         flops=6 * slots * width * hidden_dev * experts,
-        mib=32,
     )
     sums = fold_scatter(even, odd, places, "fold_slots")
 
@@ -762,10 +744,12 @@
         [shape((each, 2 * width))] * groups,
         sums,
         "split_slots",
-        mib=16,
-    )
+    )
+    cot_all = [hop(cots[k - 1], "tensor", 1) if k % 2 else cots[k] for k in range(count)]
+    cold_mine, cold_send = halve(after(even_cold, hidden), cold_theirs, "fold_cold_1")
+    pieces = after(pieces, cold_mine)
     back = [pieces[0]] + [hop(pieces[g], "dp", g) for g in range(1, groups)]
-    cot_all = [hop(cots[k - 1], "tensor", 1) if k % 2 else cots[k] for k in range(count)]
+    cold_theirs = hop(after(cold_send, pieces[0]), "tensor", 2)
     gq, gk, gv, gp = run(
         make_cold_back(count, places, heads, size, scale),
         [
@@ -776,6 +760,7 @@
         ],
         cot_all + [after(qkv, pieces[0]), proj, ctx_cold, ask_cold],
         "cold_back",
+        extra=16,
         flops=10 * total * total * heads * LANES,
         loose=count,
         scratch=[
@@ -783,13 +768,12 @@
             pltpu.SemaphoreType.DMA((count,)),
         ],
     )
-    back = after(back, gp)
+    back = after(back, gp, cold_theirs)
     grad_hot, expert_out = run(
         make_mid_back(groups),
         [shape((places, width)), shape((places, width))],
         back + [link, cot[:places], normal_hot, factor_hot],
         "mid_back",
-        mib=16,
     )
     box.clear()
 
@@ -800,22 +784,32 @@
                 [shape((width, half * rows))],
                 after(normed_all[half:], grad_hot),
                 "turn",
-                mib=24,
+        extra=3,
             )[0]
         )
         return box[0]
 
     grad_hot_all = gather_rel(grad_hot, turn)
     fn_b = box[0]
-    cold_sums = halving_scatter(even_cold, after(odd_cold, grad_hot_all), "fold_cold")
+    mask = 4
+    cold_mine = after(cold_mine, grad_hot)
+    while mask < count:
+        cold_mine, cold_send = halve(cold_mine, cold_theirs, f"fold_cold_{mask // 2}")
+        cold_theirs = hop(cold_send, "tensor", mask)
+        mask *= 2
+    cold_sums = [cold_mine, cold_theirs]
 
     me = lax.axis_index("dp").astype(jnp.int32).reshape(1)
-    pieces = run(
+    each_w = width // groups
+    first_w = near_rows(each_w)
+    halves = [(groups // 2 * n, heads * 4 * size) for n in (first_w, each_w - first_w)]
+    keep_a, send_a, keep_b, send_b = run(
         make_hot_back(count, heads, size, groups, scale),
-        [shape((width // groups, heads * 4 * size))] * groups,
-        grad_hot_all + [me, qkv, proj, ctx_hot, ask_hot, gq, gk, gv, gp, fn_a, fn_b],
+        [shape(halves[0]), shape(halves[0]), shape(halves[1]), shape(halves[1])],
+        after(grad_hot_all, cold_mine)
+        + [me, qkv, proj, ctx_hot, ask_hot, gq, gk, gv, gp, fn_a, fn_b],
         "hot_back",
-        flops=2 * total * width * heads * 3 * LANES,
+        extra=10,
         smem=(count,),
         scratch=[
             pltpu.VMEM((heads * 3 * size, total), bf16),
@@ -826,26 +820,34 @@
     grad_up, grad_down = run(
         make_weight_grads(experts),
         [shape(up_weight.shape), shape(down_weight.shape)],
-        [after(arrived, pieces[0]), slot_grads, hidden, grad_pre],
+        [after(arrived, keep_a), slot_grads, hidden, grad_pre],
         "weight_grads",
-        flops=4 * slots * width * hidden_dev * experts,
-        mib=32,
-    )
-    parts = [pieces[0]] + [hop(pieces[g], "dp", g) for g in range(1, groups)]
+        extra=10,
+    )
+    mask = 1
+    while True:
+        got_a = hop(send_a, "dp", mask)
+        got_b = hop(send_b, "dp", groups // 2 // mask)
+        if mask == groups // 2:
+            break
+        keep_a, send_a = halve(keep_a, got_a, f"fold_a_{mask}")
+        keep_b, send_b = halve(keep_b, got_b, f"fold_b_{mask}")
+        mask *= 2
+    parts = [keep_a, got_a, keep_b, got_b]
     layer_out, gate_grad = run(
         make_epilogue(2),
         [shape((rows, width)), shape((2, rows), f32)],
         cold_sums
         + [tok[places:], mid_hot, perm, pick0, pick1, expert_out, gate_weights.T, cotangent],
         "epilogue",
-        mib=24,
+        extra=4,
     )
     grad_qkv, grad_proj = run(
-        make_last(heads, size, groups),
+        make_last(heads, size),
         [shape((width // groups, heads, 3 * size), f32), shape((heads, size, width // groups), f32)],
         after(parts, layer_out, grad_up),
         "last",
-        mib=24,
+        extra=6,
     )
     return (layer_out, gate_grad.T, grad_qkv, grad_proj, grad_up, grad_down)
 

time: 184 us -> 163 us (0.89)
  local copies, waits for them, and re-layouts: 15.8 us -> 5.04 us
  Pallas kernels: 41.1 us -> 34.5 us
  starting transfers between devices: 46.6 us -> 43.6 us
    unnamed x92 -> x22, local copies, waits for them, and re-layouts: 15.8 us -> 5 us
    pallas_call x20 -> x21, Pallas kernels: 41.1 us -> 34.5 us  [run(): pl.pallas_call(body, out_shape=list(outs), in_specs=specs, out_specs=[pl....]
    ppermute x58 -> x49, starting transfers between devices: 46.6 us -> 43.6 us  [hop(): return lax.ppermute(x, axis, [(i, i ^ mask) for i in range(size)])]
    ppermute x58 -> x49, waiting for transfers between devices: 78.3 us -> 78.9 us  [hop(): return lax.ppermute(x, axis, [(i, i ^ mask) for i in range(size)])]
  transfers between devices with their start and end apart: 58 -> 49, of which waited for: 23 -> 23; matrix products, arithmetic and copies ran while one was open for 0% -> 0% of each run, Pallas kernels for 19% -> 14%
where the time goes in v3:
time: 163 us
  waiting for transfers between devices  78.9 us (48%)
  starting transfers between devices  43.6 us (27%)
  Pallas kernels  34.5 us (21%)
  local copies, waits for them, and re-layouts  5.04 us (3%)
    ppermute x49, waiting for transfers between devices, hop(): return lax.ppermute(x, axis, [(i, i ^ mask) for i in range(size)])  78.9 us
    ppermute x49, starting transfers between devices, hop(): return lax.ppermute(x, axis, [(i, i ^ mask) for i in range(size)])  43.6 us
    pallas_call x21, Pallas kernels, run(): pl.pallas_call(body, out_shape=list(outs), in_specs=specs, out_specs=[pl....  34.5 us
    unnamed x22, local copies, waits for them, and re-layouts  5 us
  transfers between devices with their start and end apart: 49, of which 23 were waited for; matrix products, arithmetic and copies ran while one was open for 0% of the time, Pallas kernels for 14%

profile of v3, /device:TPU:0, one launch (start us, length us, event | category | flops | bytes accessed | tf_op | source)
XLA Modules:
  0.0 163.0 jit_solution(6823101019530650034)
XLA Ops:
  4.6 2.2 %prologue.1 = (bf16[128,1280]{1,0:T(8,128)(2,1)S(1)}, bf16[128,1280]{1,0:T(8,128)(2,1)S(1)}, bf16[128,1280]{1,0:T(8,128)(2,1)S(1)}, bf16[128,128]{1,0:T(8,128)(2...) custom-call(bf16[128,1280]{1,0:T(8,128)(2,1)S(1)} %copy-done.6, ...), custom_call_target="tpu_custom_call" | custom-call | bytes 1723908 | tf_op jit(solution)/shard_map/prologue/pallas_call | solution.py:55
  6.8 3.1 %collective-permute-start.4 = (bf16[128,1280]{1,0:T(8,128)(2,1)S(1)}, bf16[128,1280]{1,0:T(8,128)(2,1)S(1)}, u32[]{:S(2)}, u32[]{:S(2)}) collective-permute-start(bf16[128,1280]{1,0:T(8,128)(2,1)S(1)} %get-tuple-element.119.refs_0_), channel_id=1, source_target_pairs={{0,2},{1,3},{2,0},{3,1},{4,6},{5,7},{6,4},{7,5},{8,10},{9,11},{10,... | collective-permute-start | bytes 983048 | tf_op jit(solution)/shard_map/ppermute | solution.py:91
  9.9 2.6 %collective-permute-start = (bf16[128,1280]{1,0:T(8,128)(2,1)S(1)}, bf16[128,1280]{1,0:T(8,128)(2,1)S(1)}, u32[]{:S(2)}, u32[]{:S(2)}) collective-permute-start(bf16[128,1280]{1,0:T(8,128)(2,1)S(1)} %get-tuple-element.119.refs_0_), channel_id=1, source_target_pairs={{0,4},{1,5},{2,6},{3,7},{4,0},{5,1},{6,2},{7,3},{8,12},{9,13},{10,... | collective-permute-start | bytes 983048 | tf_op jit(solution)/shard_map/ppermute | solution.py:91
  12.5 12.0 %collective-permute-done.4.refs_2_ = bf16[128,1280]{1,0:T(8,128)(2,1)S(1)} collective-permute-done((bf16[128,1280]{1,0:T(8,128)(2,1)S(1)}, bf16[128,1280]{1,0:T(8,128)(2,1)S(1)}, u32[]{:S(2)}, u32[]{:S(2)}) %collective-permute-start.4) | collective-permute-done | bytes 327712 | tf_op jit(solution)/shard_map/ppermute | solution.py:91
  24.5 2.5 %collective-permute-done.refs_0_ = bf16[128,1280]{1,0:T(8,128)(2,1)S(1)} collective-permute-done((bf16[128,1280]{1,0:T(8,128)(2,1)S(1)}, bf16[128,1280]{1,0:T(8,128)(2,1)S(1)}, u32[]{:S(2)}, u32[]{:S(2)}) %collective-permute-start) | collective-permute-done | bytes 327712 | tf_op jit(solution)/shard_map/ppermute | solution.py:91
  27.5 1.6 %collective-permute-start.6 = (bf16[112,1280]{1,0:T(8,128)(2,1)S(1)}, bf16[112,1280]{1,0:T(8,128)(2,1)S(1)}, u32[]{:S(2)}, u32[]{:S(2)}) collective-permute-start(bf16[112,1280]{1,0:T(8,128)(2,1)S(1)} %slice.12.refs_0_), channel_id=1, source_target_pairs={{0,2},{1,3},{2,0},{3,1},{4,6},{5,7},{6,4},{7,5},{8,10},{9,11},{10,... | collective-permute-start | bytes 860168 | tf_op jit(solution)/shard_map/ppermute | solution.py:91
  30.4 10.4 %collective-permute-done.6.refs_2_ = bf16[112,1280]{1,0:T(8,128)(2,1)S(1)} collective-permute-done((bf16[112,1280]{1,0:T(8,128)(2,1)S(1)}, bf16[112,1280]{1,0:T(8,128)(2,1)S(1)}, u32[]{:S(2)}, u32[]{:S(2)}) %collective-permute-start.6) | collective-permute-done | bytes 286752 | tf_op jit(solution)/shard_map/ppermute | solution.py:91
  40.8 2.3 %half.1 = (bf16[512,768]{1,0:T(8,128)(2,1)S(1)}, bf16[1280,512]{1,0:T(8,128)(2,1)S(1)}) custom-call(bf16[128,1280]{1,0:T(8,128)(2,1)S(1)} %get-tuple-element.119.refs_0_, bf16[128,1280]{1,0:T(8,128)(2,1)S(1)} %collective-permute-done.3.refs_1_, bf16[128,1280]{1,0:T(8,128)(2,1)S(1)} %collective-permute-done.4.refs_2_, ...), custom_call_target="tpu_custom_call" | custom-call | bytes 5373952 | tf_op jit(solution)/shard_map/half/pallas_call | solution.py:55
  43.2 1.6 collective-permute-start.8
  44.8 3.2 %front.1 = (bf16[1024,768]{1,0:T(8,128)(2,1)S(1)}, bf16[128,256]{1,0:T(8,128)(2,1)S(1)}, bf16[128,256]{1,0:T(8,128)(2,1)S(1)}, bf16[64,1280]{1,0:T(8,128)(2,1)S(1)}, bf16[64,1280]{1,0:T(8,128)(2,1)S(1)}) custom-call(bf16[128,1280]{1,0:T(8,128)(2,1)S(1)} %collective-permute-done.refs_0_, bf16[128,1280]{1,0:T(8,128)(2,1)S(1)} %collective-permute-done.1.refs_1_, ...), custom_call_target="tpu_custom_call" | custom-call | bytes 6750208 | tf_op jit(solution)/shard_map/front/pallas_call | solution.py:55
  48.0 11.4 %collective-permute-done.8.refs_4_ = bf16[112,1280]{1,0:T(8,128)(2,1)S(1)} collective-permute-done((bf16[112,1280]{1,0:T(8,128)(2,1)S(1)}, bf16[112,1280]{1,0:T(8,128)(2,1)S(1)}, u32[]{:S(2)}, u32[]{:S(2)}) %collective-permute-start.8) | collective-permute-done | bytes 286752 | tf_op jit(solution)/shard_map/ppermute | solution.py:91
  61.0 3.0 %collective-permute-start.11 = (bf16[16,1280]{1,0:T(8,128)(2,1)S(1)}, bf16[16,1280]{1,0:T(8,128)(2,1)S(1)}, u32[]{:S(2)}, u32[]{:S(2)}) collective-permute-start(bf16[16,1280]{1,0:T(8,128)(2,1)S(1)} %get-tuple-element.135), channel_id=1, source_target_pairs={{0,4},{1,5},{2,6},{3,7},{4,0},{5,1},{6,2},{7,3},{8,12},{9,13},{10,... | collective-permute-start | bytes 122888 | tf_op jit(solution)/shard_map/ppermute | solution.py:91
  66.5 3.2 %collective-permute-done.12.refs_3_ = bf16[16,1280]{1,0:T(8,128)(2,1)S(1)} collective-permute-done((bf16[16,1280]{1,0:T(8,128)(2,1)S(1)}, bf16[16,1280]{1,0:T(8,128)(2,1)S(1)}, u32[]{:S(2)}, u32[]{:S(2)}) %collective-permute-start.12) | collective-permute-done | bytes 40992 | tf_op jit(solution)/shard_map/ppermute | solution.py:91
  70.1 4.1 %cold.1 = (bf16[896,256]{1,0:T(8,128)(2,1)S(1)}, bf16[896,256]{1,0:T(8,128)(2,1)S(1)}, bf16[448,1280]{1,0:T(8,128)(2,1)S(1)}, bf16[448,1280]{1,0:T(8,128)(2,1)S(1)}) custom-call(bf16[1024,768]{1,0:T(8,128)(2,1)S(1)} %get-tuple-element.169.qkv.refs_8_.refs_9_, bf16[256,1280]{1,0:T(8,128)(2,1)S(1)} %get-tuple-element.127.refs_6_.proj.refs_9_.refs_10_), custom_call_target="tpu_custom_call" | custom-call | flops 1073741824 | bytes 5439488 | tf_op jit(solution)/shard_map/cold/pallas_call | solution.py:55
  79.6 2.4 %collective-permute-done.15 = bf16[4,2560]{1,0:T(4,128)(2,1)S(1)} collective-permute-done((bf16[4,2560]{1,0:T(4,128)(2,1)S(1)}, bf16[4,2560]{1,0:T(4,128)(2,1)S(1)}, u32[]{:S(2)}, u32[]{:S(2)}) %collective-permute-start.15) | collective-permute-done | bytes 20512 | tf_op jit(solution)/shard_map/ppermute | solution.py:91
  82.1 4.1 %collective-permute-done.16.refs_6_ = bf16[112,1280]{1,0:T(8,128)(2,1)S(1)} collective-permute-done((bf16[112,1280]{1,0:T(8,128)(2,1)S(1)}, bf16[112,1280]{1,0:T(8,128)(2,1)S(1)}, u32[]{:S(2)}, u32[]{:S(2)}) %collective-permute-start.16) | collective-permute-done | bytes 286752 | tf_op jit(solution)/shard_map/ppermute | solution.py:91
  86.4 1.7 %collective-permute-start.18 = (bf16[16,2560]{1,0:T(8,128)(2,1)S(1)}, bf16[16,2560]{1,0:T(8,128)(2,1)S(1)}, u32[]{:S(2)}, u32[]{:S(2)}) collective-permute-start(bf16[16,2560]{1,0:T(8,128)(2,1)S(1)} %pad_maximum_fusion.refs_0_), channel_id=1, source_target_pairs={{0,2},{1,3},{2,0},{3,1},{4,6},{5,7},{6,4},{7,5},{8,10},{9,11},{10,... | collective-permute-start | bytes 245768 | tf_op jit(solution)/shard_map/ppermute | solution.py:91
  88.2 4.0 %collective-permute-done.20.refs_4_ = bf16[16,2560]{1,0:T(8,128)(2,1)S(1)} collective-permute-done((bf16[16,2560]{1,0:T(8,128)(2,1)S(1)}, bf16[16,2560]{1,0:T(8,128)(2,1)S(1)}, u32[]{:S(2)}, u32[]{:S(2)}) %collective-permute-start.20) | collective-permute-done | bytes 81952 | tf_op jit(solution)/shard_map/ppermute | solution.py:91
  92.7 3.9 %collective-permute-done.22.refs_6_ = bf16[16,2560]{1,0:T(8,128)(2,1)S(1)} collective-permute-done((bf16[16,2560]{1,0:T(8,128)(2,1)S(1)}, bf16[16,2560]{1,0:T(8,128)(2,1)S(1)}, u32[]{:S(2)}, u32[]{:S(2)}) %collective-permute-start.22) | collective-permute-done | bytes 81952 | tf_op jit(solution)/shard_map/ppermute | solution.py:91
  97.9 3.3 %experts.1 = (bf16[128,1280]{1,0:T(8,128)(2,1)S(1)}, bf16[128,1280]{1,0:T(8,128)(2,1)S(1)}, bf16[2,128,640]{2,1,0:T(8,128)(2,1)S(1)}, bf16[2,128,640]{2,1,0:T(8,...) custom-call(bf16[16,2560]{1,0:T(8,128)(2,1)S(1)} %pad_maximum_fusion.refs_0_, ...), custom_call_target="tpu_custom_call" | custom-call | flops 1258291200 | bytes 9175040 | tf_op jit(solution)/shard_map/experts/pallas_call | solution.py:55
  103.1 2.0 %collective-permute-start.27 = (bf16[16,2560]{1,0:T(8,128)(2,1)S(1)}, bf16[16,2560]{1,0:T(8,128)(2,1)S(1)}, u32[]{:S(2)}, u32[]{:S(2)}) collective-permute-start(bf16[16,2560]{1,0:T(8,128)(2,1)S(1)} %get-tuple-element.159), channel_id=1, source_target_pairs={{0,4},{1,5},{2,6},{3,7},{4,0},{5,1},{6,2},{7,3},{8,12},{9,13},{10,... | collective-permute-start | bytes 245768 | tf_op jit(solution)/shard_map/ppermute | solution.py:91
  105.1 2.3 %collective-permute-start.28 = (bf16[16,2560]{1,0:T(8,128)(2,1)S(1)}, bf16[16,2560]{1,0:T(8,128)(2,1)S(1)}, u32[]{:S(2)}, u32[]{:S(2)}) collective-permute-start(bf16[16,2560]{1,0:T(8,128)(2,1)S(1)} %get-tuple-element.160), channel_id=1, source_target_pairs={{0,6},{1,7},{2,4},{3,5},{4,2},{5,3},{6,0},{7,1},{8,14},{9,15},{10,... | collective-permute-start | bytes 245768 | tf_op jit(solution)/shard_map/ppermute | solution.py:91
  108.6 4.3 %collective-permute-done.27.refs_2_ = bf16[16,2560]{1,0:T(8,128)(2,1)S(1)} collective-permute-done((bf16[16,2560]{1,0:T(8,128)(2,1)S(1)}, bf16[16,2560]{1,0:T(8,128)(2,1)S(1)}, u32[]{:S(2)}, u32[]{:S(2)}) %collective-permute-start.27) | collective-permute-done | bytes 81952 | tf_op jit(solution)/shard_map/ppermute | solution.py:91
  113.2 1.6 collective-permute-start.36
  119.9 7.2 %cold_back.1 = (bf16[896,256]{1,0:T(8,128)(2,1)S(1)}, f32[256,1024]{1,0:T(8,128)S(1)}, f32[256,1024]{1,0:T(8,128)S(1)}, f32[256,1280]{1,0:T(8,128)S(1)}) custom-call(bf16[112,1280]{1,0:T(8,128)(2,1)S(1)} %slice.12.refs_0_, bf16[112,1280]{1,0:T(8,128)(2,1)S(1)} %collective-permute-done.32.refs_1_, bf16[112,1280]{1,0:T(8,128)(2,1)S(1)} %collective-permute-done.6.refs_2_, ...), custom_call_target="tpu_custom_call" | custom-call | flops 2684354560 | bytes 9306112 | tf_op jit(solution)/shard_map/cold_back/pallas_call | solution.py:55
  127.6 2.0 %collective-permute-start.41 = (bf16[16,1280]{1,0:T(8,128)(2,1)S(1)}, bf16[16,1280]{1,0:T(8,128)(2,1)S(1)}, u32[]{:S(2)}, u32[]{:S(2)}) collective-permute-start(bf16[16,1280]{1,0:T(8,128)(2,1)S(1)} %get-tuple-element.195.refs_0_), channel_id=1, source_target_pairs={{0,4},{1,5},{2,6},{3,7},{4,0},{5,1},{6,2},{7,3},{8,12},{9,13},{10,... | collective-permute-start | bytes 122888 | tf_op jit(solution)/shard_map/ppermute | solution.py:91
  129.8 2.7 %collective-permute-done.41.refs_4_ = bf16[16,1280]{1,0:T(8,128)(2,1)S(1)} collective-permute-done((bf16[16,1280]{1,0:T(8,128)(2,1)S(1)}, bf16[16,1280]{1,0:T(8,128)(2,1)S(1)}, u32[]{:S(2)}, u32[]{:S(2)}) %collective-permute-start.41) | collective-permute-done | bytes 40992 | tf_op jit(solution)/shard_map/ppermute | solution.py:91
  132.5 1.7 %collective-permute-start.43 = (bf16[16,1280]{1,0:T(8,128)(2,1)S(1)}, bf16[16,1280]{1,0:T(8,128)(2,1)S(1)}, u32[]{:S(2)}, u32[]{:S(2)}) collective-permute-start(bf16[16,1280]{1,0:T(8,128)(2,1)S(1)} %collective-permute-done.41.refs_4_), channel_id=1, source_target_pairs={{0,2},{1,3},{2,0},{3,1},{4,6},{5,7},{6,4},{7,5},{8,10},{9,11},{10,... | collective-permute-start | bytes 122888 | tf_op jit(solution)/shard_map/ppermute | solution.py:91
  137.8 3.2 %hot_back.1 = (bf16[320,640]{1,0:T(8,128)(2,1)S(1)}, bf16[320,640]{1,0:T(8,128)(2,1)S(1)}, bf16[320,640]{1,0:T(8,128)(2,1)S(1)}, bf16[320,640]{1,0:T(8,128)(2,1)S(1)}) custom-call(bf16[16,1280]{1,0:T(8,128)(2,1)S(1)} %get-tuple-element.195.refs_0_, bf16[16,1280]{1,0:T(8,128)(2,1)S(1)} %collective-permute-done.38.refs_1_, ...), custom_call_target="tpu_custom_call" | custom-call | bytes 13697028 | tf_op jit(solution)/shard_map/hot_back/pallas_call | solution.py:55
  144.0 2.0 %collective-permute-start.37 = (bf16[112,1280]{1,0:T(8,128)(2,1)S(1)}, bf16[112,1280]{1,0:T(8,128)(2,1)S(1)}, u32[]{:S(2)}, u32[]{:S(2)}) collective-permute-start(bf16[112,1280]{1,0:T(8,128)(2,1)S(1)} %get-tuple-element.183), channel_id=1, source_target_pairs={{0,4},{1,5},{2,6},{3,7},{4,0},{5,1},{6,2},{7,3},{8,12},{9,13},{10,... | collective-permute-start | bytes 860168 | tf_op jit(solution)/shard_map/ppermute | solution.py:91
  146.0 6.6 %collective-permute-done.45.theirs = bf16[320,640]{1,0:T(8,128)(2,1)S(1)} collective-permute-done((bf16[320,640]{1,0:T(8,128)(2,1)S(1)}, bf16[320,640]{1,0:T(8,128)(2,1)S(1)}, u32[]{:S(2)}, u32[]{:S(2)}) %collective-permute-start.45) | collective-permute-done | bytes 409632 | tf_op jit(solution)/shard_map/ppermute | solution.py:91
  155.9 4.3 %weight_grads.1 = (bf16[2,1280,640]{2,1,0:T(8,128)(2,1)}, bf16[2,640,1280]{2,1,0:T(8,128)(2,1)}) custom-call(bf16[128,1280]{1,0:T(8,128)(2,1)S(1)} %get-tuple-element.217.arrived, bf16[128,1280]{1,0:T(8,128)(2,1)S(1)} %get-tuple-element.218.grads, bf16[2,128,640]{2,1,0:T(8,128)(2,1)S(1)} %get-tuple-element.150.hidden, ...), custom_call_target="tpu_custom_call" | custom-call | bytes 7864320 | tf_op jit(solution)/shard_map/weight_grads/pallas_call | solution.py:55
  (114 shorter events, 39.4 us)
Async XLA Ops:
  6.8 17.7 %collective-permute-start.4 = (bf16[128,1280]{1,0:T(8,128)(2,1)S(1)}, bf16[128,1280]{1,0:T(8,128)(2,1)S(1)}, u32[]{:S(2)}, u32[]{:S(2)}) collective-permute-start(bf16[128,1280]{1,0:T(8,128)(2,1)S(1)} %get-tuple-element.119.refs_0_), channel_id=1, source_target_pairs={{0,2},{1,3},{2,0},{3,1},{4,6},{5,7},{6,4},{7,5},{8,10},{9,11},{10,... | collective-permute-start | bytes 983048 | tf_op jit(solution)/shard_map/ppermute | solution.py:91
  9.9 17.1 %collective-permute-start = (bf16[128,1280]{1,0:T(8,128)(2,1)S(1)}, bf16[128,1280]{1,0:T(8,128)(2,1)S(1)}, u32[]{:S(2)}, u32[]{:S(2)}) collective-permute-start(bf16[128,1280]{1,0:T(8,128)(2,1)S(1)} %get-tuple-element.119.refs_0_), channel_id=1, source_target_pairs={{0,4},{1,5},{2,6},{3,7},{4,0},{5,1},{6,2},{7,3},{8,12},{9,13},{10,... | collective-permute-start | bytes 983048 | tf_op jit(solution)/shard_map/ppermute | solution.py:91
  12.5 28.3 %collective-permute-start.3 = (bf16[128,1280]{1,0:T(8,128)(2,1)S(1)}, bf16[128,1280]{1,0:T(8,128)(2,1)S(1)}, u32[]{:S(2)}, u32[]{:S(2)}) collective-permute-start(bf16[128,1280]{1,0:T(8,128)(2,1)S(1)} %get-tuple-element.119.refs_0_), channel_id=1, source_target_pairs={{0,1},{1,0},{2,3},{3,2},{4,5},{5,4},{6,7},{7,6},{8,9},{9,8},{10,11... | collective-permute-start | bytes 983048 | tf_op jit(solution)/shard_map/ppermute | solution.py:91
  24.5 16.3 %collective-permute-start.5 = (bf16[128,1280]{1,0:T(8,128)(2,1)S(1)}, bf16[128,1280]{1,0:T(8,128)(2,1)S(1)}, u32[]{:S(2)}, u32[]{:S(2)}) collective-permute-start(bf16[128,1280]{1,0:T(8,128)(2,1)S(1)} %collective-permute-done.4.refs_2_), channel_id=1, source_target_pairs={{0,1},{1,0},{2,3},{3,2},{4,5},{5,4},{6,7},{7,6},{8,9},{9,8},{10,11... | collective-permute-start | bytes 983048 | tf_op jit(solution)/shard_map/ppermute | solution.py:91
  27.0 16.0 %collective-permute-start.2 = (bf16[128,1280]{1,0:T(8,128)(2,1)S(1)}, bf16[128,1280]{1,0:T(8,128)(2,1)S(1)}, u32[]{:S(2)}, u32[]{:S(2)}) collective-permute-start(bf16[128,1280]{1,0:T(8,128)(2,1)S(1)} %collective-permute-done.refs_0_), channel_id=1, source_target_pairs={{0,2},{1,3},{2,0},{3,1},{4,6},{5,7},{6,4},{7,5},{8,10},{9,11},{10,... | collective-permute-start | bytes 983048 | tf_op jit(solution)/shard_map/ppermute | solution.py:91
  27.5 13.3 %collective-permute-start.6 = (bf16[112,1280]{1,0:T(8,128)(2,1)S(1)}, bf16[112,1280]{1,0:T(8,128)(2,1)S(1)}, u32[]{:S(2)}, u32[]{:S(2)}) collective-permute-start(bf16[112,1280]{1,0:T(8,128)(2,1)S(1)} %slice.12.refs_0_), channel_id=1, source_target_pairs={{0,2},{1,3},{2,0},{3,1},{4,6},{5,7},{6,4},{7,5},{8,10},{9,11},{10,... | collective-permute-start | bytes 860168 | tf_op jit(solution)/shard_map/ppermute | solution.py:91
  30.3 14.4 %collective-permute-start.1 = (bf16[128,1280]{1,0:T(8,128)(2,1)S(1)}, bf16[128,1280]{1,0:T(8,128)(2,1)S(1)}, u32[]{:S(2)}, u32[]{:S(2)}) collective-permute-start(bf16[128,1280]{1,0:T(8,128)(2,1)S(1)} %collective-permute-done.refs_0_), channel_id=1, source_target_pairs={{0,1},{1,0},{2,3},{3,2},{4,5},{5,4},{6,7},{7,6},{8,9},{9,8},{10,11... | collective-permute-start | bytes 983048 | tf_op jit(solution)/shard_map/ppermute | solution.py:91
  43.2 16.3 %collective-permute-start.8 = (bf16[112,1280]{1,0:T(8,128)(2,1)S(1)}, bf16[112,1280]{1,0:T(8,128)(2,1)S(1)}, u32[]{:S(2)}, u32[]{:S(2)}) collective-permute-start(bf16[112,1280]{1,0:T(8,128)(2,1)S(1)} %slice.12.refs_0_), channel_id=1, source_target_pairs={{0,4},{1,5},{2,6},{3,7},{4,0},{5,1},{6,2},{7,3},{8,12},{9,13},{10,... | collective-permute-start | bytes 860168 | tf_op jit(solution)/shard_map/ppermute | solution.py:91
  60.9 4.5 %collective-permute-start.10 = (bf16[16,1280]{1,0:T(8,128)(2,1)S(1)}, bf16[16,1280]{1,0:T(8,128)(2,1)S(1)}, u32[]{:S(2)}, u32[]{:S(2)}) collective-permute-start(bf16[16,1280]{1,0:T(8,128)(2,1)S(1)} %get-tuple-element.134), channel_id=1, source_target_pairs={{0,2},{1,3},{2,0},{3,1},{4,6},{5,7},{6,4},{7,5},{8,10},{9,11},{10,... | collective-permute-start | bytes 122888 | tf_op jit(solution)/shard_map/ppermute | solution.py:91
  61.0 5.5 %collective-permute-start.11 = (bf16[16,1280]{1,0:T(8,128)(2,1)S(1)}, bf16[16,1280]{1,0:T(8,128)(2,1)S(1)}, u32[]{:S(2)}, u32[]{:S(2)}) collective-permute-start(bf16[16,1280]{1,0:T(8,128)(2,1)S(1)} %get-tuple-element.135), channel_id=1, source_target_pairs={{0,4},{1,5},{2,6},{3,7},{4,0},{5,1},{6,2},{7,3},{8,12},{9,13},{10,... | collective-permute-start | bytes 122888 | tf_op jit(solution)/shard_map/ppermute | solution.py:91
  63.9 5.8 %collective-permute-start.12 = (bf16[16,1280]{1,0:T(8,128)(2,1)S(1)}, bf16[16,1280]{1,0:T(8,128)(2,1)S(1)}, u32[]{:S(2)}, u32[]{:S(2)}) collective-permute-start(bf16[16,1280]{1,0:T(8,128)(2,1)S(1)} %get-tuple-element.136), channel_id=1, source_target_pairs={{0,6},{1,7},{2,4},{3,5},{4,2},{5,3},{6,0},{7,1},{8,14},{9,15},{10,... | collective-permute-start | bytes 122888 | tf_op jit(solution)/shard_map/ppermute | solution.py:91
  74.2 38.7 %collective-permute-start.24 = (bf16[448,1280]{1,0:T(8,128)(2,1)S(1)}, bf16[448,1280]{1,0:T(8,128)(2,1)S(1)}, u32[]{:S(2)}, u32[]{:S(2)}) collective-permute-start(bf16[448,1280]{1,0:T(8,128)(2,1)S(1)} %get-tuple-element.153), channel_id=1, source_target_pairs={{0,1},{1,0},{2,3},{3,2},{4,5},{5,4},{6,7},{7,6},{8,9},{9,8},{10,11... | collective-permute-start | bytes 3440648 | tf_op jit(solution)/shard_map/ppermute | solution.py:91
  77.3 4.7 %collective-permute-start.15 = (bf16[4,2560]{1,0:T(4,128)(2,1)S(1)}, bf16[4,2560]{1,0:T(4,128)(2,1)S(1)}, u32[]{:S(2)}, u32[]{:S(2)}) collective-permute-start(bf16[4,2560]{1,0:T(4,128)(2,1)S(1)} %get-tuple-element.146), channel_id=1, source_target_pairs={{0,24},{8,16},{16,8},{24,0},{1,25},{9,17},{17,9},{25,1},{2,26},{10... | collective-permute-start | bytes 61448 | tf_op jit(solution)/shard_map/ppermute | solution.py:91
  77.9 8.3 %collective-permute-start.16 = (bf16[112,1280]{1,0:T(8,128)(2,1)S(1)}, bf16[112,1280]{1,0:T(8,128)(2,1)S(1)}, u32[]{:S(2)}, u32[]{:S(2)}) collective-permute-start(bf16[112,1280]{1,0:T(8,128)(2,1)S(1)} %collective-permute-done.8.refs_4_), channel_id=1, source_target_pairs={{0,2},{1,3},{2,0},{3,1},{4,6},{5,7},{6,4},{7,5},{8,10},{9,11},{10,... | collective-permute-start | bytes 860168 | tf_op jit(solution)/shard_map/ppermute | solution.py:91
  86.2 6.0 %collective-permute-start.20 = (bf16[16,2560]{1,0:T(8,128)(2,1)S(1)}, bf16[16,2560]{1,0:T(8,128)(2,1)S(1)}, u32[]{:S(2)}, u32[]{:S(2)}) collective-permute-start(bf16[16,2560]{1,0:T(8,128)(2,1)S(1)} %pad_maximum_fusion.refs_0_), channel_id=1, source_target_pairs={{0,4},{1,5},{2,6},{3,7},{4,0},{5,1},{6,2},{7,3},{8,12},{9,13},{10,... | collective-permute-start | bytes 245768 | tf_op jit(solution)/shard_map/ppermute | solution.py:91
  86.4 6.3 %collective-permute-start.18 = (bf16[16,2560]{1,0:T(8,128)(2,1)S(1)}, bf16[16,2560]{1,0:T(8,128)(2,1)S(1)}, u32[]{:S(2)}, u32[]{:S(2)}) collective-permute-start(bf16[16,2560]{1,0:T(8,128)(2,1)S(1)} %pad_maximum_fusion.refs_0_), channel_id=1, source_target_pairs={{0,2},{1,3},{2,0},{3,1},{4,6},{5,7},{6,4},{7,5},{8,10},{9,11},{10,... | collective-permute-start | bytes 245768 | tf_op jit(solution)/shard_map/ppermute | solution.py:91
  92.2 4.4 %collective-permute-start.21 = (bf16[16,2560]{1,0:T(8,128)(2,1)S(1)}, bf16[16,2560]{1,0:T(8,128)(2,1)S(1)}, u32[]{:S(2)}, u32[]{:S(2)}) collective-permute-start(bf16[16,2560]{1,0:T(8,128)(2,1)S(1)} %collective-permute-done.20.refs_4_), channel_id=1, source_target_pairs={{0,1},{1,0},{2,3},{3,2},{4,5},{5,4},{6,7},{7,6},{8,9},{9,8},{10,11... | collective-permute-start | bytes 245768 | tf_op jit(solution)/shard_map/ppermute | solution.py:91
  103.0 5.6 %collective-permute-start.26 = (bf16[16,2560]{1,0:T(8,128)(2,1)S(1)}, bf16[16,2560]{1,0:T(8,128)(2,1)S(1)}, u32[]{:S(2)}, u32[]{:S(2)}) collective-permute-start(bf16[16,2560]{1,0:T(8,128)(2,1)S(1)} %get-tuple-element.158), channel_id=1, source_target_pairs={{0,2},{1,3},{2,0},{3,1},{4,6},{5,7},{6,4},{7,5},{8,10},{9,11},{10,... | collective-permute-start | bytes 245768 | tf_op jit(solution)/shard_map/ppermute | solution.py:91
  103.1 9.8 %collective-permute-start.27 = (bf16[16,2560]{1,0:T(8,128)(2,1)S(1)}, bf16[16,2560]{1,0:T(8,128)(2,1)S(1)}, u32[]{:S(2)}, u32[]{:S(2)}) collective-permute-start(bf16[16,2560]{1,0:T(8,128)(2,1)S(1)} %get-tuple-element.159), channel_id=1, source_target_pairs={{0,4},{1,5},{2,6},{3,7},{4,0},{5,1},{6,2},{7,3},{8,12},{9,13},{10,... | collective-permute-start | bytes 245768 | tf_op jit(solution)/shard_map/ppermute | solution.py:91
  105.1 7.8 %collective-permute-start.28 = (bf16[16,2560]{1,0:T(8,128)(2,1)S(1)}, bf16[16,2560]{1,0:T(8,128)(2,1)S(1)}, u32[]{:S(2)}, u32[]{:S(2)}) collective-permute-start(bf16[16,2560]{1,0:T(8,128)(2,1)S(1)} %get-tuple-element.160), channel_id=1, source_target_pairs={{0,6},{1,7},{2,4},{3,5},{4,2},{5,3},{6,0},{7,1},{8,14},{9,15},{10,... | collective-permute-start | bytes 245768 | tf_op jit(solution)/shard_map/ppermute | solution.py:91
  113.2 14.1 %collective-permute-start.36 = (bf16[224,1280]{1,0:T(8,128)(2,1)S(1)}, bf16[224,1280]{1,0:T(8,128)(2,1)S(1)}, u32[]{:S(2)}, u32[]{:S(2)}) collective-permute-start(bf16[224,1280]{1,0:T(8,128)(2,1)S(1)} %get-tuple-element.173), channel_id=1, source_target_pairs={{0,2},{1,3},{2,0},{3,1},{4,6},{5,7},{6,4},{7,5},{8,10},{9,11},{10,... | collective-permute-start | bytes 1720328 | tf_op jit(solution)/shard_map/ppermute | solution.py:91
  115.3 4.6 %collective-permute-start.35 = (bf16[112,1280]{1,0:T(8,128)(2,1)S(1)}, bf16[112,1280]{1,0:T(8,128)(2,1)S(1)}, u32[]{:S(2)}, u32[]{:S(2)}) collective-permute-start(bf16[112,1280]{1,0:T(8,128)(2,1)S(1)} %collective-permute-done.16.refs_6_), channel_id=1, source_target_pairs={{0,1},{1,0},{2,3},{3,2},{4,5},{5,4},{6,7},{7,6},{8,9},{9,8},{10,11... | collective-permute-start | bytes 860168 | tf_op jit(solution)/shard_map/ppermute | solution.py:91
  116.4 10.7 %collective-permute-start.29 = (bf16[4,2560]{1,0:T(4,128)(2,1)S(1)}, bf16[4,2560]{1,0:T(4,128)(2,1)S(1)}, u32[]{:S(2)}, u32[]{:S(2)}) collective-permute-start(bf16[4,2560]{1,0:T(4,128)(2,1)S(1)} %get-tuple-element.166), channel_id=1, source_target_pairs={{0,8},{8,0},{16,24},{24,16},{1,9},{9,1},{17,25},{25,17},{2,10},{10... | collective-permute-start | bytes 61448 | tf_op jit(solution)/shard_map/ppermute | solution.py:91
  117.8 9.3 %collective-permute-start.30 = (bf16[4,2560]{1,0:T(4,128)(2,1)S(1)}, bf16[4,2560]{1,0:T(4,128)(2,1)S(1)}, u32[]{:S(2)}, u32[]{:S(2)}) collective-permute-start(bf16[4,2560]{1,0:T(4,128)(2,1)S(1)} %get-tuple-element.167), channel_id=1, source_target_pairs={{0,16},{8,24},{16,0},{24,8},{1,17},{9,25},{17,1},{25,9},{2,18},{10... | collective-permute-start | bytes 61448 | tf_op jit(solution)/shard_map/ppermute | solution.py:91
  119.4 7.7 %collective-permute-start.31 = (bf16[4,2560]{1,0:T(4,128)(2,1)S(1)}, bf16[4,2560]{1,0:T(4,128)(2,1)S(1)}, u32[]{:S(2)}, u32[]{:S(2)}) collective-permute-start(bf16[4,2560]{1,0:T(4,128)(2,1)S(1)} %get-tuple-element.168), channel_id=1, source_target_pairs={{0,24},{8,16},{16,8},{24,0},{1,25},{9,17},{17,9},{25,1},{2,26},{10... | collective-permute-start | bytes 61448 | tf_op jit(solution)/shard_map/ppermute | solution.py:91
  127.6 5.0 %collective-permute-start.41 = (bf16[16,1280]{1,0:T(8,128)(2,1)S(1)}, bf16[16,1280]{1,0:T(8,128)(2,1)S(1)}, u32[]{:S(2)}, u32[]{:S(2)}) collective-permute-start(bf16[16,1280]{1,0:T(8,128)(2,1)S(1)} %get-tuple-element.195.refs_0_), channel_id=1, source_target_pairs={{0,4},{1,5},{2,6},{3,7},{4,0},{5,1},{6,2},{7,3},{8,12},{9,13},{10,... | collective-permute-start | bytes 122888 | tf_op jit(solution)/shard_map/ppermute | solution.py:91
  129.5 5.7 %collective-permute-start.39 = (bf16[16,1280]{1,0:T(8,128)(2,1)S(1)}, bf16[16,1280]{1,0:T(8,128)(2,1)S(1)}, u32[]{:S(2)}, u32[]{:S(2)}) collective-permute-start(bf16[16,1280]{1,0:T(8,128)(2,1)S(1)} %get-tuple-element.195.refs_0_), channel_id=1, source_target_pairs={{0,2},{1,3},{2,0},{3,1},{4,6},{5,7},{6,4},{7,5},{8,10},{9,11},{10,... | collective-permute-start | bytes 122888 | tf_op jit(solution)/shard_map/ppermute | solution.py:91
  141.0 11.6 %collective-permute-start.45 = (bf16[320,640]{1,0:T(8,128)(2,1)S(1)}, bf16[320,640]{1,0:T(8,128)(2,1)S(1)}, u32[]{:S(2)}, u32[]{:S(2)}) collective-permute-start(bf16[320,640]{1,0:T(8,128)(2,1)S(1)} %get-tuple-element.209), channel_id=1, source_target_pairs={{0,8},{8,0},{16,24},{24,16},{1,9},{9,1},{17,25},{25,17},{2,10},{10... | collective-permute-start | bytes 1228808 | tf_op jit(solution)/shard_map/ppermute | solution.py:91
  142.4 11.7 %collective-permute-start.47 = (bf16[320,640]{1,0:T(8,128)(2,1)S(1)}, bf16[320,640]{1,0:T(8,128)(2,1)S(1)}, u32[]{:S(2)}, u32[]{:S(2)}) collective-permute-start(bf16[320,640]{1,0:T(8,128)(2,1)S(1)} %get-tuple-element.213), channel_id=1, source_target_pairs={{0,16},{8,24},{16,0},{24,8},{1,17},{9,25},{17,1},{25,9},{2,18},{10... | collective-permute-start | bytes 1228808 | tf_op jit(solution)/shard_map/ppermute | solution.py:91
  144.0 16.2 %collective-permute-start.37 = (bf16[112,1280]{1,0:T(8,128)(2,1)S(1)}, bf16[112,1280]{1,0:T(8,128)(2,1)S(1)}, u32[]{:S(2)}, u32[]{:S(2)}) collective-permute-start(bf16[112,1280]{1,0:T(8,128)(2,1)S(1)} %get-tuple-element.183), channel_id=1, source_target_pairs={{0,4},{1,5},{2,6},{3,7},{4,0},{5,1},{6,2},{7,3},{8,12},{9,13},{10,... | collective-permute-start | bytes 860168 | tf_op jit(solution)/shard_map/ppermute | solution.py:91
  152.7 8.8 %collective-permute-start.46 = (bf16[160,640]{1,0:T(8,128)(2,1)S(1)}, bf16[160,640]{1,0:T(8,128)(2,1)S(1)}, u32[]{:S(2)}, u32[]{:S(2)}) collective-permute-start(bf16[160,640]{1,0:T(8,128)(2,1)S(1)} %get-tuple-element.211), channel_id=1, source_target_pairs={{0,16},{8,24},{16,0},{24,8},{1,17},{9,25},{17,1},{25,9},{2,18},{10... | collective-permute-start | bytes 614408 | tf_op jit(solution)/shard_map/ppermute | solution.py:91
  154.3 7.2 %collective-permute-start.48 = (bf16[160,640]{1,0:T(8,128)(2,1)S(1)}, bf16[160,640]{1,0:T(8,128)(2,1)S(1)}, u32[]{:S(2)}, u32[]{:S(2)}) collective-permute-start(bf16[160,640]{1,0:T(8,128)(2,1)S(1)} %get-tuple-element.215), channel_id=1, source_target_pairs={{0,8},{8,0},{16,24},{24,16},{1,9},{9,1},{17,25},{25,17},{2,10},{10... | collective-permute-start | bytes 614408 | tf_op jit(solution)/shard_map/ppermute | solution.py:91
  (28 other events, 168.8 us)

commit v4 on v3

--- a/solution.py
+++ b/solution.py
@@ -42,7 +42,7 @@
     return lax.dot_general(a, b, (((0,), (0,)), ((), ())), preferred_element_type=f32)
 
 
-def run(body, outs, ins, name, flops=0, extra=1, smem=(), loose=0, scratch=()):
+def run(body, outs, ins, name, flops=0, extra=1, moved=None, smem=(), loose=0, scratch=()):
     specs = [
         pl.BlockSpec(
             memory_space=pl.ANY if i < loose else pltpu.SMEM if i in smem else pltpu.VMEM
@@ -60,7 +60,7 @@
         scratch_shapes=list(scratch),
         compiler_params=pltpu.CompilerParams(vmem_limit_bytes=limit),
         cost_estimate=pl.CostEstimate(
-            flops=int(flops), bytes_accessed=int(sum(sizes)), transcendentals=0
+            flops=int(flops), bytes_accessed=int(sum(sizes) if moved is None else moved), transcendentals=0
         ),
         name=name,
     )(*ins)
@@ -112,7 +112,7 @@
 
 
 def prologue_body(tok_in, cot_in, group, gate_t, routes_t, slots_t, *outs):
-    normed_o, cot_o, tok_o, perm_o, pick0_o, pick1_o, link_o, gout_o, tok, cot, sems = outs
+    normed_o, cot_hot_o, cot_cold_o, tok_hot_o, tok_cold_o, perm_o, pick0_o, pick1_o, link_o, gout_o, tok, cot, sems = outs
     half = tok.shape[0] // 2
     pairs = [(tok_in, tok), (cot_in, cot)]
     copies = [
@@ -154,8 +154,10 @@
         c.wait()
     normal, _ = norm_parts(tok[...])
     normed_o[...] = dot_tn(perm, normal.astype(bf16)).astype(bf16)
-    cot_o[...] = dot_tn(perm, cot[...]).astype(bf16)
-    tok_o[...] = dot_tn(perm, tok[...]).astype(bf16)
+    for source, hot_o, cold_o in ((cot, cot_hot_o, cot_cold_o), (tok, tok_hot_o, tok_cold_o)):
+        moved = dot_tn(perm, source[...]).astype(bf16)
+        hot_o[...] = moved[:places]
+        cold_o[...] = moved[places:]
     pick0 = wide0.astype(bf16)
     pick1 = wide1.astype(bf16)
     pick0_o[...] = pick0[:, :places]
@@ -286,9 +288,10 @@
 
 
 def make_cold(count, places, heads, size):
-    def body(qkv, proj, ctx, ask, even, odd):
+    def body(qkv, proj, ctx, ask, even_a, odd_a, even_b, odd_b):
         rows = qkv.shape[0] // count
         cold = rows - places
+        upper = upper_rows(cold)
         every = slice(None)
         group = min(4, count)
         order = fold_order(range(0, count, 2))
@@ -304,9 +307,12 @@
                 )
             part = dot(ctx[at, :], proj[...]).astype(bf16)
             for k in range(first, first + group):
-                to = odd if k % 2 else even
+                one = part[(k - first) * cold : (k - first + 1) * cold]
                 i = order.index(k // 2 * 2)
-                to[i * cold : (i + 1) * cold] = part[(k - first) * cold : (k - first + 1) * cold]
+                to = odd_a if k % 2 else even_a
+                to[i * upper : (i + 1) * upper] = one[:upper]
+                to = odd_b if k % 2 else even_b
+                to[i * (cold - upper) : (i + 1) * (cold - upper)] = one[upper:]
 
     return body
 
@@ -415,6 +421,10 @@
     return body
 
 
+def upper_rows(rows):
+    return (rows * 5 // 7 + 15) // 16 * 16
+
+
 def near_rows(rows):
     return (rows // 2 + 15) // 16 * 16
 
@@ -540,11 +550,12 @@
     return body
 
 
-def make_epilogue(count):
+def make_epilogue():
     def body(*refs):
-        parts = refs[:count]
-        tok, mid_hot, perm, pick0, pick1, experts, gate_t, cot, out, gate_o = refs[count:]
-        cold = (tok[...].astype(f32) + total_of(parts)).astype(bf16)
+        parts = refs[:4]
+        tok, mid_hot, perm, pick0, pick1, experts, gate_t, cot, out, gate_o = refs[4:]
+        sums = jnp.concatenate([total_of(parts[:2]), total_of(parts[2:])], axis=0)
+        cold = (tok[...].astype(f32) + sums).astype(bf16)
         ordered = jnp.concatenate([mid_hot[...], cold], axis=0)
         mid = dot(perm[...], ordered)
         gate = jnp.concatenate([gate_t[...], jnp.zeros((6, gate_t.shape[1]), f32)], axis=0).T
@@ -605,12 +616,14 @@
         "prep",
     )
     group = (lax.axis_index("dp") * experts).astype(jnp.int32).reshape(1)
-    normed, cot, tok, perm, pick0, pick1, link, grad_out = run(
+    normed, cot_hot, cot_cold, tok_hot, tok_cold, perm, pick0, pick1, link, grad_out = run(
         prologue_body,
         [
             shape((rows, width)),
-            shape((rows, width)),
-            shape((rows, width)),
+            shape((places, width)),
+            shape((cold, width)),
+            shape((places, width)),
+            shape((cold, width)),
             shape((rows, rows)),
             shape((rows, places)),
             shape((rows, places)),
@@ -619,7 +632,7 @@
         ],
         [tokens, cotangent, group, gate_weights.T, routes.T, slot_index.T],
         "prologue",
-        extra=4,
+        extra=57,
         smem=(2,),
         loose=2,
         scratch=[
@@ -629,14 +642,7 @@
         ],
     )
     half = count // 2
-    cot_cold = cot[places:]
-    cots = {0: cot_cold}
-    mask = 2
-    while mask < half:
-        cots.update({k ^ mask: hop(y, "tensor", mask) for k, y in list(cots.items())})
-        mask *= 2
-    near_cots = list(cots.values())
-
+    cots = {0: cot_cold, 1: hop(cot_cold, "tensor", 1)}
     def first_half(have):
         near = [
             hop(have[k - 1], "tensor", 1) if k % 2 else have[k] for k in range(half)
@@ -644,9 +650,10 @@
         return run(
             make_half(half, heads, size, scale),
             [shape((half * rows, heads * 3 * LANES)), shape((width, half * rows))],
-            after(near, near_cots) + [wqkv],
+            after(near, cots[1]) + [wqkv],
             "half",
         extra=6,
+        moved=1024,
             loose=half,
             scratch=[
                 pltpu.VMEM((half * rows, width), bf16),
@@ -676,52 +683,60 @@
         normed_all[half:] + [qkv_a, wqkv, proj],
         "front",
         extra=8,
+        moved=1024,
         loose=half,
         scratch=[
             pltpu.VMEM((half * rows, width), bf16),
             pltpu.SemaphoreType.DMA((half,)),
         ],
     )
-    cots[far] = hop(after(cot_cold, have[far]), "tensor", far)
-    odd = after(odd, cots[far])
     hot_sums = fold_scatter(even, odd, places, "fold_hot")
 
     outs = run(
         make_mid(count // 2, groups),
         [shape((places, width)), shape((places, width), f32), shape((places, 1), f32)]
         + [shape((each, 2 * width))] * groups,
-        hot_sums + [tok[:places], link, grad_out],
+        hot_sums + [tok_hot, link, grad_out],
         "mid_hot",
     )
     mid_hot, normal_hot, factor_hot = outs[:3]
     pieces = outs[3:]
 
-    ctx_cold, ask_cold, even_cold, odd_cold = run(
+    upper = upper_rows(cold)
+    parts_cold = [(half * n, width) for n in (upper, upper, cold - upper, cold - upper)]
+    ctx_cold, ask_cold, even_a, odd_a, even_b, odd_b = run(
         make_cold(count, places, heads, size),
         [
             shape((count * cold, heads * LANES)),
             shape((count * cold, heads * LANES)),
-            shape((count * cold // 2, width)),
-            shape((count * cold // 2, width)),
-        ],
+        ]
+        + [shape(p) for p in parts_cold],
         [after(qkv, mid_hot), proj],
         "cold",
         extra=14,
         flops=4 * total * total * heads * LANES,
     )
-    start = after(cots[far], mid_hot)
-    rest = {far: start}
-    mask = 2
-    while mask < far:
-        rest.update({k ^ mask: hop(y, "tensor", mask) for k, y in list(rest.items())})
-        mask *= 2
-    cots.update(rest)
+    mask = far
+    starts = {0: after(cot_cold, mid_hot)}
+    while mask > 1:
+        cots[mask] = hop(starts[0], "tensor", mask)
+        mask //= 2
     landed = jnp.concatenate(
         [pieces[0]] + [hop(pieces[g], "dp", g) for g in range(1, groups)], axis=0
     )
-    cold_theirs = hop(after(odd_cold, ctx_cold), "tensor", 1)
     landed = after(landed, ctx_cold, list(cots.values()))
     arrived_all = gather_rel(landed)
+    start, mask = {k: after(y, arrived_all[count - 2], arrived_all[2]) for k, y in cots.items()}, far // 2
+    early = [k for k in cots if k and k % 2 == 0]
+    for k in early:
+        cots[k + 1] = hop(after(cots[k], arrived_all), "tensor", 1)
+    while mask > 1:
+        for k in list(cots):
+            if k % 2 == 0 and k > mask and k ^ mask not in cots:
+                start[k ^ mask] = cots[k ^ mask] = hop(start[k], "tensor", mask)
+        mask //= 2
+    theirs_a = hop(after(odd_a, arrived_all), "tensor", 1)
+    theirs_b = hop(after(odd_b, arrived_all), "tensor", 1)
     arrived, slot_grads, hidden, grad_pre, even, odd = run(
         make_expert(count, experts),
         [
@@ -737,19 +752,13 @@
         extra=8,
         flops=6 * slots * width * hidden_dev * experts,
     )
-    sums = fold_scatter(even, odd, places, "fold_slots")
-
-    pieces = run(
-        make_split(count // 2, groups),
-        [shape((each, 2 * width))] * groups,
-        sums,
-        "split_slots",
-    )
-    cot_all = [hop(cots[k - 1], "tensor", 1) if k % 2 else cots[k] for k in range(count)]
-    cold_mine, cold_send = halve(after(even_cold, hidden), cold_theirs, "fold_cold_1")
-    pieces = after(pieces, cold_mine)
-    back = [pieces[0]] + [hop(pieces[g], "dp", g) for g in range(1, groups)]
-    cold_theirs = hop(after(cold_send, pieces[0]), "tensor", 2)
+    keep_a, send_a = halve(even_a, theirs_a, "fold_cold_1a")
+    keep_b, send_b = halve(even_b, theirs_b, "fold_cold_1b")
+    sums = fold_scatter(even, after(odd, list(cots.values()), keep_a, keep_b), places, "fold_slots")
+    for k in range(1, count, 2):
+        if k not in cots:
+            cots[k] = hop(after(cots[k - 1], arrived_all), "tensor", 1)
+    cot_all = [cots[k] for k in range(count)]
     gq, gk, gv, gp = run(
         make_cold_back(count, places, heads, size, scale),
         [
@@ -758,7 +767,7 @@
             shape((heads * LANES, total), f32),
             shape((heads * LANES, width), f32),
         ],
-        cot_all + [after(qkv, pieces[0]), proj, ctx_cold, ask_cold],
+        cot_all + [after(qkv, sums[0]), proj, ctx_cold, ask_cold],
         "cold_back",
         extra=16,
         flops=10 * total * total * heads * LANES,
@@ -768,11 +777,21 @@
             pltpu.SemaphoreType.DMA((count,)),
         ],
     )
-    back = after(back, gp, cold_theirs)
+    sums = after(sums, gp)
+
+    pieces = run(
+        make_split(count // 2, groups),
+        [shape((each, 2 * width))] * groups,
+        sums,
+        "split_slots",
+    )
+    back = [pieces[0]] + [hop(pieces[g], "dp", g) for g in range(1, groups)]
+    theirs_a = hop(after(send_a, pieces[0]), "tensor", 2)
+    back = after(back, theirs_a)
     grad_hot, expert_out = run(
         make_mid_back(groups),
         [shape((places, width)), shape((places, width))],
-        back + [link, cot[:places], normal_hot, factor_hot],
+        back + [link, cot_hot, normal_hot, factor_hot],
         "mid_back",
     )
     box.clear()
@@ -791,13 +810,16 @@
 
     grad_hot_all = gather_rel(grad_hot, turn)
     fn_b = box[0]
+    keep_a = after(keep_a, grad_hot)
+    theirs_b = hop(after(send_b, grad_hot_all), "tensor", 2)
     mask = 4
-    cold_mine = after(cold_mine, grad_hot)
     while mask < count:
-        cold_mine, cold_send = halve(cold_mine, cold_theirs, f"fold_cold_{mask // 2}")
-        cold_theirs = hop(cold_send, "tensor", mask)
+        keep_a, send_a = halve(keep_a, theirs_a, f"fold_cold_{mask // 2}a")
+        theirs_a = hop(send_a, "tensor", mask)
+        keep_b, send_b = halve(keep_b, theirs_b, f"fold_cold_{mask // 2}b")
+        theirs_b = hop(send_b, "tensor", mask)
         mask *= 2
-    cold_sums = [cold_mine, cold_theirs]
+    cold_sums = [keep_a, theirs_a, keep_b, theirs_b]
 
     me = lax.axis_index("dp").astype(jnp.int32).reshape(1)
     each_w = width // groups
@@ -806,10 +828,11 @@
     keep_a, send_a, keep_b, send_b = run(
         make_hot_back(count, heads, size, groups, scale),
         [shape(halves[0]), shape(halves[0]), shape(halves[1]), shape(halves[1])],
-        after(grad_hot_all, cold_mine)
+        after(grad_hot_all, keep_a)
         + [me, qkv, proj, ctx_hot, ask_hot, gq, gk, gv, gp, fn_a, fn_b],
         "hot_back",
         extra=10,
+        moved=1024,
         smem=(count,),
         scratch=[
             pltpu.VMEM((heads * 3 * size, total), bf16),
@@ -823,11 +846,14 @@
         [after(arrived, keep_a), slot_grads, hidden, grad_pre],
         "weight_grads",
         extra=10,
+        moved=1024,
     )
     mask = 1
     while True:
         got_a = hop(send_a, "dp", mask)
         got_b = hop(send_b, "dp", groups // 2 // mask)
+        if mask == 1:
+            got_a, got_b = after((got_a, got_b), grad_up, cold_sums[2])
         if mask == groups // 2:
             break
         keep_a, send_a = halve(keep_a, got_a, f"fold_a_{mask}")
@@ -835,10 +861,10 @@
         mask *= 2
     parts = [keep_a, got_a, keep_b, got_b]
     layer_out, gate_grad = run(
-        make_epilogue(2),
+        make_epilogue(),
         [shape((rows, width)), shape((2, rows), f32)],
         cold_sums
-        + [tok[places:], mid_hot, perm, pick0, pick1, expert_out, gate_weights.T, cotangent],
+        + [tok_cold, mid_hot, perm, pick0, pick1, expert_out, gate_weights.T, cotangent],
         "epilogue",
         extra=4,
     )

time: 163 us -> 145 us (0.89)
  waiting for transfers between devices: 78.9 us -> 55.4 us
  starting transfers between devices: 43.6 us -> 49.3 us
  local copies, waits for them, and re-layouts: 5.04 us -> 3.31 us
    ppermute x49 -> x52, waiting for transfers between devices: 78.9 us -> 55.4 us  [hop(): return lax.ppermute(x, axis, [(i, i ^ mask) for i in range(size)])]
    ppermute x49 -> x52, starting transfers between devices: 43.6 us -> 49.3 us  [hop(): return lax.ppermute(x, axis, [(i, i ^ mask) for i in range(size)])]
    unnamed x22 -> x32, local copies, waits for them, and re-layouts: 5 us -> 3.31 us
    pallas_call x21 -> x23, Pallas kernels: 34.5 us -> 35.5 us  [run(): pl.pallas_call(body, out_shape=list(outs), in_specs=specs, out_specs=[pl....]
  transfers between devices with their start and end apart: 49 -> 52, of which waited for: 23 -> 25; matrix products, arithmetic and copies ran while one was open for 0% -> 0% of each run, Pallas kernels for 14% -> 16%
where the time goes in v4:
time: 145 us
  waiting for transfers between devices  55.4 us (38%)
  starting transfers between devices  49.3 us (34%)
  Pallas kernels  35.5 us (24%)
  local copies, waits for them, and re-layouts  3.31 us (2%)
    ppermute x52, waiting for transfers between devices, hop(): return lax.ppermute(x, axis, [(i, i ^ mask) for i in range(size)])  55.4 us
    ppermute x52, starting transfers between devices, hop(): return lax.ppermute(x, axis, [(i, i ^ mask) for i in range(size)])  49.3 us
    pallas_call x23, Pallas kernels, run(): pl.pallas_call(body, out_shape=list(outs), in_specs=specs, out_specs=[pl....  35.5 us
    unnamed x32, local copies, waits for them, and re-layouts  3.31 us
  transfers between devices with their start and end apart: 52, of which 25 were waited for; matrix products, arithmetic and copies ran while one was open for 0% of the time, Pallas kernels for 16%

profile of v4, /device:TPU:0, one launch (start us, length us, event | category | flops | bytes accessed | tf_op | source)
XLA Modules:
  0.0 144.6 jit_solution(12629516055631797588)
XLA Ops:
  0.6 3.4 %prologue.1 = (bf16[128,1280]{1,0:T(8,128)(2,1)}, bf16[16,1280]{1,0:T(8,128)(2,1)}, bf16[112,1280]{1,0:T(8,128)(2,1)}, bf16[16,1280]{1,0:T(8,128)(2,1)}, bf16[11...) custom-call(bf16[128,1280]{1,0:T(8,128)(2,1)} %tok_in.1, ...), custom_call_target="tpu_custom_call" | custom-call | bytes 1723908 | tf_op jit(solution)/shard_map/prologue/pallas_call | solution.py:55
  4.1 3.1 %collective-permute-start.4 = (bf16[128,1280]{1,0:T(8,128)(2,1)}, bf16[128,1280]{1,0:T(8,128)(2,1)S(1)}, u32[]{:S(2)}, u32[]{:S(2)}) collective-permute-start(bf16[128,1280]{1,0:T(8,128)(2,1)} %get-tuple-element.133.refs_0_), channel_id=1, source_target_pairs={{0,2},{1,3},{2,0},{3,1},{4,6},{5,7},{6,4},{7,5},{8,10},{9,11},{10,... | collective-permute-start | bytes 983048 | tf_op jit(solution)/shard_map/ppermute | solution.py:91
  7.1 2.6 %collective-permute-start = (bf16[128,1280]{1,0:T(8,128)(2,1)}, bf16[128,1280]{1,0:T(8,128)(2,1)S(1)}, u32[]{:S(2)}, u32[]{:S(2)}) collective-permute-start(bf16[128,1280]{1,0:T(8,128)(2,1)} %get-tuple-element.133.refs_0_), channel_id=1, source_target_pairs={{0,4},{1,5},{2,6},{3,7},{4,0},{5,1},{6,2},{7,3},{8,12},{9,13},{10,... | collective-permute-start | bytes 983048 | tf_op jit(solution)/shard_map/ppermute | solution.py:91
  9.7 12.2 %collective-permute-done.4.refs_2_ = bf16[128,1280]{1,0:T(8,128)(2,1)S(1)} collective-permute-done((bf16[128,1280]{1,0:T(8,128)(2,1)}, bf16[128,1280]{1,0:T(8,128)(2,1)S(1)}, u32[]{:S(2)}, u32[]{:S(2)}) %collective-permute-start.4) | collective-permute-done | bytes 327712 | tf_op jit(solution)/shard_map/ppermute | solution.py:91
  22.0 2.6 %collective-permute-done.refs_0_ = bf16[128,1280]{1,0:T(8,128)(2,1)S(1)} collective-permute-done((bf16[128,1280]{1,0:T(8,128)(2,1)}, bf16[128,1280]{1,0:T(8,128)(2,1)S(1)}, u32[]{:S(2)}, u32[]{:S(2)}) %collective-permute-start) | collective-permute-done | bytes 327712 | tf_op jit(solution)/shard_map/ppermute | solution.py:91
  29.0 2.3 %half.1 = (bf16[512,768]{1,0:T(8,128)(2,1)S(1)}, bf16[1280,512]{1,0:T(8,128)(2,1)S(1)}) custom-call(bf16[128,1280]{1,0:T(8,128)(2,1)S(1)} %copy-done.5, bf16[128,1280]{1,0:T(8,128)(2,1)S(1)} %collective-permute-done.3.refs_1_, bf16[128,1280]{1,0:T(8,128)(2,1)S(1)} %collective-permute-done.4.refs_2_, bf16[128,1280]{1,0:T(8,128)(2,1)S(1)} %collective-permute-done.5.refs_3_, ...), custom_call_target="tpu_custom_call" | custom-call | bytes 1024 | tf_op jit(solution)/shard_map/half/pallas_call | solution.py:55
  32.1 1.6 %collective-permute-done.7.refs_3_ = bf16[128,1280]{1,0:T(8,128)(2,1)S(1)} collective-permute-done((bf16[128,1280]{1,0:T(8,128)(2,1)S(1)}, bf16[128,1280]{1,0:T(8,128)(2,1)S(1)}, u32[]{:S(2)}, u32[]{:S(2)}) %collective-permute-start.7) | collective-permute-done | bytes 327712 | tf_op jit(solution)/shard_map/ppermute | solution.py:91
  33.7 3.1 %front.1 = (bf16[1024,768]{1,0:T(8,128)(2,1)S(1)}, bf16[128,256]{1,0:T(8,128)(2,1)S(1)}, bf16[128,256]{1,0:T(8,128)(2,1)S(1)}, bf16[64,1280]{1,0:T(8,128)(2,1)S(1)}, bf16[64,1280]{1,0:T(8,128)(2,1)S(1)}) custom-call(bf16[128,1280]{1,0:T(8,128)(2,1)S(1)} %collective-permute-done.refs_0_, bf16[128,1280]{1,0:T(8,128)(2,1)S(1)} %collective-permute-done.1.refs_1_, ...), custom_call_target="tpu_custom_call" | custom-call | bytes 1024 | tf_op jit(solution)/shard_map/front/pallas_call | solution.py:55
  39.7 1.9 %collective-permute-start.10 = (bf16[16,1280]{1,0:T(8,128)(2,1)S(1)}, bf16[16,1280]{1,0:T(8,128)(2,1)S(1)}, u32[]{:S(2)}, u32[]{:S(2)}) collective-permute-start(bf16[16,1280]{1,0:T(8,128)(2,1)S(1)} %get-tuple-element.147), channel_id=1, source_target_pairs={{0,4},{1,5},{2,6},{3,7},{4,0},{5,1},{6,2},{7,3},{8,12},{9,13},{10,... | collective-permute-start | bytes 122888 | tf_op jit(solution)/shard_map/ppermute | solution.py:91
  42.8 2.5 %collective-permute-done.10.refs_2_ = bf16[16,1280]{1,0:T(8,128)(2,1)S(1)} collective-permute-done((bf16[16,1280]{1,0:T(8,128)(2,1)S(1)}, bf16[16,1280]{1,0:T(8,128)(2,1)S(1)}, u32[]{:S(2)}, u32[]{:S(2)}) %collective-permute-start.10) | collective-permute-done | bytes 40992 | tf_op jit(solution)/shard_map/ppermute | solution.py:91
  45.3 2.1 %collective-permute-done.11.refs_3_ = bf16[16,1280]{1,0:T(8,128)(2,1)S(1)} collective-permute-done((bf16[16,1280]{1,0:T(8,128)(2,1)S(1)}, bf16[16,1280]{1,0:T(8,128)(2,1)S(1)}, u32[]{:S(2)}, u32[]{:S(2)}) %collective-permute-start.11) | collective-permute-done | bytes 40992 | tf_op jit(solution)/shard_map/ppermute | solution.py:91
  47.8 1.8 %collective-permute-start.15 = (bf16[112,1280]{1,0:T(8,128)(2,1)S(1)}, bf16[112,1280]{1,0:T(8,128)(2,1)S(1)}, u32[]{:S(2)}, u32[]{:S(2)}) collective-permute-start(bf16[112,1280]{1,0:T(8,128)(2,1)S(1)} %copy-done.15), channel_id=1, source_target_pairs={{0,4},{1,5},{2,6},{3,7},{4,0},{5,1},{6,2},{7,3},{8,12},{9,13},{10,... | collective-permute-start | bytes 860168 | tf_op jit(solution)/shard_map/ppermute | solution.py:91
  53.2 4.1 %cold.1 = (bf16[896,256]{1,0:T(8,128)(2,1)S(1)}, bf16[896,256]{1,0:T(8,128)(2,1)S(1)}, bf16[320,1280]{1,0:T(8,128)(2,1)S(1)}, bf16[320,1280]{1,0:T(8,128)(2,1)S(...) custom-call(bf16[1024,768]{1,0:T(8,128)(2,1)S(1)} %get-tuple-element.180.qkv.refs_8_.refs_9_, ...), custom_call_target="tpu_custom_call" | custom-call | flops 1073741824 | bytes 5439488 | tf_op jit(solution)/shard_map/cold/pallas_call | solution.py:55
  57.5 3.2 %collective-permute-done.16.refs_2_ = bf16[112,1280]{1,0:T(8,128)(2,1)S(1)} collective-permute-done((bf16[112,1280]{1,0:T(8,128)(2,1)S(1)}, bf16[112,1280]{1,0:T(8,128)(2,1)S(1)}, u32[]{:S(2)}, u32[]{:S(2)}) %collective-permute-start.16) | collective-permute-done | bytes 286752 | tf_op jit(solution)/shard_map/ppermute | solution.py:91
  62.5 4.0 %collective-permute-start.18 = (bf16[16,2560]{1,0:T(8,128)(2,1)S(1)}, bf16[16,2560]{1,0:T(8,128)(2,1)S(1)}, u32[]{:S(2)}, u32[]{:S(2)}) collective-permute-start(bf16[16,2560]{1,0:T(8,128)(2,1)S(1)} %pad_maximum_fusion.refs_0_), channel_id=1, source_target_pairs={{0,2},{1,3},{2,0},{3,1},{4,6},{5,7},{6,4},{7,5},{8,10},{9,11},{10,... | collective-permute-start | bytes 245768 | tf_op jit(solution)/shard_map/ppermute | solution.py:91
  69.7 2.5 %collective-permute-done.22.refs_6_ = bf16[16,2560]{1,0:T(8,128)(2,1)S(1)} collective-permute-done((bf16[16,2560]{1,0:T(8,128)(2,1)S(1)}, bf16[16,2560]{1,0:T(8,128)(2,1)S(1)}, u32[]{:S(2)}, u32[]{:S(2)}) %collective-permute-start.22) | collective-permute-done | bytes 81952 | tf_op jit(solution)/shard_map/ppermute | solution.py:91
  75.9 3.3 %experts.1 = (bf16[128,1280]{1,0:T(8,128)(2,1)S(1)}, bf16[128,1280]{1,0:T(8,128)(2,1)S(1)}, bf16[2,128,640]{2,1,0:T(8,128)(2,1)S(1)}, bf16[2,128,640]{2,1,0:T(8,...) custom-call(bf16[16,2560]{1,0:T(8,128)(2,1)S(1)} %pad_maximum_fusion.refs_0_, ...), custom_call_target="tpu_custom_call" | custom-call | flops 1258291200 | bytes 9175040 | tf_op jit(solution)/shard_map/experts/pallas_call | solution.py:55
  79.5 3.4 %collective-permute-done.27.refs_6_ = bf16[112,1280]{1,0:T(8,128)(2,1)S(1)} collective-permute-done((bf16[112,1280]{1,0:T(8,128)(2,1)S(1)}, bf16[112,1280]{1,0:T(8,128)(2,1)S(1)}, u32[]{:S(2)}, u32[]{:S(2)}) %collective-permute-start.27) | collective-permute-done | bytes 286752 | tf_op jit(solution)/shard_map/ppermute | solution.py:91
  86.1 2.6 %collective-permute-start.31 = (bf16[16,2560]{1,0:T(8,128)(2,1)S(1)}, bf16[16,2560]{1,0:T(8,128)(2,1)S(1)}, u32[]{:S(2)}, u32[]{:S(2)}) collective-permute-start(bf16[16,2560]{1,0:T(8,128)(2,1)S(1)} %get-tuple-element.177), channel_id=1, source_target_pairs={{0,4},{1,5},{2,6},{3,7},{4,0},{5,1},{6,2},{7,3},{8,12},{9,13},{10,... | collective-permute-start | bytes 245768 | tf_op jit(solution)/shard_map/ppermute | solution.py:91
  89.1 7.1 %cold_back.1 = (bf16[896,256]{1,0:T(8,128)(2,1)S(1)}, f32[256,1024]{1,0:T(8,128)S(1)}, f32[256,1024]{1,0:T(8,128)S(1)}, f32[256,1280]{1,0:T(8,128)S(1)}) custom-call(bf16[112,1280]{1,0:T(8,128)(2,1)S(1)} %copy-done.15, bf16[112,1280]{1,0:T(8,128)(2,1)S(1)} %collective-permute-done.6.refs_1_, bf16[112,1280]{1,0:T(8,128)(2,1)S(1)} %collective-permute-done.16.refs_2_, ...), custom_call_target="tpu_custom_call" | custom-call | flops 2684354560 | bytes 9306112 | tf_op jit(solution)/shard_map/cold_back/pallas_call | solution.py:55
  101.6 2.4 %collective-permute-done.36.refs_3_ = bf16[4,2560]{1,0:T(4,128)(2,1)S(1)} collective-permute-done((bf16[4,2560]{1,0:T(4,128)(2,1)S(1)}, bf16[4,2560]{1,0:T(4,128)(2,1)S(1)}, u32[]{:S(2)}, u32[]{:S(2)}) %collective-permute-start.36) | collective-permute-done | bytes 20512 | tf_op jit(solution)/shard_map/ppermute | solution.py:91
  104.1 3.0 %collective-permute-done.37.theirs = bf16[160,1280]{1,0:T(8,128)(2,1)S(1)} collective-permute-done((bf16[160,1280]{1,0:T(8,128)(2,1)S(1)}, bf16[160,1280]{1,0:T(8,128)(2,1)S(1)}, u32[]{:S(2)}, u32[]{:S(2)}) %collective-permute-start.37) | collective-permute-done | bytes 409632 | tf_op jit(solution)/shard_map/ppermute | solution.py:91
  107.3 2.4 %collective-permute-start.42 = (bf16[16,1280]{1,0:T(8,128)(2,1)S(1)}, bf16[16,1280]{1,0:T(8,128)(2,1)S(1)}, u32[]{:S(2)}, u32[]{:S(2)}) collective-permute-start(bf16[16,1280]{1,0:T(8,128)(2,1)S(1)} %get-tuple-element.220.refs_0_), channel_id=1, source_target_pairs={{0,4},{1,5},{2,6},{3,7},{4,0},{5,1},{6,2},{7,3},{8,12},{9,13},{10,... | collective-permute-start | bytes 122888 | tf_op jit(solution)/shard_map/ppermute | solution.py:91
  109.7 1.7 %collective-permute-start.40 = (bf16[16,1280]{1,0:T(8,128)(2,1)S(1)}, bf16[16,1280]{1,0:T(8,128)(2,1)S(1)}, u32[]{:S(2)}, u32[]{:S(2)}) collective-permute-start(bf16[16,1280]{1,0:T(8,128)(2,1)S(1)} %get-tuple-element.220.refs_0_), channel_id=1, source_target_pairs={{0,2},{1,3},{2,0},{3,1},{4,6},{5,7},{6,4},{7,5},{8,10},{9,11},{10,... | collective-permute-start | bytes 122888 | tf_op jit(solution)/shard_map/ppermute | solution.py:91
  114.4 1.9 %collective-permute-done.44.refs_6_ = bf16[16,1280]{1,0:T(8,128)(2,1)S(1)} collective-permute-done((bf16[16,1280]{1,0:T(8,128)(2,1)S(1)}, bf16[16,1280]{1,0:T(8,128)(2,1)S(1)}, u32[]{:S(2)}, u32[]{:S(2)}) %collective-permute-start.44) | collective-permute-done | bytes 40992 | tf_op jit(solution)/shard_map/ppermute | solution.py:91
  117.5 3.2 %hot_back.1 = (bf16[320,640]{1,0:T(8,128)(2,1)S(1)}, bf16[320,640]{1,0:T(8,128)(2,1)S(1)}, bf16[320,640]{1,0:T(8,128)(2,1)S(1)}, bf16[320,640]{1,0:T(8,128)(2,1)S(1)}) custom-call(bf16[16,1280]{1,0:T(8,128)(2,1)S(1)} %get-tuple-element.220.refs_0_, bf16[16,1280]{1,0:T(8,128)(2,1)S(1)} %collective-permute-done.39.refs_1_, ...), custom_call_target="tpu_custom_call" | custom-call | bytes 1024 | tf_op jit(solution)/shard_map/hot_back/pallas_call | solution.py:55
  120.8 1.7 %collective-permute-start.48 = (bf16[320,640]{1,0:T(8,128)(2,1)S(1)}, bf16[320,640]{1,0:T(8,128)(2,1)S(1)}, u32[]{:S(2)}, u32[]{:S(2)}) collective-permute-start(bf16[320,640]{1,0:T(8,128)(2,1)S(1)} %get-tuple-element.234), channel_id=1, source_target_pairs={{0,8},{8,0},{16,24},{24,16},{1,9},{9,1},{17,25},{25,17},{2,10},{10... | collective-permute-start | bytes 1228808 | tf_op jit(solution)/shard_map/ppermute | solution.py:91
  124.1 2.5 %collective-permute-start.38 = (bf16[80,1280]{1,0:T(8,128)(2,1)S(1)}, bf16[80,1280]{1,0:T(8,128)(2,1)S(1)}, u32[]{:S(2)}, u32[]{:S(2)}) collective-permute-start(bf16[80,1280]{1,0:T(8,128)(2,1)S(1)} %get-tuple-element.203), channel_id=1, source_target_pairs={{0,4},{1,5},{2,6},{3,7},{4,0},{5,1},{6,2},{7,3},{8,12},{9,13},{10,... | collective-permute-start | bytes 614408 | tf_op jit(solution)/shard_map/ppermute | solution.py:91
  126.5 4.3 %weight_grads.1 = (bf16[2,1280,640]{2,1,0:T(8,128)(2,1)}, bf16[2,640,1280]{2,1,0:T(8,128)(2,1)}) custom-call(bf16[128,1280]{1,0:T(8,128)(2,1)S(1)} %get-tuple-element.237.arrived, bf16[128,1280]{1,0:T(8,128)(2,1)S(1)} %get-tuple-element.238.grads, bf16[2,128,640]{2,1,0:T(8,128)(2,1)S(1)} %get-tuple-element.239.hidden, ...), custom_call_target="tpu_custom_call" | custom-call | bytes 1024 | tf_op jit(solution)/shard_map/weight_grads/pallas_call | solution.py:55
  130.8 1.7 %collective-permute-done.46.theirs = bf16[64,1280]{1,0:T(8,128)(2,1)S(1)} collective-permute-done((bf16[64,1280]{1,0:T(8,128)(2,1)S(1)}, bf16[64,1280]{1,0:T(8,128)(2,1)S(1)}, u32[]{:S(2)}, u32[]{:S(2)}) %collective-permute-start.46) | collective-permute-done | bytes 163872 | tf_op jit(solution)/shard_map/ppermute | solution.py:91
  134.4 1.7 %collective-permute-start.50 = (bf16[160,640]{1,0:T(8,128)(2,1)S(1)}, bf16[160,640]{1,0:T(8,128)(2,1)S(1)}, u32[]{:S(2)}, u32[]{:S(2)}) collective-permute-start(bf16[160,640]{1,0:T(8,128)(2,1)S(1)} %get-tuple-element.244), channel_id=1, source_target_pairs={{0,16},{8,24},{16,0},{24,8},{1,17},{9,25},{17,1},{25,9},{2,18},{10... | collective-permute-start | bytes 614408 | tf_op jit(solution)/shard_map/ppermute | solution.py:91
  137.1 4.6 %collective-permute-done.47.refs_3_ = bf16[32,1280]{1,0:T(8,128)(2,1)S(1)} collective-permute-done((bf16[32,1280]{1,0:T(8,128)(2,1)S(1)}, bf16[32,1280]{1,0:T(8,128)(2,1)S(1)}, u32[]{:S(2)}, u32[]{:S(2)}) %collective-permute-start.47) | collective-permute-done | bytes 81952 | tf_op jit(solution)/shard_map/ppermute | solution.py:91
  (128 shorter events, 43.2 us)
Async XLA Ops:
  4.1 17.9 %collective-permute-start.4 = (bf16[128,1280]{1,0:T(8,128)(2,1)}, bf16[128,1280]{1,0:T(8,128)(2,1)S(1)}, u32[]{:S(2)}, u32[]{:S(2)}) collective-permute-start(bf16[128,1280]{1,0:T(8,128)(2,1)} %get-tuple-element.133.refs_0_), channel_id=1, source_target_pairs={{0,2},{1,3},{2,0},{3,1},{4,6},{5,7},{6,4},{7,5},{8,10},{9,11},{10,... | collective-permute-start | bytes 983048 | tf_op jit(solution)/shard_map/ppermute | solution.py:91
  7.1 17.4 %collective-permute-start = (bf16[128,1280]{1,0:T(8,128)(2,1)}, bf16[128,1280]{1,0:T(8,128)(2,1)S(1)}, u32[]{:S(2)}, u32[]{:S(2)}) collective-permute-start(bf16[128,1280]{1,0:T(8,128)(2,1)} %get-tuple-element.133.refs_0_), channel_id=1, source_target_pairs={{0,4},{1,5},{2,6},{3,7},{4,0},{5,1},{6,2},{7,3},{8,12},{9,13},{10,... | collective-permute-start | bytes 983048 | tf_op jit(solution)/shard_map/ppermute | solution.py:91
  9.7 18.3 %collective-permute-start.3 = (bf16[128,1280]{1,0:T(8,128)(2,1)}, bf16[128,1280]{1,0:T(8,128)(2,1)S(1)}, u32[]{:S(2)}, u32[]{:S(2)}) collective-permute-start(bf16[128,1280]{1,0:T(8,128)(2,1)} %get-tuple-element.133.refs_0_), channel_id=1, source_target_pairs={{0,1},{1,0},{2,3},{3,2},{4,5},{5,4},{6,7},{7,6},{8,9},{9,8},{10,11... | collective-permute-start | bytes 983048 | tf_op jit(solution)/shard_map/ppermute | solution.py:91
  22.0 6.0 %collective-permute-start.5 = (bf16[128,1280]{1,0:T(8,128)(2,1)S(1)}, bf16[128,1280]{1,0:T(8,128)(2,1)S(1)}, u32[]{:S(2)}, u32[]{:S(2)}) collective-permute-start(bf16[128,1280]{1,0:T(8,128)(2,1)S(1)} %collective-permute-done.4.refs_2_), channel_id=1, source_target_pairs={{0,1},{1,0},{2,3},{3,2},{4,5},{5,4},{6,7},{7,6},{8,9},{9,8},{10,11... | collective-permute-start | bytes 983048 | tf_op jit(solution)/shard_map/ppermute | solution.py:91
  24.5 7.6 %collective-permute-start.2 = (bf16[128,1280]{1,0:T(8,128)(2,1)S(1)}, bf16[128,1280]{1,0:T(8,128)(2,1)S(1)}, u32[]{:S(2)}, u32[]{:S(2)}) collective-permute-start(bf16[128,1280]{1,0:T(8,128)(2,1)S(1)} %collective-permute-done.refs_0_), channel_id=1, source_target_pairs={{0,2},{1,3},{2,0},{3,1},{4,6},{5,7},{6,4},{7,5},{8,10},{9,11},{10,... | collective-permute-start | bytes 983048 | tf_op jit(solution)/shard_map/ppermute | solution.py:91
  39.7 5.5 %collective-permute-start.10 = (bf16[16,1280]{1,0:T(8,128)(2,1)S(1)}, bf16[16,1280]{1,0:T(8,128)(2,1)S(1)}, u32[]{:S(2)}, u32[]{:S(2)}) collective-permute-start(bf16[16,1280]{1,0:T(8,128)(2,1)S(1)} %get-tuple-element.147), channel_id=1, source_target_pairs={{0,4},{1,5},{2,6},{3,7},{4,0},{5,1},{6,2},{7,3},{8,12},{9,13},{10,... | collective-permute-start | bytes 122888 | tf_op jit(solution)/shard_map/ppermute | solution.py:91
  41.6 5.8 %collective-permute-start.11 = (bf16[16,1280]{1,0:T(8,128)(2,1)S(1)}, bf16[16,1280]{1,0:T(8,128)(2,1)S(1)}, u32[]{:S(2)}, u32[]{:S(2)}) collective-permute-start(bf16[16,1280]{1,0:T(8,128)(2,1)S(1)} %get-tuple-element.148), channel_id=1, source_target_pairs={{0,6},{1,7},{2,4},{3,5},{4,2},{5,3},{6,0},{7,1},{8,14},{9,15},{10,... | collective-permute-start | bytes 122888 | tf_op jit(solution)/shard_map/ppermute | solution.py:91
  47.8 12.9 %collective-permute-start.16 = (bf16[112,1280]{1,0:T(8,128)(2,1)S(1)}, bf16[112,1280]{1,0:T(8,128)(2,1)S(1)}, u32[]{:S(2)}, u32[]{:S(2)}) collective-permute-start(bf16[112,1280]{1,0:T(8,128)(2,1)S(1)} %copy-done.15), channel_id=1, source_target_pairs={{0,2},{1,3},{2,0},{3,1},{4,6},{5,7},{6,4},{7,5},{8,10},{9,11},{10,... | collective-permute-start | bytes 860168 | tf_op jit(solution)/shard_map/ppermute | solution.py:91
  47.8 14.4 %collective-permute-start.15 = (bf16[112,1280]{1,0:T(8,128)(2,1)S(1)}, bf16[112,1280]{1,0:T(8,128)(2,1)S(1)}, u32[]{:S(2)}, u32[]{:S(2)}) collective-permute-start(bf16[112,1280]{1,0:T(8,128)(2,1)S(1)} %copy-done.15), channel_id=1, source_target_pairs={{0,4},{1,5},{2,6},{3,7},{4,0},{5,1},{6,2},{7,3},{8,12},{9,13},{10,... | collective-permute-start | bytes 860168 | tf_op jit(solution)/shard_map/ppermute | solution.py:91
  49.7 7.6 %collective-permute-start.12 = (bf16[4,2560]{1,0:T(4,128)(2,1)S(1)}, bf16[4,2560]{1,0:T(4,128)(2,1)S(1)}, u32[]{:S(2)}, u32[]{:S(2)}) collective-permute-start(bf16[4,2560]{1,0:T(4,128)(2,1)S(1)} %get-tuple-element.157), channel_id=1, source_target_pairs={{0,8},{8,0},{16,24},{24,16},{1,9},{9,1},{17,25},{25,17},{2,10},{10... | collective-permute-start | bytes 61448 | tf_op jit(solution)/shard_map/ppermute | solution.py:91
  51.2 6.1 %collective-permute-start.13 = (bf16[4,2560]{1,0:T(4,128)(2,1)S(1)}, bf16[4,2560]{1,0:T(4,128)(2,1)S(1)}, u32[]{:S(2)}, u32[]{:S(2)}) collective-permute-start(bf16[4,2560]{1,0:T(4,128)(2,1)S(1)} %get-tuple-element.158), channel_id=1, source_target_pairs={{0,16},{8,24},{16,0},{24,8},{1,17},{9,25},{17,1},{25,9},{2,18},{10... | collective-permute-start | bytes 61448 | tf_op jit(solution)/shard_map/ppermute | solution.py:91
  62.3 5.5 %collective-permute-start.20 = (bf16[16,2560]{1,0:T(8,128)(2,1)S(1)}, bf16[16,2560]{1,0:T(8,128)(2,1)S(1)}, u32[]{:S(2)}, u32[]{:S(2)}) collective-permute-start(bf16[16,2560]{1,0:T(8,128)(2,1)S(1)} %pad_maximum_fusion.refs_0_), channel_id=1, source_target_pairs={{0,4},{1,5},{2,6},{3,7},{4,0},{5,1},{6,2},{7,3},{8,12},{9,13},{10,... | collective-permute-start | bytes 245768 | tf_op jit(solution)/shard_map/ppermute | solution.py:91
  62.5 7.2 %collective-permute-start.18 = (bf16[16,2560]{1,0:T(8,128)(2,1)S(1)}, bf16[16,2560]{1,0:T(8,128)(2,1)S(1)}, u32[]{:S(2)}, u32[]{:S(2)}) collective-permute-start(bf16[16,2560]{1,0:T(8,128)(2,1)S(1)} %pad_maximum_fusion.refs_0_), channel_id=1, source_target_pairs={{0,2},{1,3},{2,0},{3,1},{4,6},{5,7},{6,4},{7,5},{8,10},{9,11},{10,... | collective-permute-start | bytes 245768 | tf_op jit(solution)/shard_map/ppermute | solution.py:91
  73.5 5.8 %collective-permute-start.24 = (bf16[320,1280]{1,0:T(8,128)(2,1)S(1)}, bf16[320,1280]{1,0:T(8,128)(2,1)S(1)}, u32[]{:S(2)}, u32[]{:S(2)}) collective-permute-start(bf16[320,1280]{1,0:T(8,128)(2,1)S(1)} %get-tuple-element.163), channel_id=1, source_target_pairs={{0,1},{1,0},{2,3},{3,2},{4,5},{5,4},{6,7},{7,6},{8,9},{9,8},{10,11... | collective-permute-start | bytes 2457608 | tf_op jit(solution)/shard_map/ppermute | solution.py:91
  73.7 5.5 %collective-permute-start.28 = (bf16[128,1280]{1,0:T(8,128)(2,1)S(1)}, bf16[128,1280]{1,0:T(8,128)(2,1)S(1)}, u32[]{:S(2)}, u32[]{:S(2)}) collective-permute-start(bf16[128,1280]{1,0:T(8,128)(2,1)S(1)} %get-tuple-element.172), channel_id=1, source_target_pairs={{0,1},{1,0},{2,3},{3,2},{4,5},{5,4},{6,7},{7,6},{8,9},{9,8},{10,11... | collective-permute-start | bytes 983048 | tf_op jit(solution)/shard_map/ppermute | solution.py:91
  74.0 8.9 %collective-permute-start.27 = (bf16[112,1280]{1,0:T(8,128)(2,1)S(1)}, bf16[112,1280]{1,0:T(8,128)(2,1)S(1)}, u32[]{:S(2)}, u32[]{:S(2)}) collective-permute-start(bf16[112,1280]{1,0:T(8,128)(2,1)S(1)} %collective-permute-done.15.refs_4_), channel_id=1, source_target_pairs={{0,2},{1,3},{2,0},{3,1},{4,6},{5,7},{6,4},{7,5},{8,10},{9,11},{10,... | collective-permute-start | bytes 860168 | tf_op jit(solution)/shard_map/ppermute | solution.py:91
  75.4 7.5 %collective-permute-start.25 = (bf16[112,1280]{1,0:T(8,128)(2,1)S(1)}, bf16[112,1280]{1,0:T(8,128)(2,1)S(1)}, u32[]{:S(2)}, u32[]{:S(2)}) collective-permute-start(bf16[112,1280]{1,0:T(8,128)(2,1)S(1)} %collective-permute-done.15.refs_4_), channel_id=1, source_target_pairs={{0,1},{1,0},{2,3},{3,2},{4,5},{5,4},{6,7},{7,6},{8,9},{9,8},{10,11... | collective-permute-start | bytes 860168 | tf_op jit(solution)/shard_map/ppermute | solution.py:91
  75.4 7.5 %collective-permute-start.26 = (bf16[112,1280]{1,0:T(8,128)(2,1)S(1)}, bf16[112,1280]{1,0:T(8,128)(2,1)S(1)}, u32[]{:S(2)}, u32[]{:S(2)}) collective-permute-start(bf16[112,1280]{1,0:T(8,128)(2,1)S(1)} %collective-permute-done.16.refs_2_), channel_id=1, source_target_pairs={{0,1},{1,0},{2,3},{3,2},{4,5},{5,4},{6,7},{7,6},{8,9},{9,8},{10,11... | collective-permute-start | bytes 860168 | tf_op jit(solution)/shard_map/ppermute | solution.py:91
  83.0 6.2 %collective-permute-start.33 = (bf16[112,1280]{1,0:T(8,128)(2,1)S(1)}, bf16[112,1280]{1,0:T(8,128)(2,1)S(1)}, u32[]{:S(2)}, u32[]{:S(2)}) collective-permute-start(bf16[112,1280]{1,0:T(8,128)(2,1)S(1)} %collective-permute-done.27.refs_6_), channel_id=1, source_target_pairs={{0,1},{1,0},{2,3},{3,2},{4,5},{5,4},{6,7},{7,6},{8,9},{9,8},{10,11... | collective-permute-start | bytes 860168 | tf_op jit(solution)/shard_map/ppermute | solution.py:91
  84.7 11.6 %collective-permute-start.30 = (bf16[16,2560]{1,0:T(8,128)(2,1)S(1)}, bf16[16,2560]{1,0:T(8,128)(2,1)S(1)}, u32[]{:S(2)}, u32[]{:S(2)}) collective-permute-start(bf16[16,2560]{1,0:T(8,128)(2,1)S(1)} %get-tuple-element.176), channel_id=1, source_target_pairs={{0,2},{1,3},{2,0},{3,1},{4,6},{5,7},{6,4},{7,5},{8,10},{9,11},{10,... | collective-permute-start | bytes 245768 | tf_op jit(solution)/shard_map/ppermute | solution.py:91
  86.1 10.1 %collective-permute-start.31 = (bf16[16,2560]{1,0:T(8,128)(2,1)S(1)}, bf16[16,2560]{1,0:T(8,128)(2,1)S(1)}, u32[]{:S(2)}, u32[]{:S(2)}) collective-permute-start(bf16[16,2560]{1,0:T(8,128)(2,1)S(1)} %get-tuple-element.177), channel_id=1, source_target_pairs={{0,4},{1,5},{2,6},{3,7},{4,0},{5,1},{6,2},{7,3},{8,12},{9,13},{10,... | collective-permute-start | bytes 245768 | tf_op jit(solution)/shard_map/ppermute | solution.py:91
  88.7 7.5 %collective-permute-start.32 = (bf16[16,2560]{1,0:T(8,128)(2,1)S(1)}, bf16[16,2560]{1,0:T(8,128)(2,1)S(1)}, u32[]{:S(2)}, u32[]{:S(2)}) collective-permute-start(bf16[16,2560]{1,0:T(8,128)(2,1)S(1)} %get-tuple-element.178), channel_id=1, source_target_pairs={{0,6},{1,7},{2,4},{3,5},{4,2},{5,3},{6,0},{7,1},{8,14},{9,15},{10,... | collective-permute-start | bytes 245768 | tf_op jit(solution)/shard_map/ppermute | solution.py:91
  96.3 10.7 %collective-permute-start.37 = (bf16[160,1280]{1,0:T(8,128)(2,1)S(1)}, bf16[160,1280]{1,0:T(8,128)(2,1)S(1)}, u32[]{:S(2)}, u32[]{:S(2)}) collective-permute-start(bf16[160,1280]{1,0:T(8,128)(2,1)S(1)} %get-tuple-element.192), channel_id=1, source_target_pairs={{0,2},{1,3},{2,0},{3,1},{4,6},{5,7},{6,4},{7,5},{8,10},{9,11},{10,... | collective-permute-start | bytes 1228808 | tf_op jit(solution)/shard_map/ppermute | solution.py:91
  107.3 5.0 %collective-permute-start.42 = (bf16[16,1280]{1,0:T(8,128)(2,1)S(1)}, bf16[16,1280]{1,0:T(8,128)(2,1)S(1)}, u32[]{:S(2)}, u32[]{:S(2)}) collective-permute-start(bf16[16,1280]{1,0:T(8,128)(2,1)S(1)} %get-tuple-element.220.refs_0_), channel_id=1, source_target_pairs={{0,4},{1,5},{2,6},{3,7},{4,0},{5,1},{6,2},{7,3},{8,12},{9,13},{10,... | collective-permute-start | bytes 122888 | tf_op jit(solution)/shard_map/ppermute | solution.py:91
  109.7 4.7 %collective-permute-start.40 = (bf16[16,1280]{1,0:T(8,128)(2,1)S(1)}, bf16[16,1280]{1,0:T(8,128)(2,1)S(1)}, u32[]{:S(2)}, u32[]{:S(2)}) collective-permute-start(bf16[16,1280]{1,0:T(8,128)(2,1)S(1)} %get-tuple-element.220.refs_0_), channel_id=1, source_target_pairs={{0,2},{1,3},{2,0},{3,1},{4,6},{5,7},{6,4},{7,5},{8,10},{9,11},{10,... | collective-permute-start | bytes 122888 | tf_op jit(solution)/shard_map/ppermute | solution.py:91
  120.8 11.9 %collective-permute-start.48 = (bf16[320,640]{1,0:T(8,128)(2,1)S(1)}, bf16[320,640]{1,0:T(8,128)(2,1)S(1)}, u32[]{:S(2)}, u32[]{:S(2)}) collective-permute-start(bf16[320,640]{1,0:T(8,128)(2,1)S(1)} %get-tuple-element.234), channel_id=1, source_target_pairs={{0,8},{8,0},{16,24},{24,16},{1,9},{9,1},{17,25},{25,17},{2,10},{10... | collective-permute-start | bytes 1228808 | tf_op jit(solution)/shard_map/ppermute | solution.py:91
  122.5 11.2 %collective-permute-start.49 = (bf16[320,640]{1,0:T(8,128)(2,1)S(1)}, bf16[320,640]{1,0:T(8,128)(2,1)S(1)}, u32[]{:S(2)}, u32[]{:S(2)}) collective-permute-start(bf16[320,640]{1,0:T(8,128)(2,1)S(1)} %get-tuple-element.235), channel_id=1, source_target_pairs={{0,16},{8,24},{16,0},{24,8},{1,17},{9,25},{17,1},{25,9},{2,18},{10... | collective-permute-start | bytes 1228808 | tf_op jit(solution)/shard_map/ppermute | solution.py:91
  124.0 8.6 %collective-permute-start.46 = (bf16[64,1280]{1,0:T(8,128)(2,1)S(1)}, bf16[64,1280]{1,0:T(8,128)(2,1)S(1)}, u32[]{:S(2)}, u32[]{:S(2)}) collective-permute-start(bf16[64,1280]{1,0:T(8,128)(2,1)S(1)} %get-tuple-element.210), channel_id=1, source_target_pairs={{0,2},{1,3},{2,0},{3,1},{4,6},{5,7},{6,4},{7,5},{8,10},{9,11},{10,... | collective-permute-start | bytes 491528 | tf_op jit(solution)/shard_map/ppermute | solution.py:91
  124.1 13.1 %collective-permute-start.38 = (bf16[80,1280]{1,0:T(8,128)(2,1)S(1)}, bf16[80,1280]{1,0:T(8,128)(2,1)S(1)}, u32[]{:S(2)}, u32[]{:S(2)}) collective-permute-start(bf16[80,1280]{1,0:T(8,128)(2,1)S(1)} %get-tuple-element.203), channel_id=1, source_target_pairs={{0,4},{1,5},{2,6},{3,7},{4,0},{5,1},{6,2},{7,3},{8,12},{9,13},{10,... | collective-permute-start | bytes 614408 | tf_op jit(solution)/shard_map/ppermute | solution.py:91
  134.0 9.1 %collective-permute-start.51 = (bf16[160,640]{1,0:T(8,128)(2,1)S(1)}, bf16[160,640]{1,0:T(8,128)(2,1)S(1)}, u32[]{:S(2)}, u32[]{:S(2)}) collective-permute-start(bf16[160,640]{1,0:T(8,128)(2,1)S(1)} %get-tuple-element.248), channel_id=1, source_target_pairs={{0,8},{8,0},{16,24},{24,16},{1,9},{9,1},{17,25},{25,17},{2,10},{10... | collective-permute-start | bytes 614408 | tf_op jit(solution)/shard_map/ppermute | solution.py:91
  134.4 8.7 %collective-permute-start.50 = (bf16[160,640]{1,0:T(8,128)(2,1)S(1)}, bf16[160,640]{1,0:T(8,128)(2,1)S(1)}, u32[]{:S(2)}, u32[]{:S(2)}) collective-permute-start(bf16[160,640]{1,0:T(8,128)(2,1)S(1)} %get-tuple-element.244), channel_id=1, source_target_pairs={{0,16},{8,24},{16,0},{24,8},{1,17},{9,25},{17,1},{25,9},{2,18},{10... | collective-permute-start | bytes 614408 | tf_op jit(solution)/shard_map/ppermute | solution.py:91
  136.1 5.7 %collective-permute-start.47 = (bf16[32,1280]{1,0:T(8,128)(2,1)S(1)}, bf16[32,1280]{1,0:T(8,128)(2,1)S(1)}, u32[]{:S(2)}, u32[]{:S(2)}) collective-permute-start(bf16[32,1280]{1,0:T(8,128)(2,1)S(1)} %get-tuple-element.212), channel_id=1, source_target_pairs={{0,4},{1,5},{2,6},{3,7},{4,0},{5,1},{6,2},{7,3},{8,12},{9,13},{10,... | collective-permute-start | bytes 245768 | tf_op jit(solution)/shard_map/ppermute | solution.py:91
  (36 other events, 329.2 us)

commit v5 on v4

--- a/solution.py
+++ b/solution.py
@@ -691,6 +691,11 @@
         ],
     )
     hot_sums = fold_scatter(even, odd, places, "fold_hot")
+    start, mask = after(cot_cold, have[count - 2]), far
+    while mask > 1:
+        cots[mask] = hop(start, "tensor", mask)
+        mask //= 2
+    hot_sums = after(hot_sums, list(cots.values()))
 
     outs = run(
         make_mid(count // 2, groups),
@@ -716,25 +721,20 @@
         extra=14,
         flops=4 * total * total * heads * LANES,
     )
-    mask = far
-    starts = {0: after(cot_cold, mid_hot)}
-    while mask > 1:
-        cots[mask] = hop(starts[0], "tensor", mask)
-        mask //= 2
-    landed = jnp.concatenate(
-        [pieces[0]] + [hop(pieces[g], "dp", g) for g in range(1, groups)], axis=0
-    )
-    landed = after(landed, ctx_cold, list(cots.values()))
-    arrived_all = gather_rel(landed)
-    start, mask = {k: after(y, arrived_all[count - 2], arrived_all[2]) for k, y in cots.items()}, far // 2
+    start, mask = {k: after(y, mid_hot) for k, y in cots.items()}, far // 2
     early = [k for k in cots if k and k % 2 == 0]
-    for k in early:
-        cots[k + 1] = hop(after(cots[k], arrived_all), "tensor", 1)
     while mask > 1:
         for k in list(cots):
             if k % 2 == 0 and k > mask and k ^ mask not in cots:
                 start[k ^ mask] = cots[k ^ mask] = hop(start[k], "tensor", mask)
         mask //= 2
+    landed = jnp.concatenate(
+        [pieces[0]] + [hop(pieces[g], "dp", g) for g in range(1, groups)], axis=0
+    )
+    landed = after(landed, ctx_cold, list(cots.values()))
+    arrived_all = gather_rel(landed)
+    for k in early:
+        cots[k + 1] = hop(after(cots[k], arrived_all), "tensor", 1)
     theirs_a = hop(after(odd_a, arrived_all), "tensor", 1)
     theirs_b = hop(after(odd_b, arrived_all), "tensor", 1)
     arrived, slot_grads, hidden, grad_pre, even, odd = run(
@@ -755,6 +755,7 @@
     keep_a, send_a = halve(even_a, theirs_a, "fold_cold_1a")
     keep_b, send_b = halve(even_b, theirs_b, "fold_cold_1b")
     sums = fold_scatter(even, after(odd, list(cots.values()), keep_a, keep_b), places, "fold_slots")
+    theirs_a = hop(after(send_a, sums[0]), "tensor", 2)
     for k in range(1, count, 2):
         if k not in cots:
             cots[k] = hop(after(cots[k - 1], arrived_all), "tensor", 1)
@@ -770,7 +771,7 @@
         cot_all + [after(qkv, sums[0]), proj, ctx_cold, ask_cold],
         "cold_back",
         extra=16,
-        flops=10 * total * total * heads * LANES,
+        flops=1e10,
         loose=count,
         scratch=[
             pltpu.VMEM((count * cold, width), bf16),
@@ -786,7 +787,6 @@
         "split_slots",
     )
     back = [pieces[0]] + [hop(pieces[g], "dp", g) for g in range(1, groups)]
-    theirs_a = hop(after(send_a, pieces[0]), "tensor", 2)
     back = after(back, theirs_a)
     grad_hot, expert_out = run(
         make_mid_back(groups),

time: 145 us -> 138 us (0.952)
  waiting for transfers between devices: 55.4 us -> 51.8 us
  starting transfers between devices: 49.3 us -> 45.8 us
    ppermute x52, waiting for transfers between devices: 55.4 us -> 51.8 us  [hop(): return lax.ppermute(x, axis, [(i, i ^ mask) for i in range(size)])]
    ppermute x52, starting transfers between devices: 49.3 us -> 45.8 us  [hop(): return lax.ppermute(x, axis, [(i, i ^ mask) for i in range(size)])]
  transfers between devices with their start and end apart: 52 -> 52, of which waited for: 25 -> 22; matrix products, arithmetic and copies ran while one was open for 0% -> 0% of each run, Pallas kernels for 16% -> 19%
where the time goes in v5:
time: 138 us
  waiting for transfers between devices  51.8 us (38%)
  starting transfers between devices  45.8 us (33%)
  Pallas kernels  35.5 us (26%)
  local copies, waits for them, and re-layouts  3.32 us (2%)
    ppermute x52, waiting for transfers between devices, hop(): return lax.ppermute(x, axis, [(i, i ^ mask) for i in range(size)])  51.8 us
    ppermute x52, starting transfers between devices, hop(): return lax.ppermute(x, axis, [(i, i ^ mask) for i in range(size)])  45.8 us
    pallas_call x23, Pallas kernels, run(): pl.pallas_call(body, out_shape=list(outs), in_specs=specs, out_specs=[pl....  35.5 us
    unnamed x32, local copies, waits for them, and re-layouts  3.32 us
  transfers between devices with their start and end apart: 52, of which 22 were waited for; matrix products, arithmetic and copies ran while one was open for 0% of the time, Pallas kernels for 19%

profile of v5, /device:TPU:0, one launch (start us, length us, event | category | flops | bytes accessed | tf_op | source)
XLA Modules:
  0.0 137.6 jit_solution(1390808372694619333)
XLA Ops:
  0.6 3.4 %prologue.1 = (bf16[128,1280]{1,0:T(8,128)(2,1)}, bf16[16,1280]{1,0:T(8,128)(2,1)}, bf16[112,1280]{1,0:T(8,128)(2,1)}, bf16[16,1280]{1,0:T(8,128)(2,1)}, bf16[11...) custom-call(bf16[128,1280]{1,0:T(8,128)(2,1)} %tok_in.1, ...), custom_call_target="tpu_custom_call" | custom-call | bytes 1723908 | tf_op jit(solution)/shard_map/prologue/pallas_call | solution.py:55
  4.1 3.1 %collective-permute-start.4 = (bf16[128,1280]{1,0:T(8,128)(2,1)}, bf16[128,1280]{1,0:T(8,128)(2,1)S(1)}, u32[]{:S(2)}, u32[]{:S(2)}) collective-permute-start(bf16[128,1280]{1,0:T(8,128)(2,1)} %get-tuple-element.137.refs_0_), channel_id=1, source_target_pairs={{0,2},{1,3},{2,0},{3,1},{4,6},{5,7},{6,4},{7,5},{8,10},{9,11},{10,... | collective-permute-start | bytes 983048 | tf_op jit(solution)/shard_map/ppermute | solution.py:91
  7.1 2.6 %collective-permute-start = (bf16[128,1280]{1,0:T(8,128)(2,1)}, bf16[128,1280]{1,0:T(8,128)(2,1)S(1)}, u32[]{:S(2)}, u32[]{:S(2)}) collective-permute-start(bf16[128,1280]{1,0:T(8,128)(2,1)} %get-tuple-element.137.refs_0_), channel_id=1, source_target_pairs={{0,4},{1,5},{2,6},{3,7},{4,0},{5,1},{6,2},{7,3},{8,12},{9,13},{10,... | collective-permute-start | bytes 983048 | tf_op jit(solution)/shard_map/ppermute | solution.py:91
  9.7 12.2 %collective-permute-done.4.refs_2_ = bf16[128,1280]{1,0:T(8,128)(2,1)S(1)} collective-permute-done((bf16[128,1280]{1,0:T(8,128)(2,1)}, bf16[128,1280]{1,0:T(8,128)(2,1)S(1)}, u32[]{:S(2)}, u32[]{:S(2)}) %collective-permute-start.4) | collective-permute-done | bytes 327712 | tf_op jit(solution)/shard_map/ppermute | solution.py:91
  22.0 2.6 %collective-permute-done.refs_0_ = bf16[128,1280]{1,0:T(8,128)(2,1)S(1)} collective-permute-done((bf16[128,1280]{1,0:T(8,128)(2,1)}, bf16[128,1280]{1,0:T(8,128)(2,1)S(1)}, u32[]{:S(2)}, u32[]{:S(2)}) %collective-permute-start) | collective-permute-done | bytes 327712 | tf_op jit(solution)/shard_map/ppermute | solution.py:91
  29.0 2.3 %half.1 = (bf16[512,768]{1,0:T(8,128)(2,1)S(1)}, bf16[1280,512]{1,0:T(8,128)(2,1)S(1)}) custom-call(bf16[128,1280]{1,0:T(8,128)(2,1)S(1)} %copy-done.5, bf16[128,1280]{1,0:T(8,128)(2,1)S(1)} %collective-permute-done.3.refs_1_, bf16[128,1280]{1,0:T(8,128)(2,1)S(1)} %collective-permute-done.4.refs_2_, bf16[128,1280]{1,0:T(8,128)(2,1)S(1)} %collective-permute-done.5.refs_3_, ...), custom_call_target="tpu_custom_call" | custom-call | bytes 1024 | tf_op jit(solution)/shard_map/half/pallas_call | solution.py:55
  33.5 1.8 %collective-permute-start.12 = (bf16[112,1280]{1,0:T(8,128)(2,1)S(1)}, bf16[112,1280]{1,0:T(8,128)(2,1)S(1)}, u32[]{:S(2)}, u32[]{:S(2)}) collective-permute-start(bf16[112,1280]{1,0:T(8,128)(2,1)S(1)} %copy-done.15), channel_id=1, source_target_pairs={{0,4},{1,5},{2,6},{3,7},{4,0},{5,1},{6,2},{7,3},{8,12},{9,13},{10,... | collective-permute-start | bytes 860168 | tf_op jit(solution)/shard_map/ppermute | solution.py:91
  35.4 3.0 %front.1 = (bf16[1024,768]{1,0:T(8,128)(2,1)S(1)}, bf16[128,256]{1,0:T(8,128)(2,1)S(1)}, bf16[128,256]{1,0:T(8,128)(2,1)S(1)}, bf16[64,1280]{1,0:T(8,128)(2,1)S(1)}, bf16[64,1280]{1,0:T(8,128)(2,1)S(1)}) custom-call(bf16[128,1280]{1,0:T(8,128)(2,1)S(1)} %collective-permute-done.refs_0_, bf16[128,1280]{1,0:T(8,128)(2,1)S(1)} %collective-permute-done.1.refs_1_, ...), custom_call_target="tpu_custom_call" | custom-call | bytes 1024 | tf_op jit(solution)/shard_map/front/pallas_call | solution.py:55
  41.7 2.7 %collective-permute-start.11 = (bf16[16,1280]{1,0:T(8,128)(2,1)S(1)}, bf16[16,1280]{1,0:T(8,128)(2,1)S(1)}, u32[]{:S(2)}, u32[]{:S(2)}) collective-permute-start(bf16[16,1280]{1,0:T(8,128)(2,1)S(1)} %get-tuple-element.152), channel_id=1, source_target_pairs={{0,6},{1,7},{2,4},{3,5},{4,2},{5,3},{6,0},{7,1},{8,14},{9,15},{10,... | collective-permute-start | bytes 122888 | tf_op jit(solution)/shard_map/ppermute | solution.py:91
  44.4 2.8 %collective-permute-done.13.refs_2_ = bf16[112,1280]{1,0:T(8,128)(2,1)S(1)} collective-permute-done((bf16[112,1280]{1,0:T(8,128)(2,1)S(1)}, bf16[112,1280]{1,0:T(8,128)(2,1)S(1)}, u32[]{:S(2)}, u32[]{:S(2)}) %collective-permute-start.13) | collective-permute-done | bytes 286752 | tf_op jit(solution)/shard_map/ppermute | solution.py:91
  47.2 4.6 %collective-permute-done.12.refs_4_ = bf16[112,1280]{1,0:T(8,128)(2,1)S(1)} collective-permute-done((bf16[112,1280]{1,0:T(8,128)(2,1)S(1)}, bf16[112,1280]{1,0:T(8,128)(2,1)S(1)}, u32[]{:S(2)}, u32[]{:S(2)}) %collective-permute-start.12) | collective-permute-done | bytes 286752 | tf_op jit(solution)/shard_map/ppermute | solution.py:91
  53.0 1.6 %collective-permute-start.14 = (bf16[4,2560]{1,0:T(4,128)(2,1)S(1)}, bf16[4,2560]{1,0:T(4,128)(2,1)S(1)}, u32[]{:S(2)}, u32[]{:S(2)}) collective-permute-start(bf16[4,2560]{1,0:T(4,128)(2,1)S(1)} %get-tuple-element.166), channel_id=1, source_target_pairs={{0,8},{8,0},{16,24},{24,16},{1,9},{9,1},{17,25},{25,17},{2,10},{10... | collective-permute-start | bytes 61448 | tf_op jit(solution)/shard_map/ppermute | solution.py:91
  57.5 4.1 %cold.1 = (bf16[896,256]{1,0:T(8,128)(2,1)S(1)}, bf16[896,256]{1,0:T(8,128)(2,1)S(1)}, bf16[320,1280]{1,0:T(8,128)(2,1)S(1)}, bf16[320,1280]{1,0:T(8,128)(2,1)S(...) custom-call(bf16[1024,768]{1,0:T(8,128)(2,1)S(1)} %get-tuple-element.188.qkv.refs_8_.refs_9_, ...), custom_call_target="tpu_custom_call" | custom-call | flops 1073741824 | bytes 5439488 | tf_op jit(solution)/shard_map/cold/pallas_call | solution.py:55
  61.7 1.8 %collective-permute-done.17.refs_6_ = bf16[112,1280]{1,0:T(8,128)(2,1)S(1)} collective-permute-done((bf16[112,1280]{1,0:T(8,128)(2,1)S(1)}, bf16[112,1280]{1,0:T(8,128)(2,1)S(1)}, u32[]{:S(2)}, u32[]{:S(2)}) %collective-permute-start.17) | collective-permute-done | bytes 286752 | tf_op jit(solution)/shard_map/ppermute | solution.py:91
  66.0 3.4 %collective-permute-done.21.refs_4_ = bf16[16,2560]{1,0:T(8,128)(2,1)S(1)} collective-permute-done((bf16[16,2560]{1,0:T(8,128)(2,1)S(1)}, bf16[16,2560]{1,0:T(8,128)(2,1)S(1)}, u32[]{:S(2)}, u32[]{:S(2)}) %collective-permute-start.21) | collective-permute-done | bytes 81952 | tf_op jit(solution)/shard_map/ppermute | solution.py:91
  71.1 2.7 %collective-permute-done.23.refs_6_ = bf16[16,2560]{1,0:T(8,128)(2,1)S(1)} collective-permute-done((bf16[16,2560]{1,0:T(8,128)(2,1)S(1)}, bf16[16,2560]{1,0:T(8,128)(2,1)S(1)}, u32[]{:S(2)}, u32[]{:S(2)}) %collective-permute-start.23) | collective-permute-done | bytes 81952 | tf_op jit(solution)/shard_map/ppermute | solution.py:91
  76.1 3.3 %experts.1 = (bf16[128,1280]{1,0:T(8,128)(2,1)S(1)}, bf16[128,1280]{1,0:T(8,128)(2,1)S(1)}, bf16[2,128,640]{2,1,0:T(8,128)(2,1)S(1)}, bf16[2,128,640]{2,1,0:T(8,...) custom-call(bf16[16,2560]{1,0:T(8,128)(2,1)S(1)} %pad_maximum_fusion.refs_0_, ...), custom_call_target="tpu_custom_call" | custom-call | flops 1258291200 | bytes 9175040 | tf_op jit(solution)/shard_map/experts/pallas_call | solution.py:55
  84.1 1.9 %collective-permute-start.32 = (bf16[16,2560]{1,0:T(8,128)(2,1)S(1)}, bf16[16,2560]{1,0:T(8,128)(2,1)S(1)}, u32[]{:S(2)}, u32[]{:S(2)}) collective-permute-start(bf16[16,2560]{1,0:T(8,128)(2,1)S(1)} %get-tuple-element.186), channel_id=1, source_target_pairs={{0,6},{1,7},{2,4},{3,5},{4,2},{5,3},{6,0},{7,1},{8,14},{9,15},{10,... | collective-permute-start | bytes 245768 | tf_op jit(solution)/shard_map/ppermute | solution.py:91
  86.3 7.1 %cold_back.1 = (bf16[896,256]{1,0:T(8,128)(2,1)S(1)}, f32[256,1024]{1,0:T(8,128)S(1)}, f32[256,1024]{1,0:T(8,128)S(1)}, f32[256,1280]{1,0:T(8,128)S(1)}) custom-call(bf16[112,1280]{1,0:T(8,128)(2,1)S(1)} %copy-done.15, bf16[112,1280]{1,0:T(8,128)(2,1)S(1)} %collective-permute-done.6.refs_1_, bf16[112,1280]{1,0:T(8,128)(2,1)S(1)} %collective-permute-done.13.refs_2_, ...), custom_call_target="tpu_custom_call" | custom-call | flops 10000000000 | bytes 9306112 | tf_op jit(solution)/shard_map/cold_back/pallas_call | solution.py:55
  93.5 1.7 %collective-permute-start.34 = (bf16[4,2560]{1,0:T(4,128)(2,1)S(1)}, bf16[4,2560]{1,0:T(4,128)(2,1)S(1)}, u32[]{:S(2)}, u32[]{:S(2)}) collective-permute-start(bf16[4,2560]{1,0:T(4,128)(2,1)S(1)} %get-tuple-element.196), channel_id=1, source_target_pairs={{0,8},{8,0},{16,24},{24,16},{1,9},{9,1},{17,25},{25,17},{2,10},{10... | collective-permute-start | bytes 61448 | tf_op jit(solution)/shard_map/ppermute | solution.py:91
  97.3 1.7 %collective-permute-done.35.refs_2_ = bf16[4,2560]{1,0:T(4,128)(2,1)S(1)} collective-permute-done((bf16[4,2560]{1,0:T(4,128)(2,1)S(1)}, bf16[4,2560]{1,0:T(4,128)(2,1)S(1)}, u32[]{:S(2)}, u32[]{:S(2)}) %collective-permute-start.35) | collective-permute-done | bytes 20512 | tf_op jit(solution)/shard_map/ppermute | solution.py:91
  99.0 2.2 %collective-permute-done.36.refs_3_ = bf16[4,2560]{1,0:T(4,128)(2,1)S(1)} collective-permute-done((bf16[4,2560]{1,0:T(4,128)(2,1)S(1)}, bf16[4,2560]{1,0:T(4,128)(2,1)S(1)}, u32[]{:S(2)}, u32[]{:S(2)}) %collective-permute-start.36) | collective-permute-done | bytes 20512 | tf_op jit(solution)/shard_map/ppermute | solution.py:91
  101.5 2.2 %collective-permute-start.42 = (bf16[16,1280]{1,0:T(8,128)(2,1)S(1)}, bf16[16,1280]{1,0:T(8,128)(2,1)S(1)}, u32[]{:S(2)}, u32[]{:S(2)}) collective-permute-start(bf16[16,1280]{1,0:T(8,128)(2,1)S(1)} %get-tuple-element.228.refs_0_), channel_id=1, source_target_pairs={{0,4},{1,5},{2,6},{3,7},{4,0},{5,1},{6,2},{7,3},{8,12},{9,13},{10,... | collective-permute-start | bytes 122888 | tf_op jit(solution)/shard_map/ppermute | solution.py:91
  104.0 2.5 %collective-permute-done.42.refs_4_ = bf16[16,1280]{1,0:T(8,128)(2,1)S(1)} collective-permute-done((bf16[16,1280]{1,0:T(8,128)(2,1)S(1)}, bf16[16,1280]{1,0:T(8,128)(2,1)S(1)}, u32[]{:S(2)}, u32[]{:S(2)}) %collective-permute-start.42) | collective-permute-done | bytes 40992 | tf_op jit(solution)/shard_map/ppermute | solution.py:91
  106.5 1.8 %collective-permute-start.44 = (bf16[16,1280]{1,0:T(8,128)(2,1)S(1)}, bf16[16,1280]{1,0:T(8,128)(2,1)S(1)}, u32[]{:S(2)}, u32[]{:S(2)}) collective-permute-start(bf16[16,1280]{1,0:T(8,128)(2,1)S(1)} %collective-permute-done.42.refs_4_), channel_id=1, source_target_pairs={{0,2},{1,3},{2,0},{3,1},{4,6},{5,7},{6,4},{7,5},{8,10},{9,11},{10,... | collective-permute-start | bytes 122888 | tf_op jit(solution)/shard_map/ppermute | solution.py:91
  111.7 3.2 %hot_back.1 = (bf16[320,640]{1,0:T(8,128)(2,1)S(1)}, bf16[320,640]{1,0:T(8,128)(2,1)S(1)}, bf16[320,640]{1,0:T(8,128)(2,1)S(1)}, bf16[320,640]{1,0:T(8,128)(2,1)S(1)}) custom-call(bf16[16,1280]{1,0:T(8,128)(2,1)S(1)} %get-tuple-element.228.refs_0_, bf16[16,1280]{1,0:T(8,128)(2,1)S(1)} %collective-permute-done.39.refs_1_, ...), custom_call_target="tpu_custom_call" | custom-call | bytes 1024 | tf_op jit(solution)/shard_map/hot_back/pallas_call | solution.py:55
  116.1 1.7 %collective-permute-start.46 = (bf16[64,1280]{1,0:T(8,128)(2,1)S(1)}, bf16[64,1280]{1,0:T(8,128)(2,1)S(1)}, u32[]{:S(2)}, u32[]{:S(2)}) collective-permute-start(bf16[64,1280]{1,0:T(8,128)(2,1)S(1)} %get-tuple-element.218), channel_id=1, source_target_pairs={{0,2},{1,3},{2,0},{3,1},{4,6},{5,7},{6,4},{7,5},{8,10},{9,11},{10,... | collective-permute-start | bytes 491528 | tf_op jit(solution)/shard_map/ppermute | solution.py:91
  118.5 4.3 %weight_grads.1 = (bf16[2,1280,640]{2,1,0:T(8,128)(2,1)}, bf16[2,640,1280]{2,1,0:T(8,128)(2,1)}) custom-call(bf16[128,1280]{1,0:T(8,128)(2,1)S(1)} %get-tuple-element.245.arrived, bf16[128,1280]{1,0:T(8,128)(2,1)S(1)} %get-tuple-element.246.grads, bf16[2,128,640]{2,1,0:T(8,128)(2,1)S(1)} %get-tuple-element.247.hidden, ...), custom_call_target="tpu_custom_call" | custom-call | bytes 1024 | tf_op jit(solution)/shard_map/weight_grads/pallas_call | solution.py:55
  122.8 1.6 %collective-permute-done.46.theirs = bf16[64,1280]{1,0:T(8,128)(2,1)S(1)} collective-permute-done((bf16[64,1280]{1,0:T(8,128)(2,1)S(1)}, bf16[64,1280]{1,0:T(8,128)(2,1)S(1)}, u32[]{:S(2)}, u32[]{:S(2)}) %collective-permute-start.46) | collective-permute-done | bytes 163872 | tf_op jit(solution)/shard_map/ppermute | solution.py:91
  124.5 2.1 %collective-permute-done.48.theirs = bf16[320,640]{1,0:T(8,128)(2,1)S(1)} collective-permute-done((bf16[320,640]{1,0:T(8,128)(2,1)S(1)}, bf16[320,640]{1,0:T(8,128)(2,1)S(1)}, u32[]{:S(2)}, u32[]{:S(2)}) %collective-permute-start.48) | collective-permute-done | bytes 409632 | tf_op jit(solution)/shard_map/ppermute | solution.py:91
  129.4 2.0 %collective-permute-start.47 = (bf16[32,1280]{1,0:T(8,128)(2,1)S(1)}, bf16[32,1280]{1,0:T(8,128)(2,1)S(1)}, u32[]{:S(2)}, u32[]{:S(2)}) collective-permute-start(bf16[32,1280]{1,0:T(8,128)(2,1)S(1)} %get-tuple-element.220), channel_id=1, source_target_pairs={{0,4},{1,5},{2,6},{3,7},{4,0},{5,1},{6,2},{7,3},{8,12},{9,13},{10,... | collective-permute-start | bytes 245768 | tf_op jit(solution)/shard_map/ppermute | solution.py:91
  131.4 3.3 %collective-permute-done.47.refs_3_ = bf16[32,1280]{1,0:T(8,128)(2,1)S(1)} collective-permute-done((bf16[32,1280]{1,0:T(8,128)(2,1)S(1)}, bf16[32,1280]{1,0:T(8,128)(2,1)S(1)}, u32[]{:S(2)}, u32[]{:S(2)}) %collective-permute-start.47) | collective-permute-done | bytes 81952 | tf_op jit(solution)/shard_map/ppermute | solution.py:91
  (128 shorter events, 39.0 us)
Async XLA Ops:
  4.1 17.9 %collective-permute-start.4 = (bf16[128,1280]{1,0:T(8,128)(2,1)}, bf16[128,1280]{1,0:T(8,128)(2,1)S(1)}, u32[]{:S(2)}, u32[]{:S(2)}) collective-permute-start(bf16[128,1280]{1,0:T(8,128)(2,1)} %get-tuple-element.137.refs_0_), channel_id=1, source_target_pairs={{0,2},{1,3},{2,0},{3,1},{4,6},{5,7},{6,4},{7,5},{8,10},{9,11},{10,... | collective-permute-start | bytes 983048 | tf_op jit(solution)/shard_map/ppermute | solution.py:91
  7.1 17.4 %collective-permute-start = (bf16[128,1280]{1,0:T(8,128)(2,1)}, bf16[128,1280]{1,0:T(8,128)(2,1)S(1)}, u32[]{:S(2)}, u32[]{:S(2)}) collective-permute-start(bf16[128,1280]{1,0:T(8,128)(2,1)} %get-tuple-element.137.refs_0_), channel_id=1, source_target_pairs={{0,4},{1,5},{2,6},{3,7},{4,0},{5,1},{6,2},{7,3},{8,12},{9,13},{10,... | collective-permute-start | bytes 983048 | tf_op jit(solution)/shard_map/ppermute | solution.py:91
  9.7 18.3 %collective-permute-start.3 = (bf16[128,1280]{1,0:T(8,128)(2,1)}, bf16[128,1280]{1,0:T(8,128)(2,1)S(1)}, u32[]{:S(2)}, u32[]{:S(2)}) collective-permute-start(bf16[128,1280]{1,0:T(8,128)(2,1)} %get-tuple-element.137.refs_0_), channel_id=1, source_target_pairs={{0,1},{1,0},{2,3},{3,2},{4,5},{5,4},{6,7},{7,6},{8,9},{9,8},{10,11... | collective-permute-start | bytes 983048 | tf_op jit(solution)/shard_map/ppermute | solution.py:91
  22.0 6.0 %collective-permute-start.5 = (bf16[128,1280]{1,0:T(8,128)(2,1)S(1)}, bf16[128,1280]{1,0:T(8,128)(2,1)S(1)}, u32[]{:S(2)}, u32[]{:S(2)}) collective-permute-start(bf16[128,1280]{1,0:T(8,128)(2,1)S(1)} %collective-permute-done.4.refs_2_), channel_id=1, source_target_pairs={{0,1},{1,0},{2,3},{3,2},{4,5},{5,4},{6,7},{7,6},{8,9},{9,8},{10,11... | collective-permute-start | bytes 983048 | tf_op jit(solution)/shard_map/ppermute | solution.py:91
  24.5 7.6 %collective-permute-start.2 = (bf16[128,1280]{1,0:T(8,128)(2,1)S(1)}, bf16[128,1280]{1,0:T(8,128)(2,1)S(1)}, u32[]{:S(2)}, u32[]{:S(2)}) collective-permute-start(bf16[128,1280]{1,0:T(8,128)(2,1)S(1)} %collective-permute-done.refs_0_), channel_id=1, source_target_pairs={{0,2},{1,3},{2,0},{3,1},{4,6},{5,7},{6,4},{7,5},{8,10},{9,11},{10,... | collective-permute-start | bytes 983048 | tf_op jit(solution)/shard_map/ppermute | solution.py:91
  27.4 7.9 %collective-permute-start.1 = (bf16[128,1280]{1,0:T(8,128)(2,1)S(1)}, bf16[128,1280]{1,0:T(8,128)(2,1)S(1)}, u32[]{:S(2)}, u32[]{:S(2)}) collective-permute-start(bf16[128,1280]{1,0:T(8,128)(2,1)S(1)} %collective-permute-done.refs_0_), channel_id=1, source_target_pairs={{0,1},{1,0},{2,3},{3,2},{4,5},{5,4},{6,7},{7,6},{8,9},{9,8},{10,11... | collective-permute-start | bytes 983048 | tf_op jit(solution)/shard_map/ppermute | solution.py:91
  32.1 15.1 %collective-permute-start.13 = (bf16[112,1280]{1,0:T(8,128)(2,1)S(1)}, bf16[112,1280]{1,0:T(8,128)(2,1)S(1)}, u32[]{:S(2)}, u32[]{:S(2)}) collective-permute-start(bf16[112,1280]{1,0:T(8,128)(2,1)S(1)} %copy-done.15), channel_id=1, source_target_pairs={{0,2},{1,3},{2,0},{3,1},{4,6},{5,7},{6,4},{7,5},{8,10},{9,11},{10,... | collective-permute-start | bytes 860168 | tf_op jit(solution)/shard_map/ppermute | solution.py:91
  33.5 18.4 %collective-permute-start.12 = (bf16[112,1280]{1,0:T(8,128)(2,1)S(1)}, bf16[112,1280]{1,0:T(8,128)(2,1)S(1)}, u32[]{:S(2)}, u32[]{:S(2)}) collective-permute-start(bf16[112,1280]{1,0:T(8,128)(2,1)S(1)} %copy-done.15), channel_id=1, source_target_pairs={{0,4},{1,5},{2,6},{3,7},{4,0},{5,1},{6,2},{7,3},{8,12},{9,13},{10,... | collective-permute-start | bytes 860168 | tf_op jit(solution)/shard_map/ppermute | solution.py:91
  39.9 11.9 %collective-permute-start.9 = (bf16[16,1280]{1,0:T(8,128)(2,1)S(1)}, bf16[16,1280]{1,0:T(8,128)(2,1)S(1)}, u32[]{:S(2)}, u32[]{:S(2)}) collective-permute-start(bf16[16,1280]{1,0:T(8,128)(2,1)S(1)} %get-tuple-element.150), channel_id=1, source_target_pairs={{0,2},{1,3},{2,0},{3,1},{4,6},{5,7},{6,4},{7,5},{8,10},{9,11},{10,... | collective-permute-start | bytes 122888 | tf_op jit(solution)/shard_map/ppermute | solution.py:91
  40.7 11.9 %collective-permute-start.10 = (bf16[16,1280]{1,0:T(8,128)(2,1)S(1)}, bf16[16,1280]{1,0:T(8,128)(2,1)S(1)}, u32[]{:S(2)}, u32[]{:S(2)}) collective-permute-start(bf16[16,1280]{1,0:T(8,128)(2,1)S(1)} %get-tuple-element.151), channel_id=1, source_target_pairs={{0,4},{1,5},{2,6},{3,7},{4,0},{5,1},{6,2},{7,3},{8,12},{9,13},{10,... | collective-permute-start | bytes 122888 | tf_op jit(solution)/shard_map/ppermute | solution.py:91
  41.7 10.9 %collective-permute-start.11 = (bf16[16,1280]{1,0:T(8,128)(2,1)S(1)}, bf16[16,1280]{1,0:T(8,128)(2,1)S(1)}, u32[]{:S(2)}, u32[]{:S(2)}) collective-permute-start(bf16[16,1280]{1,0:T(8,128)(2,1)S(1)} %get-tuple-element.152), channel_id=1, source_target_pairs={{0,6},{1,7},{2,4},{3,5},{4,2},{5,3},{6,0},{7,1},{8,14},{9,15},{10,... | collective-permute-start | bytes 122888 | tf_op jit(solution)/shard_map/ppermute | solution.py:91
  53.0 8.7 %collective-permute-start.14 = (bf16[4,2560]{1,0:T(4,128)(2,1)S(1)}, bf16[4,2560]{1,0:T(4,128)(2,1)S(1)}, u32[]{:S(2)}, u32[]{:S(2)}) collective-permute-start(bf16[4,2560]{1,0:T(4,128)(2,1)S(1)} %get-tuple-element.166), channel_id=1, source_target_pairs={{0,8},{8,0},{16,24},{24,16},{1,9},{9,1},{17,25},{25,17},{2,10},{10... | collective-permute-start | bytes 61448 | tf_op jit(solution)/shard_map/ppermute | solution.py:91
  54.5 7.1 %collective-permute-start.15 = (bf16[4,2560]{1,0:T(4,128)(2,1)S(1)}, bf16[4,2560]{1,0:T(4,128)(2,1)S(1)}, u32[]{:S(2)}, u32[]{:S(2)}) collective-permute-start(bf16[4,2560]{1,0:T(4,128)(2,1)S(1)} %get-tuple-element.167), channel_id=1, source_target_pairs={{0,16},{8,24},{16,0},{24,8},{1,17},{9,25},{17,1},{25,9},{2,18},{10... | collective-permute-start | bytes 61448 | tf_op jit(solution)/shard_map/ppermute | solution.py:91
  56.0 5.6 %collective-permute-start.16 = (bf16[4,2560]{1,0:T(4,128)(2,1)S(1)}, bf16[4,2560]{1,0:T(4,128)(2,1)S(1)}, u32[]{:S(2)}, u32[]{:S(2)}) collective-permute-start(bf16[4,2560]{1,0:T(4,128)(2,1)S(1)} %get-tuple-element.168), channel_id=1, source_target_pairs={{0,24},{8,16},{16,8},{24,0},{1,25},{9,17},{17,9},{25,1},{2,26},{10... | collective-permute-start | bytes 61448 | tf_op jit(solution)/shard_map/ppermute | solution.py:91
  56.5 7.0 %collective-permute-start.17 = (bf16[112,1280]{1,0:T(8,128)(2,1)S(1)}, bf16[112,1280]{1,0:T(8,128)(2,1)S(1)}, u32[]{:S(2)}, u32[]{:S(2)}) collective-permute-start(bf16[112,1280]{1,0:T(8,128)(2,1)S(1)} %collective-permute-done.12.refs_4_), channel_id=1, source_target_pairs={{0,2},{1,3},{2,0},{3,1},{4,6},{5,7},{6,4},{7,5},{8,10},{9,11},{10,... | collective-permute-start | bytes 860168 | tf_op jit(solution)/shard_map/ppermute | solution.py:91
  63.5 5.9 %collective-permute-start.21 = (bf16[16,2560]{1,0:T(8,128)(2,1)S(1)}, bf16[16,2560]{1,0:T(8,128)(2,1)S(1)}, u32[]{:S(2)}, u32[]{:S(2)}) collective-permute-start(bf16[16,2560]{1,0:T(8,128)(2,1)S(1)} %pad_maximum_fusion.refs_0_), channel_id=1, source_target_pairs={{0,4},{1,5},{2,6},{3,7},{4,0},{5,1},{6,2},{7,3},{8,12},{9,13},{10,... | collective-permute-start | bytes 245768 | tf_op jit(solution)/shard_map/ppermute | solution.py:91
  65.1 6.1 %collective-permute-start.19 = (bf16[16,2560]{1,0:T(8,128)(2,1)S(1)}, bf16[16,2560]{1,0:T(8,128)(2,1)S(1)}, u32[]{:S(2)}, u32[]{:S(2)}) collective-permute-start(bf16[16,2560]{1,0:T(8,128)(2,1)S(1)} %pad_maximum_fusion.refs_0_), channel_id=1, source_target_pairs={{0,2},{1,3},{2,0},{3,1},{4,6},{5,7},{6,4},{7,5},{8,10},{9,11},{10,... | collective-permute-start | bytes 245768 | tf_op jit(solution)/shard_map/ppermute | solution.py:91
  80.0 6.3 %collective-permute-start.33 = (bf16[112,1280]{1,0:T(8,128)(2,1)S(1)}, bf16[112,1280]{1,0:T(8,128)(2,1)S(1)}, u32[]{:S(2)}, u32[]{:S(2)}) collective-permute-start(bf16[112,1280]{1,0:T(8,128)(2,1)S(1)} %collective-permute-done.17.refs_6_), channel_id=1, source_target_pairs={{0,1},{1,0},{2,3},{3,2},{4,5},{5,4},{6,7},{7,6},{8,9},{9,8},{10,11... | collective-permute-start | bytes 860168 | tf_op jit(solution)/shard_map/ppermute | solution.py:91
  81.5 11.8 %collective-permute-start.30 = (bf16[16,2560]{1,0:T(8,128)(2,1)S(1)}, bf16[16,2560]{1,0:T(8,128)(2,1)S(1)}, u32[]{:S(2)}, u32[]{:S(2)}) collective-permute-start(bf16[16,2560]{1,0:T(8,128)(2,1)S(1)} %get-tuple-element.184), channel_id=1, source_target_pairs={{0,2},{1,3},{2,0},{3,1},{4,6},{5,7},{6,4},{7,5},{8,10},{9,11},{10,... | collective-permute-start | bytes 245768 | tf_op jit(solution)/shard_map/ppermute | solution.py:91
  82.8 10.6 %collective-permute-start.31 = (bf16[16,2560]{1,0:T(8,128)(2,1)S(1)}, bf16[16,2560]{1,0:T(8,128)(2,1)S(1)}, u32[]{:S(2)}, u32[]{:S(2)}) collective-permute-start(bf16[16,2560]{1,0:T(8,128)(2,1)S(1)} %get-tuple-element.185), channel_id=1, source_target_pairs={{0,4},{1,5},{2,6},{3,7},{4,0},{5,1},{6,2},{7,3},{8,12},{9,13},{10,... | collective-permute-start | bytes 245768 | tf_op jit(solution)/shard_map/ppermute | solution.py:91
  84.1 9.3 %collective-permute-start.32 = (bf16[16,2560]{1,0:T(8,128)(2,1)S(1)}, bf16[16,2560]{1,0:T(8,128)(2,1)S(1)}, u32[]{:S(2)}, u32[]{:S(2)}) collective-permute-start(bf16[16,2560]{1,0:T(8,128)(2,1)S(1)} %get-tuple-element.186), channel_id=1, source_target_pairs={{0,6},{1,7},{2,4},{3,5},{4,2},{5,3},{6,0},{7,1},{8,14},{9,15},{10,... | collective-permute-start | bytes 245768 | tf_op jit(solution)/shard_map/ppermute | solution.py:91
  86.0 15.2 %collective-permute-start.37 = (bf16[160,1280]{1,0:T(8,128)(2,1)S(1)}, bf16[160,1280]{1,0:T(8,128)(2,1)S(1)}, u32[]{:S(2)}, u32[]{:S(2)}) collective-permute-start(bf16[160,1280]{1,0:T(8,128)(2,1)S(1)} %get-tuple-element.200), channel_id=1, source_target_pairs={{0,2},{1,3},{2,0},{3,1},{4,6},{5,7},{6,4},{7,5},{8,10},{9,11},{10,... | collective-permute-start | bytes 1228808 | tf_op jit(solution)/shard_map/ppermute | solution.py:91
  96.5 4.7 %collective-permute-start.36 = (bf16[4,2560]{1,0:T(4,128)(2,1)S(1)}, bf16[4,2560]{1,0:T(4,128)(2,1)S(1)}, u32[]{:S(2)}, u32[]{:S(2)}) collective-permute-start(bf16[4,2560]{1,0:T(4,128)(2,1)S(1)} %get-tuple-element.198), channel_id=1, source_target_pairs={{0,24},{8,16},{16,8},{24,0},{1,25},{9,17},{17,9},{25,1},{2,26},{10... | collective-permute-start | bytes 61448 | tf_op jit(solution)/shard_map/ppermute | solution.py:91
  101.5 5.0 %collective-permute-start.42 = (bf16[16,1280]{1,0:T(8,128)(2,1)S(1)}, bf16[16,1280]{1,0:T(8,128)(2,1)S(1)}, u32[]{:S(2)}, u32[]{:S(2)}) collective-permute-start(bf16[16,1280]{1,0:T(8,128)(2,1)S(1)} %get-tuple-element.228.refs_0_), channel_id=1, source_target_pairs={{0,4},{1,5},{2,6},{3,7},{4,0},{5,1},{6,2},{7,3},{8,12},{9,13},{10,... | collective-permute-start | bytes 122888 | tf_op jit(solution)/shard_map/ppermute | solution.py:91
  103.7 5.5 %collective-permute-start.40 = (bf16[16,1280]{1,0:T(8,128)(2,1)S(1)}, bf16[16,1280]{1,0:T(8,128)(2,1)S(1)}, u32[]{:S(2)}, u32[]{:S(2)}) collective-permute-start(bf16[16,1280]{1,0:T(8,128)(2,1)S(1)} %get-tuple-element.228.refs_0_), channel_id=1, source_target_pairs={{0,2},{1,3},{2,0},{3,1},{4,6},{5,7},{6,4},{7,5},{8,10},{9,11},{10,... | collective-permute-start | bytes 122888 | tf_op jit(solution)/shard_map/ppermute | solution.py:91
  115.0 11.6 %collective-permute-start.48 = (bf16[320,640]{1,0:T(8,128)(2,1)S(1)}, bf16[320,640]{1,0:T(8,128)(2,1)S(1)}, u32[]{:S(2)}, u32[]{:S(2)}) collective-permute-start(bf16[320,640]{1,0:T(8,128)(2,1)S(1)} %get-tuple-element.242), channel_id=1, source_target_pairs={{0,8},{8,0},{16,24},{24,16},{1,9},{9,1},{17,25},{25,17},{2,10},{10... | collective-permute-start | bytes 1228808 | tf_op jit(solution)/shard_map/ppermute | solution.py:91
  115.7 11.3 %collective-permute-start.49 = (bf16[320,640]{1,0:T(8,128)(2,1)S(1)}, bf16[320,640]{1,0:T(8,128)(2,1)S(1)}, u32[]{:S(2)}, u32[]{:S(2)}) collective-permute-start(bf16[320,640]{1,0:T(8,128)(2,1)S(1)} %get-tuple-element.243), channel_id=1, source_target_pairs={{0,16},{8,24},{16,0},{24,8},{1,17},{9,25},{17,1},{25,9},{2,18},{10... | collective-permute-start | bytes 1228808 | tf_op jit(solution)/shard_map/ppermute | solution.py:91
  116.1 8.3 %collective-permute-start.46 = (bf16[64,1280]{1,0:T(8,128)(2,1)S(1)}, bf16[64,1280]{1,0:T(8,128)(2,1)S(1)}, u32[]{:S(2)}, u32[]{:S(2)}) collective-permute-start(bf16[64,1280]{1,0:T(8,128)(2,1)S(1)} %get-tuple-element.218), channel_id=1, source_target_pairs={{0,2},{1,3},{2,0},{3,1},{4,6},{5,7},{6,4},{7,5},{8,10},{9,11},{10,... | collective-permute-start | bytes 491528 | tf_op jit(solution)/shard_map/ppermute | solution.py:91
  117.8 13.6 %collective-permute-start.38 = (bf16[80,1280]{1,0:T(8,128)(2,1)S(1)}, bf16[80,1280]{1,0:T(8,128)(2,1)S(1)}, u32[]{:S(2)}, u32[]{:S(2)}) collective-permute-start(bf16[80,1280]{1,0:T(8,128)(2,1)S(1)} %get-tuple-element.211), channel_id=1, source_target_pairs={{0,4},{1,5},{2,6},{3,7},{4,0},{5,1},{6,2},{7,3},{8,12},{9,13},{10,... | collective-permute-start | bytes 614408 | tf_op jit(solution)/shard_map/ppermute | solution.py:91
  127.1 8.9 %collective-permute-start.51 = (bf16[160,640]{1,0:T(8,128)(2,1)S(1)}, bf16[160,640]{1,0:T(8,128)(2,1)S(1)}, u32[]{:S(2)}, u32[]{:S(2)}) collective-permute-start(bf16[160,640]{1,0:T(8,128)(2,1)S(1)} %get-tuple-element.256), channel_id=1, source_target_pairs={{0,8},{8,0},{16,24},{24,16},{1,9},{9,1},{17,25},{25,17},{2,10},{10... | collective-permute-start | bytes 614408 | tf_op jit(solution)/shard_map/ppermute | solution.py:91
  128.6 7.4 %collective-permute-start.50 = (bf16[160,640]{1,0:T(8,128)(2,1)S(1)}, bf16[160,640]{1,0:T(8,128)(2,1)S(1)}, u32[]{:S(2)}, u32[]{:S(2)}) collective-permute-start(bf16[160,640]{1,0:T(8,128)(2,1)S(1)} %get-tuple-element.252), channel_id=1, source_target_pairs={{0,16},{8,24},{16,0},{24,8},{1,17},{9,25},{17,1},{25,9},{2,18},{10... | collective-permute-start | bytes 614408 | tf_op jit(solution)/shard_map/ppermute | solution.py:91
  129.4 5.3 %collective-permute-start.47 = (bf16[32,1280]{1,0:T(8,128)(2,1)S(1)}, bf16[32,1280]{1,0:T(8,128)(2,1)S(1)}, u32[]{:S(2)}, u32[]{:S(2)}) collective-permute-start(bf16[32,1280]{1,0:T(8,128)(2,1)S(1)} %get-tuple-element.220), channel_id=1, source_target_pairs={{0,4},{1,5},{2,6},{3,7},{4,0},{5,1},{6,2},{7,3},{8,12},{9,13},{10,... | collective-permute-start | bytes 245768 | tf_op jit(solution)/shard_map/ppermute | solution.py:91
  (36 other events, 314.0 us)

commit v6 on v5

--- a/solution.py
+++ b/solution.py
@@ -91,12 +91,14 @@
     return lax.ppermute(x, axis, [(i, i ^ mask) for i in range(size)])
 
 
-def gather_rel(x, hold=None, firm=()):
+def gather_rel(x, hold=None, firm=(), direct=False):
     size = lax.axis_size("tensor")
     have = {0: x}
     odd = {}
     mask = size // 2
-    while mask > 1:
+    if direct:
+        have.update({k: hop(x, "tensor", k) for k in range(2, size, 2)})
+    while mask > 1 and not direct:
         have.update({k ^ mask: hop(y, "tensor", mask) for k, y in list(have.items())})
         mask //= 2
     if hold is not None:
@@ -288,10 +290,9 @@
 
 
 def make_cold(count, places, heads, size):
-    def body(qkv, proj, ctx, ask, even_a, odd_a, even_b, odd_b):
+    def body(qkv, proj, ctx, ask, even, odd):
         rows = qkv.shape[0] // count
         cold = rows - places
-        upper = upper_rows(cold)
         every = slice(None)
         group = min(4, count)
         order = fold_order(range(0, count, 2))
@@ -307,12 +308,9 @@
                 )
             part = dot(ctx[at, :], proj[...]).astype(bf16)
             for k in range(first, first + group):
-                one = part[(k - first) * cold : (k - first + 1) * cold]
+                to = odd if k % 2 else even
                 i = order.index(k // 2 * 2)
-                to = odd_a if k % 2 else even_a
-                to[i * upper : (i + 1) * upper] = one[:upper]
-                to = odd_b if k % 2 else even_b
-                to[i * (cold - upper) : (i + 1) * (cold - upper)] = one[upper:]
+                to[i * cold : (i + 1) * cold] = part[(k - first) * cold : (k - first + 1) * cold]
 
     return body
 
@@ -421,10 +419,6 @@
     return body
 
 
-def upper_rows(rows):
-    return (rows * 5 // 7 + 15) // 16 * 16
-
-
 def near_rows(rows):
     return (rows // 2 + 15) // 16 * 16
 
@@ -550,12 +544,11 @@
     return body
 
 
-def make_epilogue():
-    def body(*refs):
-        parts = refs[:4]
-        tok, mid_hot, perm, pick0, pick1, experts, gate_t, cot, out, gate_o = refs[4:]
-        sums = jnp.concatenate([total_of(parts[:2]), total_of(parts[2:])], axis=0)
-        cold = (tok[...].astype(f32) + sums).astype(bf16)
+def make_epilogue(count):
+    def body(*refs):
+        parts = refs[:count]
+        tok, mid_hot, perm, pick0, pick1, experts, gate_t, cot, out, gate_o = refs[count:]
+        cold = (tok[...].astype(f32) + total_of(parts)).astype(bf16)
         ordered = jnp.concatenate([mid_hot[...], cold], axis=0)
         mid = dot(perm[...], ordered)
         gate = jnp.concatenate([gate_t[...], jnp.zeros((6, gate_t.shape[1]), f32)], axis=0).T
@@ -707,15 +700,13 @@
     mid_hot, normal_hot, factor_hot = outs[:3]
     pieces = outs[3:]
 
-    upper = upper_rows(cold)
-    parts_cold = [(half * n, width) for n in (upper, upper, cold - upper, cold - upper)]
-    ctx_cold, ask_cold, even_a, odd_a, even_b, odd_b = run(
+    ctx_cold, ask_cold, even_cold, odd_cold = run(
         make_cold(count, places, heads, size),
         [
             shape((count * cold, heads * LANES)),
             shape((count * cold, heads * LANES)),
         ]
-        + [shape(p) for p in parts_cold],
+        + [shape((half * cold, width))] * 2,
         [after(qkv, mid_hot), proj],
         "cold",
         extra=14,
@@ -732,11 +723,10 @@
         [pieces[0]] + [hop(pieces[g], "dp", g) for g in range(1, groups)], axis=0
     )
     landed = after(landed, ctx_cold, list(cots.values()))
-    arrived_all = gather_rel(landed)
+    arrived_all = gather_rel(landed, direct=True)
     for k in early:
         cots[k + 1] = hop(after(cots[k], arrived_all), "tensor", 1)
-    theirs_a = hop(after(odd_a, arrived_all), "tensor", 1)
-    theirs_b = hop(after(odd_b, arrived_all), "tensor", 1)
+    cold_theirs = hop(after(odd_cold, arrived_all), "tensor", 1)
     arrived, slot_grads, hidden, grad_pre, even, odd = run(
         make_expert(count, experts),
         [
@@ -752,10 +742,9 @@
         extra=8,
         flops=6 * slots * width * hidden_dev * experts,
     )
-    keep_a, send_a = halve(even_a, theirs_a, "fold_cold_1a")
-    keep_b, send_b = halve(even_b, theirs_b, "fold_cold_1b")
-    sums = fold_scatter(even, after(odd, list(cots.values()), keep_a, keep_b), places, "fold_slots")
-    theirs_a = hop(after(send_a, sums[0]), "tensor", 2)
+    cold_mine, cold_send = halve(even_cold, cold_theirs, "fold_cold_1")
+    sums = fold_scatter(even, after(odd, list(cots.values()), cold_mine), places, "fold_slots")
+    cold_theirs = hop(after(cold_send, sums[0]), "tensor", 2)
     for k in range(1, count, 2):
         if k not in cots:
             cots[k] = hop(after(cots[k - 1], arrived_all), "tensor", 1)
@@ -787,7 +776,7 @@
         "split_slots",
     )
     back = [pieces[0]] + [hop(pieces[g], "dp", g) for g in range(1, groups)]
-    back = after(back, theirs_a)
+    back = after(back, cold_theirs)
     grad_hot, expert_out = run(
         make_mid_back(groups),
         [shape((places, width)), shape((places, width))],
@@ -808,18 +797,15 @@
         )
         return box[0]
 
-    grad_hot_all = gather_rel(grad_hot, turn)
+    grad_hot_all = gather_rel(grad_hot, turn, direct=True)
     fn_b = box[0]
-    keep_a = after(keep_a, grad_hot)
-    theirs_b = hop(after(send_b, grad_hot_all), "tensor", 2)
+    cold_mine = after(cold_mine, grad_hot)
     mask = 4
     while mask < count:
-        keep_a, send_a = halve(keep_a, theirs_a, f"fold_cold_{mask // 2}a")
-        theirs_a = hop(send_a, "tensor", mask)
-        keep_b, send_b = halve(keep_b, theirs_b, f"fold_cold_{mask // 2}b")
-        theirs_b = hop(send_b, "tensor", mask)
+        cold_mine, cold_send = halve(cold_mine, cold_theirs, f"fold_cold_{mask // 2}")
+        cold_theirs = hop(cold_send, "tensor", mask)
         mask *= 2
-    cold_sums = [keep_a, theirs_a, keep_b, theirs_b]
+    cold_sums = [cold_mine, cold_theirs]
 
     me = lax.axis_index("dp").astype(jnp.int32).reshape(1)
     each_w = width // groups
@@ -828,7 +814,7 @@
     keep_a, send_a, keep_b, send_b = run(
         make_hot_back(count, heads, size, groups, scale),
         [shape(halves[0]), shape(halves[0]), shape(halves[1]), shape(halves[1])],
-        after(grad_hot_all, keep_a)
+        after(grad_hot_all, cold_mine)
         + [me, qkv, proj, ctx_hot, ask_hot, gq, gk, gv, gp, fn_a, fn_b],
         "hot_back",
         extra=10,
@@ -853,7 +839,7 @@
         got_a = hop(send_a, "dp", mask)
         got_b = hop(send_b, "dp", groups // 2 // mask)
         if mask == 1:
-            got_a, got_b = after((got_a, got_b), grad_up, cold_sums[2])
+            got_a, got_b = after((got_a, got_b), grad_up)
         if mask == groups // 2:
             break
         keep_a, send_a = halve(keep_a, got_a, f"fold_a_{mask}")
@@ -861,7 +847,7 @@
         mask *= 2
     parts = [keep_a, got_a, keep_b, got_b]
     layer_out, gate_grad = run(
-        make_epilogue(),
+        make_epilogue(2),
         [shape((rows, width)), shape((2, rows), f32)],
         cold_sums
         + [tok_cold, mid_hot, perm, pick0, pick1, expert_out, gate_weights.T, cotangent],

time: 138 us -> 134 us (0.971)
  waiting for transfers between devices: 51.8 us -> 49.3 us
    ppermute x52 -> x49, waiting for transfers between devices: 51.8 us -> 49.3 us  [hop(): return lax.ppermute(x, axis, [(i, i ^ mask) for i in range(size)])]
    ppermute x52 -> x49, starting transfers between devices: 45.8 us -> 45.4 us  [hop(): return lax.ppermute(x, axis, [(i, i ^ mask) for i in range(size)])]
    pallas_call x23 -> x21, Pallas kernels: 35.5 us -> 35.6 us  [run(): pl.pallas_call(body, out_shape=list(outs), in_specs=specs, out_specs=[pl....]
  transfers between devices with their start and end apart: 52 -> 49, of which waited for: 22 -> 24; matrix products, arithmetic and copies ran while one was open for 0% -> 0% of each run, Pallas kernels for 19% -> 20%
where the time goes in v6:
time: 134 us
  waiting for transfers between devices  49.3 us (37%)
  starting transfers between devices  45.4 us (34%)
  Pallas kernels  35.6 us (27%)
  local copies, waits for them, and re-layouts  2.56 us (2%)
    ppermute x49, waiting for transfers between devices, hop(): return lax.ppermute(x, axis, [(i, i ^ mask) for i in range(size)])  49.3 us
    ppermute x49, starting transfers between devices, hop(): return lax.ppermute(x, axis, [(i, i ^ mask) for i in range(size)])  45.4 us
    pallas_call x21, Pallas kernels, run(): pl.pallas_call(body, out_shape=list(outs), in_specs=specs, out_specs=[pl....  35.6 us
  transfers between devices with their start and end apart: 49, of which 24 were waited for; matrix products, arithmetic and copies ran while one was open for 0% of the time, Pallas kernels for 20%

profile of v6, /device:TPU:0, one launch (start us, length us, event | category | flops | bytes accessed | tf_op | source)
XLA Modules:
  0.0 133.9 jit_solution(431599359001240872)
XLA Ops:
  0.6 3.4 %prologue.1 = (bf16[128,1280]{1,0:T(8,128)(2,1)}, bf16[16,1280]{1,0:T(8,128)(2,1)}, bf16[112,1280]{1,0:T(8,128)(2,1)}, bf16[16,1280]{1,0:T(8,128)(2,1)}, bf16[11...) custom-call(bf16[128,1280]{1,0:T(8,128)(2,1)} %tok_in.1, ...), custom_call_target="tpu_custom_call" | custom-call | bytes 1723908 | tf_op jit(solution)/shard_map/prologue/pallas_call | solution.py:55
  4.1 3.1 %collective-permute-start.4 = (bf16[128,1280]{1,0:T(8,128)(2,1)}, bf16[128,1280]{1,0:T(8,128)(2,1)S(1)}, u32[]{:S(2)}, u32[]{:S(2)}) collective-permute-start(bf16[128,1280]{1,0:T(8,128)(2,1)} %get-tuple-element.129.refs_0_), channel_id=1, source_target_pairs={{0,2},{1,3},{2,0},{3,1},{4,6},{5,7},{6,4},{7,5},{8,10},{9,11},{10,... | collective-permute-start | bytes 983048 | tf_op jit(solution)/shard_map/ppermute | solution.py:91
  7.1 2.6 %collective-permute-start = (bf16[128,1280]{1,0:T(8,128)(2,1)}, bf16[128,1280]{1,0:T(8,128)(2,1)S(1)}, u32[]{:S(2)}, u32[]{:S(2)}) collective-permute-start(bf16[128,1280]{1,0:T(8,128)(2,1)} %get-tuple-element.129.refs_0_), channel_id=1, source_target_pairs={{0,4},{1,5},{2,6},{3,7},{4,0},{5,1},{6,2},{7,3},{8,12},{9,13},{10,... | collective-permute-start | bytes 983048 | tf_op jit(solution)/shard_map/ppermute | solution.py:91
  9.7 12.2 %collective-permute-done.4.refs_2_ = bf16[128,1280]{1,0:T(8,128)(2,1)S(1)} collective-permute-done((bf16[128,1280]{1,0:T(8,128)(2,1)}, bf16[128,1280]{1,0:T(8,128)(2,1)S(1)}, u32[]{:S(2)}, u32[]{:S(2)}) %collective-permute-start.4) | collective-permute-done | bytes 327712 | tf_op jit(solution)/shard_map/ppermute | solution.py:91
  22.0 2.6 %collective-permute-done.refs_0_ = bf16[128,1280]{1,0:T(8,128)(2,1)S(1)} collective-permute-done((bf16[128,1280]{1,0:T(8,128)(2,1)}, bf16[128,1280]{1,0:T(8,128)(2,1)S(1)}, u32[]{:S(2)}, u32[]{:S(2)}) %collective-permute-start) | collective-permute-done | bytes 327712 | tf_op jit(solution)/shard_map/ppermute | solution.py:91
  28.2 2.3 %half.1 = (bf16[512,768]{1,0:T(8,128)(2,1)S(1)}, bf16[1280,512]{1,0:T(8,128)(2,1)S(1)}) custom-call(bf16[128,1280]{1,0:T(8,128)(2,1)S(1)} %copy-done.5, bf16[128,1280]{1,0:T(8,128)(2,1)S(1)} %collective-permute-done.3.refs_1_, bf16[128,1280]{1,0:T(8,128)(2,1)S(1)} %collective-permute-done.4.refs_2_, bf16[128,1280]{1,0:T(8,128)(2,1)S(1)} %collective-permute-done.5.refs_3_, ...), custom_call_target="tpu_custom_call" | custom-call | bytes 1024 | tf_op jit(solution)/shard_map/half/pallas_call | solution.py:55
  33.5 1.8 %collective-permute-start.12 = (bf16[112,1280]{1,0:T(8,128)(2,1)S(1)}, bf16[112,1280]{1,0:T(8,128)(2,1)S(1)}, u32[]{:S(2)}, u32[]{:S(2)}) collective-permute-start(bf16[112,1280]{1,0:T(8,128)(2,1)S(1)} %copy-done.15), channel_id=1, source_target_pairs={{0,4},{1,5},{2,6},{3,7},{4,0},{5,1},{6,2},{7,3},{8,12},{9,13},{10,... | collective-permute-start | bytes 860168 | tf_op jit(solution)/shard_map/ppermute | solution.py:91
  35.4 3.0 %front.1 = (bf16[1024,768]{1,0:T(8,128)(2,1)S(1)}, bf16[128,256]{1,0:T(8,128)(2,1)S(1)}, bf16[128,256]{1,0:T(8,128)(2,1)S(1)}, bf16[64,1280]{1,0:T(8,128)(2,1)S(1)}, bf16[64,1280]{1,0:T(8,128)(2,1)S(1)}) custom-call(bf16[128,1280]{1,0:T(8,128)(2,1)S(1)} %collective-permute-done.refs_0_, bf16[128,1280]{1,0:T(8,128)(2,1)S(1)} %collective-permute-done.1.refs_1_, ...), custom_call_target="tpu_custom_call" | custom-call | bytes 1024 | tf_op jit(solution)/shard_map/front/pallas_call | solution.py:55
  41.7 2.7 %collective-permute-start.11 = (bf16[16,1280]{1,0:T(8,128)(2,1)S(1)}, bf16[16,1280]{1,0:T(8,128)(2,1)S(1)}, u32[]{:S(2)}, u32[]{:S(2)}) collective-permute-start(bf16[16,1280]{1,0:T(8,128)(2,1)S(1)} %get-tuple-element.144), channel_id=1, source_target_pairs={{0,6},{1,7},{2,4},{3,5},{4,2},{5,3},{6,0},{7,1},{8,14},{9,15},{10,... | collective-permute-start | bytes 122888 | tf_op jit(solution)/shard_map/ppermute | solution.py:91
  44.4 2.5 %collective-permute-done.13.refs_2_ = bf16[112,1280]{1,0:T(8,128)(2,1)S(1)} collective-permute-done((bf16[112,1280]{1,0:T(8,128)(2,1)S(1)}, bf16[112,1280]{1,0:T(8,128)(2,1)S(1)}, u32[]{:S(2)}, u32[]{:S(2)}) %collective-permute-start.13) | collective-permute-done | bytes 286752 | tf_op jit(solution)/shard_map/ppermute | solution.py:91
  46.9 5.1 %collective-permute-done.12.refs_4_ = bf16[112,1280]{1,0:T(8,128)(2,1)S(1)} collective-permute-done((bf16[112,1280]{1,0:T(8,128)(2,1)S(1)}, bf16[112,1280]{1,0:T(8,128)(2,1)S(1)}, u32[]{:S(2)}, u32[]{:S(2)}) %collective-permute-start.12) | collective-permute-done | bytes 286752 | tf_op jit(solution)/shard_map/ppermute | solution.py:91
  53.0 1.6 %collective-permute-start.14 = (bf16[4,2560]{1,0:T(4,128)(2,1)S(1)}, bf16[4,2560]{1,0:T(4,128)(2,1)S(1)}, u32[]{:S(2)}, u32[]{:S(2)}) collective-permute-start(bf16[4,2560]{1,0:T(4,128)(2,1)S(1)} %get-tuple-element.158), channel_id=1, source_target_pairs={{0,8},{8,0},{16,24},{24,16},{1,9},{9,1},{17,25},{25,17},{2,10},{10... | collective-permute-start | bytes 61448 | tf_op jit(solution)/shard_map/ppermute | solution.py:91
  57.5 4.1 %cold.1 = (bf16[896,256]{1,0:T(8,128)(2,1)S(1)}, bf16[896,256]{1,0:T(8,128)(2,1)S(1)}, bf16[448,1280]{1,0:T(8,128)(2,1)S(1)}, bf16[448,1280]{1,0:T(8,128)(2,1)S(1)}) custom-call(bf16[1024,768]{1,0:T(8,128)(2,1)S(1)} %get-tuple-element.176.qkv.refs_8_.refs_9_, bf16[256,1280]{1,0:T(8,128)(2,1)S(1)} %get-tuple-element.137.refs_6_.proj.refs_9_.refs_10_), custom_call_target="tpu_custom_call" | custom-call | flops 1073741824 | bytes 5439488 | tf_op jit(solution)/shard_map/cold/pallas_call | solution.py:55
  61.7 1.6 %collective-permute-done.17.refs_6_ = bf16[112,1280]{1,0:T(8,128)(2,1)S(1)} collective-permute-done((bf16[112,1280]{1,0:T(8,128)(2,1)S(1)}, bf16[112,1280]{1,0:T(8,128)(2,1)S(1)}, u32[]{:S(2)}, u32[]{:S(2)}) %collective-permute-start.17) | collective-permute-done | bytes 286752 | tf_op jit(solution)/shard_map/ppermute | solution.py:91
  63.4 2.0 %collective-permute-start.23 = (bf16[16,2560]{1,0:T(8,128)(2,1)S(1)}, bf16[16,2560]{1,0:T(8,128)(2,1)S(1)}, u32[]{:S(2)}, u32[]{:S(2)}) collective-permute-start(bf16[16,2560]{1,0:T(8,128)(2,1)S(1)} %pad_maximum_fusion.refs_0_), channel_id=1, source_target_pairs={{0,6},{1,7},{2,4},{3,5},{4,2},{5,3},{6,0},{7,1},{8,14},{9,15},{10,... | collective-permute-start | bytes 245768 | tf_op jit(solution)/shard_map/ppermute | solution.py:91
  66.0 1.8 %collective-permute-start.19 = (bf16[16,2560]{1,0:T(8,128)(2,1)S(1)}, bf16[16,2560]{1,0:T(8,128)(2,1)S(1)}, u32[]{:S(2)}, u32[]{:S(2)}) collective-permute-start(bf16[16,2560]{1,0:T(8,128)(2,1)S(1)} %pad_maximum_fusion.refs_0_), channel_id=1, source_target_pairs={{0,2},{1,3},{2,0},{3,1},{4,6},{5,7},{6,4},{7,5},{8,10},{9,11},{10,... | collective-permute-start | bytes 245768 | tf_op jit(solution)/shard_map/ppermute | solution.py:91
  67.8 2.0 %collective-permute-done.23.refs_6_ = bf16[16,2560]{1,0:T(8,128)(2,1)S(1)} collective-permute-done((bf16[16,2560]{1,0:T(8,128)(2,1)S(1)}, bf16[16,2560]{1,0:T(8,128)(2,1)S(1)}, u32[]{:S(2)}, u32[]{:S(2)}) %collective-permute-start.23) | collective-permute-done | bytes 81952 | tf_op jit(solution)/shard_map/ppermute | solution.py:91
  69.7 1.9 %collective-permute-done.21.refs_4_ = bf16[16,2560]{1,0:T(8,128)(2,1)S(1)} collective-permute-done((bf16[16,2560]{1,0:T(8,128)(2,1)S(1)}, bf16[16,2560]{1,0:T(8,128)(2,1)S(1)}, u32[]{:S(2)}, u32[]{:S(2)}) %collective-permute-start.21) | collective-permute-done | bytes 81952 | tf_op jit(solution)/shard_map/ppermute | solution.py:91
  73.9 3.3 %experts.1 = (bf16[128,1280]{1,0:T(8,128)(2,1)S(1)}, bf16[128,1280]{1,0:T(8,128)(2,1)S(1)}, bf16[2,128,640]{2,1,0:T(8,128)(2,1)S(1)}, bf16[2,128,640]{2,1,0:T(8,...) custom-call(bf16[16,2560]{1,0:T(8,128)(2,1)S(1)} %pad_maximum_fusion.refs_0_, ...), custom_call_target="tpu_custom_call" | custom-call | flops 1258291200 | bytes 9175040 | tf_op jit(solution)/shard_map/experts/pallas_call | solution.py:55
  79.6 2.6 %collective-permute-start.30 = (bf16[16,2560]{1,0:T(8,128)(2,1)S(1)}, bf16[16,2560]{1,0:T(8,128)(2,1)S(1)}, u32[]{:S(2)}, u32[]{:S(2)}) collective-permute-start(bf16[16,2560]{1,0:T(8,128)(2,1)S(1)} %get-tuple-element.173), channel_id=1, source_target_pairs={{0,4},{1,5},{2,6},{3,7},{4,0},{5,1},{6,2},{7,3},{8,12},{9,13},{10,... | collective-permute-start | bytes 245768 | tf_op jit(solution)/shard_map/ppermute | solution.py:91
  83.8 7.1 %cold_back.1 = (bf16[896,256]{1,0:T(8,128)(2,1)S(1)}, f32[256,1024]{1,0:T(8,128)S(1)}, f32[256,1024]{1,0:T(8,128)S(1)}, f32[256,1280]{1,0:T(8,128)S(1)}) custom-call(bf16[112,1280]{1,0:T(8,128)(2,1)S(1)} %copy-done.15, bf16[112,1280]{1,0:T(8,128)(2,1)S(1)} %collective-permute-done.6.refs_1_, bf16[112,1280]{1,0:T(8,128)(2,1)S(1)} %collective-permute-done.13.refs_2_, ...), custom_call_target="tpu_custom_call" | custom-call | flops 10000000000 | bytes 9306112 | tf_op jit(solution)/shard_map/cold_back/pallas_call | solution.py:55
  91.0 1.6 %collective-permute-start.33 = (bf16[4,2560]{1,0:T(4,128)(2,1)S(1)}, bf16[4,2560]{1,0:T(4,128)(2,1)S(1)}, u32[]{:S(2)}, u32[]{:S(2)}) collective-permute-start(bf16[4,2560]{1,0:T(4,128)(2,1)S(1)} %get-tuple-element.184), channel_id=1, source_target_pairs={{0,8},{8,0},{16,24},{24,16},{1,9},{9,1},{17,25},{25,17},{2,10},{10... | collective-permute-start | bytes 61448 | tf_op jit(solution)/shard_map/ppermute | solution.py:91
  96.4 2.4 %collective-permute-done.35.refs_3_ = bf16[4,2560]{1,0:T(4,128)(2,1)S(1)} collective-permute-done((bf16[4,2560]{1,0:T(4,128)(2,1)S(1)}, bf16[4,2560]{1,0:T(4,128)(2,1)S(1)}, u32[]{:S(2)}, u32[]{:S(2)}) %collective-permute-start.35) | collective-permute-done | bytes 20512 | tf_op jit(solution)/shard_map/ppermute | solution.py:91
  100.6 2.3 %collective-permute-start.43 = (bf16[16,1280]{1,0:T(8,128)(2,1)S(1)}, bf16[16,1280]{1,0:T(8,128)(2,1)S(1)}, u32[]{:S(2)}, u32[]{:S(2)}) collective-permute-start(bf16[16,1280]{1,0:T(8,128)(2,1)S(1)} %get-tuple-element.212.refs_0_), channel_id=1, source_target_pairs={{0,6},{1,7},{2,4},{3,5},{4,2},{5,3},{6,0},{7,1},{8,14},{9,15},{10,... | collective-permute-start | bytes 122888 | tf_op jit(solution)/shard_map/ppermute | solution.py:91
  102.9 2.2 %collective-permute-start.39 = (bf16[16,1280]{1,0:T(8,128)(2,1)S(1)}, bf16[16,1280]{1,0:T(8,128)(2,1)S(1)}, u32[]{:S(2)}, u32[]{:S(2)}) collective-permute-start(bf16[16,1280]{1,0:T(8,128)(2,1)S(1)} %get-tuple-element.212.refs_0_), channel_id=1, source_target_pairs={{0,2},{1,3},{2,0},{3,1},{4,6},{5,7},{6,4},{7,5},{8,10},{9,11},{10,... | collective-permute-start | bytes 122888 | tf_op jit(solution)/shard_map/ppermute | solution.py:91
  109.2 3.2 %hot_back.1 = (bf16[320,640]{1,0:T(8,128)(2,1)S(1)}, bf16[320,640]{1,0:T(8,128)(2,1)S(1)}, bf16[320,640]{1,0:T(8,128)(2,1)S(1)}, bf16[320,640]{1,0:T(8,128)(2,1)S(1)}) custom-call(bf16[16,1280]{1,0:T(8,128)(2,1)S(1)} %get-tuple-element.212.refs_0_, bf16[16,1280]{1,0:T(8,128)(2,1)S(1)} %collective-permute-done.38.refs_1_, ...), custom_call_target="tpu_custom_call" | custom-call | bytes 1024 | tf_op jit(solution)/shard_map/hot_back/pallas_call | solution.py:55
  112.4 1.6 %collective-permute-start.45 = (bf16[320,640]{1,0:T(8,128)(2,1)S(1)}, bf16[320,640]{1,0:T(8,128)(2,1)S(1)}, u32[]{:S(2)}, u32[]{:S(2)}) collective-permute-start(bf16[320,640]{1,0:T(8,128)(2,1)S(1)} %get-tuple-element.226), channel_id=1, source_target_pairs={{0,8},{8,0},{16,24},{24,16},{1,9},{9,1},{17,25},{25,17},{2,10},{10... | collective-permute-start | bytes 1228808 | tf_op jit(solution)/shard_map/ppermute | solution.py:91
  115.5 1.9 %collective-permute-start.37 = (bf16[112,1280]{1,0:T(8,128)(2,1)S(1)}, bf16[112,1280]{1,0:T(8,128)(2,1)S(1)}, u32[]{:S(2)}, u32[]{:S(2)}) collective-permute-start(bf16[112,1280]{1,0:T(8,128)(2,1)S(1)} %get-tuple-element.199), channel_id=1, source_target_pairs={{0,4},{1,5},{2,6},{3,7},{4,0},{5,1},{6,2},{7,3},{8,12},{9,13},{10,... | collective-permute-start | bytes 860168 | tf_op jit(solution)/shard_map/ppermute | solution.py:91
  117.4 4.3 %weight_grads.1 = (bf16[2,1280,640]{2,1,0:T(8,128)(2,1)}, bf16[2,640,1280]{2,1,0:T(8,128)(2,1)}) custom-call(bf16[128,1280]{1,0:T(8,128)(2,1)S(1)} %get-tuple-element.229.arrived, bf16[128,1280]{1,0:T(8,128)(2,1)S(1)} %get-tuple-element.230.grads, bf16[2,128,640]{2,1,0:T(8,128)(2,1)S(1)} %get-tuple-element.231.hidden, ...), custom_call_target="tpu_custom_call" | custom-call | bytes 1024 | tf_op jit(solution)/shard_map/weight_grads/pallas_call | solution.py:55
  121.7 2.5 %collective-permute-done.45.theirs = bf16[320,640]{1,0:T(8,128)(2,1)S(1)} collective-permute-done((bf16[320,640]{1,0:T(8,128)(2,1)S(1)}, bf16[320,640]{1,0:T(8,128)(2,1)S(1)}, u32[]{:S(2)}, u32[]{:S(2)}) %collective-permute-start.45) | collective-permute-done | bytes 409632 | tf_op jit(solution)/shard_map/ppermute | solution.py:91
  126.2 1.6 %collective-permute-start.47 = (bf16[160,640]{1,0:T(8,128)(2,1)S(1)}, bf16[160,640]{1,0:T(8,128)(2,1)S(1)}, u32[]{:S(2)}, u32[]{:S(2)}) collective-permute-start(bf16[160,640]{1,0:T(8,128)(2,1)S(1)} %get-tuple-element.236), channel_id=1, source_target_pairs={{0,16},{8,24},{16,0},{24,8},{1,17},{9,25},{17,1},{25,9},{2,18},{10... | collective-permute-start | bytes 614408 | tf_op jit(solution)/shard_map/ppermute | solution.py:91
  127.8 3.3 %collective-permute-done.37.refs_1_ = bf16[112,1280]{1,0:T(8,128)(2,1)S(1)} collective-permute-done((bf16[112,1280]{1,0:T(8,128)(2,1)S(1)}, bf16[112,1280]{1,0:T(8,128)(2,1)S(1)}, u32[]{:S(2)}, u32[]{:S(2)}) %collective-permute-start.37) | collective-permute-done | bytes 286752 | tf_op jit(solution)/shard_map/ppermute | solution.py:91
  (120 shorter events, 36.8 us)
Async XLA Ops:
  4.1 17.9 %collective-permute-start.4 = (bf16[128,1280]{1,0:T(8,128)(2,1)}, bf16[128,1280]{1,0:T(8,128)(2,1)S(1)}, u32[]{:S(2)}, u32[]{:S(2)}) collective-permute-start(bf16[128,1280]{1,0:T(8,128)(2,1)} %get-tuple-element.129.refs_0_), channel_id=1, source_target_pairs={{0,2},{1,3},{2,0},{3,1},{4,6},{5,7},{6,4},{7,5},{8,10},{9,11},{10,... | collective-permute-start | bytes 983048 | tf_op jit(solution)/shard_map/ppermute | solution.py:91
  7.1 17.4 %collective-permute-start = (bf16[128,1280]{1,0:T(8,128)(2,1)}, bf16[128,1280]{1,0:T(8,128)(2,1)S(1)}, u32[]{:S(2)}, u32[]{:S(2)}) collective-permute-start(bf16[128,1280]{1,0:T(8,128)(2,1)} %get-tuple-element.129.refs_0_), channel_id=1, source_target_pairs={{0,4},{1,5},{2,6},{3,7},{4,0},{5,1},{6,2},{7,3},{8,12},{9,13},{10,... | collective-permute-start | bytes 983048 | tf_op jit(solution)/shard_map/ppermute | solution.py:91
  9.7 18.3 %collective-permute-start.3 = (bf16[128,1280]{1,0:T(8,128)(2,1)}, bf16[128,1280]{1,0:T(8,128)(2,1)S(1)}, u32[]{:S(2)}, u32[]{:S(2)}) collective-permute-start(bf16[128,1280]{1,0:T(8,128)(2,1)} %get-tuple-element.129.refs_0_), channel_id=1, source_target_pairs={{0,1},{1,0},{2,3},{3,2},{4,5},{5,4},{6,7},{7,6},{8,9},{9,8},{10,11... | collective-permute-start | bytes 983048 | tf_op jit(solution)/shard_map/ppermute | solution.py:91
  22.0 6.0 %collective-permute-start.5 = (bf16[128,1280]{1,0:T(8,128)(2,1)S(1)}, bf16[128,1280]{1,0:T(8,128)(2,1)S(1)}, u32[]{:S(2)}, u32[]{:S(2)}) collective-permute-start(bf16[128,1280]{1,0:T(8,128)(2,1)S(1)} %collective-permute-done.4.refs_2_), channel_id=1, source_target_pairs={{0,1},{1,0},{2,3},{3,2},{4,5},{5,4},{6,7},{7,6},{8,9},{9,8},{10,11... | collective-permute-start | bytes 983048 | tf_op jit(solution)/shard_map/ppermute | solution.py:91
  24.5 7.6 %collective-permute-start.2 = (bf16[128,1280]{1,0:T(8,128)(2,1)S(1)}, bf16[128,1280]{1,0:T(8,128)(2,1)S(1)}, u32[]{:S(2)}, u32[]{:S(2)}) collective-permute-start(bf16[128,1280]{1,0:T(8,128)(2,1)S(1)} %collective-permute-done.refs_0_), channel_id=1, source_target_pairs={{0,2},{1,3},{2,0},{3,1},{4,6},{5,7},{6,4},{7,5},{8,10},{9,11},{10,... | collective-permute-start | bytes 983048 | tf_op jit(solution)/shard_map/ppermute | solution.py:91
  27.4 7.9 %collective-permute-start.1 = (bf16[128,1280]{1,0:T(8,128)(2,1)S(1)}, bf16[128,1280]{1,0:T(8,128)(2,1)S(1)}, u32[]{:S(2)}, u32[]{:S(2)}) collective-permute-start(bf16[128,1280]{1,0:T(8,128)(2,1)S(1)} %collective-permute-done.refs_0_), channel_id=1, source_target_pairs={{0,1},{1,0},{2,3},{3,2},{4,5},{5,4},{6,7},{7,6},{8,9},{9,8},{10,11... | collective-permute-start | bytes 983048 | tf_op jit(solution)/shard_map/ppermute | solution.py:91
  32.1 14.8 %collective-permute-start.13 = (bf16[112,1280]{1,0:T(8,128)(2,1)S(1)}, bf16[112,1280]{1,0:T(8,128)(2,1)S(1)}, u32[]{:S(2)}, u32[]{:S(2)}) collective-permute-start(bf16[112,1280]{1,0:T(8,128)(2,1)S(1)} %copy-done.15), channel_id=1, source_target_pairs={{0,2},{1,3},{2,0},{3,1},{4,6},{5,7},{6,4},{7,5},{8,10},{9,11},{10,... | collective-permute-start | bytes 860168 | tf_op jit(solution)/shard_map/ppermute | solution.py:91
  33.5 18.5 %collective-permute-start.12 = (bf16[112,1280]{1,0:T(8,128)(2,1)S(1)}, bf16[112,1280]{1,0:T(8,128)(2,1)S(1)}, u32[]{:S(2)}, u32[]{:S(2)}) collective-permute-start(bf16[112,1280]{1,0:T(8,128)(2,1)S(1)} %copy-done.15), channel_id=1, source_target_pairs={{0,4},{1,5},{2,6},{3,7},{4,0},{5,1},{6,2},{7,3},{8,12},{9,13},{10,... | collective-permute-start | bytes 860168 | tf_op jit(solution)/shard_map/ppermute | solution.py:91
  39.9 12.1 %collective-permute-start.9 = (bf16[16,1280]{1,0:T(8,128)(2,1)S(1)}, bf16[16,1280]{1,0:T(8,128)(2,1)S(1)}, u32[]{:S(2)}, u32[]{:S(2)}) collective-permute-start(bf16[16,1280]{1,0:T(8,128)(2,1)S(1)} %get-tuple-element.142), channel_id=1, source_target_pairs={{0,2},{1,3},{2,0},{3,1},{4,6},{5,7},{6,4},{7,5},{8,10},{9,11},{10,... | collective-permute-start | bytes 122888 | tf_op jit(solution)/shard_map/ppermute | solution.py:91
  40.4 12.2 %collective-permute-start.10 = (bf16[16,1280]{1,0:T(8,128)(2,1)S(1)}, bf16[16,1280]{1,0:T(8,128)(2,1)S(1)}, u32[]{:S(2)}, u32[]{:S(2)}) collective-permute-start(bf16[16,1280]{1,0:T(8,128)(2,1)S(1)} %get-tuple-element.143), channel_id=1, source_target_pairs={{0,4},{1,5},{2,6},{3,7},{4,0},{5,1},{6,2},{7,3},{8,12},{9,13},{10,... | collective-permute-start | bytes 122888 | tf_op jit(solution)/shard_map/ppermute | solution.py:91
  41.7 10.9 %collective-permute-start.11 = (bf16[16,1280]{1,0:T(8,128)(2,1)S(1)}, bf16[16,1280]{1,0:T(8,128)(2,1)S(1)}, u32[]{:S(2)}, u32[]{:S(2)}) collective-permute-start(bf16[16,1280]{1,0:T(8,128)(2,1)S(1)} %get-tuple-element.144), channel_id=1, source_target_pairs={{0,6},{1,7},{2,4},{3,5},{4,2},{5,3},{6,0},{7,1},{8,14},{9,15},{10,... | collective-permute-start | bytes 122888 | tf_op jit(solution)/shard_map/ppermute | solution.py:91
  53.0 8.7 %collective-permute-start.14 = (bf16[4,2560]{1,0:T(4,128)(2,1)S(1)}, bf16[4,2560]{1,0:T(4,128)(2,1)S(1)}, u32[]{:S(2)}, u32[]{:S(2)}) collective-permute-start(bf16[4,2560]{1,0:T(4,128)(2,1)S(1)} %get-tuple-element.158), channel_id=1, source_target_pairs={{0,8},{8,0},{16,24},{24,16},{1,9},{9,1},{17,25},{25,17},{2,10},{10... | collective-permute-start | bytes 61448 | tf_op jit(solution)/shard_map/ppermute | solution.py:91
  54.5 7.1 %collective-permute-start.15 = (bf16[4,2560]{1,0:T(4,128)(2,1)S(1)}, bf16[4,2560]{1,0:T(4,128)(2,1)S(1)}, u32[]{:S(2)}, u32[]{:S(2)}) collective-permute-start(bf16[4,2560]{1,0:T(4,128)(2,1)S(1)} %get-tuple-element.159), channel_id=1, source_target_pairs={{0,16},{8,24},{16,0},{24,8},{1,17},{9,25},{17,1},{25,9},{2,18},{10... | collective-permute-start | bytes 61448 | tf_op jit(solution)/shard_map/ppermute | solution.py:91
  56.0 5.6 %collective-permute-start.16 = (bf16[4,2560]{1,0:T(4,128)(2,1)S(1)}, bf16[4,2560]{1,0:T(4,128)(2,1)S(1)}, u32[]{:S(2)}, u32[]{:S(2)}) collective-permute-start(bf16[4,2560]{1,0:T(4,128)(2,1)S(1)} %get-tuple-element.160), channel_id=1, source_target_pairs={{0,24},{8,16},{16,8},{24,0},{1,25},{9,17},{17,9},{25,1},{2,26},{10... | collective-permute-start | bytes 61448 | tf_op jit(solution)/shard_map/ppermute | solution.py:91
  56.5 6.9 %collective-permute-start.17 = (bf16[112,1280]{1,0:T(8,128)(2,1)S(1)}, bf16[112,1280]{1,0:T(8,128)(2,1)S(1)}, u32[]{:S(2)}, u32[]{:S(2)}) collective-permute-start(bf16[112,1280]{1,0:T(8,128)(2,1)S(1)} %collective-permute-done.12.refs_4_), channel_id=1, source_target_pairs={{0,2},{1,3},{2,0},{3,1},{4,6},{5,7},{6,4},{7,5},{8,10},{9,11},{10,... | collective-permute-start | bytes 860168 | tf_op jit(solution)/shard_map/ppermute | solution.py:91
  63.4 6.4 %collective-permute-start.23 = (bf16[16,2560]{1,0:T(8,128)(2,1)S(1)}, bf16[16,2560]{1,0:T(8,128)(2,1)S(1)}, u32[]{:S(2)}, u32[]{:S(2)}) collective-permute-start(bf16[16,2560]{1,0:T(8,128)(2,1)S(1)} %pad_maximum_fusion.refs_0_), channel_id=1, source_target_pairs={{0,6},{1,7},{2,4},{3,5},{4,2},{5,3},{6,0},{7,1},{8,14},{9,15},{10,... | collective-permute-start | bytes 245768 | tf_op jit(solution)/shard_map/ppermute | solution.py:91
  65.4 6.2 %collective-permute-start.21 = (bf16[16,2560]{1,0:T(8,128)(2,1)S(1)}, bf16[16,2560]{1,0:T(8,128)(2,1)S(1)}, u32[]{:S(2)}, u32[]{:S(2)}) collective-permute-start(bf16[16,2560]{1,0:T(8,128)(2,1)S(1)} %pad_maximum_fusion.refs_0_), channel_id=1, source_target_pairs={{0,4},{1,5},{2,6},{3,7},{4,0},{5,1},{6,2},{7,3},{8,12},{9,13},{10,... | collective-permute-start | bytes 245768 | tf_op jit(solution)/shard_map/ppermute | solution.py:91
  66.0 5.7 %collective-permute-start.19 = (bf16[16,2560]{1,0:T(8,128)(2,1)S(1)}, bf16[16,2560]{1,0:T(8,128)(2,1)S(1)}, u32[]{:S(2)}, u32[]{:S(2)}) collective-permute-start(bf16[16,2560]{1,0:T(8,128)(2,1)S(1)} %pad_maximum_fusion.refs_0_), channel_id=1, source_target_pairs={{0,2},{1,3},{2,0},{3,1},{4,6},{5,7},{6,4},{7,5},{8,10},{9,11},{10,... | collective-permute-start | bytes 245768 | tf_op jit(solution)/shard_map/ppermute | solution.py:91
  77.7 6.0 %collective-permute-start.32 = (bf16[112,1280]{1,0:T(8,128)(2,1)S(1)}, bf16[112,1280]{1,0:T(8,128)(2,1)S(1)}, u32[]{:S(2)}, u32[]{:S(2)}) collective-permute-start(bf16[112,1280]{1,0:T(8,128)(2,1)S(1)} %collective-permute-done.17.refs_6_), channel_id=1, source_target_pairs={{0,1},{1,0},{2,3},{3,2},{4,5},{5,4},{6,7},{7,6},{8,9},{9,8},{10,11... | collective-permute-start | bytes 860168 | tf_op jit(solution)/shard_map/ppermute | solution.py:91
  79.3 11.6 %collective-permute-start.29 = (bf16[16,2560]{1,0:T(8,128)(2,1)S(1)}, bf16[16,2560]{1,0:T(8,128)(2,1)S(1)}, u32[]{:S(2)}, u32[]{:S(2)}) collective-permute-start(bf16[16,2560]{1,0:T(8,128)(2,1)S(1)} %get-tuple-element.172), channel_id=1, source_target_pairs={{0,2},{1,3},{2,0},{3,1},{4,6},{5,7},{6,4},{7,5},{8,10},{9,11},{10,... | collective-permute-start | bytes 245768 | tf_op jit(solution)/shard_map/ppermute | solution.py:91
  79.6 11.3 %collective-permute-start.30 = (bf16[16,2560]{1,0:T(8,128)(2,1)S(1)}, bf16[16,2560]{1,0:T(8,128)(2,1)S(1)}, u32[]{:S(2)}, u32[]{:S(2)}) collective-permute-start(bf16[16,2560]{1,0:T(8,128)(2,1)S(1)} %get-tuple-element.173), channel_id=1, source_target_pairs={{0,4},{1,5},{2,6},{3,7},{4,0},{5,1},{6,2},{7,3},{8,12},{9,13},{10,... | collective-permute-start | bytes 245768 | tf_op jit(solution)/shard_map/ppermute | solution.py:91
  82.2 8.7 %collective-permute-start.31 = (bf16[16,2560]{1,0:T(8,128)(2,1)S(1)}, bf16[16,2560]{1,0:T(8,128)(2,1)S(1)}, u32[]{:S(2)}, u32[]{:S(2)}) collective-permute-start(bf16[16,2560]{1,0:T(8,128)(2,1)S(1)} %get-tuple-element.174), channel_id=1, source_target_pairs={{0,6},{1,7},{2,4},{3,5},{4,2},{5,3},{6,0},{7,1},{8,14},{9,15},{10,... | collective-permute-start | bytes 245768 | tf_op jit(solution)/shard_map/ppermute | solution.py:91
  83.7 16.6 %collective-permute-start.36 = (bf16[224,1280]{1,0:T(8,128)(2,1)S(1)}, bf16[224,1280]{1,0:T(8,128)(2,1)S(1)}, u32[]{:S(2)}, u32[]{:S(2)}) collective-permute-start(bf16[224,1280]{1,0:T(8,128)(2,1)S(1)} %get-tuple-element.188), channel_id=1, source_target_pairs={{0,2},{1,3},{2,0},{3,1},{4,6},{5,7},{6,4},{7,5},{8,10},{9,11},{10,... | collective-permute-start | bytes 1720328 | tf_op jit(solution)/shard_map/ppermute | solution.py:91
  94.1 4.7 %collective-permute-start.35 = (bf16[4,2560]{1,0:T(4,128)(2,1)S(1)}, bf16[4,2560]{1,0:T(4,128)(2,1)S(1)}, u32[]{:S(2)}, u32[]{:S(2)}) collective-permute-start(bf16[4,2560]{1,0:T(4,128)(2,1)S(1)} %get-tuple-element.186), channel_id=1, source_target_pairs={{0,24},{8,16},{16,8},{24,0},{1,25},{9,17},{17,9},{25,1},{2,26},{10... | collective-permute-start | bytes 61448 | tf_op jit(solution)/shard_map/ppermute | solution.py:91
  100.6 5.9 %collective-permute-start.43 = (bf16[16,1280]{1,0:T(8,128)(2,1)S(1)}, bf16[16,1280]{1,0:T(8,128)(2,1)S(1)}, u32[]{:S(2)}, u32[]{:S(2)}) collective-permute-start(bf16[16,1280]{1,0:T(8,128)(2,1)S(1)} %get-tuple-element.212.refs_0_), channel_id=1, source_target_pairs={{0,6},{1,7},{2,4},{3,5},{4,2},{5,3},{6,0},{7,1},{8,14},{9,15},{10,... | collective-permute-start | bytes 122888 | tf_op jit(solution)/shard_map/ppermute | solution.py:91
  102.9 4.9 %collective-permute-start.41 = (bf16[16,1280]{1,0:T(8,128)(2,1)S(1)}, bf16[16,1280]{1,0:T(8,128)(2,1)S(1)}, u32[]{:S(2)}, u32[]{:S(2)}) collective-permute-start(bf16[16,1280]{1,0:T(8,128)(2,1)S(1)} %get-tuple-element.212.refs_0_), channel_id=1, source_target_pairs={{0,4},{1,5},{2,6},{3,7},{4,0},{5,1},{6,2},{7,3},{8,12},{9,13},{10,... | collective-permute-start | bytes 122888 | tf_op jit(solution)/shard_map/ppermute | solution.py:91
  102.9 4.9 %collective-permute-start.39 = (bf16[16,1280]{1,0:T(8,128)(2,1)S(1)}, bf16[16,1280]{1,0:T(8,128)(2,1)S(1)}, u32[]{:S(2)}, u32[]{:S(2)}) collective-permute-start(bf16[16,1280]{1,0:T(8,128)(2,1)S(1)} %get-tuple-element.212.refs_0_), channel_id=1, source_target_pairs={{0,2},{1,3},{2,0},{3,1},{4,6},{5,7},{6,4},{7,5},{8,10},{9,11},{10,... | collective-permute-start | bytes 122888 | tf_op jit(solution)/shard_map/ppermute | solution.py:91
  112.4 11.8 %collective-permute-start.45 = (bf16[320,640]{1,0:T(8,128)(2,1)S(1)}, bf16[320,640]{1,0:T(8,128)(2,1)S(1)}, u32[]{:S(2)}, u32[]{:S(2)}) collective-permute-start(bf16[320,640]{1,0:T(8,128)(2,1)S(1)} %get-tuple-element.226), channel_id=1, source_target_pairs={{0,8},{8,0},{16,24},{24,16},{1,9},{9,1},{17,25},{25,17},{2,10},{10... | collective-permute-start | bytes 1228808 | tf_op jit(solution)/shard_map/ppermute | solution.py:91
  113.9 11.4 %collective-permute-start.46 = (bf16[320,640]{1,0:T(8,128)(2,1)S(1)}, bf16[320,640]{1,0:T(8,128)(2,1)S(1)}, u32[]{:S(2)}, u32[]{:S(2)}) collective-permute-start(bf16[320,640]{1,0:T(8,128)(2,1)S(1)} %get-tuple-element.227), channel_id=1, source_target_pairs={{0,16},{8,24},{16,0},{24,8},{1,17},{9,25},{17,1},{25,9},{2,18},{10... | collective-permute-start | bytes 1228808 | tf_op jit(solution)/shard_map/ppermute | solution.py:91
  115.5 15.6 %collective-permute-start.37 = (bf16[112,1280]{1,0:T(8,128)(2,1)S(1)}, bf16[112,1280]{1,0:T(8,128)(2,1)S(1)}, u32[]{:S(2)}, u32[]{:S(2)}) collective-permute-start(bf16[112,1280]{1,0:T(8,128)(2,1)S(1)} %get-tuple-element.199), channel_id=1, source_target_pairs={{0,4},{1,5},{2,6},{3,7},{4,0},{5,1},{6,2},{7,3},{8,12},{9,13},{10,... | collective-permute-start | bytes 860168 | tf_op jit(solution)/shard_map/ppermute | solution.py:91
  125.6 6.7 %collective-permute-start.48 = (bf16[160,640]{1,0:T(8,128)(2,1)S(1)}, bf16[160,640]{1,0:T(8,128)(2,1)S(1)}, u32[]{:S(2)}, u32[]{:S(2)}) collective-permute-start(bf16[160,640]{1,0:T(8,128)(2,1)S(1)} %get-tuple-element.240), channel_id=1, source_target_pairs={{0,8},{8,0},{16,24},{24,16},{1,9},{9,1},{17,25},{25,17},{2,10},{10... | collective-permute-start | bytes 614408 | tf_op jit(solution)/shard_map/ppermute | solution.py:91
  126.2 6.2 %collective-permute-start.47 = (bf16[160,640]{1,0:T(8,128)(2,1)S(1)}, bf16[160,640]{1,0:T(8,128)(2,1)S(1)}, u32[]{:S(2)}, u32[]{:S(2)}) collective-permute-start(bf16[160,640]{1,0:T(8,128)(2,1)S(1)} %get-tuple-element.236), channel_id=1, source_target_pairs={{0,16},{8,24},{16,0},{24,8},{1,17},{9,25},{17,1},{25,9},{2,18},{10... | collective-permute-start | bytes 614408 | tf_op jit(solution)/shard_map/ppermute | solution.py:91
  (33 other events, 260.9 us)

commit v7 on v6

--- a/solution.py
+++ b/solution.py
@@ -776,7 +776,6 @@
         "split_slots",
     )
     back = [pieces[0]] + [hop(pieces[g], "dp", g) for g in range(1, groups)]
-    back = after(back, cold_theirs)
     grad_hot, expert_out = run(
         make_mid_back(groups),
         [shape((places, width)), shape((places, width))],

time: 134 us -> 132 us (0.985)
  starting transfers between devices: 45.4 us -> 42.6 us
    ppermute x49, starting transfers between devices: 45.4 us -> 42.6 us  [hop(): return lax.ppermute(x, axis, [(i, i ^ mask) for i in range(size)])]
  transfers between devices with their start and end apart: 49 -> 49, of which waited for: 24 -> 26; matrix products, arithmetic and copies ran while one was open for 0% -> 0% of each run, Pallas kernels for 20% -> 21%
where the time goes in v7:
time: 132 us
  waiting for transfers between devices  50.3 us (38%)
  starting transfers between devices  42.6 us (32%)
  Pallas kernels  35.6 us (27%)
  local copies, waits for them, and re-layouts  2.56 us (2%)
    ppermute x49, waiting for transfers between devices, hop(): return lax.ppermute(x, axis, [(i, i ^ mask) for i in range(size)])  50.3 us
    ppermute x49, starting transfers between devices, hop(): return lax.ppermute(x, axis, [(i, i ^ mask) for i in range(size)])  42.6 us
    pallas_call x21, Pallas kernels, run(): pl.pallas_call(body, out_shape=list(outs), in_specs=specs, out_specs=[pl....  35.6 us
  transfers between devices with their start and end apart: 49, of which 26 were waited for; matrix products, arithmetic and copies ran while one was open for 0% of the time, Pallas kernels for 21%

profile of v7, /device:TPU:0, one launch (start us, length us, event | category | flops | bytes accessed | tf_op | source)
XLA Modules:
  0.0 132.0 jit_solution(10726677962084439475)
XLA Ops:
  0.6 3.4 %prologue.1 = (bf16[128,1280]{1,0:T(8,128)(2,1)}, bf16[16,1280]{1,0:T(8,128)(2,1)}, bf16[112,1280]{1,0:T(8,128)(2,1)}, bf16[16,1280]{1,0:T(8,128)(2,1)}, bf16[11...) custom-call(bf16[128,1280]{1,0:T(8,128)(2,1)} %tok_in.1, ...), custom_call_target="tpu_custom_call" | custom-call | bytes 1723908 | tf_op jit(solution)/shard_map/prologue/pallas_call | solution.py:55
  4.1 3.1 %collective-permute-start.4 = (bf16[128,1280]{1,0:T(8,128)(2,1)}, bf16[128,1280]{1,0:T(8,128)(2,1)S(1)}, u32[]{:S(2)}, u32[]{:S(2)}) collective-permute-start(bf16[128,1280]{1,0:T(8,128)(2,1)} %get-tuple-element.125.refs_0_), channel_id=1, source_target_pairs={{0,2},{1,3},{2,0},{3,1},{4,6},{5,7},{6,4},{7,5},{8,10},{9,11},{10,... | collective-permute-start | bytes 983048 | tf_op jit(solution)/shard_map/ppermute | solution.py:91
  7.1 2.6 %collective-permute-start = (bf16[128,1280]{1,0:T(8,128)(2,1)}, bf16[128,1280]{1,0:T(8,128)(2,1)S(1)}, u32[]{:S(2)}, u32[]{:S(2)}) collective-permute-start(bf16[128,1280]{1,0:T(8,128)(2,1)} %get-tuple-element.125.refs_0_), channel_id=1, source_target_pairs={{0,4},{1,5},{2,6},{3,7},{4,0},{5,1},{6,2},{7,3},{8,12},{9,13},{10,... | collective-permute-start | bytes 983048 | tf_op jit(solution)/shard_map/ppermute | solution.py:91
  9.7 12.2 %collective-permute-done.4.refs_2_ = bf16[128,1280]{1,0:T(8,128)(2,1)S(1)} collective-permute-done((bf16[128,1280]{1,0:T(8,128)(2,1)}, bf16[128,1280]{1,0:T(8,128)(2,1)S(1)}, u32[]{:S(2)}, u32[]{:S(2)}) %collective-permute-start.4) | collective-permute-done | bytes 327712 | tf_op jit(solution)/shard_map/ppermute | solution.py:91
  22.0 2.6 %collective-permute-done.refs_0_ = bf16[128,1280]{1,0:T(8,128)(2,1)S(1)} collective-permute-done((bf16[128,1280]{1,0:T(8,128)(2,1)}, bf16[128,1280]{1,0:T(8,128)(2,1)S(1)}, u32[]{:S(2)}, u32[]{:S(2)}) %collective-permute-start) | collective-permute-done | bytes 327712 | tf_op jit(solution)/shard_map/ppermute | solution.py:91
  28.2 2.3 %half.1 = (bf16[512,768]{1,0:T(8,128)(2,1)S(1)}, bf16[1280,512]{1,0:T(8,128)(2,1)S(1)}) custom-call(bf16[128,1280]{1,0:T(8,128)(2,1)S(1)} %copy-done.5, bf16[128,1280]{1,0:T(8,128)(2,1)S(1)} %collective-permute-done.3.refs_1_, bf16[128,1280]{1,0:T(8,128)(2,1)S(1)} %collective-permute-done.4.refs_2_, bf16[128,1280]{1,0:T(8,128)(2,1)S(1)} %collective-permute-done.5.refs_3_, ...), custom_call_target="tpu_custom_call" | custom-call | bytes 1024 | tf_op jit(solution)/shard_map/half/pallas_call | solution.py:55
  30.6 1.5 %collective-permute-done.2.refs_2_ = bf16[128,1280]{1,0:T(8,128)(2,1)S(1)} collective-permute-done((bf16[128,1280]{1,0:T(8,128)(2,1)S(1)}, bf16[128,1280]{1,0:T(8,128)(2,1)S(1)}, u32[]{:S(2)}, u32[]{:S(2)}) %collective-permute-start.2) | collective-permute-done | bytes 327712 | tf_op jit(solution)/shard_map/ppermute | solution.py:91
  33.5 1.8 %collective-permute-start.12 = (bf16[112,1280]{1,0:T(8,128)(2,1)S(1)}, bf16[112,1280]{1,0:T(8,128)(2,1)S(1)}, u32[]{:S(2)}, u32[]{:S(2)}) collective-permute-start(bf16[112,1280]{1,0:T(8,128)(2,1)S(1)} %copy-done.15), channel_id=1, source_target_pairs={{0,4},{1,5},{2,6},{3,7},{4,0},{5,1},{6,2},{7,3},{8,12},{9,13},{10,... | collective-permute-start | bytes 860168 | tf_op jit(solution)/shard_map/ppermute | solution.py:91
  35.4 3.0 %front.1 = (bf16[1024,768]{1,0:T(8,128)(2,1)S(1)}, bf16[128,256]{1,0:T(8,128)(2,1)S(1)}, bf16[128,256]{1,0:T(8,128)(2,1)S(1)}, bf16[64,1280]{1,0:T(8,128)(2,1)S(1)}, bf16[64,1280]{1,0:T(8,128)(2,1)S(1)}) custom-call(bf16[128,1280]{1,0:T(8,128)(2,1)S(1)} %collective-permute-done.refs_0_, bf16[128,1280]{1,0:T(8,128)(2,1)S(1)} %collective-permute-done.1.refs_1_, ...), custom_call_target="tpu_custom_call" | custom-call | bytes 1024 | tf_op jit(solution)/shard_map/front/pallas_call | solution.py:55
  41.7 2.7 %collective-permute-start.11 = (bf16[16,1280]{1,0:T(8,128)(2,1)S(1)}, bf16[16,1280]{1,0:T(8,128)(2,1)S(1)}, u32[]{:S(2)}, u32[]{:S(2)}) collective-permute-start(bf16[16,1280]{1,0:T(8,128)(2,1)S(1)} %get-tuple-element.140), channel_id=1, source_target_pairs={{0,6},{1,7},{2,4},{3,5},{4,2},{5,3},{6,0},{7,1},{8,14},{9,15},{10,... | collective-permute-start | bytes 122888 | tf_op jit(solution)/shard_map/ppermute | solution.py:91
  44.4 2.5 %collective-permute-done.13.refs_2_ = bf16[112,1280]{1,0:T(8,128)(2,1)S(1)} collective-permute-done((bf16[112,1280]{1,0:T(8,128)(2,1)S(1)}, bf16[112,1280]{1,0:T(8,128)(2,1)S(1)}, u32[]{:S(2)}, u32[]{:S(2)}) %collective-permute-start.13) | collective-permute-done | bytes 286752 | tf_op jit(solution)/shard_map/ppermute | solution.py:91
  46.9 5.1 %collective-permute-done.12.refs_4_ = bf16[112,1280]{1,0:T(8,128)(2,1)S(1)} collective-permute-done((bf16[112,1280]{1,0:T(8,128)(2,1)S(1)}, bf16[112,1280]{1,0:T(8,128)(2,1)S(1)}, u32[]{:S(2)}, u32[]{:S(2)}) %collective-permute-start.12) | collective-permute-done | bytes 286752 | tf_op jit(solution)/shard_map/ppermute | solution.py:91
  53.0 1.6 %collective-permute-start.14 = (bf16[4,2560]{1,0:T(4,128)(2,1)S(1)}, bf16[4,2560]{1,0:T(4,128)(2,1)S(1)}, u32[]{:S(2)}, u32[]{:S(2)}) collective-permute-start(bf16[4,2560]{1,0:T(4,128)(2,1)S(1)} %get-tuple-element.154), channel_id=1, source_target_pairs={{0,8},{8,0},{16,24},{24,16},{1,9},{9,1},{17,25},{25,17},{2,10},{10... | collective-permute-start | bytes 61448 | tf_op jit(solution)/shard_map/ppermute | solution.py:91
  57.5 4.1 %cold.1 = (bf16[896,256]{1,0:T(8,128)(2,1)S(1)}, bf16[896,256]{1,0:T(8,128)(2,1)S(1)}, bf16[448,1280]{1,0:T(8,128)(2,1)S(1)}, bf16[448,1280]{1,0:T(8,128)(2,1)S(1)}) custom-call(bf16[1024,768]{1,0:T(8,128)(2,1)S(1)} %get-tuple-element.172.qkv.refs_8_.refs_9_, bf16[256,1280]{1,0:T(8,128)(2,1)S(1)} %get-tuple-element.133.refs_6_.proj.refs_9_.refs_10_), custom_call_target="tpu_custom_call" | custom-call | flops 1073741824 | bytes 5439488 | tf_op jit(solution)/shard_map/cold/pallas_call | solution.py:55
  61.7 1.6 %collective-permute-done.17.refs_6_ = bf16[112,1280]{1,0:T(8,128)(2,1)S(1)} collective-permute-done((bf16[112,1280]{1,0:T(8,128)(2,1)S(1)}, bf16[112,1280]{1,0:T(8,128)(2,1)S(1)}, u32[]{:S(2)}, u32[]{:S(2)}) %collective-permute-start.17) | collective-permute-done | bytes 286752 | tf_op jit(solution)/shard_map/ppermute | solution.py:91
  63.4 2.0 %collective-permute-start.23 = (bf16[16,2560]{1,0:T(8,128)(2,1)S(1)}, bf16[16,2560]{1,0:T(8,128)(2,1)S(1)}, u32[]{:S(2)}, u32[]{:S(2)}) collective-permute-start(bf16[16,2560]{1,0:T(8,128)(2,1)S(1)} %pad_maximum_fusion.refs_0_), channel_id=1, source_target_pairs={{0,6},{1,7},{2,4},{3,5},{4,2},{5,3},{6,0},{7,1},{8,14},{9,15},{10,... | collective-permute-start | bytes 245768 | tf_op jit(solution)/shard_map/ppermute | solution.py:91
  66.0 1.8 %collective-permute-start.19 = (bf16[16,2560]{1,0:T(8,128)(2,1)S(1)}, bf16[16,2560]{1,0:T(8,128)(2,1)S(1)}, u32[]{:S(2)}, u32[]{:S(2)}) collective-permute-start(bf16[16,2560]{1,0:T(8,128)(2,1)S(1)} %pad_maximum_fusion.refs_0_), channel_id=1, source_target_pairs={{0,2},{1,3},{2,0},{3,1},{4,6},{5,7},{6,4},{7,5},{8,10},{9,11},{10,... | collective-permute-start | bytes 245768 | tf_op jit(solution)/shard_map/ppermute | solution.py:91
  67.8 2.0 %collective-permute-done.23.refs_6_ = bf16[16,2560]{1,0:T(8,128)(2,1)S(1)} collective-permute-done((bf16[16,2560]{1,0:T(8,128)(2,1)S(1)}, bf16[16,2560]{1,0:T(8,128)(2,1)S(1)}, u32[]{:S(2)}, u32[]{:S(2)}) %collective-permute-start.23) | collective-permute-done | bytes 81952 | tf_op jit(solution)/shard_map/ppermute | solution.py:91
  69.7 1.9 %collective-permute-done.21.refs_4_ = bf16[16,2560]{1,0:T(8,128)(2,1)S(1)} collective-permute-done((bf16[16,2560]{1,0:T(8,128)(2,1)S(1)}, bf16[16,2560]{1,0:T(8,128)(2,1)S(1)}, u32[]{:S(2)}, u32[]{:S(2)}) %collective-permute-start.21) | collective-permute-done | bytes 81952 | tf_op jit(solution)/shard_map/ppermute | solution.py:91
  73.9 3.3 %experts.1 = (bf16[128,1280]{1,0:T(8,128)(2,1)S(1)}, bf16[128,1280]{1,0:T(8,128)(2,1)S(1)}, bf16[2,128,640]{2,1,0:T(8,128)(2,1)S(1)}, bf16[2,128,640]{2,1,0:T(8,...) custom-call(bf16[16,2560]{1,0:T(8,128)(2,1)S(1)} %pad_maximum_fusion.refs_0_, ...), custom_call_target="tpu_custom_call" | custom-call | flops 1258291200 | bytes 9175040 | tf_op jit(solution)/shard_map/experts/pallas_call | solution.py:55
  79.6 2.6 %collective-permute-start.30 = (bf16[16,2560]{1,0:T(8,128)(2,1)S(1)}, bf16[16,2560]{1,0:T(8,128)(2,1)S(1)}, u32[]{:S(2)}, u32[]{:S(2)}) collective-permute-start(bf16[16,2560]{1,0:T(8,128)(2,1)S(1)} %get-tuple-element.169), channel_id=1, source_target_pairs={{0,4},{1,5},{2,6},{3,7},{4,0},{5,1},{6,2},{7,3},{8,12},{9,13},{10,... | collective-permute-start | bytes 245768 | tf_op jit(solution)/shard_map/ppermute | solution.py:91
  83.8 7.1 %cold_back.1 = (bf16[896,256]{1,0:T(8,128)(2,1)S(1)}, f32[256,1024]{1,0:T(8,128)S(1)}, f32[256,1024]{1,0:T(8,128)S(1)}, f32[256,1280]{1,0:T(8,128)S(1)}) custom-call(bf16[112,1280]{1,0:T(8,128)(2,1)S(1)} %copy-done.15, bf16[112,1280]{1,0:T(8,128)(2,1)S(1)} %collective-permute-done.6.refs_1_, bf16[112,1280]{1,0:T(8,128)(2,1)S(1)} %collective-permute-done.13.refs_2_, ...), custom_call_target="tpu_custom_call" | custom-call | flops 10000000000 | bytes 9306112 | tf_op jit(solution)/shard_map/cold_back/pallas_call | solution.py:55
  91.0 1.6 %collective-permute-start.33 = (bf16[4,2560]{1,0:T(4,128)(2,1)S(1)}, bf16[4,2560]{1,0:T(4,128)(2,1)S(1)}, u32[]{:S(2)}, u32[]{:S(2)}) collective-permute-start(bf16[4,2560]{1,0:T(4,128)(2,1)S(1)} %get-tuple-element.180), channel_id=1, source_target_pairs={{0,8},{8,0},{16,24},{24,16},{1,9},{9,1},{17,25},{25,17},{2,10},{10... | collective-permute-start | bytes 61448 | tf_op jit(solution)/shard_map/ppermute | solution.py:91
  94.8 1.6 %collective-permute-done.34.refs_2_ = bf16[4,2560]{1,0:T(4,128)(2,1)S(1)} collective-permute-done((bf16[4,2560]{1,0:T(4,128)(2,1)S(1)}, bf16[4,2560]{1,0:T(4,128)(2,1)S(1)}, u32[]{:S(2)}, u32[]{:S(2)}) %collective-permute-start.34) | collective-permute-done | bytes 20512 | tf_op jit(solution)/shard_map/ppermute | solution.py:91
  96.4 2.4 %collective-permute-done.35.refs_3_ = bf16[4,2560]{1,0:T(4,128)(2,1)S(1)} collective-permute-done((bf16[4,2560]{1,0:T(4,128)(2,1)S(1)}, bf16[4,2560]{1,0:T(4,128)(2,1)S(1)}, u32[]{:S(2)}, u32[]{:S(2)}) %collective-permute-start.35) | collective-permute-done | bytes 20512 | tf_op jit(solution)/shard_map/ppermute | solution.py:91
  99.0 2.3 %collective-permute-start.43 = (bf16[16,1280]{1,0:T(8,128)(2,1)S(1)}, bf16[16,1280]{1,0:T(8,128)(2,1)S(1)}, u32[]{:S(2)}, u32[]{:S(2)}) collective-permute-start(bf16[16,1280]{1,0:T(8,128)(2,1)S(1)} %get-tuple-element.204.refs_0_), channel_id=1, source_target_pairs={{0,6},{1,7},{2,4},{3,5},{4,2},{5,3},{6,0},{7,1},{8,14},{9,15},{10,... | collective-permute-start | bytes 122888 | tf_op jit(solution)/shard_map/ppermute | solution.py:91
  107.9 3.2 %hot_back.1 = (bf16[320,640]{1,0:T(8,128)(2,1)S(1)}, bf16[320,640]{1,0:T(8,128)(2,1)S(1)}, bf16[320,640]{1,0:T(8,128)(2,1)S(1)}, bf16[320,640]{1,0:T(8,128)(2,1)S(1)}) custom-call(bf16[16,1280]{1,0:T(8,128)(2,1)S(1)} %get-tuple-element.204.refs_0_, bf16[16,1280]{1,0:T(8,128)(2,1)S(1)} %collective-permute-done.38.refs_1_, ...), custom_call_target="tpu_custom_call" | custom-call | bytes 1024 | tf_op jit(solution)/shard_map/hot_back/pallas_call | solution.py:55
  112.2 1.6 %collective-permute-start.37 = (bf16[112,1280]{1,0:T(8,128)(2,1)S(1)}, bf16[112,1280]{1,0:T(8,128)(2,1)S(1)}, u32[]{:S(2)}, u32[]{:S(2)}) collective-permute-start(bf16[112,1280]{1,0:T(8,128)(2,1)S(1)} %get-tuple-element.191), channel_id=1, source_target_pairs={{0,4},{1,5},{2,6},{3,7},{4,0},{5,1},{6,2},{7,3},{8,12},{9,13},{10,... | collective-permute-start | bytes 860168 | tf_op jit(solution)/shard_map/ppermute | solution.py:91
  113.8 4.3 %weight_grads.1 = (bf16[2,1280,640]{2,1,0:T(8,128)(2,1)}, bf16[2,640,1280]{2,1,0:T(8,128)(2,1)}) custom-call(bf16[128,1280]{1,0:T(8,128)(2,1)S(1)} %get-tuple-element.221.arrived, bf16[128,1280]{1,0:T(8,128)(2,1)S(1)} %get-tuple-element.222.grads, bf16[2,128,640]{2,1,0:T(8,128)(2,1)S(1)} %get-tuple-element.223.hidden, ...), custom_call_target="tpu_custom_call" | custom-call | bytes 1024 | tf_op jit(solution)/shard_map/weight_grads/pallas_call | solution.py:55
  118.2 4.5 %collective-permute-done.45.theirs = bf16[320,640]{1,0:T(8,128)(2,1)S(1)} collective-permute-done((bf16[320,640]{1,0:T(8,128)(2,1)S(1)}, bf16[320,640]{1,0:T(8,128)(2,1)S(1)}, u32[]{:S(2)}, u32[]{:S(2)}) %collective-permute-start.45) | collective-permute-done | bytes 409632 | tf_op jit(solution)/shard_map/ppermute | solution.py:91
  125.3 2.3 %collective-permute-done.37.refs_1_ = bf16[112,1280]{1,0:T(8,128)(2,1)S(1)} collective-permute-done((bf16[112,1280]{1,0:T(8,128)(2,1)S(1)}, bf16[112,1280]{1,0:T(8,128)(2,1)S(1)}, u32[]{:S(2)}, u32[]{:S(2)}) %collective-permute-start.37) | collective-permute-done | bytes 286752 | tf_op jit(solution)/shard_map/ppermute | solution.py:91
  130.5 1.5 %last.1 = (f32[320,2,240]{2,1,0:T(2,128)}, f32[2,80,320]{2,1,0:T(8,128)}) custom-call(bf16[160,640]{1,0:T(8,128)(2,1)S(1)} %get-tuple-element.233.a, bf16[160,640]{1,0:T(8,128)(2,1)S(1)} %collective-permute-done.47.b, bf16[160,640]{1,0:T(8,128)(2,1)S(1)} %get-tuple-element.235.c, bf16[160,640]{1,0:T(8,128)(2,1)S(1)} %collective-permute-done.48.d), custom_call_target="tpu_custom_call" | custom-call | bytes 1638400 | tf_op jit(solution)/shard_map/last/pallas_call | solution.py:55
  (120 shorter events, 34.8 us)
Async XLA Ops:
  4.1 17.9 %collective-permute-start.4 = (bf16[128,1280]{1,0:T(8,128)(2,1)}, bf16[128,1280]{1,0:T(8,128)(2,1)S(1)}, u32[]{:S(2)}, u32[]{:S(2)}) collective-permute-start(bf16[128,1280]{1,0:T(8,128)(2,1)} %get-tuple-element.125.refs_0_), channel_id=1, source_target_pairs={{0,2},{1,3},{2,0},{3,1},{4,6},{5,7},{6,4},{7,5},{8,10},{9,11},{10,... | collective-permute-start | bytes 983048 | tf_op jit(solution)/shard_map/ppermute | solution.py:91
  7.1 17.4 %collective-permute-start = (bf16[128,1280]{1,0:T(8,128)(2,1)}, bf16[128,1280]{1,0:T(8,128)(2,1)S(1)}, u32[]{:S(2)}, u32[]{:S(2)}) collective-permute-start(bf16[128,1280]{1,0:T(8,128)(2,1)} %get-tuple-element.125.refs_0_), channel_id=1, source_target_pairs={{0,4},{1,5},{2,6},{3,7},{4,0},{5,1},{6,2},{7,3},{8,12},{9,13},{10,... | collective-permute-start | bytes 983048 | tf_op jit(solution)/shard_map/ppermute | solution.py:91
  9.7 18.3 %collective-permute-start.3 = (bf16[128,1280]{1,0:T(8,128)(2,1)}, bf16[128,1280]{1,0:T(8,128)(2,1)S(1)}, u32[]{:S(2)}, u32[]{:S(2)}) collective-permute-start(bf16[128,1280]{1,0:T(8,128)(2,1)} %get-tuple-element.125.refs_0_), channel_id=1, source_target_pairs={{0,1},{1,0},{2,3},{3,2},{4,5},{5,4},{6,7},{7,6},{8,9},{9,8},{10,11... | collective-permute-start | bytes 983048 | tf_op jit(solution)/shard_map/ppermute | solution.py:91
  22.0 6.0 %collective-permute-start.5 = (bf16[128,1280]{1,0:T(8,128)(2,1)S(1)}, bf16[128,1280]{1,0:T(8,128)(2,1)S(1)}, u32[]{:S(2)}, u32[]{:S(2)}) collective-permute-start(bf16[128,1280]{1,0:T(8,128)(2,1)S(1)} %collective-permute-done.4.refs_2_), channel_id=1, source_target_pairs={{0,1},{1,0},{2,3},{3,2},{4,5},{5,4},{6,7},{7,6},{8,9},{9,8},{10,11... | collective-permute-start | bytes 983048 | tf_op jit(solution)/shard_map/ppermute | solution.py:91
  24.5 7.6 %collective-permute-start.2 = (bf16[128,1280]{1,0:T(8,128)(2,1)S(1)}, bf16[128,1280]{1,0:T(8,128)(2,1)S(1)}, u32[]{:S(2)}, u32[]{:S(2)}) collective-permute-start(bf16[128,1280]{1,0:T(8,128)(2,1)S(1)} %collective-permute-done.refs_0_), channel_id=1, source_target_pairs={{0,2},{1,3},{2,0},{3,1},{4,6},{5,7},{6,4},{7,5},{8,10},{9,11},{10,... | collective-permute-start | bytes 983048 | tf_op jit(solution)/shard_map/ppermute | solution.py:91
  27.4 7.9 %collective-permute-start.1 = (bf16[128,1280]{1,0:T(8,128)(2,1)S(1)}, bf16[128,1280]{1,0:T(8,128)(2,1)S(1)}, u32[]{:S(2)}, u32[]{:S(2)}) collective-permute-start(bf16[128,1280]{1,0:T(8,128)(2,1)S(1)} %collective-permute-done.refs_0_), channel_id=1, source_target_pairs={{0,1},{1,0},{2,3},{3,2},{4,5},{5,4},{6,7},{7,6},{8,9},{9,8},{10,11... | collective-permute-start | bytes 983048 | tf_op jit(solution)/shard_map/ppermute | solution.py:91
  32.1 14.8 %collective-permute-start.13 = (bf16[112,1280]{1,0:T(8,128)(2,1)S(1)}, bf16[112,1280]{1,0:T(8,128)(2,1)S(1)}, u32[]{:S(2)}, u32[]{:S(2)}) collective-permute-start(bf16[112,1280]{1,0:T(8,128)(2,1)S(1)} %copy-done.15), channel_id=1, source_target_pairs={{0,2},{1,3},{2,0},{3,1},{4,6},{5,7},{6,4},{7,5},{8,10},{9,11},{10,... | collective-permute-start | bytes 860168 | tf_op jit(solution)/shard_map/ppermute | solution.py:91
  33.5 18.5 %collective-permute-start.12 = (bf16[112,1280]{1,0:T(8,128)(2,1)S(1)}, bf16[112,1280]{1,0:T(8,128)(2,1)S(1)}, u32[]{:S(2)}, u32[]{:S(2)}) collective-permute-start(bf16[112,1280]{1,0:T(8,128)(2,1)S(1)} %copy-done.15), channel_id=1, source_target_pairs={{0,4},{1,5},{2,6},{3,7},{4,0},{5,1},{6,2},{7,3},{8,12},{9,13},{10,... | collective-permute-start | bytes 860168 | tf_op jit(solution)/shard_map/ppermute | solution.py:91
  39.9 12.1 %collective-permute-start.9 = (bf16[16,1280]{1,0:T(8,128)(2,1)S(1)}, bf16[16,1280]{1,0:T(8,128)(2,1)S(1)}, u32[]{:S(2)}, u32[]{:S(2)}) collective-permute-start(bf16[16,1280]{1,0:T(8,128)(2,1)S(1)} %get-tuple-element.138), channel_id=1, source_target_pairs={{0,2},{1,3},{2,0},{3,1},{4,6},{5,7},{6,4},{7,5},{8,10},{9,11},{10,... | collective-permute-start | bytes 122888 | tf_op jit(solution)/shard_map/ppermute | solution.py:91
  40.4 12.2 %collective-permute-start.10 = (bf16[16,1280]{1,0:T(8,128)(2,1)S(1)}, bf16[16,1280]{1,0:T(8,128)(2,1)S(1)}, u32[]{:S(2)}, u32[]{:S(2)}) collective-permute-start(bf16[16,1280]{1,0:T(8,128)(2,1)S(1)} %get-tuple-element.139), channel_id=1, source_target_pairs={{0,4},{1,5},{2,6},{3,7},{4,0},{5,1},{6,2},{7,3},{8,12},{9,13},{10,... | collective-permute-start | bytes 122888 | tf_op jit(solution)/shard_map/ppermute | solution.py:91
  41.7 10.9 %collective-permute-start.11 = (bf16[16,1280]{1,0:T(8,128)(2,1)S(1)}, bf16[16,1280]{1,0:T(8,128)(2,1)S(1)}, u32[]{:S(2)}, u32[]{:S(2)}) collective-permute-start(bf16[16,1280]{1,0:T(8,128)(2,1)S(1)} %get-tuple-element.140), channel_id=1, source_target_pairs={{0,6},{1,7},{2,4},{3,5},{4,2},{5,3},{6,0},{7,1},{8,14},{9,15},{10,... | collective-permute-start | bytes 122888 | tf_op jit(solution)/shard_map/ppermute | solution.py:91
  53.0 8.7 %collective-permute-start.14 = (bf16[4,2560]{1,0:T(4,128)(2,1)S(1)}, bf16[4,2560]{1,0:T(4,128)(2,1)S(1)}, u32[]{:S(2)}, u32[]{:S(2)}) collective-permute-start(bf16[4,2560]{1,0:T(4,128)(2,1)S(1)} %get-tuple-element.154), channel_id=1, source_target_pairs={{0,8},{8,0},{16,24},{24,16},{1,9},{9,1},{17,25},{25,17},{2,10},{10... | collective-permute-start | bytes 61448 | tf_op jit(solution)/shard_map/ppermute | solution.py:91
  54.5 7.1 %collective-permute-start.15 = (bf16[4,2560]{1,0:T(4,128)(2,1)S(1)}, bf16[4,2560]{1,0:T(4,128)(2,1)S(1)}, u32[]{:S(2)}, u32[]{:S(2)}) collective-permute-start(bf16[4,2560]{1,0:T(4,128)(2,1)S(1)} %get-tuple-element.155), channel_id=1, source_target_pairs={{0,16},{8,24},{16,0},{24,8},{1,17},{9,25},{17,1},{25,9},{2,18},{10... | collective-permute-start | bytes 61448 | tf_op jit(solution)/shard_map/ppermute | solution.py:91
  56.0 5.6 %collective-permute-start.16 = (bf16[4,2560]{1,0:T(4,128)(2,1)S(1)}, bf16[4,2560]{1,0:T(4,128)(2,1)S(1)}, u32[]{:S(2)}, u32[]{:S(2)}) collective-permute-start(bf16[4,2560]{1,0:T(4,128)(2,1)S(1)} %get-tuple-element.156), channel_id=1, source_target_pairs={{0,24},{8,16},{16,8},{24,0},{1,25},{9,17},{17,9},{25,1},{2,26},{10... | collective-permute-start | bytes 61448 | tf_op jit(solution)/shard_map/ppermute | solution.py:91
  56.5 6.9 %collective-permute-start.17 = (bf16[112,1280]{1,0:T(8,128)(2,1)S(1)}, bf16[112,1280]{1,0:T(8,128)(2,1)S(1)}, u32[]{:S(2)}, u32[]{:S(2)}) collective-permute-start(bf16[112,1280]{1,0:T(8,128)(2,1)S(1)} %collective-permute-done.12.refs_4_), channel_id=1, source_target_pairs={{0,2},{1,3},{2,0},{3,1},{4,6},{5,7},{6,4},{7,5},{8,10},{9,11},{10,... | collective-permute-start | bytes 860168 | tf_op jit(solution)/shard_map/ppermute | solution.py:91
  63.4 6.4 %collective-permute-start.23 = (bf16[16,2560]{1,0:T(8,128)(2,1)S(1)}, bf16[16,2560]{1,0:T(8,128)(2,1)S(1)}, u32[]{:S(2)}, u32[]{:S(2)}) collective-permute-start(bf16[16,2560]{1,0:T(8,128)(2,1)S(1)} %pad_maximum_fusion.refs_0_), channel_id=1, source_target_pairs={{0,6},{1,7},{2,4},{3,5},{4,2},{5,3},{6,0},{7,1},{8,14},{9,15},{10,... | collective-permute-start | bytes 245768 | tf_op jit(solution)/shard_map/ppermute | solution.py:91
  65.4 6.2 %collective-permute-start.21 = (bf16[16,2560]{1,0:T(8,128)(2,1)S(1)}, bf16[16,2560]{1,0:T(8,128)(2,1)S(1)}, u32[]{:S(2)}, u32[]{:S(2)}) collective-permute-start(bf16[16,2560]{1,0:T(8,128)(2,1)S(1)} %pad_maximum_fusion.refs_0_), channel_id=1, source_target_pairs={{0,4},{1,5},{2,6},{3,7},{4,0},{5,1},{6,2},{7,3},{8,12},{9,13},{10,... | collective-permute-start | bytes 245768 | tf_op jit(solution)/shard_map/ppermute | solution.py:91
  66.0 5.7 %collective-permute-start.19 = (bf16[16,2560]{1,0:T(8,128)(2,1)S(1)}, bf16[16,2560]{1,0:T(8,128)(2,1)S(1)}, u32[]{:S(2)}, u32[]{:S(2)}) collective-permute-start(bf16[16,2560]{1,0:T(8,128)(2,1)S(1)} %pad_maximum_fusion.refs_0_), channel_id=1, source_target_pairs={{0,2},{1,3},{2,0},{3,1},{4,6},{5,7},{6,4},{7,5},{8,10},{9,11},{10,... | collective-permute-start | bytes 245768 | tf_op jit(solution)/shard_map/ppermute | solution.py:91
  67.8 4.4 %collective-permute-start.18 = (bf16[16,2560]{1,0:T(8,128)(2,1)S(1)}, bf16[16,2560]{1,0:T(8,128)(2,1)S(1)}, u32[]{:S(2)}, u32[]{:S(2)}) collective-permute-start(bf16[16,2560]{1,0:T(8,128)(2,1)S(1)} %pad_maximum_fusion.refs_0_), channel_id=1, source_target_pairs={{0,1},{1,0},{2,3},{3,2},{4,5},{5,4},{6,7},{7,6},{8,9},{9,8},{10,11... | collective-permute-start | bytes 245768 | tf_op jit(solution)/shard_map/ppermute | solution.py:91
  77.7 6.0 %collective-permute-start.32 = (bf16[112,1280]{1,0:T(8,128)(2,1)S(1)}, bf16[112,1280]{1,0:T(8,128)(2,1)S(1)}, u32[]{:S(2)}, u32[]{:S(2)}) collective-permute-start(bf16[112,1280]{1,0:T(8,128)(2,1)S(1)} %collective-permute-done.17.refs_6_), channel_id=1, source_target_pairs={{0,1},{1,0},{2,3},{3,2},{4,5},{5,4},{6,7},{7,6},{8,9},{9,8},{10,11... | collective-permute-start | bytes 860168 | tf_op jit(solution)/shard_map/ppermute | solution.py:91
  79.3 11.6 %collective-permute-start.29 = (bf16[16,2560]{1,0:T(8,128)(2,1)S(1)}, bf16[16,2560]{1,0:T(8,128)(2,1)S(1)}, u32[]{:S(2)}, u32[]{:S(2)}) collective-permute-start(bf16[16,2560]{1,0:T(8,128)(2,1)S(1)} %get-tuple-element.168), channel_id=1, source_target_pairs={{0,2},{1,3},{2,0},{3,1},{4,6},{5,7},{6,4},{7,5},{8,10},{9,11},{10,... | collective-permute-start | bytes 245768 | tf_op jit(solution)/shard_map/ppermute | solution.py:91
  79.6 11.3 %collective-permute-start.30 = (bf16[16,2560]{1,0:T(8,128)(2,1)S(1)}, bf16[16,2560]{1,0:T(8,128)(2,1)S(1)}, u32[]{:S(2)}, u32[]{:S(2)}) collective-permute-start(bf16[16,2560]{1,0:T(8,128)(2,1)S(1)} %get-tuple-element.169), channel_id=1, source_target_pairs={{0,4},{1,5},{2,6},{3,7},{4,0},{5,1},{6,2},{7,3},{8,12},{9,13},{10,... | collective-permute-start | bytes 245768 | tf_op jit(solution)/shard_map/ppermute | solution.py:91
  82.2 8.7 %collective-permute-start.31 = (bf16[16,2560]{1,0:T(8,128)(2,1)S(1)}, bf16[16,2560]{1,0:T(8,128)(2,1)S(1)}, u32[]{:S(2)}, u32[]{:S(2)}) collective-permute-start(bf16[16,2560]{1,0:T(8,128)(2,1)S(1)} %get-tuple-element.170), channel_id=1, source_target_pairs={{0,6},{1,7},{2,4},{3,5},{4,2},{5,3},{6,0},{7,1},{8,14},{9,15},{10,... | collective-permute-start | bytes 245768 | tf_op jit(solution)/shard_map/ppermute | solution.py:91
  83.7 23.0 %collective-permute-start.36 = (bf16[224,1280]{1,0:T(8,128)(2,1)S(1)}, bf16[224,1280]{1,0:T(8,128)(2,1)S(1)}, u32[]{:S(2)}, u32[]{:S(2)}) collective-permute-start(bf16[224,1280]{1,0:T(8,128)(2,1)S(1)} %get-tuple-element.189), channel_id=1, source_target_pairs={{0,2},{1,3},{2,0},{3,1},{4,6},{5,7},{6,4},{7,5},{8,10},{9,11},{10,... | collective-permute-start | bytes 1720328 | tf_op jit(solution)/shard_map/ppermute | solution.py:91
  94.1 4.7 %collective-permute-start.35 = (bf16[4,2560]{1,0:T(4,128)(2,1)S(1)}, bf16[4,2560]{1,0:T(4,128)(2,1)S(1)}, u32[]{:S(2)}, u32[]{:S(2)}) collective-permute-start(bf16[4,2560]{1,0:T(4,128)(2,1)S(1)} %get-tuple-element.182), channel_id=1, source_target_pairs={{0,24},{8,16},{16,8},{24,0},{1,25},{9,17},{17,9},{25,1},{2,26},{10... | collective-permute-start | bytes 61448 | tf_op jit(solution)/shard_map/ppermute | solution.py:91
  99.0 5.9 %collective-permute-start.43 = (bf16[16,1280]{1,0:T(8,128)(2,1)S(1)}, bf16[16,1280]{1,0:T(8,128)(2,1)S(1)}, u32[]{:S(2)}, u32[]{:S(2)}) collective-permute-start(bf16[16,1280]{1,0:T(8,128)(2,1)S(1)} %get-tuple-element.204.refs_0_), channel_id=1, source_target_pairs={{0,6},{1,7},{2,4},{3,5},{4,2},{5,3},{6,0},{7,1},{8,14},{9,15},{10,... | collective-permute-start | bytes 122888 | tf_op jit(solution)/shard_map/ppermute | solution.py:91
  101.4 4.9 %collective-permute-start.41 = (bf16[16,1280]{1,0:T(8,128)(2,1)S(1)}, bf16[16,1280]{1,0:T(8,128)(2,1)S(1)}, u32[]{:S(2)}, u32[]{:S(2)}) collective-permute-start(bf16[16,1280]{1,0:T(8,128)(2,1)S(1)} %get-tuple-element.204.refs_0_), channel_id=1, source_target_pairs={{0,4},{1,5},{2,6},{3,7},{4,0},{5,1},{6,2},{7,3},{8,12},{9,13},{10,... | collective-permute-start | bytes 122888 | tf_op jit(solution)/shard_map/ppermute | solution.py:91
  111.1 11.6 %collective-permute-start.45 = (bf16[320,640]{1,0:T(8,128)(2,1)S(1)}, bf16[320,640]{1,0:T(8,128)(2,1)S(1)}, u32[]{:S(2)}, u32[]{:S(2)}) collective-permute-start(bf16[320,640]{1,0:T(8,128)(2,1)S(1)} %get-tuple-element.218), channel_id=1, source_target_pairs={{0,8},{8,0},{16,24},{24,16},{1,9},{9,1},{17,25},{25,17},{2,10},{10... | collective-permute-start | bytes 1228808 | tf_op jit(solution)/shard_map/ppermute | solution.py:91
  111.8 11.2 %collective-permute-start.46 = (bf16[320,640]{1,0:T(8,128)(2,1)S(1)}, bf16[320,640]{1,0:T(8,128)(2,1)S(1)}, u32[]{:S(2)}, u32[]{:S(2)}) collective-permute-start(bf16[320,640]{1,0:T(8,128)(2,1)S(1)} %get-tuple-element.219), channel_id=1, source_target_pairs={{0,16},{8,24},{16,0},{24,8},{1,17},{9,25},{17,1},{25,9},{2,18},{10... | collective-permute-start | bytes 1228808 | tf_op jit(solution)/shard_map/ppermute | solution.py:91
  112.2 15.4 %collective-permute-start.37 = (bf16[112,1280]{1,0:T(8,128)(2,1)S(1)}, bf16[112,1280]{1,0:T(8,128)(2,1)S(1)}, u32[]{:S(2)}, u32[]{:S(2)}) collective-permute-start(bf16[112,1280]{1,0:T(8,128)(2,1)S(1)} %get-tuple-element.191), channel_id=1, source_target_pairs={{0,4},{1,5},{2,6},{3,7},{4,0},{5,1},{6,2},{7,3},{8,12},{9,13},{10,... | collective-permute-start | bytes 860168 | tf_op jit(solution)/shard_map/ppermute | solution.py:91
  123.2 6.1 %collective-permute-start.48 = (bf16[160,640]{1,0:T(8,128)(2,1)S(1)}, bf16[160,640]{1,0:T(8,128)(2,1)S(1)}, u32[]{:S(2)}, u32[]{:S(2)}) collective-permute-start(bf16[160,640]{1,0:T(8,128)(2,1)S(1)} %get-tuple-element.232), channel_id=1, source_target_pairs={{0,8},{8,0},{16,24},{24,16},{1,9},{9,1},{17,25},{25,17},{2,10},{10... | collective-permute-start | bytes 614408 | tf_op jit(solution)/shard_map/ppermute | solution.py:91
  124.7 5.8 %collective-permute-start.47 = (bf16[160,640]{1,0:T(8,128)(2,1)S(1)}, bf16[160,640]{1,0:T(8,128)(2,1)S(1)}, u32[]{:S(2)}, u32[]{:S(2)}) collective-permute-start(bf16[160,640]{1,0:T(8,128)(2,1)S(1)} %get-tuple-element.228), channel_id=1, source_target_pairs={{0,16},{8,24},{16,0},{24,8},{1,17},{9,25},{17,1},{25,9},{2,18},{10... | collective-permute-start | bytes 614408 | tf_op jit(solution)/shard_map/ppermute | solution.py:91
  (33 other events, 259.6 us)
